TPU v7x, 32 devices: a whole 2x2x4 slice. The times are simulated.
32 devices in a mesh: groups: 2 (over y), rows: 16 (over z, x, core).
Axes of the slice: x: 2, y: 2, z: 4, core: 2. Of those that a mesh axis runs over, the one named last changes fastest.
Arguments:
- grad: bfloat16 [12288, 2880], P(('groups', 'rows')), parts along dimension 0, may hold values from -40 to 40
- moment: bfloat16 [12288, 2880], P(('groups', 'rows')), parts along dimension 0, may hold values from -6 to 6
- second: float32 [12288, 64], P(('groups', 'rows')), parts along dimension 0, may hold values from 0.05 to 2
- basis: bfloat16 [128, 2880], P(('groups', 'rows')), parts along dimension 0, may hold values from -0.109375 to 0.109375
Outputs:
- update: bfloat16 [12288, 2880], P(('groups', 'rows')), parts along dimension 0
- moment_next: bfloat16 [12288, 2880], P(('groups', 'rows')), parts along dimension 0
- second_next: float32 [12288, 64], P(('groups', 'rows')), parts along dimension 0
- basis_next: float32 [128, 2880], P(('groups', 'rows')), parts along dimension 0
There are 2 independent parts, one for each index of `groups`. A program takes and returns all parts, laid end to end along the dimension named above; each array names one. Nothing has to cross between parts.
All inputs are finite; a program needn't handle non-finite values.
Results may differ from a plain program's by a relative error of at most 0.0065.
Values may be sent and summed in bfloat16 or wider, within the bound.
No kernel may reach another device: no remote copies, remote signals or barrier semaphores. Data moves between devices by JAX's collectives and lax.ppermute only.
A program may use at most 128 MiB of HBM per device.

v0:
```python
import jax
import jax.numpy as jnp
from jax import lax
from jax.sharding import PartitionSpec as P


def shards(grad, moment, second, basis):
    moment_next = (0.9 * moment.astype(jnp.float32) + 0.1 * grad.astype(jnp.float32)).astype(
        jnp.bfloat16
    )
    local_rows = grad.shape[0]
    own_count = basis.shape[0]
    stacked = jnp.concatenate([grad, moment_next], 0)
    whole_basis = lax.all_gather(basis, "rows", axis=0, tiled=True)
    rotated = lax.dot_general(
        stacked, whole_basis, (((1,), (1,)), ((), ())), preferred_element_type=jnp.float32
    )
    rot_grad = rotated[:local_rows]
    rot_moment = rotated[local_rows:]
    rot_rounded = rot_grad.astype(jnp.bfloat16)
    second_next = 0.95 * second + 0.05 * rot_grad * rot_grad
    scaled = (rot_moment / (jnp.sqrt(second_next) + 1e-08)).astype(jnp.bfloat16)
    back = jnp.dot(scaled, whole_basis, preferred_element_type=jnp.float32)
    update, second_next = (back.astype(jnp.bfloat16), second_next)
    partial_value = lax.dot_general(
        rot_rounded, grad, (((0,), (0,)), ((), ())), preferred_element_type=jnp.float32
    )
    summed = lax.psum(partial_value, "rows")
    offset = lax.axis_index("rows") * own_count
    power = lax.dynamic_slice_in_dim(summed, offset, own_count, 0)
    basis_next = power / jnp.sqrt(jnp.mean(power * power, axis=1, keepdims=True) + 1e-06)
    return (update, moment_next, second_next, basis_next)


def solution(mesh):
    placed = (
        P(("groups", "rows"), None),
        P(("groups", "rows"), None),
        P(("groups", "rows"), None),
        P(("groups", "rows"), None),
    )
    return jax.shard_map(
        shards,
        mesh=mesh,
        in_specs=placed,
        out_specs=(
            P(("groups", "rows"), None),
            P(("groups", "rows"), None),
            P(("groups", "rows"), None),
            P(("groups", "rows"), None),
        ),
        check_vma=False,
    )
```

profile of v0, /device:TPU:0, one launch (start us, length us, event | category | flops | bytes accessed | tf_op | source)
XLA Modules:
  0.0 136.4 jit_solution(13591645299343601200)
XLA Ops:
  7.2 0.0 all-reduce.2.cloned.1.call-start
  7.2 24.3 %all-gather = bf16[16,4,2880]{2,1,0:T(4,128)(2,1)S(1)} all-gather(bf16[1,4,2880]{2,1,0:T(4,128)(2,1)} %bitcast.4), channel_id=1, replica_groups=mesh['groups'=2,'rows'=16] {'rows'}, dimensions={0}, use_global_device_ids=true | all-gather | bytes 391680 | tf_op jit(solution)/shard_map/all_gather | solution.py:14
  31.6 0.2 reshape.17
  31.7 0.0 copy-start
  31.7 3.3 %add_convert_fusion = bf16[384,2880]{0,1:T(8,128)(2,1)S(1)} fusion(bf16[384,2880]{0,1:T(8,128)(2,1)} %param.4, bf16[384,2880]{0,1:T(8,128)(2,1)} %param.5), kind=kLoop, calls=%fused_computation.4 | loop fusion | flops 6635520 | bytes 6635520 | tf_op jit(solution)/shard_map/convert_element_type | solution.py:8
  35.1 0.0 copy-done
  35.1 0.0 copy-start.1
  35.1 0.8 fusion
  35.9 0.6 copy-done.1
  36.4 0.0 copy-start.3
  36.4 1.7 %fusion.6 = f32[64,2880]{1,0:T(8,128)} fusion(bf16[384,2880]{0,1:T(8,128)(2,1)S(1)} %copy-done, f32[768,64]{0,1:T(8,128)S(1)} %fusion), kind=kOutput, calls=%fused_computation.11 | convolution fusion | flops 141557760 | bytes 2998272 | tf_op jit(solution)/shard_map/dot_general | solution.py:25
  38.1 0.0 all-reduce.2.cloned.1.call-update
  38.1 0.0 copy-done.3
  38.2 0.0 copy-start.2
  38.2 2.2 %convolution_convert_fusion = bf16[384,2880]{0,1:T(8,128)(2,1)} fusion(bf16[64,2880]{1,0:T(8,128)(2,1)S(1)} %reshape.17, f32[768,64]{0,1:T(8,128)S(1)} %fusion, f32[384,64]{0,1:T(8,128)S(1)} %fusion.4), kind=kOutput, calls=%fused_computation.5 | convolution fusion | flops 142737408 | bytes 2785280 | tf_op jit(solution)/shard_map/dot_general | solution.py:23
  40.4 86.5 %all-reduce.2.cloned.1.call-done = f32[64,2880]{1,0:T(8,128)} async-done(((f32[64,2880]{1,0:T(8,128)}), f32[64,2880]{1,0:T(8,128)}) %all-reduce.2.cloned.1.call-update) | async-done | bytes 737296 | tf_op jit(solution)/shard_map/psum | solution.py:28
  126.9 1.0 multiply_reduce_fusion
  127.9 1.6 %dynamic-slice_divide_fusion = f32[4,2880]{1,0:T(4,128)} fusion(f32[64,2880]{1,0:T(8,128)} %all-reduce.2.cloned.1.call-done, s32[]{:T(128)S(6)} %select_n.3, f32[4]{0:T(128)S(1)} %add_sqrt_fusion), kind=kLoop, calls=%fused_computation.14 | loop fusion | flops 11520 | bytes 92180 | tf_op jit(solution)/shard_map/div | solution.py:31
  129.5 0.0 copy-done.2
  (2 shorter events, 0.0 us)
Async XLA Ops:
  7.2 119.7 %all-reduce.2.cloned.1.call-start = ((), (), s32[]{:S(2)}) async-start(), calls=%async_computation | async-start | bytes 1507328 | tf_op jit(solution)/shard_map/psum | solution.py:28
  31.7 3.3 %copy-start = (bf16[384,2880]{0,1:T(8,128)(2,1)S(1)}, bf16[384,2880]{0,1:T(8,128)(2,1)}, u32[]{:S(2)}) copy-start(bf16[384,2880]{0,1:T(8,128)(2,1)} %param.4) | copy-start | bytes 6635524
  35.1 1.4 copy-start.1
  36.4 1.7 %copy-start.3 = (f32[384,64]{0,1:T(8,128)S(1)}, f32[384,64]{0,1:T(8,128)}, u32[]{:S(2)}) copy-start(f32[384,64]{0,1:T(8,128)} %param.6) | copy-start | bytes 294916
  38.2 91.3 %copy-start.2 = (f32[384,64]{0,1:T(8,128)}, f32[384,64]{0,1:T(8,128)S(1)}, u32[]{:S(2)}) copy-start(f32[384,64]{0,1:T(8,128)S(1)} %fusion.4) | copy-start | bytes 294916
Sparse Core Ops, SparseCore 0:
  38.3 88.5 all-reduce.1
where the time goes:
time: 137 us; the launch traced here: 136 us
  waiting for transfers between devices  86.5 us (63%)
  blocking collectives  24.3 us (18%)
  between operations  14.1 us (10%)
  other arithmetic  5.99 us (4%)
  matrix products  4.61 us (3%)
    psum x1, waiting for transfers between devices, shards(): summed = lax.psum(partial_value, 'rows')  86.5 us
    all_gather x1, blocking collectives, shards(): whole_basis = lax.all_gather(basis, 'rows', axis=0, tiled=True)  24.3 us
    convert_element_type x1, other arithmetic, shards(): (0.9 * moment.astype(jnp.float32) + 0.1 * grad.astype(jnp.float32)).astyp...  3.33 us
  transfers between devices with their start and end apart: 1, of which 1 were waited for; matrix products, arithmetic and copies ran while one was open for 2% of the time, Pallas kernels for 0%

commit v1 on v0

v1 whole, which is shorter than its diff:
```python
import jax
import jax.numpy as jnp
from jax import lax
from jax.sharding import PartitionSpec as P


def shards(n, grad, moment, second, basis):
    bits = n.bit_length() - 1
    me = lax.axis_index("rows")
    own = basis.shape[0]
    rows, depth = grad.shape

    def exchange(value, bit):
        return lax.ppermute(value, "rows", [(i, i ^ (1 << bit)) for i in range(n)])

    def reorder(value):
        value = value.reshape((2,) * bits + (own, rows))
        for bit in range(bits):
            axis = bits - 1 - bit
            value = jnp.where((me >> bit) & 1, jnp.flip(value, axis), value)
        return value

    held = basis
    for bit in reversed(range(bits)):
        held = jnp.concatenate([held, exchange(held, bit)], 0)

    moment_next = (0.9 * moment.astype(jnp.float32) + 0.1 * grad.astype(jnp.float32)).astype(
        jnp.bfloat16
    )
    rot_grad = lax.dot_general(
        held, grad, (((1,), (1,)), ((), ())), preferred_element_type=jnp.float32
    )
    partial = jnp.dot(rot_grad.astype(jnp.bfloat16), grad, preferred_element_type=jnp.float32)
    for bit in range(bits):
        half = partial.shape[0] // 2
        partial = partial[:half] + exchange(partial[half:].astype(jnp.bfloat16), bit).astype(
            jnp.float32
        )
    basis_next = partial / jnp.sqrt(jnp.mean(partial * partial, axis=1, keepdims=True) + 1e-06)

    rot_moment = lax.dot_general(
        held, moment_next, (((1,), (1,)), ((), ())), preferred_element_type=jnp.float32
    )
    turn = tuple(reversed(range(bits))) + (bits, bits + 1)
    mine = reorder(second.T).transpose(turn).reshape(n * own, rows)
    mine = 0.95 * mine + 0.05 * rot_grad * rot_grad
    scaled = (rot_moment / (jnp.sqrt(mine) + 1e-08)).astype(jnp.bfloat16)
    update = lax.dot_general(
        scaled, held, (((0,), (0,)), ((), ())), preferred_element_type=jnp.float32
    ).astype(jnp.bfloat16)
    back = mine.reshape((2,) * bits + (own, rows)).transpose(turn)
    second_next = reorder(back).reshape(n * own, rows).T
    return update, moment_next, second_next, basis_next


def solution(mesh):
    n = mesh.shape["rows"]
    placed = P(("groups", "rows"), None)
    return jax.shard_map(
        lambda *arrays: shards(n, *arrays),
        mesh=mesh,
        in_specs=(placed,) * 4,
        out_specs=(placed,) * 4,
        check_vma=False,
    )
```

time: 137 us -> 42 us (0.31)
  waiting for transfers between devices: 86.5 us -> 16.7 us
  blocking collectives: 24.3 us -> 0 us
  between operations: 14.1 us -> 0.83 us
  starting transfers between devices: 0.04 us -> 10.9 us
    psum x1 -> x0, waiting for transfers between devices: 86.5 us -> none  [shards(): summed = lax.psum(partial_value, 'rows')]
    all_gather x1 -> x0, blocking collectives: 24.3 us -> none  [shards(): whole_basis = lax.all_gather(basis, 'rows', axis=0, tiled=True)]
    ppermute x0 -> x8, waiting for transfers between devices: none -> 16.7 us  [exchange(): return lax.ppermute(value, 'rows', [(i, i ^ 1 << bit) for i in range(n)])]
    ppermute x0 -> x8, starting transfers between devices: none -> 10.9 us  [exchange(): return lax.ppermute(value, 'rows', [(i, i ^ 1 << bit) for i in range(n)])]
    reshape x0 -> x4, local copies, waits for them, and re-layouts: none -> 1.64 us  [the longest x2 0.93 us: reorder(): value = value.reshape((2,) * bits + (own, rows))]
  transfers between devices with their start and end apart: 1 -> 8, of which waited for: 1 -> 6; matrix products, arithmetic and copies ran while one was open for 2% -> 26% of each run, Pallas kernels for 0% -> 0%
where the time goes in v1:
time: 42 us; the launch traced here: 41.8 us
  waiting for transfers between devices  16.7 us (40%)
  starting transfers between devices  10.9 us (26%)
  other arithmetic  5.75 us (14%)
  matrix products  5.63 us (13%)
  local copies, waits for them, and re-layouts  1.92 us (5%)
  between operations  0.83 us (2%)
    ppermute x8, waiting for transfers between devices, exchange(): return lax.ppermute(value, 'rows', [(i, i ^ 1 << bit) for i in range(n)])  16.7 us
    ppermute x8, starting transfers between devices, exchange(): return lax.ppermute(value, 'rows', [(i, i ^ 1 << bit) for i in range(n)])  10.9 us
    convert_element_type x1, other arithmetic, shards(): (0.9 * moment.astype(jnp.float32) + 0.1 * grad.astype(jnp.float32)).astyp...  4.54 us
    dot_general x1, matrix products, shards(): lax.dot_general(scaled, held, (((0,), (0,)), ((), ())), preferred_element...  4.37 us
    reshape x2, local copies, waits for them, and re-layouts, reorder(): value = value.reshape((2,) * bits + (own, rows))  0.93 us
  transfers between devices with their start and end apart: 8, of which 6 were waited for; matrix products, arithmetic and copies ran while one was open for 26% of the time, Pallas kernels for 0%

profile of v1, /device:TPU:0, one launch (start us, length us, event | category | flops | bytes accessed | tf_op | source)
XLA Modules:
  0.0 41.8 jit_solution(11028094983918775216)
XLA Ops:
  0.6 4.1 %collective-permute-start = (bf16[4,2880]{1,0:T(4,128)(2,1)}, bf16[4,2880]{1,0:T(4,128)(2,1)S(1)}, u32[]{:S(2)}, u32[]{:S(2)}) collective-permute-start(bf16[4,2880]{1,0:T(4,128)(2,1)} %param.7), channel_id=1, source_target_pairs={{0,8},{1,9},{2,10},{3,11},{4,12},{5,13},{6,14},{7,15},{8,0},{9,1},... | collective-permute-start | bytes 69128 | tf_op jit(solution)/shard_map/ppermute | solution.py:14
  4.7 0.9 %reshape.28 = f32[2,2,2,2,4,384]{5,4,3,2,1,0:T(4,128)S(1)} reshape(f32[64,384]{1,0:T(8,128)} %bitcast.13) | data formatting | bytes 196608 | tf_op jit(solution)/shard_map/reshape | solution.py:17
  5.7 0.0 copy-start.1
  5.7 4.5 %add_convert_fusion = bf16[384,2880]{0,1:T(8,128)(2,1)} fusion(bf16[384,2880]{0,1:T(8,128)(2,1)} %param.4, bf16[384,2880]{0,1:T(8,128)(2,1)} %param.5), kind=kLoop, calls=%fused_computation | loop fusion | flops 6635520 | bytes 6635520 | tf_op jit(solution)/shard_map/convert_element_type | solution.py:27
  10.2 0.0 copy-start
  10.3 0.0 collective-permute-done
  10.3 0.0 copy-done.1
  10.3 1.6 %collective-permute-start.1 = (bf16[8,2880]{1,0:T(8,128)(2,1)S(1)}, bf16[8,2880]{1,0:T(8,128)(2,1)S(1)}, u32[]{:S(2)}, u32[]{:S(2)}) collective-permute-start(bf16[8,2880]{1,0:T(8,128)(2,1)S(1)} %pad_maximum_fusion.2), channel_id=1, source_target_pairs={{0,4},{1,5},{2,6},{3,7},{4,0},{5,1},{6,2},{7,3},{8,12},{9,13},{10,... | collective-permute-start | bytes 138248 | tf_op jit(solution)/shard_map/ppermute | solution.py:14
  12.0 2.5 %collective-permute-done.1 = bf16[8,2880]{1,0:T(8,128)(2,1)S(1)} collective-permute-done((bf16[8,2880]{1,0:T(8,128)(2,1)S(1)}, bf16[8,2880]{1,0:T(8,128)(2,1)S(1)}, u32[]{:S(2)}, u32[]{:S(2)}) %collective-permute-start.1) | collective-permute-done | bytes 46112 | tf_op jit(solution)/shard_map/ppermute | solution.py:14
  14.5 1.6 %collective-permute-start.2 = (bf16[16,2880]{1,0:T(8,128)(2,1)S(1)}, bf16[16,2880]{1,0:T(8,128)(2,1)S(1)}, u32[]{:S(2)}, u32[]{:S(2)}) collective-permute-start(bf16[16,2880]{1,0:T(8,128)(2,1)S(1)} %pad_maximum_fusion.1), channel_id=1, source_target_pairs={{0,2},{1,3},{2,0},{3,1},{4,6},{5,7},{6,4},{7,5},{8,10},{9,11},{10,... | collective-permute-start | bytes 276488 | tf_op jit(solution)/shard_map/ppermute | solution.py:14
  16.1 3.1 %collective-permute-done.2 = bf16[16,2880]{1,0:T(8,128)(2,1)S(1)} collective-permute-done((bf16[16,2880]{1,0:T(8,128)(2,1)S(1)}, bf16[16,2880]{1,0:T(8,128)(2,1)S(1)}, u32[]{:S(2)}, u32[]{:S(2)}) %collective-permute-start.2) | collective-permute-done | bytes 92192 | tf_op jit(solution)/shard_map/ppermute | solution.py:14
  19.2 0.1 collective-permute-start.3
  19.3 1.3 %collective-permute-done.3 = bf16[32,2880]{1,0:T(8,128)(2,1)S(1)} collective-permute-done((bf16[32,2880]{1,0:T(8,128)(2,1)S(1)}, bf16[32,2880]{1,0:T(8,128)(2,1)S(1)}, u32[]{:S(2)}, u32[]{:S(2)}) %collective-permute-start.3) | collective-permute-done | bytes 184352 | tf_op jit(solution)/shard_map/ppermute | solution.py:14
  20.7 0.2 concatenate.18
  20.9 0.0 copy-done
  20.9 0.5 %fusion.3 = (f32[64,384]{1,0:T(8,128)S(1)}, bf16[64,384]{1,0:T(8,128)(2,1)S(1)}) fusion(f32[64,384]{1,0:T(8,128)S(1)} %mul.43, bf16[64,2880]{1,0:T(8,128)(2,1)S(1)} %concatenate.18, bf16[384,2880]{0,1:T(8,128)(2,1)S(1)} %copy-done), kind=kOutput, calls=%fused_computation.20 | convolution fusion | flops 141656064 | bytes 2826240 | tf_op jit(solution)/shard_map/dot_general | solution.py:30
  21.3 0.8 %fusion.6 = f32[64,2880]{1,0:T(8,128)S(1)} fusion(bf16[384,2880]{0,1:T(8,128)(2,1)S(1)} %copy-done, bf16[64,384]{1,0:T(8,128)(2,1)S(1)} %get-tuple-element.5), kind=kOutput, calls=%fused_computation.26 | convolution fusion | flops 141557760 | bytes 2998272 | tf_op jit(solution)/shard_map/dot_general | solution.py:33
  22.2 0.2 collective-permute-start.4
  22.4 4.4 %convolution_convert_fusion = bf16[384,2880]{0,1:T(8,128)(2,1)} fusion(bf16[64,2880]{1,0:T(8,128)(2,1)S(1)} %concatenate.18, bf16[384,2880]{0,1:T(8,128)(2,1)} %add_convert_fusion, f32[64,384]{1,0:T(8,128)S(1)} %get-tuple-element.4), kind=kOutput, calls=%fused_computation.1 | convolution fusion | flops 284295168 | bytes 4890624 | tf_op jit(solution)/shard_map/dot_general | solution.py:48
  26.8 0.0 collective-permute-done.4
  26.9 1.6 %collective-permute-start.5 = (bf16[16,2880]{1,0:T(8,128)(2,1)S(1)}, bf16[16,2880]{1,0:T(8,128)(2,1)S(1)}, u32[]{:S(2)}, u32[]{:S(2)}) collective-permute-start(bf16[16,2880]{1,0:T(8,128)(2,1)S(1)} %slice.57), channel_id=1, source_target_pairs={{0,2},{1,3},{2,0},{3,1},{4,6},{5,7},{6,4},{7,5},{8,10},{9,11},{10,... | collective-permute-start | bytes 276488 | tf_op jit(solution)/shard_map/ppermute | solution.py:14
  28.5 3.5 %collective-permute-done.5 = bf16[16,2880]{1,0:T(8,128)(2,1)S(1)} collective-permute-done((bf16[16,2880]{1,0:T(8,128)(2,1)S(1)}, bf16[16,2880]{1,0:T(8,128)(2,1)S(1)}, u32[]{:S(2)}, u32[]{:S(2)}) %collective-permute-start.5) | collective-permute-done | bytes 92192 | tf_op jit(solution)/shard_map/ppermute | solution.py:14
  32.0 1.6 %collective-permute-start.6 = (bf16[8,2880]{1,0:T(8,128)(2,1)S(1)}, bf16[8,2880]{1,0:T(8,128)(2,1)S(1)}, u32[]{:S(2)}, u32[]{:S(2)}) collective-permute-start(bf16[8,2880]{1,0:T(8,128)(2,1)S(1)} %slice.58), channel_id=1, source_target_pairs={{0,4},{1,5},{2,6},{3,7},{4,0},{5,1},{6,2},{7,3},{8,12},{9,13},{10,... | collective-permute-start | bytes 138248 | tf_op jit(solution)/shard_map/ppermute | solution.py:14
  33.6 2.5 %collective-permute-done.6 = bf16[8,2880]{1,0:T(8,128)(2,1)S(1)} collective-permute-done((bf16[8,2880]{1,0:T(8,128)(2,1)S(1)}, bf16[8,2880]{1,0:T(8,128)(2,1)S(1)}, u32[]{:S(2)}, u32[]{:S(2)}) %collective-permute-start.6) | collective-permute-done | bytes 46112 | tf_op jit(solution)/shard_map/ppermute | solution.py:14
  36.1 0.2 collective-permute-start.7
  36.3 0.7 %reshape.30 = f32[64,384]{1,0:T(8,128)} reshape(f32[2,2,2,2,4,384]{5,4,3,2,1,0:T(4,128)S(1)} %copy.10) | data formatting | bytes 196608 | tf_op jit(solution)/shard_map/reshape | solution.py:52
  37.0 3.9 %collective-permute-done.7 = bf16[4,2880]{1,0:T(4,128)(2,1)S(1)} collective-permute-done((bf16[4,2880]{1,0:T(4,128)(2,1)S(1)}, bf16[4,2880]{1,0:T(4,128)(2,1)S(1)}, u32[]{:S(2)}, u32[]{:S(2)}) %collective-permute-start.7) | collective-permute-done | bytes 23072 | tf_op jit(solution)/shard_map/ppermute | solution.py:14
  40.9 0.1 multiply_reduce_fusion
  41.1 0.7 %fusion.9 = f32[4,2880]{1,0:T(4,128)} fusion(bf16[4,2880]{1,0:T(4,128)(2,1)S(1)} %collective-permute-done.7, f32[8,2880]{1,0:T(8,128)S(1)} %slice_add_fusion.2, f32[4]{0:T(128)S(1)} %add_sqrt_fusion), kind=kLoop, calls=%fused_computation.33 | loop fusion | flops 34560 | bytes 115216 | tf_op jit(solution)/shard_map/div | solution.py:39
  (23 shorter events, 0.5 us)
Async XLA Ops:
  0.6 9.6 %collective-permute-start = (bf16[4,2880]{1,0:T(4,128)(2,1)}, bf16[4,2880]{1,0:T(4,128)(2,1)S(1)}, u32[]{:S(2)}, u32[]{:S(2)}) collective-permute-start(bf16[4,2880]{1,0:T(4,128)(2,1)} %param.7), channel_id=1, source_target_pairs={{0,8},{1,9},{2,10},{3,11},{4,12},{5,13},{6,14},{7,15},{8,0},{9,1},... | collective-permute-start | bytes 69128 | tf_op jit(solution)/shard_map/ppermute | solution.py:14
  5.7 4.6 %copy-start.1 = (bf16[4,2880]{1,0:T(4,128)(2,1)S(1)}, bf16[4,2880]{1,0:T(4,128)(2,1)}, u32[]{:S(2)}) copy-start(bf16[4,2880]{1,0:T(4,128)(2,1)} %param.7) | copy-start | bytes 69124
  10.2 10.6 %copy-start = (bf16[384,2880]{0,1:T(8,128)(2,1)S(1)}, bf16[384,2880]{0,1:T(8,128)(2,1)}, u32[]{:S(2)}) copy-start(bf16[384,2880]{0,1:T(8,128)(2,1)} %param.4) | copy-start | bytes 6635524
  10.3 4.1 %collective-permute-start.1 = (bf16[8,2880]{1,0:T(8,128)(2,1)S(1)}, bf16[8,2880]{1,0:T(8,128)(2,1)S(1)}, u32[]{:S(2)}, u32[]{:S(2)}) collective-permute-start(bf16[8,2880]{1,0:T(8,128)(2,1)S(1)} %pad_maximum_fusion.2), channel_id=1, source_target_pairs={{0,4},{1,5},{2,6},{3,7},{4,0},{5,1},{6,2},{7,3},{8,12},{9,13},{10,... | collective-permute-start | bytes 138248 | tf_op jit(solution)/shard_map/ppermute | solution.py:14
  14.5 4.6 %collective-permute-start.2 = (bf16[16,2880]{1,0:T(8,128)(2,1)S(1)}, bf16[16,2880]{1,0:T(8,128)(2,1)S(1)}, u32[]{:S(2)}, u32[]{:S(2)}) collective-permute-start(bf16[16,2880]{1,0:T(8,128)(2,1)S(1)} %pad_maximum_fusion.1), channel_id=1, source_target_pairs={{0,2},{1,3},{2,0},{3,1},{4,6},{5,7},{6,4},{7,5},{8,10},{9,11},{10,... | collective-permute-start | bytes 276488 | tf_op jit(solution)/shard_map/ppermute | solution.py:14
  19.2 1.5 %collective-permute-start.3 = (bf16[32,2880]{1,0:T(8,128)(2,1)S(1)}, bf16[32,2880]{1,0:T(8,128)(2,1)S(1)}, u32[]{:S(2)}, u32[]{:S(2)}) collective-permute-start(bf16[32,2880]{1,0:T(8,128)(2,1)S(1)} %pad_maximum_fusion), channel_id=1, source_target_pairs={{0,1},{1,0},{2,3},{3,2},{4,5},{5,4},{6,7},{7,6},{8,9},{9,8},{10,11... | collective-permute-start | bytes 552968 | tf_op jit(solution)/shard_map/ppermute | solution.py:14
  22.2 4.6 %collective-permute-start.4 = (bf16[32,2880]{1,0:T(8,128)(2,1)S(1)}, bf16[32,2880]{1,0:T(8,128)(2,1)S(1)}, u32[]{:S(2)}, u32[]{:S(2)}) collective-permute-start(bf16[32,2880]{1,0:T(8,128)(2,1)S(1)} %slice.56), channel_id=1, source_target_pairs={{0,1},{1,0},{2,3},{3,2},{4,5},{5,4},{6,7},{7,6},{8,9},{9,8},{10,11... | collective-permute-start | bytes 552968 | tf_op jit(solution)/shard_map/ppermute | solution.py:14
  26.9 5.0 %collective-permute-start.5 = (bf16[16,2880]{1,0:T(8,128)(2,1)S(1)}, bf16[16,2880]{1,0:T(8,128)(2,1)S(1)}, u32[]{:S(2)}, u32[]{:S(2)}) collective-permute-start(bf16[16,2880]{1,0:T(8,128)(2,1)S(1)} %slice.57), channel_id=1, source_target_pairs={{0,2},{1,3},{2,0},{3,1},{4,6},{5,7},{6,4},{7,5},{8,10},{9,11},{10,... | collective-permute-start | bytes 276488 | tf_op jit(solution)/shard_map/ppermute | solution.py:14
  32.0 4.1 %collective-permute-start.6 = (bf16[8,2880]{1,0:T(8,128)(2,1)S(1)}, bf16[8,2880]{1,0:T(8,128)(2,1)S(1)}, u32[]{:S(2)}, u32[]{:S(2)}) collective-permute-start(bf16[8,2880]{1,0:T(8,128)(2,1)S(1)} %slice.58), channel_id=1, source_target_pairs={{0,4},{1,5},{2,6},{3,7},{4,0},{5,1},{6,2},{7,3},{8,12},{9,13},{10,... | collective-permute-start | bytes 138248 | tf_op jit(solution)/shard_map/ppermute | solution.py:14
  36.1 4.8 %collective-permute-start.7 = (bf16[4,2880]{1,0:T(4,128)(2,1)S(1)}, bf16[4,2880]{1,0:T(4,128)(2,1)S(1)}, u32[]{:S(2)}, u32[]{:S(2)}) collective-permute-start(bf16[4,2880]{1,0:T(4,128)(2,1)S(1)} %slice.59), channel_id=1, source_target_pairs={{0,8},{1,9},{2,10},{3,11},{4,12},{5,13},{6,14},{7,15},{8,0},{9,1},... | collective-permute-start | bytes 69128 | tf_op jit(solution)/shard_map/ppermute | solution.py:14

commit v2 on v1

v2 whole, which is shorter than its diff:
```python
import jax
import jax.numpy as jnp
import numpy as np
from jax import lax
from jax.experimental import pallas as pl
from jax.experimental.pallas import tpu as pltpu
from jax.sharding import PartitionSpec as P

PARTS = 3


def moment_kernel(*refs):
    grad, moment, out = refs[0], refs[1], refs[-1]
    out[...] = (0.9 * moment[...].astype(jnp.float32) + 0.1 * grad[...].astype(jnp.float32)).astype(
        jnp.bfloat16
    )


def moment_part(part, grad, moment, after, so_far):
    depth, rows = grad.shape
    steps = 3
    size = depth // (PARTS * steps)
    block = pl.BlockSpec((size, rows), lambda i: (part * steps + i, 0))
    anywhere = pl.BlockSpec(memory_space=pl.ANY)
    extra = (after,) if so_far is None else (after, so_far)
    return pl.pallas_call(
        moment_kernel,
        grid=(steps,),
        in_specs=[block, block] + [anywhere] * len(extra),
        out_specs=block,
        out_shape=jax.ShapeDtypeStruct((depth, rows), jnp.bfloat16),
        input_output_aliases={} if so_far is None else {3: 0},
        cost_estimate=pl.CostEstimate(
            flops=3 * size * steps * rows, bytes_accessed=6 * size * steps * rows, transcendentals=0
        ),
        name="moment",
    )(grad, moment, *extra)


def shards(n, grad, moment, second, basis):
    bits = n.bit_length() - 1
    chip_bits = bits - 1
    me = lax.axis_index("rows")
    own = basis.shape[0]
    rows, depth = grad.shape

    def half_of(i):
        return i.bit_count() & 1

    orders = (
        tuple(reversed(range(chip_bits))),
        (0,) + tuple(reversed(range(1, chip_bits))),
    )

    def exchange(value, step):
        pairs = [(i, i ^ (2 << orders[half_of(i)][step]) ^ 1) for i in range(n)]
        return lax.ppermute(value, "rows", pairs)

    def across(value):
        return lax.ppermute(value, "rows", [(i, i ^ 1) for i in range(n)])

    parity = me
    for shift in (4, 2, 1):
        parity = parity ^ (parity >> shift)
    my_half = parity & 1

    grad_t, moment_t = grad.T, moment.T
    other_grad = across(grad)

    held = basis
    moment_next = None
    for step in range(chip_bits):
        come = exchange(held, step)
        if step < PARTS:
            moment_next = moment_part(step, grad_t, moment_t, held, moment_next)
            come, moment_next = lax.optimization_barrier((come, moment_next))
        held = jnp.concatenate([held, come], 0)
    for step in range(chip_bits, PARTS):
        moment_next = moment_part(step, grad_t, moment_t, held, moment_next)

    def rotate(basis_rows, values):
        return lax.dot_general(
            basis_rows, values, (((1,), (1,)), ((), ())), preferred_element_type=jnp.float32
        )

    rot_own = rotate(held, grad)
    rot_other = rotate(held, other_grad)
    rot_own, rot_other = lax.optimization_barrier((rot_own, rot_other))
    partial = jnp.dot(rot_own.astype(jnp.bfloat16), grad, preferred_element_type=jnp.float32)
    partial += jnp.dot(rot_other.astype(jnp.bfloat16), other_grad, preferred_element_type=jnp.float32)
    held_later, partial = lax.optimization_barrier((held, partial))
    whole = jnp.concatenate([held, across(held_later)], 0)
    rot_grad = jnp.concatenate([rot_own, rotate(whole[rot_own.shape[0] :], grad)], 0)
    rot_moment = lax.dot_general(
        whole, moment_next, (((1,), (0,)), ((), ())), preferred_element_type=jnp.float32
    )

    cube = (2,) * bits + (own, rows)
    odd = np.array([half_of(o) for o in range(n // 2)]).reshape((2,) * chip_bits + (1, 1, 1)) == 1

    def flips(value):
        for bit in range(bits):
            axis = bits - 1 - bit
            value = jnp.where((me >> bit) & 1, jnp.flip(value, axis), value)
        return value

    def swap(value):
        return jnp.where(odd, jnp.flip(value, chip_bits), value)

    turns = tuple(tuple(chip_bits - 1 - b for b in reversed(order)) for order in orders)
    rest = (chip_bits, chip_bits + 1)

    def turned(value, turn, back):
        turn = tuple(np.argsort(turn)) if back else turn
        return value.transpose(turn + rest)

    def by_half(first, back):
        pair = [turned(first, turn, back) for turn in turns]
        return jnp.where(my_half == 0, pair[0], pair[1]), jnp.where(my_half == 0, pair[1], pair[0])

    placed = swap(flips(second.T.reshape(cube)))
    mine = by_half(placed[(slice(None),) * chip_bits + (0,)], False)[0]
    theirs = by_half(placed[(slice(None),) * chip_bits + (1,)], False)[1]
    both = jnp.concatenate([mine.reshape(-1, rows), theirs.reshape(-1, rows)], 0)
    both = 0.95 * both + 0.05 * rot_grad * rot_grad
    scaled = (rot_moment / (jnp.sqrt(both) + 1e-08)).astype(jnp.bfloat16)
    both, scaled = lax.optimization_barrier((both, scaled))
    def shrink(partial, step, *beside):
        half = partial.shape[0] // 2
        come = exchange(partial[half:].astype(jnp.bfloat16), step)
        if beside:
            come, *beside = lax.optimization_barrier((come, *beside))
        return partial[:half] + come.astype(jnp.float32), beside

    partial, (both, scaled) = shrink(partial, chip_bits - 1, both, scaled)
    update = lax.dot_general(
        scaled, whole, (((0,), (0,)), ((), ())), preferred_element_type=jnp.float32
    ).astype(jnp.bfloat16)
    partial, (update,) = shrink(partial, chip_bits - 2, update)
    for step in reversed(range(chip_bits - 2)):
        partial, _ = shrink(partial, step)
    basis_next = partial / jnp.sqrt(jnp.mean(partial * partial, axis=1, keepdims=True) + 1e-06)
    count = rot_own.shape[0]
    half_cube = (2,) * chip_bits + (own, rows)
    mine = by_half(both[:count].reshape(half_cube), True)[0]
    theirs = by_half(both[count:].reshape(half_cube), True)[1]
    back = flips(swap(jnp.stack([mine, theirs], chip_bits)))
    second_next = back.reshape(n * own, rows).T
    return update, moment_next.T, second_next, basis_next


def solution(mesh):
    n = mesh.shape["rows"]
    placed = P(("groups", "rows"), None)
    return jax.shard_map(
        lambda *arrays: shards(n, *arrays),
        mesh=mesh,
        in_specs=(placed,) * 4,
        out_specs=(placed,) * 4,
        check_vma=False,
    )
```

time: 42 us -> 38 us (0.905)
  waiting for transfers between devices: 16.7 us -> 2.42 us
  Pallas kernels: 0 us -> 9.77 us
  matrix products: 5.63 us -> 10.3 us
  other arithmetic: 5.75 us -> 1.44 us
    ppermute x8, waiting for transfers between devices: 16.7 us -> 2.42 us  [the longest x6 2.41 us: exchange(): return lax.ppermute(value, 'rows', pairs)]
    pallas_call x0 -> x3, Pallas kernels: none -> 9.77 us  [moment_part(): pl.pallas_call(moment_kernel, grid=(steps,), in_specs=[block, block] + [a...]
    dot_general x3 -> x7, matrix products: 5.63 us -> 10.3 us  [the longest x3 2.96 us: rotate(): lax.dot_general(basis_rows, values, (((1,), (1,)), ((), ())), preferred_e...]
    convert_element_type x1 -> x0, other arithmetic: 4.54 us -> none  [shards(): (0.9 * moment.astype(jnp.float32) + 0.1 * grad.astype(jnp.float32)).astyp...]
    reshape x4 -> x7, local copies, waits for them, and re-layouts: 1.64 us -> 1.68 us  [the longest x2 0.93 us: shards(): placed = swap(flips(second.T.reshape(cube)))]
  transfers between devices with their start and end apart: 8 -> 8, of which waited for: 6 -> 3; matrix products, arithmetic and copies ran while one was open for 26% -> 20% of each run, Pallas kernels for 0% -> 26%
where the time goes in v2:
time: 38 us; the launch traced here: 37.6 us
  starting transfers between devices  10.7 us (28%)
  matrix products  10.3 us (27%)
  Pallas kernels  9.77 us (26%)
  waiting for transfers between devices  2.42 us (6%)
  local copies, waits for them, and re-layouts  1.95 us (5%)
  other arithmetic  1.44 us (4%)
  between operations  0.97 us (3%)
    ppermute x6, starting transfers between devices, exchange(): return lax.ppermute(value, 'rows', pairs)  9.97 us
    pallas_call x3, Pallas kernels, moment_part(): pl.pallas_call(moment_kernel, grid=(steps,), in_specs=[block, block] + [a...  9.77 us
    dot_general x3, matrix products, rotate(): lax.dot_general(basis_rows, values, (((1,), (1,)), ((), ())), preferred_e...  2.96 us
    ppermute x6, waiting for transfers between devices, exchange(): return lax.ppermute(value, 'rows', pairs)  2.41 us
    dot_general x1, matrix products, shards(): jnp.dot(rot_other.astype(jnp.bfloat16), other_grad, preferred_element_typ...  2.37 us
    dot_general x1, matrix products, shards(): lax.dot_general(scaled, whole, (((0,), (0,)), ((), ())), preferred_elemen...  2.16 us
    dot_general x1, matrix products, shards(): lax.dot_general(whole, moment_next, (((1,), (0,)), ((), ())), preferred_e...  2.09 us
    reshape x2, local copies, waits for them, and re-layouts, shards(): placed = swap(flips(second.T.reshape(cube)))  0.93 us
  transfers between devices with their start and end apart: 8, of which 3 were waited for; matrix products, arithmetic and copies ran while one was open for 20% of the time, Pallas kernels for 26%

profile of v2, /device:TPU:0, one launch (start us, length us, event | category | flops | bytes accessed | tf_op | source)
XLA Modules:
  0.0 37.6 jit_solution(1164256808286707219)
XLA Ops:
  0.6 3.5 %collective-permute-start = (bf16[4,2880]{1,0:T(4,128)(2,1)}, bf16[4,2880]{1,0:T(4,128)(2,1)S(1)}, u32[]{:S(2)}, u32[]{:S(2)}) collective-permute-start(bf16[4,2880]{1,0:T(4,128)(2,1)} %refs_2_.1), channel_id=1, source_target_pairs={{0,9},{1,2},{2,1},{3,10},{4,7},{5,12},{6,15},{7,4},{8,11},{9,0},{1... | collective-permute-start | bytes 69128 | tf_op jit(solution)/shard_map/ppermute | solution.py:57
  4.2 0.0 collective-permute-start.3
  4.2 0.9 %reshape.34 = f32[2,2,2,2,4,384]{5,4,3,2,1,0:T(4,128)S(1)} reshape(f32[64,384]{1,0:T(8,128)} %bitcast.62) | data formatting | bytes 196608 | tf_op jit(solution)/shard_map/reshape | solution.py:121
  5.2 0.0 copy-start.1
  5.3 0.0 copy-start.4
  5.3 3.2 %moment.3.refs_3_ = bf16[2880,384]{1,0:T(8,128)(2,1)} custom-call(bf16[2880,384]{1,0:T(8,128)(2,1)} %bitcast.55, bf16[2880,384]{1,0:T(8,128)(2,1)} %bitcast.59, bf16[4,2880]{1,0:T(4,128)(2,1)} %refs_2_.1), custom_call_target="tpu_custom_call" | custom-call | flops 1105920 | bytes 2211840 | tf_op jit(solution)/shard_map/moment/pallas_call | solution.py:26
  8.5 0.0 collective-permute-done
  8.5 0.0 copy-done.1
  8.5 0.0 copy-start.3
  8.5 1.9 %collective-permute-start.1 = (bf16[8,2880]{1,0:T(8,128)(2,1)S(1)}, bf16[8,2880]{1,0:T(8,128)(2,1)S(1)}, u32[]{:S(2)}, u32[]{:S(2)}) collective-permute-start(bf16[8,2880]{1,0:T(8,128)(2,1)S(1)} %pad_maximum_fusion.3.refs_2_), channel_id=1, source_target_pairs={{0,5},{1,8},{2,11},{3,6},{4,13},{5,0},{6,3},{7,14},{8,1},{9,12},{1... | collective-permute-start | bytes 138248 | tf_op jit(solution)/shard_map/ppermute | solution.py:57
  10.4 0.0 copy-done.4
  10.4 0.1 reverse_select_fusion.5
  10.5 0.0 copy-done.3
  10.5 3.2 %moment.4.refs_3_ = bf16[2880,384]{1,0:T(8,128)(2,1)} custom-call(bf16[2880,384]{1,0:T(8,128)(2,1)} %bitcast.56, bf16[2880,384]{1,0:T(8,128)(2,1)} %bitcast.60, bf16[8,2880]{1,0:T(8,128)(2,1)} %copy-done.3, bf16[2880,384]{1,0:T(8,128)(2,1)} %moment.3.refs_3_), custom_call_target="tpu_custom_call", output_to_operand_aliasing={{}: (3, {})} | custom-call | flops 1105920 | bytes 2211840 | tf_op jit(solution)/shard_map/moment/pallas_call | solution.py:26
  13.7 0.0 collective-permute-done.1
  13.8 0.0 copy-start.2
  13.8 1.0 %collective-permute-start.2 = (bf16[16,2880]{1,0:T(8,128)(2,1)S(1)}, bf16[16,2880]{1,0:T(8,128)(2,1)S(1)}, u32[]{:S(2)}, u32[]{:S(2)}) collective-permute-start(bf16[16,2880]{1,0:T(8,128)(2,1)S(1)} %pad_maximum_fusion.2.refs_2_), channel_id=1, source_target_pairs={{0,3},{1,4},{2,7},{3,0},{4,1},{5,6},{6,5},{7,2},{8,13},{9,10},{10,... | collective-permute-start | bytes 276488 | tf_op jit(solution)/shard_map/ppermute | solution.py:57
  14.8 0.0 copy-done.2
  14.8 0.0 copy-start
  14.9 3.4 %moment.5 = bf16[2880,384]{1,0:T(8,128)(2,1)} custom-call(bf16[2880,384]{1,0:T(8,128)(2,1)} %bitcast.57, bf16[2880,384]{1,0:T(8,128)(2,1)} %bitcast.61, bf16[16,2880]{1,0:T(8,128)(2,1)} %copy-done.2, bf16[2880,384]{1,0:T(8,128)(2,1)} %moment.4.refs_3_), custom_call_target="tpu_custom_call", output_to_operand_aliasing={{}: (3, {})} | custom-call | flops 1105920 | bytes 2211840 | tf_op jit(solution)/shard_map/moment/pallas_call | solution.py:26
  18.2 0.0 collective-permute-done.2
  18.2 0.0 copy-done
  18.2 0.4 %fusion.9 = f32[32,384]{1,0:T(8,128)S(1)} fusion(bf16[384,2880]{0,1:T(8,128)(2,1)S(1)} %copy-done, bf16[16,2880]{1,0:T(8,128)(2,1)S(1)} %collective-permute-done.2, bf16[8,2880]{1,0:T(8,128)(2,1)S(1)} %collective-permute-done.1, bf16[4,2880]{1,0:T(4,128)(2,1)S(1)} %collective-permute-done, bf16[4,2880]{1,0:T(4,128)(2,1)S(1)} %copy-done.1), kind=kOutput, calls=%fused_computation.42 | convolution fusion | flops 71516160 | bytes 2445312 | tf_op jit(solution)/shard_map/dot_general | solution.py:82
  18.7 0.0 collective-permute-done.3
  18.8 2.1 %fusion.8 = bf16[32,384]{1,0:T(8,128)(2,1)S(1)} fusion(bf16[384,2880]{0,1:T(8,128)(2,1)} %collective-permute-done.3, bf16[16,2880]{1,0:T(8,128)(2,1)S(1)} %collective-permute-done.2, bf16[8,2880]{1,0:T(8,128)(2,1)S(1)} %collective-permute-done.1, bf16[4,2880]{1,0:T(4,128)(2,1)S(1)} %collective-permute-done, bf16[4,2880]{1,0:T(4,128)(2,1)S(1)} %copy-done.1), kind=kOutput, calls=%fused_computation.41 | convolution fusion | flops 71516160 | bytes 2420736 | tf_op jit(solution)/shard_map/dot_general | solution.py:82
  20.8 0.7 %fusion.5 = f32[32,2880]{1,0:T(8,128)S(1)} fusion(bf16[384,2880]{0,1:T(8,128)(2,1)S(1)} %copy-done, f32[32,384]{1,0:T(8,128)S(1)} %fusion.9), kind=kOutput, calls=%fused_computation.37 | convolution fusion | flops 70791168 | bytes 2629632 | tf_op jit(solution)/shard_map/dot_general | solution.py:89
  21.6 2.4 %convolution_add_fusion = f32[32,2880]{1,0:T(8,128)S(1)} fusion(f32[32,2880]{1,0:T(8,128)S(1)} %fusion.5, bf16[384,2880]{0,1:T(8,128)(2,1)} %collective-permute-done.3, bf16[32,384]{1,0:T(8,128)(2,1)S(1)} %fusion.8), kind=kOutput, calls=%fused_computation.1 | convolution fusion | flops 70871040 | bytes 2973696 | tf_op jit(solution)/shard_map/dot_general | solution.py:90
  24.0 0.7 %collective-permute-start.5 = (bf16[32,2880]{1,0:T(8,128)(2,1)S(1)}, bf16[32,2880]{1,0:T(8,128)(2,1)S(1)}, u32[]{:S(2)}, u32[]{:S(2)}) collective-permute-start(bf16[32,2880]{1,0:T(8,128)(2,1)S(1)} %pad_maximum_fusion), channel_id=1, source_target_pairs={{0,1},{1,0},{2,3},{3,2},{4,5},{5,4},{6,7},{7,6},{8,9},{9,8},{10,11... | collective-permute-start | bytes 552968 | tf_op jit(solution)/shard_map/ppermute | solution.py:60
  24.8 1.0 %collective-permute-start.4 = (bf16[16,2880]{1,0:T(8,128)(2,1)S(1)}, bf16[16,2880]{1,0:T(8,128)(2,1)S(1)}, u32[]{:S(2)}, u32[]{:S(2)}) collective-permute-start(bf16[16,2880]{1,0:T(8,128)(2,1)S(1)} %slice.62), channel_id=1, source_target_pairs={{0,3},{1,4},{2,7},{3,0},{4,1},{5,6},{6,5},{7,2},{8,13},{9,10},{10,... | collective-permute-start | bytes 276488 | tf_op jit(solution)/shard_map/ppermute | solution.py:57
  25.8 0.0 collective-permute-done.5
  25.8 0.4 %fusion.12 = f32[32,384]{1,0:T(8,128)S(1)} fusion(bf16[32,2880]{1,0:T(8,128)(2,1)S(1)} %collective-permute-done.5, bf16[384,2880]{0,1:T(8,128)(2,1)S(1)} %copy-done), kind=kOutput, calls=%fused_computation.45 | convolution fusion | flops 70778880 | bytes 2445312 | tf_op jit(solution)/shard_map/dot_general | solution.py:82
  26.3 0.2 concatenate.26
  26.4 2.1 %fusion = bf16[64,384]{1,0:T(8,128)(2,1)S(1)} fusion(bf16[64,2880]{1,0:T(8,128)(2,1)S(1)} %concatenate.26, bf16[2880,384]{1,0:T(8,128)(2,1)} %moment.5, f32[64,384]{1,0:T(8,128)S(1)} %fusion.1), kind=kOutput, calls=%fused_computation.3 | convolution fusion | flops 141631488 | bytes 2727936 | tf_op jit(solution)/shard_map/dot_general | solution.py:94
  28.5 0.3 collective-permute-done.4
  28.9 0.6 %collective-permute-start.6 = (bf16[8,2880]{1,0:T(8,128)(2,1)S(1)}, bf16[8,2880]{1,0:T(8,128)(2,1)S(1)}, u32[]{:S(2)}, u32[]{:S(2)}) collective-permute-start(bf16[8,2880]{1,0:T(8,128)(2,1)S(1)} %slice.63), channel_id=1, source_target_pairs={{0,5},{1,8},{2,11},{3,6},{4,13},{5,0},{6,3},{7,14},{8,1},{9,12},{1... | collective-permute-start | bytes 138248 | tf_op jit(solution)/shard_map/ppermute | solution.py:57
  29.5 2.2 %convolution_convert_fusion = bf16[384,2880]{0,1:T(8,128)(2,1)} fusion(bf16[64,384]{1,0:T(8,128)(2,1)S(1)} %fusion, bf16[64,2880]{1,0:T(8,128)(2,1)S(1)} %concatenate.26), kind=kOutput, calls=%fused_computation | convolution fusion | flops 142663680 | bytes 2629632 | tf_op jit(solution)/shard_map/dot_general | solution.py:136
  31.8 0.1 reverse_select_fusion.4
  32.0 0.5 %collective-permute-done.6 = bf16[8,2880]{1,0:T(8,128)(2,1)S(1)} collective-permute-done((bf16[8,2880]{1,0:T(8,128)(2,1)S(1)}, bf16[8,2880]{1,0:T(8,128)(2,1)S(1)}, u32[]{:S(2)}, u32[]{:S(2)}) %collective-permute-start.6) | collective-permute-done | bytes 46112 | tf_op jit(solution)/shard_map/ppermute | solution.py:57
  32.5 1.9 %collective-permute-start.7 = (bf16[4,2880]{1,0:T(4,128)(2,1)S(1)}, bf16[4,2880]{1,0:T(4,128)(2,1)S(1)}, u32[]{:S(2)}, u32[]{:S(2)}) collective-permute-start(bf16[4,2880]{1,0:T(4,128)(2,1)S(1)} %slice.64), channel_id=1, source_target_pairs={{0,9},{1,2},{2,1},{3,10},{4,7},{5,12},{6,15},{7,4},{8,11},{9,0},{1... | collective-permute-start | bytes 69128 | tf_op jit(solution)/shard_map/ppermute | solution.py:57
  34.4 0.7 %reshape.39 = f32[64,384]{1,0:T(8,128)} reshape(f32[2,2,2,2,4,384]{5,4,3,2,1,0:T(4,128)S(1)} %copy.21) | data formatting | bytes 196608 | tf_op jit(solution)/shard_map/reshape | solution.py:148
  35.1 1.6 %collective-permute-done.7 = bf16[4,2880]{1,0:T(4,128)(2,1)S(1)} collective-permute-done((bf16[4,2880]{1,0:T(4,128)(2,1)S(1)}, bf16[4,2880]{1,0:T(4,128)(2,1)S(1)}, u32[]{:S(2)}, u32[]{:S(2)}) %collective-permute-start.7) | collective-permute-done | bytes 23072 | tf_op jit(solution)/shard_map/ppermute | solution.py:57
  36.7 0.1 multiply_reduce_fusion
  36.9 0.7 %fusion.7 = f32[4,2880]{1,0:T(4,128)} fusion(bf16[4,2880]{1,0:T(4,128)(2,1)S(1)} %collective-permute-done.7, f32[8,2880]{1,0:T(8,128)S(1)} %slice_add_fusion, f32[4]{0:T(128)S(1)} %add_sqrt_fusion), kind=kLoop, calls=%fused_computation.39 | loop fusion | flops 34560 | bytes 115216 | tf_op jit(solution)/shard_map/div | solution.py:142
  (29 shorter events, 0.6 us)
Async XLA Ops:
  0.6 7.8 %collective-permute-start = (bf16[4,2880]{1,0:T(4,128)(2,1)}, bf16[4,2880]{1,0:T(4,128)(2,1)S(1)}, u32[]{:S(2)}, u32[]{:S(2)}) collective-permute-start(bf16[4,2880]{1,0:T(4,128)(2,1)} %refs_2_.1), channel_id=1, source_target_pairs={{0,9},{1,2},{2,1},{3,10},{4,7},{5,12},{6,15},{7,4},{8,11},{9,0},{1... | collective-permute-start | bytes 69128 | tf_op jit(solution)/shard_map/ppermute | solution.py:57
  4.2 14.6 %collective-permute-start.3 = (bf16[384,2880]{0,1:T(8,128)(2,1)}, bf16[384,2880]{0,1:T(8,128)(2,1)}, u32[]{:S(2)}, u32[]{:S(2)}) collective-permute-start(bf16[384,2880]{0,1:T(8,128)(2,1)} %param.5), channel_id=1, source_target_pairs={{0,1},{1,0},{2,3},{3,2},{4,5},{5,4},{6,7},{7,6},{8,9},{9,8},{10,11... | collective-permute-start | bytes 6635528 | tf_op jit(solution)/shard_map/ppermute | solution.py:60
  5.2 3.2 %copy-start.1 = (bf16[4,2880]{1,0:T(4,128)(2,1)S(1)}, bf16[4,2880]{1,0:T(4,128)(2,1)}, u32[]{:S(2)}) copy-start(bf16[4,2880]{1,0:T(4,128)(2,1)} %refs_2_.1) | copy-start | bytes 69124
  5.3 5.2 %copy-start.4 = (pred[2,2,2]{0,1,2:T(4,128)(4,1)S(1)}, pred[2,2,2]{0,1,2:T(4,128)(4,1)}, u32[]{:S(2)}) copy-start(pred[2,2,2]{0,1,2:T(4,128)(4,1)} %constant.40) | copy-start | bytes 28
  8.5 2.0 %copy-start.3 = (bf16[8,2880]{1,0:T(8,128)(2,1)}, bf16[8,2880]{1,0:T(8,128)(2,1)S(1)}, u32[]{:S(2)}) copy-start(bf16[8,2880]{1,0:T(8,128)(2,1)S(1)} %pad_maximum_fusion.3.refs_2_) | copy-start | bytes 138244
  8.5 5.2 %collective-permute-start.1 = (bf16[8,2880]{1,0:T(8,128)(2,1)S(1)}, bf16[8,2880]{1,0:T(8,128)(2,1)S(1)}, u32[]{:S(2)}, u32[]{:S(2)}) collective-permute-start(bf16[8,2880]{1,0:T(8,128)(2,1)S(1)} %pad_maximum_fusion.3.refs_2_), channel_id=1, source_target_pairs={{0,5},{1,8},{2,11},{3,6},{4,13},{5,0},{6,3},{7,14},{8,1},{9,12},{1... | collective-permute-start | bytes 138248 | tf_op jit(solution)/shard_map/ppermute | solution.py:57
  13.8 1.0 %copy-start.2 = (bf16[16,2880]{1,0:T(8,128)(2,1)}, bf16[16,2880]{1,0:T(8,128)(2,1)S(1)}, u32[]{:S(2)}) copy-start(bf16[16,2880]{1,0:T(8,128)(2,1)S(1)} %pad_maximum_fusion.2.refs_2_) | copy-start | bytes 276484
  13.8 4.4 %collective-permute-start.2 = (bf16[16,2880]{1,0:T(8,128)(2,1)S(1)}, bf16[16,2880]{1,0:T(8,128)(2,1)S(1)}, u32[]{:S(2)}, u32[]{:S(2)}) collective-permute-start(bf16[16,2880]{1,0:T(8,128)(2,1)S(1)} %pad_maximum_fusion.2.refs_2_), channel_id=1, source_target_pairs={{0,3},{1,4},{2,7},{3,0},{4,1},{5,6},{6,5},{7,2},{8,13},{9,10},{10,... | collective-permute-start | bytes 276488 | tf_op jit(solution)/shard_map/ppermute | solution.py:57
  14.8 3.4 %copy-start = (bf16[384,2880]{0,1:T(8,128)(2,1)S(1)}, bf16[384,2880]{0,1:T(8,128)(2,1)}, u32[]{:S(2)}) copy-start(bf16[384,2880]{0,1:T(8,128)(2,1)} %param.5) | copy-start | bytes 6635524
  24.0 1.8 %collective-permute-start.5 = (bf16[32,2880]{1,0:T(8,128)(2,1)S(1)}, bf16[32,2880]{1,0:T(8,128)(2,1)S(1)}, u32[]{:S(2)}, u32[]{:S(2)}) collective-permute-start(bf16[32,2880]{1,0:T(8,128)(2,1)S(1)} %pad_maximum_fusion), channel_id=1, source_target_pairs={{0,1},{1,0},{2,3},{3,2},{4,5},{5,4},{6,7},{7,6},{8,9},{9,8},{10,11... | collective-permute-start | bytes 552968 | tf_op jit(solution)/shard_map/ppermute | solution.py:60
  24.8 4.1 %collective-permute-start.4 = (bf16[16,2880]{1,0:T(8,128)(2,1)S(1)}, bf16[16,2880]{1,0:T(8,128)(2,1)S(1)}, u32[]{:S(2)}, u32[]{:S(2)}) collective-permute-start(bf16[16,2880]{1,0:T(8,128)(2,1)S(1)} %slice.62), channel_id=1, source_target_pairs={{0,3},{1,4},{2,7},{3,0},{4,1},{5,6},{6,5},{7,2},{8,13},{9,10},{10,... | collective-permute-start | bytes 276488 | tf_op jit(solution)/shard_map/ppermute | solution.py:57
  28.9 3.6 %collective-permute-start.6 = (bf16[8,2880]{1,0:T(8,128)(2,1)S(1)}, bf16[8,2880]{1,0:T(8,128)(2,1)S(1)}, u32[]{:S(2)}, u32[]{:S(2)}) collective-permute-start(bf16[8,2880]{1,0:T(8,128)(2,1)S(1)} %slice.63), channel_id=1, source_target_pairs={{0,5},{1,8},{2,11},{3,6},{4,13},{5,0},{6,3},{7,14},{8,1},{9,12},{1... | collective-permute-start | bytes 138248 | tf_op jit(solution)/shard_map/ppermute | solution.py:57
  32.5 4.2 %collective-permute-start.7 = (bf16[4,2880]{1,0:T(4,128)(2,1)S(1)}, bf16[4,2880]{1,0:T(4,128)(2,1)S(1)}, u32[]{:S(2)}, u32[]{:S(2)}) collective-permute-start(bf16[4,2880]{1,0:T(4,128)(2,1)S(1)} %slice.64), channel_id=1, source_target_pairs={{0,9},{1,2},{2,1},{3,10},{4,7},{5,12},{6,15},{7,4},{8,11},{9,0},{1... | collective-permute-start | bytes 69128 | tf_op jit(solution)/shard_map/ppermute | solution.py:57

commit v3 on v2

--- a/solution.py
+++ b/solution.py
@@ -2,40 +2,7 @@
 import jax.numpy as jnp
 import numpy as np
 from jax import lax
-from jax.experimental import pallas as pl
-from jax.experimental.pallas import tpu as pltpu
 from jax.sharding import PartitionSpec as P
-
-PARTS = 3
-
-
-def moment_kernel(*refs):
-    grad, moment, out = refs[0], refs[1], refs[-1]
-    out[...] = (0.9 * moment[...].astype(jnp.float32) + 0.1 * grad[...].astype(jnp.float32)).astype(
-        jnp.bfloat16
-    )
-
-
-def moment_part(part, grad, moment, after, so_far):
-    depth, rows = grad.shape
-    steps = 3
-    size = depth // (PARTS * steps)
-    block = pl.BlockSpec((size, rows), lambda i: (part * steps + i, 0))
-    anywhere = pl.BlockSpec(memory_space=pl.ANY)
-    extra = (after,) if so_far is None else (after, so_far)
-    return pl.pallas_call(
-        moment_kernel,
-        grid=(steps,),
-        in_specs=[block, block] + [anywhere] * len(extra),
-        out_specs=block,
-        out_shape=jax.ShapeDtypeStruct((depth, rows), jnp.bfloat16),
-        input_output_aliases={} if so_far is None else {3: 0},
-        cost_estimate=pl.CostEstimate(
-            flops=3 * size * steps * rows, bytes_accessed=6 * size * steps * rows, transcendentals=0
-        ),
-        name="moment",
-    )(grad, moment, *extra)
-
 
 def shards(n, grad, moment, second, basis):
     bits = n.bit_length() - 1
@@ -64,19 +31,21 @@
         parity = parity ^ (parity >> shift)
     my_half = parity & 1
 
-    grad_t, moment_t = grad.T, moment.T
     other_grad = across(grad)
 
     held = basis
-    moment_next = None
     for step in range(chip_bits):
+        if step == 2:
+            held, moment = lax.optimization_barrier((held, moment))
         come = exchange(held, step)
-        if step < PARTS:
-            moment_next = moment_part(step, grad_t, moment_t, held, moment_next)
+        if step == 0:
+            come, other_grad = lax.optimization_barrier((come, other_grad))
+        if step == 2:
+            moment_next = (
+                0.9 * moment.astype(jnp.float32) + 0.1 * grad.astype(jnp.float32)
+            ).astype(jnp.bfloat16)
             come, moment_next = lax.optimization_barrier((come, moment_next))
         held = jnp.concatenate([held, come], 0)
-    for step in range(chip_bits, PARTS):
-        moment_next = moment_part(step, grad_t, moment_t, held, moment_next)
 
     def rotate(basis_rows, values):
         return lax.dot_general(
@@ -92,7 +61,7 @@
     whole = jnp.concatenate([held, across(held_later)], 0)
     rot_grad = jnp.concatenate([rot_own, rotate(whole[rot_own.shape[0] :], grad)], 0)
     rot_moment = lax.dot_general(
-        whole, moment_next, (((1,), (0,)), ((), ())), preferred_element_type=jnp.float32
+        whole, moment_next, (((1,), (1,)), ((), ())), preferred_element_type=jnp.float32
     )
 
     cube = (2,) * bits + (own, rows)
@@ -146,7 +115,7 @@
     theirs = by_half(both[count:].reshape(half_cube), True)[1]
     back = flips(swap(jnp.stack([mine, theirs], chip_bits)))
     second_next = back.reshape(n * own, rows).T
-    return update, moment_next.T, second_next, basis_next
+    return update, moment_next, second_next, basis_next
 
 
 def solution(mesh):

time: 38 us -> 39.7 us (1.045)
  Pallas kernels: 9.77 us -> 0 us
  other arithmetic: 1.44 us -> 8.72 us
  matrix products: 10.3 us -> 5.43 us
  waiting for transfers between devices: 2.42 us -> 6.49 us
  starting transfers between devices: 10.7 us -> 13.3 us
  local copies, waits for them, and re-layouts: 1.95 us -> 4.38 us
    pallas_call x3 -> x0, Pallas kernels: 9.77 us -> none  [moment_part(): pl.pallas_call(moment_kernel, grid=(steps,), in_specs=[block, block] + [a...]
    convert_element_type x0 -> x1, other arithmetic: none -> 4.53 us  [shards(): moment_next = (0.9 * moment.astype(jnp.float32) + 0.1 * grad.astype(jnp.f...]
    ppermute x6, waiting for transfers between devices: 2.41 us -> 6.49 us  [exchange(): return lax.ppermute(value, 'rows', pairs)]
    ppermute x6, starting transfers between devices: 9.97 us -> 12.3 us  [exchange(): return lax.ppermute(value, 'rows', pairs)]
    dot_general x3, matrix products: 2.96 us -> 1.33 us  [rotate(): lax.dot_general(basis_rows, values, (((1,), (1,)), ((), ())), preferred_e...]
    dot_general x1, matrix products: 2.37 us -> 0.75 us  [shards(): jnp.dot(rot_other.astype(jnp.bfloat16), other_grad, preferred_element_typ...]
    dot_general x1, matrix products: 2.09 us -> 0.46 us  [shards(): lax.dot_general(whole, moment_next, (((1,), (1,)), ((), ())), preferred_e...]
    concatenate x3 -> x2, other arithmetic: 0.12 us -> 1.57 us  [shards(): held = jnp.concatenate([held, come], 0)]
  transfers between devices with their start and end apart: 8 -> 8, of which waited for: 3 -> 4; matrix products, arithmetic and copies ran while one was open for 20% -> 26% of each run, Pallas kernels for 26% -> 0%
where the time goes in v3:
time: 39.7 us; the launch traced here: 39.3 us
  starting transfers between devices  13.3 us (34%)
  other arithmetic  8.72 us (22%)
  waiting for transfers between devices  6.49 us (16%)
  matrix products  5.43 us (14%)
  local copies, waits for them, and re-layouts  4.38 us (11%)
  between operations  0.96 us (2%)
    ppermute x6, starting transfers between devices, exchange(): return lax.ppermute(value, 'rows', pairs)  12.3 us
    ppermute x6, waiting for transfers between devices, exchange(): return lax.ppermute(value, 'rows', pairs)  6.49 us
    convert_element_type x1, other arithmetic, shards(): moment_next = (0.9 * moment.astype(jnp.float32) + 0.1 * grad.astype(jnp.f...  4.53 us
    dot_general x1, matrix products, shards(): lax.dot_general(scaled, whole, (((0,), (0,)), ((), ())), preferred_elemen...  2.15 us
    concatenate x2, other arithmetic, shards(): held = jnp.concatenate([held, come], 0)  1.57 us
    dot_general x3, matrix products, rotate(): lax.dot_general(basis_rows, values, (((1,), (1,)), ((), ())), preferred_e...  1.33 us
    unnamed x16, local copies, waits for them, and re-layouts  1.19 us
    ppermute x2, starting transfers between devices, across(): return lax.ppermute(value, 'rows', [(i, i ^ 1) for i in range(n)])  1.06 us
  transfers between devices with their start and end apart: 8, of which 4 were waited for; matrix products, arithmetic and copies ran while one was open for 26% of the time, Pallas kernels for 0%

profile of v3, /device:TPU:0, one launch (start us, length us, event | category | flops | bytes accessed | tf_op | source)
XLA Modules:
  0.0 39.3 jit_solution(6362968181120654985)
XLA Ops:
  0.6 0.5 %collective-permute-start.1 = (bf16[384,2880]{0,1:T(8,128)(2,1)}, bf16[384,2880]{0,1:T(8,128)(2,1)S(1)}, u32[]{:S(2)}, u32[]{:S(2)}) collective-permute-start(bf16[384,2880]{0,1:T(8,128)(2,1)} %param.5), channel_id=1, source_target_pairs={{0,1},{1,0},{2,3},{3,2},{4,5},{5,4},{6,7},{7,6},{8,9},{9,8},{10,11... | collective-permute-start | bytes 6635528 | tf_op jit(solution)/shard_map/ppermute | solution.py:27
  1.1 3.7 %collective-permute-start = (bf16[4,2880]{1,0:T(4,128)(2,1)}, bf16[4,2880]{1,0:T(4,128)(2,1)S(1)}, u32[]{:S(2)}, u32[]{:S(2)}) collective-permute-start(bf16[4,2880]{1,0:T(4,128)(2,1)} %param.8), channel_id=1, source_target_pairs={{0,9},{1,2},{2,1},{3,10},{4,7},{5,12},{6,15},{7,4},{8,11},{9,0},{1... | collective-permute-start | bytes 69128 | tf_op jit(solution)/shard_map/ppermute | solution.py:24
  4.8 0.9 %reshape.34 = f32[2,2,2,2,4,384]{5,4,3,2,1,0:T(4,128)S(1)} reshape(f32[64,384]{1,0:T(8,128)} %bitcast.54) | data formatting | bytes 196608 | tf_op jit(solution)/shard_map/reshape | solution.py:90
  5.9 0.8 %reverse_select_fusion.5 = f32[2,2,2,2,4,384]{5,4,0,1,2,3:T(4,128)S(1)} fusion(f32[2,2,2,2,4,384]{5,4,0,1,2,3:T(4,128)S(1)} %reverse_select_fusion.6, pred[2,2,2]{0,1,2:T(4,128)(4,1)} %constant.44), kind=kLoop, calls=%fused_computation.13 | loop fusion | flops 24576 | bytes 196616 | tf_op jit(solution)/shard_map/jit(_where)/select_n | solution.py:77
  6.7 0.0 collective-permute-done
  6.7 0.0 collective-permute-done.1
  6.7 0.0 copy-start.2
  6.7 0.8 %pad_maximum_fusion.2 = bf16[8,2880]{1,0:T(8,128)(2,1)S(1)} fusion(bf16[4,2880]{1,0:T(4,128)(2,1)S(1)} %collective-permute-done, bf16[4,2880]{1,0:T(4,128)(2,1)} %param.8), kind=kLoop, calls=%fused_computation.33 | loop fusion | flops 92160 | bytes 92160 | tf_op jit(solution)/shard_map/concatenate | solution.py:48
  7.5 1.5 %collective-permute-start.2 = (bf16[8,2880]{1,0:T(8,128)(2,1)S(1)}, bf16[8,2880]{1,0:T(8,128)(2,1)S(1)}, u32[]{:S(2)}, u32[]{:S(2)}) collective-permute-start(bf16[8,2880]{1,0:T(8,128)(2,1)S(1)} %pad_maximum_fusion.2), channel_id=1, source_target_pairs={{0,5},{1,8},{2,11},{3,6},{4,13},{5,0},{6,3},{7,14},{8,1},{9,12},{1... | collective-permute-start | bytes 138248 | tf_op jit(solution)/shard_map/ppermute | solution.py:24
  9.0 0.6 %fusion.9 = (f32[2,2,2,1,4,384]{5,4,0,1,2,3:T(4,128)}, f32[2,2,2,4,384]{4,3,0,1,2:T(4,128)}) fusion(f32[2,2,2,2,4,384]{5,4,0,1,2,3:T(4,128)S(1)} %reverse_select_fusion.5), kind=kLoop, calls=%fused_computation.47 | loop fusion | bytes 196608 | tf_op jit(solution)/shard_map/slice | solution.py:91
  9.7 1.4 %collective-permute-done.2 = bf16[8,2880]{1,0:T(8,128)(2,1)S(1)} collective-permute-done((bf16[8,2880]{1,0:T(8,128)(2,1)S(1)}, bf16[8,2880]{1,0:T(8,128)(2,1)S(1)}, u32[]{:S(2)}, u32[]{:S(2)}) %collective-permute-start.2) | collective-permute-done | bytes 46112 | tf_op jit(solution)/shard_map/ppermute | solution.py:24
  11.1 0.0 copy-done.2
  11.1 0.8 %pad_maximum_fusion.1 = bf16[16,2880]{1,0:T(8,128)(2,1)S(1)} fusion(bf16[8,2880]{1,0:T(8,128)(2,1)S(1)} %collective-permute-done.2, bf16[4,2880]{1,0:T(4,128)(2,1)S(1)} %collective-permute-done, bf16[4,2880]{1,0:T(4,128)(2,1)} %param.8), kind=kLoop, calls=%fused_computation.23 | loop fusion | flops 276480 | bytes 184320 | tf_op jit(solution)/shard_map/concatenate | solution.py:48
  11.9 0.0 copy-start
  11.9 2.1 %collective-permute-start.3 = (bf16[16,2880]{1,0:T(8,128)(2,1)S(1)}, bf16[16,2880]{1,0:T(8,128)(2,1)S(1)}, u32[]{:S(2)}, u32[]{:S(2)}) collective-permute-start(bf16[16,2880]{1,0:T(8,128)(2,1)S(1)} %pad_maximum_fusion.1), channel_id=1, source_target_pairs={{0,3},{1,4},{2,7},{3,0},{4,1},{5,6},{6,5},{7,2},{8,13},{9,10},{10,... | collective-permute-start | bytes 276488 | tf_op jit(solution)/shard_map/ppermute | solution.py:24
  14.0 4.5 %add_convert_fusion = bf16[384,2880]{0,1:T(8,128)(2,1)} fusion(bf16[384,2880]{0,1:T(8,128)(2,1)} %param.5, bf16[384,2880]{0,1:T(8,128)(2,1)} %param.6), kind=kLoop, calls=%fused_computation | loop fusion | flops 6635520 | bytes 6635520 | tf_op jit(solution)/shard_map/convert_element_type | solution.py:46
  18.5 0.0 collective-permute-done.3
  18.6 0.0 copy-done
  18.6 0.4 %fusion.10 = f32[32,384]{1,0:T(8,128)S(1)} fusion(bf16[32,2880]{1,0:T(8,128)(2,1)S(1)} %get-tuple-element.29, bf16[384,2880]{0,1:T(8,128)(2,1)S(1)} %copy-done), kind=kOutput, calls=%fused_computation.48 | convolution fusion | flops 70778880 | bytes 2445312 | tf_op jit(solution)/shard_map/dot_general | solution.py:51
  19.0 1.1 %copy-done.3 = bf16[384,2880]{0,1:T(8,128)(2,1)S(1)} copy-done((bf16[384,2880]{0,1:T(8,128)(2,1)S(1)}, bf16[384,2880]{0,1:T(8,128)(2,1)}, u32[]{:S(2)}) %copy-start.3) | copy-done | bytes 2211864
  20.1 0.4 %fusion.11 = bf16[32,384]{1,0:T(8,128)(2,1)S(1)} fusion(bf16[32,2880]{1,0:T(8,128)(2,1)S(1)} %get-tuple-element.29, bf16[384,2880]{0,1:T(8,128)(2,1)S(1)} %copy-done.3), kind=kOutput, calls=%fused_computation.49 | convolution fusion | flops 70778880 | bytes 2420736 | tf_op jit(solution)/shard_map/dot_general | solution.py:51
  20.6 0.0 copy-start.4
  20.6 0.0 copy-start.5
  20.6 0.7 %fusion.5 = f32[32,2880]{1,0:T(8,128)S(1)} fusion(bf16[384,2880]{0,1:T(8,128)(2,1)S(1)} %copy-done, f32[32,384]{1,0:T(8,128)S(1)} %fusion.10), kind=kOutput, calls=%fused_computation.37 | convolution fusion | flops 70791168 | bytes 2629632 | tf_op jit(solution)/shard_map/dot_general | solution.py:58
  21.3 0.7 %convolution_add_fusion = f32[32,2880]{1,0:T(8,128)S(1)} fusion(f32[32,2880]{1,0:T(8,128)S(1)} %fusion.5, bf16[384,2880]{0,1:T(8,128)(2,1)S(1)} %copy-done.3, bf16[32,384]{1,0:T(8,128)(2,1)S(1)} %fusion.11), kind=kOutput, calls=%fused_computation.2 | convolution fusion | flops 70871040 | bytes 2973696 | tf_op jit(solution)/shard_map/dot_general | solution.py:59
  22.1 0.5 %collective-permute-start.5 = (bf16[32,2880]{1,0:T(8,128)(2,1)S(1)}, bf16[32,2880]{1,0:T(8,128)(2,1)S(1)}, u32[]{:S(2)}, u32[]{:S(2)}) collective-permute-start(bf16[32,2880]{1,0:T(8,128)(2,1)S(1)} %get-tuple-element.29), channel_id=1, source_target_pairs={{0,1},{1,0},{2,3},{3,2},{4,5},{5,4},{6,7},{7,6},{8,9},{9,8},{10,11... | collective-permute-start | bytes 552968 | tf_op jit(solution)/shard_map/ppermute | solution.py:27
  22.6 0.0 copy-done.4
  22.7 0.0 copy-done.5
  22.7 0.6 %bitcast_select_fusion = (f32[2,2,2,4,384]{4,3,2,1,0:T(4,128)}, f32[2,2,2,4,384]{4,3,2,1,0:T(4,128)S(1)}) fusion(f32[2,2,2,1,4,384]{5,4,0,1,2,3:T(4,128)S(1)} %copy-done.4, pred[]{:T(512)S(6)} %eq.2, f32[2,2,2,2,4,384]{5,4,0,1,2,3:T(4,128)S(1)} %reverse_select_fusion.5, f32[2,2,2,4,384]{4,3,0,1,2:T(4,128)S(1)} %copy-done.5), kind=kLoop, calls=%fused_computation.24 | loop fusion | flops 24576 | bytes 245761 | tf_op jit(solution)/shard_map/jit(_where)/select_n | solution.py:88
  23.3 0.8 %reshape.35 = f32[32,384]{1,0:T(8,128)S(1)} reshape(f32[2,2,2,4,384]{4,3,2,1,0:T(4,128)} %get-tuple-element.46) | data formatting | bytes 98304 | tf_op jit(solution)/shard_map/reshape | solution.py:93
  24.1 0.0 copy-start.1
  24.2 1.6 %collective-permute-start.4 = (bf16[16,2880]{1,0:T(8,128)(2,1)S(1)}, bf16[16,2880]{1,0:T(8,128)(2,1)S(1)}, u32[]{:S(2)}, u32[]{:S(2)}) collective-permute-start(bf16[16,2880]{1,0:T(8,128)(2,1)S(1)} %slice.62), channel_id=1, source_target_pairs={{0,3},{1,4},{2,7},{3,0},{4,1},{5,6},{6,5},{7,2},{8,13},{9,10},{10,... | collective-permute-start | bytes 276488 | tf_op jit(solution)/shard_map/ppermute | solution.py:24
  25.8 0.0 collective-permute-done.5
  25.8 0.4 %fusion.12 = f32[32,384]{1,0:T(8,128)S(1)} fusion(bf16[32,2880]{1,0:T(8,128)(2,1)S(1)} %collective-permute-done.5, bf16[384,2880]{0,1:T(8,128)(2,1)S(1)} %copy-done), kind=kOutput, calls=%fused_computation.50 | convolution fusion | flops 70778880 | bytes 2445312 | tf_op jit(solution)/shard_map/dot_general | solution.py:51
  26.3 0.0 copy-done.1
  26.3 0.5 %fusion = bf16[64,384]{1,0:T(8,128)(2,1)S(1)} fusion(bf16[64,2880]{1,0:T(8,128)(2,1)S(1)} %constant_dynamic-update-slice_fusion.2, bf16[384,2880]{0,1:T(8,128)(2,1)S(1)} %copy-done.1, f32[64,384]{1,0:T(8,128)S(1)} %fusion.1), kind=kOutput, calls=%fused_computation.4 | convolution fusion | flops 141631488 | bytes 2727936 | tf_op jit(solution)/shard_map/dot_general | solution.py:63
  26.8 0.0 copy-start.6
  26.8 1.5 %collective-permute-done.4 = bf16[16,2880]{1,0:T(8,128)(2,1)S(1)} collective-permute-done((bf16[16,2880]{1,0:T(8,128)(2,1)S(1)}, bf16[16,2880]{1,0:T(8,128)(2,1)S(1)}, u32[]{:S(2)}, u32[]{:S(2)}) %collective-permute-start.4) | collective-permute-done | bytes 92192 | tf_op jit(solution)/shard_map/ppermute | solution.py:24
  28.2 2.2 %convolution_convert_fusion = bf16[384,2880]{0,1:T(8,128)(2,1)} fusion(bf16[64,384]{1,0:T(8,128)(2,1)S(1)} %fusion, bf16[64,2880]{1,0:T(8,128)(2,1)S(1)} %constant_dynamic-update-slice_fusion.2), kind=kOutput, calls=%fused_computation.1 | convolution fusion | flops 142663680 | bytes 2629632 | tf_op jit(solution)/shard_map/dot_general | solution.py:105
  30.4 0.4 %collective-permute-start.6 = (bf16[8,2880]{1,0:T(8,128)(2,1)S(1)}, bf16[8,2880]{1,0:T(8,128)(2,1)S(1)}, u32[]{:S(2)}, u32[]{:S(2)}) collective-permute-start(bf16[8,2880]{1,0:T(8,128)(2,1)S(1)} %slice.63), channel_id=1, source_target_pairs={{0,5},{1,8},{2,11},{3,6},{4,13},{5,0},{6,3},{7,14},{8,1},{9,12},{1... | collective-permute-start | bytes 138248 | tf_op jit(solution)/shard_map/ppermute | solution.py:24
  31.0 0.0 copy-done.6
  31.0 0.1 reverse_select_fusion.4
  31.2 2.8 %collective-permute-done.6 = bf16[8,2880]{1,0:T(8,128)(2,1)S(1)} collective-permute-done((bf16[8,2880]{1,0:T(8,128)(2,1)S(1)}, bf16[8,2880]{1,0:T(8,128)(2,1)S(1)}, u32[]{:S(2)}, u32[]{:S(2)}) %collective-permute-start.6) | collective-permute-done | bytes 46112 | tf_op jit(solution)/shard_map/ppermute | solution.py:24
  34.0 2.9 %collective-permute-start.7 = (bf16[4,2880]{1,0:T(4,128)(2,1)S(1)}, bf16[4,2880]{1,0:T(4,128)(2,1)S(1)}, u32[]{:S(2)}, u32[]{:S(2)}) collective-permute-start(bf16[4,2880]{1,0:T(4,128)(2,1)S(1)} %slice.64), channel_id=1, source_target_pairs={{0,9},{1,2},{2,1},{3,10},{4,7},{5,12},{6,15},{7,4},{8,11},{9,0},{1... | collective-permute-start | bytes 69128 | tf_op jit(solution)/shard_map/ppermute | solution.py:24
  37.0 0.7 %reshape.39 = f32[64,384]{1,0:T(8,128)} reshape(f32[2,2,2,2,4,384]{5,4,3,2,1,0:T(4,128)S(1)} %copy.19) | data formatting | bytes 196608 | tf_op jit(solution)/shard_map/reshape | solution.py:117
  37.7 0.8 %collective-permute-done.7 = bf16[4,2880]{1,0:T(4,128)(2,1)S(1)} collective-permute-done((bf16[4,2880]{1,0:T(4,128)(2,1)S(1)}, bf16[4,2880]{1,0:T(4,128)(2,1)S(1)}, u32[]{:S(2)}, u32[]{:S(2)}) %collective-permute-start.7) | collective-permute-done | bytes 23072 | tf_op jit(solution)/shard_map/ppermute | solution.py:24
  38.5 0.1 multiply_reduce_fusion
  38.6 0.7 %fusion.7 = f32[4,2880]{1,0:T(4,128)} fusion(bf16[4,2880]{1,0:T(4,128)(2,1)S(1)} %collective-permute-done.7, f32[8,2880]{1,0:T(8,128)S(1)} %slice_add_fusion, f32[4]{0:T(128)S(1)} %add_sqrt_fusion), kind=kLoop, calls=%fused_computation.39 | loop fusion | flops 34560 | bytes 115216 | tf_op jit(solution)/shard_map/div | solution.py:111
  (27 shorter events, 0.4 us)
Async XLA Ops:
  0.6 6.1 %collective-permute-start.1 = (bf16[384,2880]{0,1:T(8,128)(2,1)}, bf16[384,2880]{0,1:T(8,128)(2,1)S(1)}, u32[]{:S(2)}, u32[]{:S(2)}) collective-permute-start(bf16[384,2880]{0,1:T(8,128)(2,1)} %param.5), channel_id=1, source_target_pairs={{0,1},{1,0},{2,3},{3,2},{4,5},{5,4},{6,7},{7,6},{8,9},{9,8},{10,11... | collective-permute-start | bytes 6635528 | tf_op jit(solution)/shard_map/ppermute | solution.py:27
  1.1 5.5 %collective-permute-start = (bf16[4,2880]{1,0:T(4,128)(2,1)}, bf16[4,2880]{1,0:T(4,128)(2,1)S(1)}, u32[]{:S(2)}, u32[]{:S(2)}) collective-permute-start(bf16[4,2880]{1,0:T(4,128)(2,1)} %param.8), channel_id=1, source_target_pairs={{0,9},{1,2},{2,1},{3,10},{4,7},{5,12},{6,15},{7,4},{8,11},{9,0},{1... | collective-permute-start | bytes 69128 | tf_op jit(solution)/shard_map/ppermute | solution.py:24
  6.7 4.4 %copy-start.2 = (bf16[384,2880]{0,1:T(8,128)(2,1)}, bf16[384,2880]{0,1:T(8,128)(2,1)S(1)}, u32[]{:S(2)}) copy-start(bf16[384,2880]{0,1:T(8,128)(2,1)S(1)} %collective-permute-done.1) | copy-start | bytes 6635524
  7.5 3.6 %collective-permute-start.2 = (bf16[8,2880]{1,0:T(8,128)(2,1)S(1)}, bf16[8,2880]{1,0:T(8,128)(2,1)S(1)}, u32[]{:S(2)}, u32[]{:S(2)}) collective-permute-start(bf16[8,2880]{1,0:T(8,128)(2,1)S(1)} %pad_maximum_fusion.2), channel_id=1, source_target_pairs={{0,5},{1,8},{2,11},{3,6},{4,13},{5,0},{6,3},{7,14},{8,1},{9,12},{1... | collective-permute-start | bytes 138248 | tf_op jit(solution)/shard_map/ppermute | solution.py:24
  11.9 6.7 %copy-start = (bf16[384,2880]{0,1:T(8,128)(2,1)S(1)}, bf16[384,2880]{0,1:T(8,128)(2,1)}, u32[]{:S(2)}) copy-start(bf16[384,2880]{0,1:T(8,128)(2,1)} %param.5) | copy-start | bytes 6635524
  11.9 6.7 %collective-permute-start.3 = (bf16[16,2880]{1,0:T(8,128)(2,1)S(1)}, bf16[16,2880]{1,0:T(8,128)(2,1)S(1)}, u32[]{:S(2)}, u32[]{:S(2)}) collective-permute-start(bf16[16,2880]{1,0:T(8,128)(2,1)S(1)} %pad_maximum_fusion.1), channel_id=1, source_target_pairs={{0,3},{1,4},{2,7},{3,0},{4,1},{5,6},{6,5},{7,2},{8,13},{9,10},{10,... | collective-permute-start | bytes 276488 | tf_op jit(solution)/shard_map/ppermute | solution.py:24
  18.5 1.6 %copy-start.3 = (bf16[384,2880]{0,1:T(8,128)(2,1)S(1)}, bf16[384,2880]{0,1:T(8,128)(2,1)}, u32[]{:S(2)}) copy-start(bf16[384,2880]{0,1:T(8,128)(2,1)} %copy-done.2) | copy-start | bytes 6635524
  20.6 2.1 %copy-start.4 = (f32[2,2,2,1,4,384]{5,4,0,1,2,3:T(4,128)S(1)}, f32[2,2,2,1,4,384]{5,4,0,1,2,3:T(4,128)}, u32[]{:S(2)}) copy-start(f32[2,2,2,1,4,384]{5,4,0,1,2,3:T(4,128)} %get-tuple-element.40) | copy-start | bytes 147460
  20.6 2.1 %copy-start.5 = (f32[2,2,2,4,384]{4,3,0,1,2:T(4,128)S(1)}, f32[2,2,2,4,384]{4,3,0,1,2:T(4,128)}, u32[]{:S(2)}) copy-start(f32[2,2,2,4,384]{4,3,0,1,2:T(4,128)} %get-tuple-element.41) | copy-start | bytes 147460
  22.1 3.7 %collective-permute-start.5 = (bf16[32,2880]{1,0:T(8,128)(2,1)S(1)}, bf16[32,2880]{1,0:T(8,128)(2,1)S(1)}, u32[]{:S(2)}, u32[]{:S(2)}) collective-permute-start(bf16[32,2880]{1,0:T(8,128)(2,1)S(1)} %get-tuple-element.29), channel_id=1, source_target_pairs={{0,1},{1,0},{2,3},{3,2},{4,5},{5,4},{6,7},{7,6},{8,9},{9,8},{10,11... | collective-permute-start | bytes 552968 | tf_op jit(solution)/shard_map/ppermute | solution.py:27
  24.1 2.1 %copy-start.1 = (bf16[384,2880]{0,1:T(8,128)(2,1)S(1)}, bf16[384,2880]{0,1:T(8,128)(2,1)}, u32[]{:S(2)}) copy-start(bf16[384,2880]{0,1:T(8,128)(2,1)} %add_convert_fusion) | copy-start | bytes 6635524
  24.2 4.1 %collective-permute-start.4 = (bf16[16,2880]{1,0:T(8,128)(2,1)S(1)}, bf16[16,2880]{1,0:T(8,128)(2,1)S(1)}, u32[]{:S(2)}, u32[]{:S(2)}) collective-permute-start(bf16[16,2880]{1,0:T(8,128)(2,1)S(1)} %slice.62), channel_id=1, source_target_pairs={{0,3},{1,4},{2,7},{3,0},{4,1},{5,6},{6,5},{7,2},{8,13},{9,10},{10,... | collective-permute-start | bytes 276488 | tf_op jit(solution)/shard_map/ppermute | solution.py:24
  26.8 4.2 %copy-start.6 = (pred[2,2,2]{0,1,2:T(4,128)(4,1)S(1)}, pred[2,2,2]{0,1,2:T(4,128)(4,1)}, u32[]{:S(2)}) copy-start(pred[2,2,2]{0,1,2:T(4,128)(4,1)} %constant.44) | copy-start | bytes 28
  30.4 3.6 %collective-permute-start.6 = (bf16[8,2880]{1,0:T(8,128)(2,1)S(1)}, bf16[8,2880]{1,0:T(8,128)(2,1)S(1)}, u32[]{:S(2)}, u32[]{:S(2)}) collective-permute-start(bf16[8,2880]{1,0:T(8,128)(2,1)S(1)} %slice.63), channel_id=1, source_target_pairs={{0,5},{1,8},{2,11},{3,6},{4,13},{5,0},{6,3},{7,14},{8,1},{9,12},{1... | collective-permute-start | bytes 138248 | tf_op jit(solution)/shard_map/ppermute | solution.py:24
  34.0 4.4 %collective-permute-start.7 = (bf16[4,2880]{1,0:T(4,128)(2,1)S(1)}, bf16[4,2880]{1,0:T(4,128)(2,1)S(1)}, u32[]{:S(2)}, u32[]{:S(2)}) collective-permute-start(bf16[4,2880]{1,0:T(4,128)(2,1)S(1)} %slice.64), channel_id=1, source_target_pairs={{0,9},{1,2},{2,1},{3,10},{4,7},{5,12},{6,15},{7,4},{8,11},{9,0},{1... | collective-permute-start | bytes 69128 | tf_op jit(solution)/shard_map/ppermute | solution.py:24

commit v4 on v1

v4 whole, which is shorter than its diff:
```python
import functools

import jax
import jax.numpy as jnp
from jax import lax
from jax.experimental import pallas as pl
from jax.experimental.pallas import tpu as pltpu
from jax.sharding import PartitionSpec as P

INSIDE = pl.BlockSpec(memory_space=pltpu.VMEM)
ANYWHERE = pl.BlockSpec(memory_space=pl.ANY)
PARAMS = pltpu.CompilerParams(vmem_limit_bytes=24 << 20)


def inside(value):
    return pltpu.with_memory_space_constraint(value, pltpu.VMEM)


def tie(*values):
    return lax.optimization_barrier(values)


def cuts(depth, size):
    return [(at, min(size, depth - at)) for at in range(0, depth, size)]


def odd(i):
    return i.bit_count() & 1


def dot(left, right, dims):
    return lax.dot_general(left, right, (dims, ((), ())), preferred_element_type=jnp.float32)


def moment_kernel(grad, moment, held, stored, sems):
    copies = []
    for i, (at, size) in enumerate(cuts(grad.shape[0], 960)):
        part = pl.ds(at, size)
        held[part] = (
            0.9 * moment[part].astype(jnp.float32) + 0.1 * grad[part].astype(jnp.float32)
        ).astype(jnp.bfloat16)
        copy = pltpu.make_async_copy(held.at[part], stored.at[part], sems.at[i])
        copy.start()
        copies.append(copy)
    for copy in copies:
        copy.wait()


def new_moment(grad, moment):
    return pl.pallas_call(
        moment_kernel,
        in_specs=[INSIDE, INSIDE],
        out_specs=[INSIDE, ANYWHERE],
        out_shape=[
            pltpu.VMEM(grad.shape, grad.dtype),
            jax.ShapeDtypeStruct(grad.shape, grad.dtype),
        ],
        scratch_shapes=[pltpu.SemaphoreType.DMA((len(cuts(grad.shape[0], 960)),))],
        compiler_params=PARAMS,
        name="moment",
    )(inside(grad), inside(moment))


def power_kernel(basis, grad, other, rot, kept, sent):
    rot_own = dot(basis[...], grad[...], ((1,), (0,)))
    rot_other = dot(basis[...], other[...], ((1,), (0,)))
    rot[...] = rot_own
    rot_own = rot_own.astype(jnp.bfloat16)
    rot_other = rot_other.astype(jnp.bfloat16)
    half = kept.shape[0]
    for at, size in cuts(grad.shape[0], 768):
        part = pl.ds(at, size)
        product = dot(rot_own, grad[part], ((1,), (1,))) + dot(rot_other, other[part], ((1,), (1,)))
        kept[:, part] = product[:half]
        sent[:, part] = product[half:].astype(jnp.bfloat16)


def power_products(basis, grad, other):
    count, depth = basis.shape
    rows = grad.shape[1]
    return pl.pallas_call(
        power_kernel,
        in_specs=[INSIDE] * 3,
        out_specs=[INSIDE] * 3,
        out_shape=[
            pltpu.VMEM((count, rows), jnp.float32),
            pltpu.VMEM((count // 2, depth), jnp.float32),
            pltpu.VMEM((count // 2, depth), jnp.bfloat16),
        ],
        compiler_params=PARAMS,
        name="power",
    )(inside(basis), inside(grad), inside(other))


def scale_kernel(orders, own, basis, grad, moment, rot_half, second, scaled, second_next, rot, mom):
    me = lax.axis_index("rows")
    core, chip = me & 1, me >> 1
    bits = len(orders[0])
    parity = functools.reduce(lambda a, b: a ^ b, [(me >> b) & 1 for b in range(bits + 1)])
    count = rot_half.shape[0]
    rot[:count] = rot_half[...]
    rot[count:] = dot(basis[count:], grad[...], ((1,), (0,)))
    mom[...] = dot(basis[...], moment[...], ((1,), (0,)))

    def place(offset, order):
        return sum(((offset >> bit) & 1) << step for step, bit in enumerate(order)) * own

    for half in range(2):

        @pl.when(parity == half)
        def _():
            for offset in range(1 << bits):
                mine = pl.ds(place(offset, orders[half]), own)
                theirs = pl.ds(count + place(offset, orders[1 - half]), own)
                first = core == odd(offset)
                tile = pl.ds(pl.multiple_of((chip ^ offset) * 2 * own, 2 * own), 2 * own)

                def joined(ref):
                    a, b = ref[mine], ref[theirs]
                    return jnp.where(
                        first, jnp.concatenate([a, b], 0), jnp.concatenate([b, a], 0)
                    )

                turned = joined(rot)
                value = 0.95 * second[tile] + 0.05 * turned * turned
                second_next[tile] = value
                ratio = joined(mom) / (jnp.sqrt(value) + 1e-08)
                rot[mine] = jnp.where(first, ratio[:own], ratio[own:])
                rot[theirs] = jnp.where(first, ratio[own:], ratio[:own])

    scaled[...] = rot[...].astype(jnp.bfloat16)


def scaled_rotation(orders, own, basis, grad, moment, rot_half, second):
    count, rows = basis.shape[0], grad.shape[1]
    return pl.pallas_call(
        functools.partial(scale_kernel, orders, own),
        in_specs=[INSIDE] * 5,
        out_specs=[INSIDE] * 2,
        out_shape=[
            pltpu.VMEM((count, rows), jnp.bfloat16),
            jax.ShapeDtypeStruct((count, rows), jnp.float32),
        ],
        scratch_shapes=[pltpu.VMEM((count, rows), jnp.float32)] * 2,
        compiler_params=PARAMS,
        name="scale",
    )(*map(inside, (basis, grad, moment, rot_half, second)))


def update_kernel(basis, scaled, out, held, sems):
    copies = []
    for i, (at, size) in enumerate(cuts(out.shape[0], 640)):
        part = pl.ds(at, size)
        held[part] = dot(basis[:, part], scaled[...], ((0,), (0,))).astype(jnp.bfloat16)
        copy = pltpu.make_async_copy(held.at[part], out.at[part], sems.at[i])
        copy.start()
        copies.append(copy)
    for copy in copies:
        copy.wait()


def new_update(basis, scaled):
    depth, rows = basis.shape[1], scaled.shape[1]
    return pl.pallas_call(
        update_kernel,
        in_specs=[INSIDE] * 2,
        out_specs=ANYWHERE,
        out_shape=jax.ShapeDtypeStruct((depth, rows), jnp.bfloat16),
        scratch_shapes=[
            pltpu.VMEM((depth, rows), jnp.bfloat16),
            pltpu.SemaphoreType.DMA((len(cuts(depth, 640)),)),
        ],
        compiler_params=PARAMS,
        name="update",
    )(inside(basis), inside(scaled))


def shards(n, grad, moment, second, basis):
    bits = n.bit_length() - 2
    own = basis.shape[0]
    orders = (tuple(reversed(range(bits))), (0,) + tuple(reversed(range(1, bits))))

    def exchange(value, step):
        pairs = [(i, i ^ (2 << orders[odd(i)][step]) ^ 1) for i in range(n)]
        return lax.ppermute(value, "rows", pairs)

    def across(value):
        return lax.ppermute(value, "rows", [(i, i ^ 1) for i in range(n)])

    grad, moment, second = grad.T, moment.T, second.T
    other = across(grad.T).T

    held = basis
    for step in range(bits):
        if step == 1:
            held, moment = tie(held, moment)
        come = exchange(held, step)
        if step == 0:
            come, other = tie(come, other)
        if step == 1:
            moment_in, moment_next = new_moment(grad, moment)
            come, moment_in, moment_next = tie(come, moment_in, moment_next)
        held = jnp.concatenate([held, come], 0)

    rot_half, kept, sent = power_products(held, grad, other)
    come = exchange(sent, bits - 1)
    held, _ = tie(held, sent)
    whole = jnp.concatenate([held, across(held)], 0)
    come, whole = tie(come, whole)
    for step in reversed(range(bits)):
        kept = kept + come.astype(jnp.float32)
        if step == 0:
            break
        half = kept.shape[0] // 2
        come = exchange(kept[half:].astype(jnp.bfloat16), step - 1)
        kept = kept[:half]
        if step == bits - 1:
            whole, kept = tie(whole, kept)
            scaled, second_next = scaled_rotation(
                orders, own, whole, grad, moment_in, rot_half, second
            )
            come, scaled, second_next = tie(come, scaled, second_next)
        if step == bits - 2:
            scaled, kept = tie(scaled, kept)
            update = new_update(whole, scaled)
            come, update = tie(come, update)
    basis_next = kept / jnp.sqrt(jnp.mean(kept * kept, axis=1, keepdims=True) + 1e-06)
    return update.T, moment_next.T, second_next.T, basis_next


def solution(mesh):
    n = mesh.shape["rows"]
    placed = P(("groups", "rows"), None)
    return jax.shard_map(
        lambda *arrays: shards(n, *arrays),
        mesh=mesh,
        in_specs=(placed,) * 4,
        out_specs=(placed,) * 4,
        check_vma=False,
    )
```

time: 42 us -> 34.3 us (0.82)
  waiting for transfers between devices: 16.7 us -> 8.38 us
  Pallas kernels: 0 us -> 7.03 us
  matrix products: 5.63 us -> 0 us
  other arithmetic: 5.75 us -> 1.7 us
  starting transfers between devices: 10.9 us -> 12.9 us
  local copies, waits for them, and re-layouts: 1.92 us -> 3.31 us
    ppermute x8, waiting for transfers between devices: 16.7 us -> 8.38 us  [the longest x6 8.37 us: exchange(): return lax.ppermute(value, 'rows', pairs)]
    pallas_call x0 -> x4, Pallas kernels: none -> 7.03 us  [the longest x1 2.07 us: power_products(): pl.pallas_call(power_kernel, in_specs=[INSIDE] * 3, out_specs=[INSIDE] *...]
    dot_general x3 -> x0, matrix products: 5.63 us -> none  [the longest x1 4.37 us: shards(): lax.dot_general(scaled, held, (((0,), (0,)), ((), ())), preferred_element...]
    convert_element_type x1 -> x0, other arithmetic: 4.54 us -> none  [shards(): (0.9 * moment.astype(jnp.float32) + 0.1 * grad.astype(jnp.float32)).astyp...]
    unnamed x4 -> x8, local copies, waits for them, and re-layouts: 0.01 us -> 3.27 us
    ppermute x8, starting transfers between devices: 10.9 us -> 12.9 us  [the longest x6 11.2 us: exchange(): return lax.ppermute(value, 'rows', pairs)]
    reshape x4 -> x0, local copies, waits for them, and re-layouts: 1.64 us -> none  [the longest x2 0.93 us: reorder(): value = value.reshape((2,) * bits + (own, rows))]
    concatenate x3, other arithmetic: 0.12 us -> 0.81 us  [the longest x2 0.78 us: shards(): held = jnp.concatenate([held, come], 0)]
  transfers between devices with their start and end apart: 8 -> 8, of which waited for: 6 -> 5; matrix products, arithmetic and copies ran while one was open for 26% -> 0% of each run, Pallas kernels for 0% -> 15%
where the time goes in v4:
time: 34.3 us; the launch traced here: 34.1 us
  starting transfers between devices  12.9 us (38%)
  waiting for transfers between devices  8.38 us (24%)
  Pallas kernels  7.03 us (20%)
  local copies, waits for them, and re-layouts  3.31 us (10%)
  other arithmetic  1.7 us (5%)
  between operations  0.71 us (2%)
    ppermute x6, starting transfers between devices, exchange(): return lax.ppermute(value, 'rows', pairs)  11.2 us
    ppermute x6, waiting for transfers between devices, exchange(): return lax.ppermute(value, 'rows', pairs)  8.37 us
    unnamed x8, local copies, waits for them, and re-layouts  3.27 us
    pallas_call x1, Pallas kernels, power_products(): pl.pallas_call(power_kernel, in_specs=[INSIDE] * 3, out_specs=[INSIDE] *...  2.07 us
    ppermute x2, starting transfers between devices, across(): return lax.ppermute(value, 'rows', [(i, i ^ 1) for i in range(n)])  1.73 us
    pallas_call x1, Pallas kernels, new_update(): pl.pallas_call(update_kernel, in_specs=[INSIDE] * 2, out_specs=ANYWHERE,...  1.72 us
    pallas_call x1, Pallas kernels, new_moment(): pl.pallas_call(moment_kernel, in_specs=[INSIDE, INSIDE], out_specs=[INSID...  1.7 us
    pallas_call x1, Pallas kernels, scaled_rotation(): pl.pallas_call(functools.partial(scale_kernel, orders, own), in_specs=[IN...  1.54 us
  transfers between devices with their start and end apart: 8, of which 5 were waited for; matrix products, arithmetic and copies ran while one was open for 0% of the time, Pallas kernels for 15%

profile of v4, /device:TPU:0, one launch (start us, length us, event | category | flops | bytes accessed | tf_op | source)
XLA Modules:
  0.0 34.1 jit_solution(5842154802399562112)
XLA Ops:
  0.6 0.5 %collective-permute-start.1 = (bf16[384,2880]{0,1:T(8,128)(2,1)}, bf16[384,2880]{0,1:T(8,128)(2,1)S(1)}, u32[]{:S(2)}, u32[]{:S(2)}) collective-permute-start(bf16[384,2880]{0,1:T(8,128)(2,1)} %param.4), channel_id=1, source_target_pairs={{0,1},{1,0},{2,3},{3,2},{4,5},{5,4},{6,7},{7,6},{8,9},{9,8},{10,11... | collective-permute-start | bytes 6635528 | tf_op jit(solution)/shard_map/ppermute | solution.py:188
  1.1 3.7 %collective-permute-start = (bf16[4,2880]{1,0:T(4,128)(2,1)}, bf16[4,2880]{1,0:T(4,128)(2,1)S(1)}, u32[]{:S(2)}, u32[]{:S(2)}) collective-permute-start(bf16[4,2880]{1,0:T(4,128)(2,1)} %param.7), channel_id=1, source_target_pairs={{0,9},{1,2},{2,1},{3,10},{4,7},{5,12},{6,15},{7,4},{8,11},{9,0},{1... | collective-permute-start | bytes 69128 | tf_op jit(solution)/shard_map/ppermute | solution.py:185
  4.8 1.7 %collective-permute-done = bf16[4,2880]{1,0:T(4,128)(2,1)S(1)} collective-permute-done((bf16[4,2880]{1,0:T(4,128)(2,1)}, bf16[4,2880]{1,0:T(4,128)(2,1)S(1)}, u32[]{:S(2)}, u32[]{:S(2)}) %collective-permute-start) | collective-permute-done | bytes 23072 | tf_op jit(solution)/shard_map/ppermute | solution.py:185
  6.6 0.0 collective-permute-done.1
  6.6 0.8 %pad_maximum_fusion.2 = bf16[8,2880]{1,0:T(8,128)(2,1)S(1)} fusion(bf16[4,2880]{1,0:T(4,128)(2,1)S(1)} %collective-permute-done, bf16[4,2880]{1,0:T(4,128)(2,1)} %param.7), kind=kLoop, calls=%fused_computation.6 | loop fusion | flops 92160 | bytes 92160 | tf_op jit(solution)/shard_map/concatenate | solution.py:203
  7.3 1.7 %collective-permute-start.2 = (bf16[8,2880]{1,0:T(8,128)(2,1)S(1)}, bf16[8,2880]{1,0:T(8,128)(2,1)S(1)}, u32[]{:S(2)}, u32[]{:S(2)}) collective-permute-start(bf16[8,2880]{1,0:T(8,128)(2,1)S(1)} %pad_maximum_fusion.2), channel_id=1, source_target_pairs={{0,5},{1,8},{2,11},{3,6},{4,13},{5,0},{6,3},{7,14},{8,1},{9,12},{1... | collective-permute-start | bytes 138248 | tf_op jit(solution)/shard_map/ppermute | solution.py:185
  9.0 0.0 copy-start
  9.0 1.6 %copy-done = bf16[384,2880]{0,1:T(8,128)(2,1)S(1)} copy-done((bf16[384,2880]{0,1:T(8,128)(2,1)S(1)}, bf16[384,2880]{0,1:T(8,128)(2,1)}, u32[]{:S(2)}) %copy-start) | copy-done | bytes 2211864
  10.7 0.0 copy-start.1
  10.7 1.6 %copy-done.1 = bf16[384,2880]{0,1:T(8,128)(2,1)S(1)} copy-done((bf16[384,2880]{0,1:T(8,128)(2,1)S(1)}, bf16[384,2880]{0,1:T(8,128)(2,1)}, u32[]{:S(2)}) %copy-start.1) | copy-done | bytes 2211864
  12.3 1.7 %moment.1 = (bf16[2880,384]{1,0:T(8,128)(2,1)S(1)}, bf16[2880,384]{1,0:T(8,128)(2,1)}) custom-call(bf16[2880,384]{1,0:T(8,128)(2,1)S(1)} %bitcast.7, bf16[2880,384]{1,0:T(8,128)(2,1)S(1)} %bitcast.10), custom_call_target="tpu_custom_call" | custom-call | tf_op jit(solution)/shard_map/moment/pallas_call | solution.py:50
  14.0 0.0 collective-permute-done.2
  14.0 1.3 %collective-permute-start.3 = (bf16[16,2880]{1,0:T(8,128)(2,1)S(1)}, bf16[16,2880]{1,0:T(8,128)(2,1)S(1)}, u32[]{:S(2)}, u32[]{:S(2)}) collective-permute-start(bf16[16,2880]{1,0:T(8,128)(2,1)S(1)} %pad_maximum_fusion.1), channel_id=1, source_target_pairs={{0,3},{1,4},{2,7},{3,0},{4,1},{5,6},{6,5},{7,2},{8,13},{9,10},{10,... | collective-permute-start | bytes 276488 | tf_op jit(solution)/shard_map/ppermute | solution.py:185
  15.4 2.7 %collective-permute-done.3 = bf16[16,2880]{1,0:T(8,128)(2,1)S(1)} collective-permute-done((bf16[16,2880]{1,0:T(8,128)(2,1)S(1)}, bf16[16,2880]{1,0:T(8,128)(2,1)S(1)}, u32[]{:S(2)}, u32[]{:S(2)}) %collective-permute-start.3) | collective-permute-done | bytes 92192 | tf_op jit(solution)/shard_map/ppermute | solution.py:185
  18.1 0.0 copy-start.2
  18.1 2.1 %power.1 = (f32[32,384]{1,0:T(8,128)S(1)}, f32[16,2880]{1,0:T(8,128)S(1)}, bf16[16,2880]{1,0:T(8,128)(2,1)S(1)}) custom-call(bf16[32,2880]{1,0:T(8,128)(2,1)S(1)} %constant_dynamic-update-slice_fusion.basis, bf16[2880,384]{1,0:T(8,128)(2,1)S(1)} %bitcast.8, bf16[2880,384]{1,0:T(8,128)(2,1)S(1)} %bitcast.11), custom_call_target="tpu_custom_call" | custom-call | tf_op jit(solution)/shard_map/power/pallas_call | solution.py:81
  20.2 1.2 %collective-permute-start.5 = (bf16[32,2880]{1,0:T(8,128)(2,1)S(1)}, bf16[32,2880]{1,0:T(8,128)(2,1)S(1)}, u32[]{:S(2)}, u32[]{:S(2)}) collective-permute-start(bf16[32,2880]{1,0:T(8,128)(2,1)S(1)} %constant_dynamic-update-slice_fusion.basis), channel_id=1, source_target_pairs={{0,1},{1,0},{2,3},{3,2},{4,5},{5,4},{6,7},{7,6},{8,9},{9,8},{10,11... | collective-permute-start | bytes 552968 | tf_op jit(solution)/shard_map/ppermute | solution.py:188
  21.4 1.2 %collective-permute-start.4 = (bf16[16,2880]{1,0:T(8,128)(2,1)S(1)}, bf16[16,2880]{1,0:T(8,128)(2,1)S(1)}, u32[]{:S(2)}, u32[]{:S(2)}) collective-permute-start(bf16[16,2880]{1,0:T(8,128)(2,1)S(1)} %get-tuple-element.37), channel_id=1, source_target_pairs={{0,3},{1,4},{2,7},{3,0},{4,1},{5,6},{6,5},{7,2},{8,13},{9,10},{10,... | collective-permute-start | bytes 276488 | tf_op jit(solution)/shard_map/ppermute | solution.py:185
  22.6 0.0 collective-permute-done.5
  22.7 2.7 %collective-permute-done.4 = bf16[16,2880]{1,0:T(8,128)(2,1)S(1)} collective-permute-done((bf16[16,2880]{1,0:T(8,128)(2,1)S(1)}, bf16[16,2880]{1,0:T(8,128)(2,1)S(1)}, u32[]{:S(2)}, u32[]{:S(2)}) %collective-permute-start.4) | collective-permute-done | bytes 92192 | tf_op jit(solution)/shard_map/ppermute | solution.py:185
  25.4 1.4 %collective-permute-start.6 = (bf16[8,2880]{1,0:T(8,128)(2,1)S(1)}, bf16[8,2880]{1,0:T(8,128)(2,1)S(1)}, u32[]{:S(2)}, u32[]{:S(2)}) collective-permute-start(bf16[8,2880]{1,0:T(8,128)(2,1)S(1)} %slice.24), channel_id=1, source_target_pairs={{0,5},{1,8},{2,11},{3,6},{4,13},{5,0},{6,3},{7,14},{8,1},{9,12},{1... | collective-permute-start | bytes 138248 | tf_op jit(solution)/shard_map/ppermute | solution.py:185
  26.8 0.0 copy-done.2
  26.8 1.5 %scale.1 = (bf16[64,384]{1,0:T(8,128)(2,1)S(1)}, f32[64,384]{1,0:T(8,128)}) custom-call(bf16[64,2880]{1,0:T(8,128)(2,1)S(1)} %pad_maximum_fusion.basis, bf16[2880,384]{1,0:T(8,128)(2,1)S(1)} %bitcast.9, bf16[2880,384]{1,0:T(8,128)(2,1)S(1)} %get-tuple-element.44.moment, f32[32,384]{1,0:T(8,128)S(1)} %get-tuple-element.45.rot_half, f32[64,384]{1,0:T(8,128)S(1)} %bitcast.12), custom_call_target="tpu_custom_call" | custom-call | tf_op jit(solution)/shard_map/scale/pallas_call | solution.py:136
  28.4 0.6 %collective-permute-done.6 = bf16[8,2880]{1,0:T(8,128)(2,1)S(1)} collective-permute-done((bf16[8,2880]{1,0:T(8,128)(2,1)S(1)}, bf16[8,2880]{1,0:T(8,128)(2,1)S(1)}, u32[]{:S(2)}, u32[]{:S(2)}) %collective-permute-start.6) | collective-permute-done | bytes 46112 | tf_op jit(solution)/shard_map/ppermute | solution.py:185
  29.0 1.9 %collective-permute-start.7 = (bf16[4,2880]{1,0:T(4,128)(2,1)S(1)}, bf16[4,2880]{1,0:T(4,128)(2,1)S(1)}, u32[]{:S(2)}, u32[]{:S(2)}) collective-permute-start(bf16[4,2880]{1,0:T(4,128)(2,1)S(1)} %slice.25), channel_id=1, source_target_pairs={{0,9},{1,2},{2,1},{3,10},{4,7},{5,12},{6,15},{7,4},{8,11},{9,0},{1... | collective-permute-start | bytes 69128 | tf_op jit(solution)/shard_map/ppermute | solution.py:185
  30.9 1.7 %update.1 = bf16[2880,384]{1,0:T(8,128)(2,1)} custom-call(bf16[64,2880]{1,0:T(8,128)(2,1)S(1)} %pad_maximum_fusion.basis, bf16[64,384]{1,0:T(8,128)(2,1)S(1)} %get-tuple-element.50.scaled), custom_call_target="tpu_custom_call" | custom-call | tf_op jit(solution)/shard_map/update/pallas_call | solution.py:164
  32.6 0.6 %collective-permute-done.7 = bf16[4,2880]{1,0:T(4,128)(2,1)S(1)} collective-permute-done((bf16[4,2880]{1,0:T(4,128)(2,1)S(1)}, bf16[4,2880]{1,0:T(4,128)(2,1)S(1)}, u32[]{:S(2)}, u32[]{:S(2)}) %collective-permute-start.7) | collective-permute-done | bytes 23072 | tf_op jit(solution)/shard_map/ppermute | solution.py:185
  33.2 0.1 multiply_reduce_fusion
  33.4 0.7 %fusion = f32[4,2880]{1,0:T(4,128)} fusion(f32[4,2880]{1,0:T(4,128)S(1)} %slice.21, bf16[4,2880]{1,0:T(4,128)(2,1)S(1)} %collective-permute-done.7, f32[4]{0:T(128)S(1)} %add_sqrt_fusion), kind=kLoop, calls=%fused_computation.9 | loop fusion | flops 34560 | bytes 115216 | tf_op jit(solution)/shard_map/div | solution.py:227
  (12 shorter events, 0.1 us)
Async XLA Ops:
  0.6 5.9 %collective-permute-start.1 = (bf16[384,2880]{0,1:T(8,128)(2,1)}, bf16[384,2880]{0,1:T(8,128)(2,1)S(1)}, u32[]{:S(2)}, u32[]{:S(2)}) collective-permute-start(bf16[384,2880]{0,1:T(8,128)(2,1)} %param.4), channel_id=1, source_target_pairs={{0,1},{1,0},{2,3},{3,2},{4,5},{5,4},{6,7},{7,6},{8,9},{9,8},{10,11... | collective-permute-start | bytes 6635528 | tf_op jit(solution)/shard_map/ppermute | solution.py:188
  1.1 5.4 %collective-permute-start = (bf16[4,2880]{1,0:T(4,128)(2,1)}, bf16[4,2880]{1,0:T(4,128)(2,1)S(1)}, u32[]{:S(2)}, u32[]{:S(2)}) collective-permute-start(bf16[4,2880]{1,0:T(4,128)(2,1)} %param.7), channel_id=1, source_target_pairs={{0,9},{1,2},{2,1},{3,10},{4,7},{5,12},{6,15},{7,4},{8,11},{9,0},{1... | collective-permute-start | bytes 69128 | tf_op jit(solution)/shard_map/ppermute | solution.py:185
  7.3 6.6 %collective-permute-start.2 = (bf16[8,2880]{1,0:T(8,128)(2,1)S(1)}, bf16[8,2880]{1,0:T(8,128)(2,1)S(1)}, u32[]{:S(2)}, u32[]{:S(2)}) collective-permute-start(bf16[8,2880]{1,0:T(8,128)(2,1)S(1)} %pad_maximum_fusion.2), channel_id=1, source_target_pairs={{0,5},{1,8},{2,11},{3,6},{4,13},{5,0},{6,3},{7,14},{8,1},{9,12},{1... | collective-permute-start | bytes 138248 | tf_op jit(solution)/shard_map/ppermute | solution.py:185
  9.0 1.6 %copy-start = (bf16[384,2880]{0,1:T(8,128)(2,1)S(1)}, bf16[384,2880]{0,1:T(8,128)(2,1)}, u32[]{:S(2)}) copy-start(bf16[384,2880]{0,1:T(8,128)(2,1)} %param.4) | copy-start | bytes 6635524
  10.7 1.6 %copy-start.1 = (bf16[384,2880]{0,1:T(8,128)(2,1)S(1)}, bf16[384,2880]{0,1:T(8,128)(2,1)}, u32[]{:S(2)}) copy-start(bf16[384,2880]{0,1:T(8,128)(2,1)} %param.5) | copy-start | bytes 6635524
  14.0 4.1 %collective-permute-start.3 = (bf16[16,2880]{1,0:T(8,128)(2,1)S(1)}, bf16[16,2880]{1,0:T(8,128)(2,1)S(1)}, u32[]{:S(2)}, u32[]{:S(2)}) collective-permute-start(bf16[16,2880]{1,0:T(8,128)(2,1)S(1)} %pad_maximum_fusion.1), channel_id=1, source_target_pairs={{0,3},{1,4},{2,7},{3,0},{4,1},{5,6},{6,5},{7,2},{8,13},{9,10},{10,... | collective-permute-start | bytes 276488 | tf_op jit(solution)/shard_map/ppermute | solution.py:185
  18.1 8.7 %copy-start.2 = (f32[384,64]{0,1:T(8,128)S(1)}, f32[384,64]{0,1:T(8,128)}, u32[]{:S(2)}) copy-start(f32[384,64]{0,1:T(8,128)} %param.6) | copy-start | bytes 294916
  20.2 2.4 %collective-permute-start.5 = (bf16[32,2880]{1,0:T(8,128)(2,1)S(1)}, bf16[32,2880]{1,0:T(8,128)(2,1)S(1)}, u32[]{:S(2)}, u32[]{:S(2)}) collective-permute-start(bf16[32,2880]{1,0:T(8,128)(2,1)S(1)} %constant_dynamic-update-slice_fusion.basis), channel_id=1, source_target_pairs={{0,1},{1,0},{2,3},{3,2},{4,5},{5,4},{6,7},{7,6},{8,9},{9,8},{10,11... | collective-permute-start | bytes 552968 | tf_op jit(solution)/shard_map/ppermute | solution.py:188
  21.4 4.0 %collective-permute-start.4 = (bf16[16,2880]{1,0:T(8,128)(2,1)S(1)}, bf16[16,2880]{1,0:T(8,128)(2,1)S(1)}, u32[]{:S(2)}, u32[]{:S(2)}) collective-permute-start(bf16[16,2880]{1,0:T(8,128)(2,1)S(1)} %get-tuple-element.37), channel_id=1, source_target_pairs={{0,3},{1,4},{2,7},{3,0},{4,1},{5,6},{6,5},{7,2},{8,13},{9,10},{10,... | collective-permute-start | bytes 276488 | tf_op jit(solution)/shard_map/ppermute | solution.py:185
  25.4 3.6 %collective-permute-start.6 = (bf16[8,2880]{1,0:T(8,128)(2,1)S(1)}, bf16[8,2880]{1,0:T(8,128)(2,1)S(1)}, u32[]{:S(2)}, u32[]{:S(2)}) collective-permute-start(bf16[8,2880]{1,0:T(8,128)(2,1)S(1)} %slice.24), channel_id=1, source_target_pairs={{0,5},{1,8},{2,11},{3,6},{4,13},{5,0},{6,3},{7,14},{8,1},{9,12},{1... | collective-permute-start | bytes 138248 | tf_op jit(solution)/shard_map/ppermute | solution.py:185
  29.0 4.2 %collective-permute-start.7 = (bf16[4,2880]{1,0:T(4,128)(2,1)S(1)}, bf16[4,2880]{1,0:T(4,128)(2,1)S(1)}, u32[]{:S(2)}, u32[]{:S(2)}) collective-permute-start(bf16[4,2880]{1,0:T(4,128)(2,1)S(1)} %slice.25), channel_id=1, source_target_pairs={{0,9},{1,2},{2,1},{3,10},{4,7},{5,12},{6,15},{7,4},{8,11},{9,0},{1... | collective-permute-start | bytes 69128 | tf_op jit(solution)/shard_map/ppermute | solution.py:185

commit v5 on v4

--- a/solution.py
+++ b/solution.py
@@ -30,6 +30,31 @@
 
 def dot(left, right, dims):
     return lax.dot_general(left, right, (dims, ((), ())), preferred_element_type=jnp.float32)
+
+
+def load_kernel(*refs):
+    count = len(refs) // 2
+    sems = refs[-1]
+    copies = [
+        pltpu.make_async_copy(refs[i], refs[count + i], sems.at[i]) for i in range(count)
+    ]
+    for copy in copies:
+        copy.start()
+    for copy in copies:
+        copy.wait()
+
+
+def load(*values):
+    out = pl.pallas_call(
+        load_kernel,
+        in_specs=[pl.BlockSpec(memory_space=pltpu.HBM)] * len(values),
+        out_specs=[INSIDE] * len(values),
+        out_shape=[pltpu.VMEM(value.shape, value.dtype) for value in values],
+        scratch_shapes=[pltpu.SemaphoreType.DMA((len(values),))],
+        compiler_params=PARAMS,
+        name="load",
+    )(*[pltpu.with_memory_space_constraint(value, pltpu.HBM) for value in values])
+    return out
 
 
 def moment_kernel(grad, moment, held, stored, sems):
@@ -188,25 +213,28 @@
         return lax.ppermute(value, "rows", [(i, i ^ 1) for i in range(n)])
 
     grad, moment, second = grad.T, moment.T, second.T
-    other = across(grad.T).T
-
-    held = basis
-    for step in range(bits):
-        if step == 1:
+
+    come = exchange(basis, 0)
+    grad, held = load(grad, basis)
+    come, grad, held = tie(come, grad, held)
+    other = across(grad)
+    held = jnp.concatenate([held, come], 0)
+    for step in range(1, bits):
+        if step == bits - 1:
             held, moment = tie(held, moment)
         come = exchange(held, step)
-        if step == 0:
-            come, other = tie(come, other)
-        if step == 1:
-            moment_in, moment_next = new_moment(grad, moment)
-            come, moment_in, moment_next = tie(come, moment_in, moment_next)
+        if step == bits - 1:
+            (moment,) = load(moment)
+            come, moment, other = tie(come, moment, other)
         held = jnp.concatenate([held, come], 0)
 
     rot_half, kept, sent = power_products(held, grad, other)
     come = exchange(sent, bits - 1)
-    held, _ = tie(held, sent)
-    whole = jnp.concatenate([held, across(held)], 0)
-    come, whole = tie(come, whole)
+    moment, _ = tie(moment, sent)
+    moment_in, moment_next = new_moment(grad, moment)
+    held, _ = tie(held, moment_in)
+    theirs = across(held)
+    come, moment_in, moment_next = tie(come, moment_in, moment_next)
     for step in reversed(range(bits)):
         kept = kept + come.astype(jnp.float32)
         if step == 0:
@@ -215,7 +243,8 @@
         come = exchange(kept[half:].astype(jnp.bfloat16), step - 1)
         kept = kept[:half]
         if step == bits - 1:
-            whole, kept = tie(whole, kept)
+            theirs, kept = tie(theirs, kept)
+            whole = jnp.concatenate([held, theirs], 0)
             scaled, second_next = scaled_rotation(
                 orders, own, whole, grad, moment_in, rot_half, second
             )

time: 34.3 us -> 30.9 us (0.901)
  waiting for transfers between devices: 8.38 us -> 4.1 us
  Pallas kernels: 7.03 us -> 10.3 us
  local copies, waits for them, and re-layouts: 3.31 us -> 0.09 us
  starting transfers between devices: 12.9 us -> 14.5 us
  other arithmetic: 1.7 us -> 0.98 us
    ppermute x6, waiting for transfers between devices: 8.37 us -> 3.54 us  [exchange(): return lax.ppermute(value, 'rows', pairs)]
    pallas_call x0 -> x2, Pallas kernels: none -> 3.27 us  [load(): pl.pallas_call(load_kernel, in_specs=[pl.BlockSpec(memory_space=pltpu.HBM...]
    unnamed x8 -> x4, local copies, waits for them, and re-layouts: 3.27 us -> 0.02 us
    ppermute x6, starting transfers between devices: 11.2 us -> 12.8 us  [exchange(): return lax.ppermute(value, 'rows', pairs)]
    concatenate x2, other arithmetic: 0.78 us -> 0.08 us  [shards(): held = jnp.concatenate([held, come], 0)]
    ppermute x2, waiting for transfers between devices: 0.01 us -> 0.56 us  [across(): return lax.ppermute(value, 'rows', [(i, i ^ 1) for i in range(n)])]
  transfers between devices with their start and end apart: 8 -> 8, of which waited for: 5 -> 5; matrix products, arithmetic and copies ran while one was open for 0% -> 1% of each run, Pallas kernels for 15% -> 27%
where the time goes in v5:
time: 30.9 us; the launch traced here: 30.7 us
  starting transfers between devices  14.5 us (47%)
  Pallas kernels  10.3 us (33%)
  waiting for transfers between devices  4.1 us (13%)
  other arithmetic  0.98 us (3%)
  between operations  0.74 us (2%)
    ppermute x6, starting transfers between devices, exchange(): return lax.ppermute(value, 'rows', pairs)  12.8 us
    ppermute x6, waiting for transfers between devices, exchange(): return lax.ppermute(value, 'rows', pairs)  3.54 us
    pallas_call x2, Pallas kernels, load(): pl.pallas_call(load_kernel, in_specs=[pl.BlockSpec(memory_space=pltpu.HBM...  3.27 us
    pallas_call x1, Pallas kernels, power_products(): pl.pallas_call(power_kernel, in_specs=[INSIDE] * 3, out_specs=[INSIDE] *...  2.07 us
    pallas_call x1, Pallas kernels, new_update(): pl.pallas_call(update_kernel, in_specs=[INSIDE] * 2, out_specs=ANYWHERE,...  1.71 us
    ppermute x2, starting transfers between devices, across(): return lax.ppermute(value, 'rows', [(i, i ^ 1) for i in range(n)])  1.71 us
    pallas_call x1, Pallas kernels, new_moment(): pl.pallas_call(moment_kernel, in_specs=[INSIDE, INSIDE], out_specs=[INSID...  1.7 us
    pallas_call x1, Pallas kernels, scaled_rotation(): pl.pallas_call(functools.partial(scale_kernel, orders, own), in_specs=[IN...  1.54 us
  transfers between devices with their start and end apart: 8, of which 5 were waited for; matrix products, arithmetic and copies ran while one was open for 1% of the time, Pallas kernels for 27%

profile of v5, /device:TPU:0, one launch (start us, length us, event | category | flops | bytes accessed | tf_op | source)
XLA Modules:
  0.0 30.7 jit_solution(6874022269118265406)
XLA Ops:
  0.6 3.5 %collective-permute-start = (bf16[4,2880]{1,0:T(4,128)(2,1)}, bf16[4,2880]{1,0:T(4,128)(2,1)S(1)}, u32[]{:S(2)}, u32[]{:S(2)}) collective-permute-start(bf16[4,2880]{1,0:T(4,128)(2,1)} %refs_1_.1), channel_id=1, source_target_pairs={{0,9},{1,2},{2,1},{3,10},{4,7},{5,12},{6,15},{7,4},{8,11},{9,0},{1... | collective-permute-start | bytes 69128 | tf_op jit(solution)/shard_map/ppermute | solution.py:210
  4.2 1.6 %load.2 = (bf16[2880,384]{1,0:T(8,128)(2,1)S(1)}, bf16[4,2880]{1,0:T(4,128)(2,1)S(1)}) custom-call(bf16[2880,384]{1,0:T(8,128)(2,1)} %bitcast.8, bf16[4,2880]{1,0:T(4,128)(2,1)} %refs_1_.1), custom_call_target="tpu_custom_call" | custom-call | tf_op jit(solution)/shard_map/load/pallas_call | solution.py:48
  5.8 0.1 collective-permute-done
  5.9 0.0 collective-permute-start.3
  5.9 1.9 %collective-permute-start.1 = (bf16[8,2880]{1,0:T(8,128)(2,1)S(1)}, bf16[8,2880]{1,0:T(8,128)(2,1)S(1)}, u32[]{:S(2)}, u32[]{:S(2)}) collective-permute-start(bf16[8,2880]{1,0:T(8,128)(2,1)S(1)} %pad_maximum_fusion.1), channel_id=1, source_target_pairs={{0,5},{1,8},{2,11},{3,6},{4,13},{5,0},{6,3},{7,14},{8,1},{9,12},{1... | collective-permute-start | bytes 138248 | tf_op jit(solution)/shard_map/ppermute | solution.py:210
  7.9 1.8 %collective-permute-done.1 = bf16[8,2880]{1,0:T(8,128)(2,1)S(1)} collective-permute-done((bf16[8,2880]{1,0:T(8,128)(2,1)S(1)}, bf16[8,2880]{1,0:T(8,128)(2,1)S(1)}, u32[]{:S(2)}, u32[]{:S(2)}) %collective-permute-start.1) | collective-permute-done | bytes 46112 | tf_op jit(solution)/shard_map/ppermute | solution.py:210
  9.7 1.7 %collective-permute-start.2 = (bf16[16,2880]{1,0:T(8,128)(2,1)S(1)}, bf16[16,2880]{1,0:T(8,128)(2,1)S(1)}, u32[]{:S(2)}, u32[]{:S(2)}) collective-permute-start(bf16[16,2880]{1,0:T(8,128)(2,1)S(1)} %pad_maximum_fusion), channel_id=1, source_target_pairs={{0,3},{1,4},{2,7},{3,0},{4,1},{5,6},{6,5},{7,2},{8,13},{9,10},{10,... | collective-permute-start | bytes 276488 | tf_op jit(solution)/shard_map/ppermute | solution.py:210
  11.4 1.6 %load.3.moment = bf16[2880,384]{1,0:T(8,128)(2,1)S(1)} custom-call(bf16[2880,384]{1,0:T(8,128)(2,1)} %bitcast.9), custom_call_target="tpu_custom_call" | custom-call | tf_op jit(solution)/shard_map/load/pallas_call | solution.py:48
  13.0 0.7 %collective-permute-done.2 = bf16[16,2880]{1,0:T(8,128)(2,1)S(1)} collective-permute-done((bf16[16,2880]{1,0:T(8,128)(2,1)S(1)}, bf16[16,2880]{1,0:T(8,128)(2,1)S(1)}, u32[]{:S(2)}, u32[]{:S(2)}) %collective-permute-start.2) | collective-permute-done | bytes 92192 | tf_op jit(solution)/shard_map/ppermute | solution.py:210
  13.7 0.0 collective-permute-done.3.other
  13.8 2.1 %power.1 = (f32[32,384]{1,0:T(8,128)S(1)}, f32[16,2880]{1,0:T(8,128)S(1)}, bf16[16,2880]{1,0:T(8,128)(2,1)S(1)}) custom-call(bf16[32,2880]{1,0:T(8,128)(2,1)S(1)} %constant_dynamic-update-slice_fusion.basis, bf16[2880,384]{1,0:T(8,128)(2,1)S(1)} %get-tuple-element.41.grad, bf16[2880,384]{1,0:T(8,128)(2,1)S(1)} %collective-permute-done.3.other), custom_call_target="tpu_custom_call" | custom-call | tf_op jit(solution)/shard_map/power/pallas_call | solution.py:106
  15.8 0.0 copy-start
  15.8 2.0 %collective-permute-start.5 = (bf16[16,2880]{1,0:T(8,128)(2,1)S(1)}, bf16[16,2880]{1,0:T(8,128)(2,1)S(1)}, u32[]{:S(2)}, u32[]{:S(2)}) collective-permute-start(bf16[16,2880]{1,0:T(8,128)(2,1)S(1)} %get-tuple-element.45), channel_id=1, source_target_pairs={{0,3},{1,4},{2,7},{3,0},{4,1},{5,6},{6,5},{7,2},{8,13},{9,10},{10,... | collective-permute-start | bytes 276488 | tf_op jit(solution)/shard_map/ppermute | solution.py:210
  17.8 1.7 %moment.1 = (bf16[2880,384]{1,0:T(8,128)(2,1)S(1)}, bf16[2880,384]{1,0:T(8,128)(2,1)}) custom-call(bf16[2880,384]{1,0:T(8,128)(2,1)S(1)} %get-tuple-element.41.grad, bf16[2880,384]{1,0:T(8,128)(2,1)S(1)} %load.3.moment), custom_call_target="tpu_custom_call" | custom-call | tf_op jit(solution)/shard_map/moment/pallas_call | solution.py:75
  19.5 1.7 %collective-permute-start.4 = (bf16[32,2880]{1,0:T(8,128)(2,1)S(1)}, bf16[32,2880]{1,0:T(8,128)(2,1)S(1)}, u32[]{:S(2)}, u32[]{:S(2)}) collective-permute-start(bf16[32,2880]{1,0:T(8,128)(2,1)S(1)} %constant_dynamic-update-slice_fusion.basis), channel_id=1, source_target_pairs={{0,1},{1,0},{2,3},{3,2},{4,5},{5,4},{6,7},{7,6},{8,9},{9,8},{10,11... | collective-permute-start | bytes 552968 | tf_op jit(solution)/shard_map/ppermute | solution.py:213
  21.2 0.0 collective-permute-done.5
  21.3 0.4 %collective-permute-start.6 = (bf16[8,2880]{1,0:T(8,128)(2,1)S(1)}, bf16[8,2880]{1,0:T(8,128)(2,1)S(1)}, u32[]{:S(2)}, u32[]{:S(2)}) collective-permute-start(bf16[8,2880]{1,0:T(8,128)(2,1)S(1)} %slice.24), channel_id=1, source_target_pairs={{0,5},{1,8},{2,11},{3,6},{4,13},{5,0},{6,3},{7,14},{8,1},{9,12},{1... | collective-permute-start | bytes 138248 | tf_op jit(solution)/shard_map/ppermute | solution.py:210
  21.7 0.6 %collective-permute-done.4 = bf16[32,2880]{1,0:T(8,128)(2,1)S(1)} collective-permute-done((bf16[32,2880]{1,0:T(8,128)(2,1)S(1)}, bf16[32,2880]{1,0:T(8,128)(2,1)S(1)}, u32[]{:S(2)}, u32[]{:S(2)}) %collective-permute-start.4) | collective-permute-done | bytes 184352 | tf_op jit(solution)/shard_map/ppermute | solution.py:213
  22.3 0.0 copy-done
  22.3 1.5 %scale.1 = (bf16[64,384]{1,0:T(8,128)(2,1)S(1)}, f32[64,384]{1,0:T(8,128)}) custom-call(bf16[64,2880]{1,0:T(8,128)(2,1)S(1)} %constant_dynamic-update-slice_fusion.2.basis, bf16[2880,384]{1,0:T(8,128)(2,1)S(1)} %get-tuple-element.41.grad, bf16[2880,384]{1,0:T(8,128)(2,1)S(1)} %get-tuple-element.54.moment, f32[32,384]{1,0:T(8,128)S(1)} %get-tuple-element.55.rot_half, ...), custom_call_target="tpu_custom_call" | custom-call | tf_op jit(solution)/shard_map/scale/pallas_call | solution.py:161
  23.8 1.0 %collective-permute-done.6 = bf16[8,2880]{1,0:T(8,128)(2,1)S(1)} collective-permute-done((bf16[8,2880]{1,0:T(8,128)(2,1)S(1)}, bf16[8,2880]{1,0:T(8,128)(2,1)S(1)}, u32[]{:S(2)}, u32[]{:S(2)}) %collective-permute-start.6) | collective-permute-done | bytes 46112 | tf_op jit(solution)/shard_map/ppermute | solution.py:210
  24.9 3.2 %collective-permute-start.7 = (bf16[4,2880]{1,0:T(4,128)(2,1)S(1)}, bf16[4,2880]{1,0:T(4,128)(2,1)S(1)}, u32[]{:S(2)}, u32[]{:S(2)}) collective-permute-start(bf16[4,2880]{1,0:T(4,128)(2,1)S(1)} %slice.25), channel_id=1, source_target_pairs={{0,9},{1,2},{2,1},{3,10},{4,7},{5,12},{6,15},{7,4},{8,11},{9,0},{1... | collective-permute-start | bytes 69128 | tf_op jit(solution)/shard_map/ppermute | solution.py:210
  28.1 1.7 %update.1 = bf16[2880,384]{1,0:T(8,128)(2,1)} custom-call(bf16[64,2880]{1,0:T(8,128)(2,1)S(1)} %constant_dynamic-update-slice_fusion.2.basis, bf16[64,384]{1,0:T(8,128)(2,1)S(1)} %get-tuple-element.60.scaled), custom_call_target="tpu_custom_call" | custom-call | tf_op jit(solution)/shard_map/update/pallas_call | solution.py:189
  29.8 0.0 collective-permute-done.7
  29.9 0.1 multiply_reduce_fusion
  30.0 0.7 %fusion = f32[4,2880]{1,0:T(4,128)} fusion(f32[4,2880]{1,0:T(4,128)S(1)} %slice.21, bf16[4,2880]{1,0:T(4,128)(2,1)S(1)} %collective-permute-done.7, f32[4]{0:T(128)S(1)} %add_sqrt_fusion), kind=kLoop, calls=%fused_computation.8 | loop fusion | flops 34560 | bytes 115216 | tf_op jit(solution)/shard_map/div | solution.py:256
  (13 shorter events, 0.2 us)
Async XLA Ops:
  0.6 5.3 %collective-permute-start = (bf16[4,2880]{1,0:T(4,128)(2,1)}, bf16[4,2880]{1,0:T(4,128)(2,1)S(1)}, u32[]{:S(2)}, u32[]{:S(2)}) collective-permute-start(bf16[4,2880]{1,0:T(4,128)(2,1)} %refs_1_.1), channel_id=1, source_target_pairs={{0,9},{1,2},{2,1},{3,10},{4,7},{5,12},{6,15},{7,4},{8,11},{9,0},{1... | collective-permute-start | bytes 69128 | tf_op jit(solution)/shard_map/ppermute | solution.py:210
  5.9 7.8 %collective-permute-start.3 = (bf16[2880,384]{1,0:T(8,128)(2,1)S(1)}, bf16[2880,384]{1,0:T(8,128)(2,1)S(1)}, u32[]{:S(2)}, u32[]{:S(2)}) collective-permute-start(bf16[2880,384]{1,0:T(8,128)(2,1)S(1)} %get-tuple-element.41.grad), channel_id=1, source_target_pairs={{0,1},{1,0},{2,3},{3,2},{4,5},{5,4},{6,7},{7,6},{8,9},{9,8},{10,11... | collective-permute-start | bytes 6635528 | tf_op jit(solution)/shard_map/ppermute | solution.py:213
  5.9 3.7 %collective-permute-start.1 = (bf16[8,2880]{1,0:T(8,128)(2,1)S(1)}, bf16[8,2880]{1,0:T(8,128)(2,1)S(1)}, u32[]{:S(2)}, u32[]{:S(2)}) collective-permute-start(bf16[8,2880]{1,0:T(8,128)(2,1)S(1)} %pad_maximum_fusion.1), channel_id=1, source_target_pairs={{0,5},{1,8},{2,11},{3,6},{4,13},{5,0},{6,3},{7,14},{8,1},{9,12},{1... | collective-permute-start | bytes 138248 | tf_op jit(solution)/shard_map/ppermute | solution.py:210
  9.7 4.1 %collective-permute-start.2 = (bf16[16,2880]{1,0:T(8,128)(2,1)S(1)}, bf16[16,2880]{1,0:T(8,128)(2,1)S(1)}, u32[]{:S(2)}, u32[]{:S(2)}) collective-permute-start(bf16[16,2880]{1,0:T(8,128)(2,1)S(1)} %pad_maximum_fusion), channel_id=1, source_target_pairs={{0,3},{1,4},{2,7},{3,0},{4,1},{5,6},{6,5},{7,2},{8,13},{9,10},{10,... | collective-permute-start | bytes 276488 | tf_op jit(solution)/shard_map/ppermute | solution.py:210
  15.8 6.5 %copy-start = (f32[384,64]{0,1:T(8,128)S(1)}, f32[384,64]{0,1:T(8,128)}, u32[]{:S(2)}) copy-start(f32[384,64]{0,1:T(8,128)} %param.6) | copy-start | bytes 294916
  15.8 5.4 %collective-permute-start.5 = (bf16[16,2880]{1,0:T(8,128)(2,1)S(1)}, bf16[16,2880]{1,0:T(8,128)(2,1)S(1)}, u32[]{:S(2)}, u32[]{:S(2)}) collective-permute-start(bf16[16,2880]{1,0:T(8,128)(2,1)S(1)} %get-tuple-element.45), channel_id=1, source_target_pairs={{0,3},{1,4},{2,7},{3,0},{4,1},{5,6},{6,5},{7,2},{8,13},{9,10},{10,... | collective-permute-start | bytes 276488 | tf_op jit(solution)/shard_map/ppermute | solution.py:210
  19.5 2.8 %collective-permute-start.4 = (bf16[32,2880]{1,0:T(8,128)(2,1)S(1)}, bf16[32,2880]{1,0:T(8,128)(2,1)S(1)}, u32[]{:S(2)}, u32[]{:S(2)}) collective-permute-start(bf16[32,2880]{1,0:T(8,128)(2,1)S(1)} %constant_dynamic-update-slice_fusion.basis), channel_id=1, source_target_pairs={{0,1},{1,0},{2,3},{3,2},{4,5},{5,4},{6,7},{7,6},{8,9},{9,8},{10,11... | collective-permute-start | bytes 552968 | tf_op jit(solution)/shard_map/ppermute | solution.py:213
  21.3 3.6 %collective-permute-start.6 = (bf16[8,2880]{1,0:T(8,128)(2,1)S(1)}, bf16[8,2880]{1,0:T(8,128)(2,1)S(1)}, u32[]{:S(2)}, u32[]{:S(2)}) collective-permute-start(bf16[8,2880]{1,0:T(8,128)(2,1)S(1)} %slice.24), channel_id=1, source_target_pairs={{0,5},{1,8},{2,11},{3,6},{4,13},{5,0},{6,3},{7,14},{8,1},{9,12},{1... | collective-permute-start | bytes 138248 | tf_op jit(solution)/shard_map/ppermute | solution.py:210
  24.9 5.0 %collective-permute-start.7 = (bf16[4,2880]{1,0:T(4,128)(2,1)S(1)}, bf16[4,2880]{1,0:T(4,128)(2,1)S(1)}, u32[]{:S(2)}, u32[]{:S(2)}) collective-permute-start(bf16[4,2880]{1,0:T(4,128)(2,1)S(1)} %slice.25), channel_id=1, source_target_pairs={{0,9},{1,2},{2,1},{3,10},{4,7},{5,12},{6,15},{7,4},{8,11},{9,0},{1... | collective-permute-start | bytes 69128 | tf_op jit(solution)/shard_map/ppermute | solution.py:210

commit v6 on v5

--- a/solution.py
+++ b/solution.py
@@ -203,7 +203,8 @@
 def shards(n, grad, moment, second, basis):
     bits = n.bit_length() - 2
     own = basis.shape[0]
-    orders = (tuple(reversed(range(bits))), (0,) + tuple(reversed(range(1, bits))))
+    far, near = (bits - 1,), tuple(reversed(range(bits - 1)))
+    orders = (far + near, far + near[-1:] + near[:-1])
 
     def exchange(value, step):
         pairs = [(i, i ^ (2 << orders[odd(i)][step]) ^ 1) for i in range(n)]

time: 30.9 us -> 29.8 us (0.964)
  starting transfers between devices: 14.5 us -> 13.9 us
  waiting for transfers between devices: 4.1 us -> 3.63 us
    ppermute x2, starting transfers between devices: 1.71 us -> 0.87 us  [across(): return lax.ppermute(value, 'rows', [(i, i ^ 1) for i in range(n)])]
    ppermute x2, waiting for transfers between devices: 0.56 us -> 0.01 us  [across(): return lax.ppermute(value, 'rows', [(i, i ^ 1) for i in range(n)])]
  transfers between devices with their start and end apart: 8 -> 8, of which waited for: 5 -> 5; matrix products, arithmetic and copies ran while one was open for 1% -> 1% of each run, Pallas kernels for 27% -> 28%
where the time goes in v6:
time: 29.8 us; the launch traced here: 29.6 us
  starting transfers between devices  13.9 us (47%)
  Pallas kernels  10.3 us (35%)
  waiting for transfers between devices  3.63 us (12%)
  other arithmetic  0.97 us (3%)
  between operations  0.72 us (2%)
    ppermute x6, starting transfers between devices, exchange(): return lax.ppermute(value, 'rows', pairs)  13 us
    ppermute x6, waiting for transfers between devices, exchange(): return lax.ppermute(value, 'rows', pairs)  3.62 us
    pallas_call x2, Pallas kernels, load(): pl.pallas_call(load_kernel, in_specs=[pl.BlockSpec(memory_space=pltpu.HBM...  3.27 us
    pallas_call x1, Pallas kernels, power_products(): pl.pallas_call(power_kernel, in_specs=[INSIDE] * 3, out_specs=[INSIDE] *...  2.08 us
    pallas_call x1, Pallas kernels, new_update(): pl.pallas_call(update_kernel, in_specs=[INSIDE] * 2, out_specs=ANYWHERE,...  1.72 us
    pallas_call x1, Pallas kernels, new_moment(): pl.pallas_call(moment_kernel, in_specs=[INSIDE, INSIDE], out_specs=[INSID...  1.7 us
    pallas_call x1, Pallas kernels, scaled_rotation(): pl.pallas_call(functools.partial(scale_kernel, orders, own), in_specs=[IN...  1.54 us
    ppermute x2, starting transfers between devices, across(): return lax.ppermute(value, 'rows', [(i, i ^ 1) for i in range(n)])  0.87 us
  transfers between devices with their start and end apart: 8, of which 5 were waited for; matrix products, arithmetic and copies ran while one was open for 1% of the time, Pallas kernels for 28%

profile of v6, /device:TPU:0, one launch (start us, length us, event | category | flops | bytes accessed | tf_op | source)
XLA Modules:
  0.0 29.6 jit_solution(15428718565826887912)
XLA Ops:
  0.6 3.5 %collective-permute-start = (bf16[4,2880]{1,0:T(4,128)(2,1)}, bf16[4,2880]{1,0:T(4,128)(2,1)S(1)}, u32[]{:S(2)}, u32[]{:S(2)}) collective-permute-start(bf16[4,2880]{1,0:T(4,128)(2,1)} %refs_1_.1), channel_id=1, source_target_pairs={{0,9},{1,8},{2,11},{3,10},{4,13},{5,12},{6,15},{7,14},{8,1},{9,0},... | collective-permute-start | bytes 69128 | tf_op jit(solution)/shard_map/ppermute | solution.py:211
  4.2 1.6 %load.2 = (bf16[2880,384]{1,0:T(8,128)(2,1)S(1)}, bf16[4,2880]{1,0:T(4,128)(2,1)S(1)}) custom-call(bf16[2880,384]{1,0:T(8,128)(2,1)} %bitcast.8, bf16[4,2880]{1,0:T(4,128)(2,1)} %refs_1_.1), custom_call_target="tpu_custom_call" | custom-call | tf_op jit(solution)/shard_map/load/pallas_call | solution.py:48
  5.8 0.1 collective-permute-done
  6.0 0.6 %collective-permute-start.3 = (bf16[2880,384]{1,0:T(8,128)(2,1)S(1)}, bf16[2880,384]{1,0:T(8,128)(2,1)S(1)}, u32[]{:S(2)}, u32[]{:S(2)}) collective-permute-start(bf16[2880,384]{1,0:T(8,128)(2,1)S(1)} %get-tuple-element.41.grad), channel_id=1, source_target_pairs={{0,1},{1,0},{2,3},{3,2},{4,5},{5,4},{6,7},{7,6},{8,9},{9,8},{10,11... | collective-permute-start | bytes 6635528 | tf_op jit(solution)/shard_map/ppermute | solution.py:214
  6.6 1.7 %collective-permute-start.1 = (bf16[8,2880]{1,0:T(8,128)(2,1)S(1)}, bf16[8,2880]{1,0:T(8,128)(2,1)S(1)}, u32[]{:S(2)}, u32[]{:S(2)}) collective-permute-start(bf16[8,2880]{1,0:T(8,128)(2,1)S(1)} %pad_maximum_fusion.1), channel_id=1, source_target_pairs={{0,5},{1,2},{2,1},{3,6},{4,7},{5,0},{6,3},{7,4},{8,11},{9,12},{10,... | collective-permute-start | bytes 138248 | tf_op jit(solution)/shard_map/ppermute | solution.py:211
  8.3 1.9 %collective-permute-done.1 = bf16[8,2880]{1,0:T(8,128)(2,1)S(1)} collective-permute-done((bf16[8,2880]{1,0:T(8,128)(2,1)S(1)}, bf16[8,2880]{1,0:T(8,128)(2,1)S(1)}, u32[]{:S(2)}, u32[]{:S(2)}) %collective-permute-start.1) | collective-permute-done | bytes 46112 | tf_op jit(solution)/shard_map/ppermute | solution.py:211
  10.2 1.6 %collective-permute-start.2 = (bf16[16,2880]{1,0:T(8,128)(2,1)S(1)}, bf16[16,2880]{1,0:T(8,128)(2,1)S(1)}, u32[]{:S(2)}, u32[]{:S(2)}) collective-permute-start(bf16[16,2880]{1,0:T(8,128)(2,1)S(1)} %pad_maximum_fusion), channel_id=1, source_target_pairs={{0,3},{1,4},{2,7},{3,0},{4,1},{5,6},{6,5},{7,2},{8,13},{9,10},{10,... | collective-permute-start | bytes 276488 | tf_op jit(solution)/shard_map/ppermute | solution.py:211
  11.8 1.6 %load.3.moment = bf16[2880,384]{1,0:T(8,128)(2,1)S(1)} custom-call(bf16[2880,384]{1,0:T(8,128)(2,1)} %bitcast.9), custom_call_target="tpu_custom_call" | custom-call | tf_op jit(solution)/shard_map/load/pallas_call | solution.py:48
  13.5 0.8 %collective-permute-done.2 = bf16[16,2880]{1,0:T(8,128)(2,1)S(1)} collective-permute-done((bf16[16,2880]{1,0:T(8,128)(2,1)S(1)}, bf16[16,2880]{1,0:T(8,128)(2,1)S(1)}, u32[]{:S(2)}, u32[]{:S(2)}) %collective-permute-start.2) | collective-permute-done | bytes 92192 | tf_op jit(solution)/shard_map/ppermute | solution.py:211
  14.3 0.0 collective-permute-done.3.other
  14.3 2.1 %power.1 = (f32[32,384]{1,0:T(8,128)S(1)}, f32[16,2880]{1,0:T(8,128)S(1)}, bf16[16,2880]{1,0:T(8,128)(2,1)S(1)}) custom-call(bf16[32,2880]{1,0:T(8,128)(2,1)S(1)} %constant_dynamic-update-slice_fusion.basis, bf16[2880,384]{1,0:T(8,128)(2,1)S(1)} %get-tuple-element.41.grad, bf16[2880,384]{1,0:T(8,128)(2,1)S(1)} %collective-permute-done.3.other), custom_call_target="tpu_custom_call" | custom-call | tf_op jit(solution)/shard_map/power/pallas_call | solution.py:106
  16.4 0.0 copy-start
  16.4 1.5 %collective-permute-start.5 = (bf16[16,2880]{1,0:T(8,128)(2,1)S(1)}, bf16[16,2880]{1,0:T(8,128)(2,1)S(1)}, u32[]{:S(2)}, u32[]{:S(2)}) collective-permute-start(bf16[16,2880]{1,0:T(8,128)(2,1)S(1)} %get-tuple-element.45), channel_id=1, source_target_pairs={{0,3},{1,4},{2,7},{3,0},{4,1},{5,6},{6,5},{7,2},{8,13},{9,10},{10,... | collective-permute-start | bytes 276488 | tf_op jit(solution)/shard_map/ppermute | solution.py:211
  17.9 1.7 %moment.1 = (bf16[2880,384]{1,0:T(8,128)(2,1)S(1)}, bf16[2880,384]{1,0:T(8,128)(2,1)}) custom-call(bf16[2880,384]{1,0:T(8,128)(2,1)S(1)} %get-tuple-element.41.grad, bf16[2880,384]{1,0:T(8,128)(2,1)S(1)} %load.3.moment), custom_call_target="tpu_custom_call" | custom-call | tf_op jit(solution)/shard_map/moment/pallas_call | solution.py:75
  19.6 0.3 collective-permute-start.4
  19.9 0.5 %collective-permute-done.5 = bf16[16,2880]{1,0:T(8,128)(2,1)S(1)} collective-permute-done((bf16[16,2880]{1,0:T(8,128)(2,1)S(1)}, bf16[16,2880]{1,0:T(8,128)(2,1)S(1)}, u32[]{:S(2)}, u32[]{:S(2)}) %collective-permute-start.5) | collective-permute-done | bytes 92192 | tf_op jit(solution)/shard_map/ppermute | solution.py:211
  20.4 1.7 %collective-permute-start.6 = (bf16[8,2880]{1,0:T(8,128)(2,1)S(1)}, bf16[8,2880]{1,0:T(8,128)(2,1)S(1)}, u32[]{:S(2)}, u32[]{:S(2)}) collective-permute-start(bf16[8,2880]{1,0:T(8,128)(2,1)S(1)} %slice.24), channel_id=1, source_target_pairs={{0,5},{1,2},{2,1},{3,6},{4,7},{5,0},{6,3},{7,4},{8,11},{9,12},{10,... | collective-permute-start | bytes 138248 | tf_op jit(solution)/shard_map/ppermute | solution.py:211
  22.1 0.0 collective-permute-done.4
  22.1 0.0 copy-done
  22.2 1.5 %scale.1 = (bf16[64,384]{1,0:T(8,128)(2,1)S(1)}, f32[64,384]{1,0:T(8,128)}) custom-call(bf16[64,2880]{1,0:T(8,128)(2,1)S(1)} %constant_dynamic-update-slice_fusion.2.basis, bf16[2880,384]{1,0:T(8,128)(2,1)S(1)} %get-tuple-element.41.grad, bf16[2880,384]{1,0:T(8,128)(2,1)S(1)} %get-tuple-element.54.moment, f32[32,384]{1,0:T(8,128)S(1)} %get-tuple-element.55.rot_half, ...), custom_call_target="tpu_custom_call" | custom-call | tf_op jit(solution)/shard_map/scale/pallas_call | solution.py:161
  23.7 0.3 %collective-permute-done.6 = bf16[8,2880]{1,0:T(8,128)(2,1)S(1)} collective-permute-done((bf16[8,2880]{1,0:T(8,128)(2,1)S(1)}, bf16[8,2880]{1,0:T(8,128)(2,1)S(1)}, u32[]{:S(2)}, u32[]{:S(2)}) %collective-permute-start.6) | collective-permute-done | bytes 46112 | tf_op jit(solution)/shard_map/ppermute | solution.py:211
  24.0 3.0 %collective-permute-start.7 = (bf16[4,2880]{1,0:T(4,128)(2,1)S(1)}, bf16[4,2880]{1,0:T(4,128)(2,1)S(1)}, u32[]{:S(2)}, u32[]{:S(2)}) collective-permute-start(bf16[4,2880]{1,0:T(4,128)(2,1)S(1)} %slice.25), channel_id=1, source_target_pairs={{0,9},{1,8},{2,11},{3,10},{4,13},{5,12},{6,15},{7,14},{8,1},{9,0},... | collective-permute-start | bytes 69128 | tf_op jit(solution)/shard_map/ppermute | solution.py:211
  27.0 1.7 %update.1 = bf16[2880,384]{1,0:T(8,128)(2,1)} custom-call(bf16[64,2880]{1,0:T(8,128)(2,1)S(1)} %constant_dynamic-update-slice_fusion.2.basis, bf16[64,384]{1,0:T(8,128)(2,1)S(1)} %get-tuple-element.60.scaled), custom_call_target="tpu_custom_call" | custom-call | tf_op jit(solution)/shard_map/update/pallas_call | solution.py:189
  28.7 0.0 collective-permute-done.7
  28.7 0.1 multiply_reduce_fusion
  28.9 0.7 %fusion = f32[4,2880]{1,0:T(4,128)} fusion(f32[4,2880]{1,0:T(4,128)S(1)} %slice.21, bf16[4,2880]{1,0:T(4,128)(2,1)S(1)} %collective-permute-done.7, f32[4]{0:T(128)S(1)} %add_sqrt_fusion), kind=kLoop, calls=%fused_computation.8 | loop fusion | flops 34560 | bytes 115216 | tf_op jit(solution)/shard_map/div | solution.py:257
  (13 shorter events, 0.2 us)
Async XLA Ops:
  0.6 5.3 %collective-permute-start = (bf16[4,2880]{1,0:T(4,128)(2,1)}, bf16[4,2880]{1,0:T(4,128)(2,1)S(1)}, u32[]{:S(2)}, u32[]{:S(2)}) collective-permute-start(bf16[4,2880]{1,0:T(4,128)(2,1)} %refs_1_.1), channel_id=1, source_target_pairs={{0,9},{1,8},{2,11},{3,10},{4,13},{5,12},{6,15},{7,14},{8,1},{9,0},... | collective-permute-start | bytes 69128 | tf_op jit(solution)/shard_map/ppermute | solution.py:211
  6.0 8.3 %collective-permute-start.3 = (bf16[2880,384]{1,0:T(8,128)(2,1)S(1)}, bf16[2880,384]{1,0:T(8,128)(2,1)S(1)}, u32[]{:S(2)}, u32[]{:S(2)}) collective-permute-start(bf16[2880,384]{1,0:T(8,128)(2,1)S(1)} %get-tuple-element.41.grad), channel_id=1, source_target_pairs={{0,1},{1,0},{2,3},{3,2},{4,5},{5,4},{6,7},{7,6},{8,9},{9,8},{10,11... | collective-permute-start | bytes 6635528 | tf_op jit(solution)/shard_map/ppermute | solution.py:214
  6.6 3.6 %collective-permute-start.1 = (bf16[8,2880]{1,0:T(8,128)(2,1)S(1)}, bf16[8,2880]{1,0:T(8,128)(2,1)S(1)}, u32[]{:S(2)}, u32[]{:S(2)}) collective-permute-start(bf16[8,2880]{1,0:T(8,128)(2,1)S(1)} %pad_maximum_fusion.1), channel_id=1, source_target_pairs={{0,5},{1,2},{2,1},{3,6},{4,7},{5,0},{6,3},{7,4},{8,11},{9,12},{10,... | collective-permute-start | bytes 138248 | tf_op jit(solution)/shard_map/ppermute | solution.py:211
  10.2 4.1 %collective-permute-start.2 = (bf16[16,2880]{1,0:T(8,128)(2,1)S(1)}, bf16[16,2880]{1,0:T(8,128)(2,1)S(1)}, u32[]{:S(2)}, u32[]{:S(2)}) collective-permute-start(bf16[16,2880]{1,0:T(8,128)(2,1)S(1)} %pad_maximum_fusion), channel_id=1, source_target_pairs={{0,3},{1,4},{2,7},{3,0},{4,1},{5,6},{6,5},{7,2},{8,13},{9,10},{10,... | collective-permute-start | bytes 276488 | tf_op jit(solution)/shard_map/ppermute | solution.py:211
  16.4 5.8 %copy-start = (f32[384,64]{0,1:T(8,128)S(1)}, f32[384,64]{0,1:T(8,128)}, u32[]{:S(2)}) copy-start(f32[384,64]{0,1:T(8,128)} %param.6) | copy-start | bytes 294916
  16.4 4.0 %collective-permute-start.5 = (bf16[16,2880]{1,0:T(8,128)(2,1)S(1)}, bf16[16,2880]{1,0:T(8,128)(2,1)S(1)}, u32[]{:S(2)}, u32[]{:S(2)}) collective-permute-start(bf16[16,2880]{1,0:T(8,128)(2,1)S(1)} %get-tuple-element.45), channel_id=1, source_target_pairs={{0,3},{1,4},{2,7},{3,0},{4,1},{5,6},{6,5},{7,2},{8,13},{9,10},{10,... | collective-permute-start | bytes 276488 | tf_op jit(solution)/shard_map/ppermute | solution.py:211
  19.6 2.5 %collective-permute-start.4 = (bf16[32,2880]{1,0:T(8,128)(2,1)S(1)}, bf16[32,2880]{1,0:T(8,128)(2,1)S(1)}, u32[]{:S(2)}, u32[]{:S(2)}) collective-permute-start(bf16[32,2880]{1,0:T(8,128)(2,1)S(1)} %constant_dynamic-update-slice_fusion.basis), channel_id=1, source_target_pairs={{0,1},{1,0},{2,3},{3,2},{4,5},{5,4},{6,7},{7,6},{8,9},{9,8},{10,11... | collective-permute-start | bytes 552968 | tf_op jit(solution)/shard_map/ppermute | solution.py:214
  20.4 3.6 %collective-permute-start.6 = (bf16[8,2880]{1,0:T(8,128)(2,1)S(1)}, bf16[8,2880]{1,0:T(8,128)(2,1)S(1)}, u32[]{:S(2)}, u32[]{:S(2)}) collective-permute-start(bf16[8,2880]{1,0:T(8,128)(2,1)S(1)} %slice.24), channel_id=1, source_target_pairs={{0,5},{1,2},{2,1},{3,6},{4,7},{5,0},{6,3},{7,4},{8,11},{9,12},{10,... | collective-permute-start | bytes 138248 | tf_op jit(solution)/shard_map/ppermute | solution.py:211
  24.0 4.7 %collective-permute-start.7 = (bf16[4,2880]{1,0:T(4,128)(2,1)S(1)}, bf16[4,2880]{1,0:T(4,128)(2,1)S(1)}, u32[]{:S(2)}, u32[]{:S(2)}) collective-permute-start(bf16[4,2880]{1,0:T(4,128)(2,1)S(1)} %slice.25), channel_id=1, source_target_pairs={{0,9},{1,8},{2,11},{3,10},{4,13},{5,12},{6,15},{7,14},{8,1},{9,0},... | collective-permute-start | bytes 69128 | tf_op jit(solution)/shard_map/ppermute | solution.py:211

commit v7 on v6

--- a/solution.py
+++ b/solution.py
@@ -86,26 +86,42 @@
     )(inside(grad), inside(moment))
 
 
-def power_kernel(basis, grad, other, rot, kept, sent):
+def transpose_kernel(value, out):
+    out[...] = value[...].T
+
+
+def transposed(value):
+    return pl.pallas_call(
+        transpose_kernel,
+        in_specs=[INSIDE],
+        out_specs=INSIDE,
+        out_shape=pltpu.VMEM(value.shape[::-1], value.dtype),
+        compiler_params=PARAMS,
+        name="transpose",
+    )(inside(value))
+
+
+def power_kernel(basis, grad, other, grad_rows, other_rows, rot, kept, sent):
     rot_own = dot(basis[...], grad[...], ((1,), (0,)))
     rot_other = dot(basis[...], other[...], ((1,), (0,)))
     rot[...] = rot_own
-    rot_own = rot_own.astype(jnp.bfloat16)
-    rot_other = rot_other.astype(jnp.bfloat16)
+    both = jnp.concatenate([rot_own, rot_other], 1).astype(jnp.bfloat16)
     half = kept.shape[0]
     for at, size in cuts(grad.shape[0], 768):
         part = pl.ds(at, size)
-        product = dot(rot_own, grad[part], ((1,), (1,))) + dot(rot_other, other[part], ((1,), (1,)))
+        rows = jnp.concatenate([grad_rows[:, part], other_rows[:, part]], 0)
+        product = dot(both, rows, ((1,), (0,)))
         kept[:, part] = product[:half]
         sent[:, part] = product[half:].astype(jnp.bfloat16)
 
 
-def power_products(basis, grad, other):
+def power_products(*operands):
+    basis, grad = operands[:2]
     count, depth = basis.shape
     rows = grad.shape[1]
     return pl.pallas_call(
         power_kernel,
-        in_specs=[INSIDE] * 3,
+        in_specs=[INSIDE] * len(operands),
         out_specs=[INSIDE] * 3,
         out_shape=[
             pltpu.VMEM((count, rows), jnp.float32),
@@ -114,7 +130,7 @@
         ],
         compiler_params=PARAMS,
         name="power",
-    )(inside(basis), inside(grad), inside(other))
+    )(*map(inside, operands))
 
 
 def scale_kernel(orders, own, basis, grad, moment, rot_half, second, scaled, second_next, rot, mom):
@@ -221,15 +237,22 @@
     other = across(grad)
     held = jnp.concatenate([held, come], 0)
     for step in range(1, bits):
+        if step == 1:
+            held, grad = tie(held, grad)
         if step == bits - 1:
             held, moment = tie(held, moment)
         come = exchange(held, step)
+        if step == 1:
+            grad_rows = transposed(grad)
+            come, grad_rows = tie(come, grad_rows)
         if step == bits - 1:
             (moment,) = load(moment)
-            come, moment, other = tie(come, moment, other)
+            moment, other = tie(moment, other)
+            other_rows = transposed(other)
+            come, moment, other, other_rows = tie(come, moment, other, other_rows)
         held = jnp.concatenate([held, come], 0)
 
-    rot_half, kept, sent = power_products(held, grad, other)
+    rot_half, kept, sent = power_products(held, grad, other, grad_rows, other_rows)
     come = exchange(sent, bits - 1)
     moment, _ = tie(moment, sent)
     moment_in, moment_next = new_moment(grad, moment)

time: 29.8 us -> 29.3 us (0.983)
  waiting for transfers between devices: 3.63 us -> 2.28 us
  Pallas kernels: 10.3 us -> 11.1 us
    ppermute x6, waiting for transfers between devices: 3.62 us -> 2.28 us  [exchange(): return lax.ppermute(value, 'rows', pairs)]
    pallas_call x1 -> x3, Pallas kernels: 2.08 us -> 2.83 us  [the longest x1 1.55 us: power_products(): pl.pallas_call(power_kernel, in_specs=[INSIDE] * len(operands), out_specs...]
  transfers between devices with their start and end apart: 8 -> 8, of which waited for: 5 -> 5; matrix products, arithmetic and copies ran while one was open for 1% -> 0% of each run, Pallas kernels for 28% -> 33%
where the time goes in v7:
time: 29.3 us; the launch traced here: 29.1 us
  starting transfers between devices  13.9 us (47%)
  Pallas kernels  11.1 us (38%)
  waiting for transfers between devices  2.28 us (8%)
  other arithmetic  0.93 us (3%)
  between operations  0.75 us (3%)
    ppermute x6, starting transfers between devices, exchange(): return lax.ppermute(value, 'rows', pairs)  13.1 us
    pallas_call x2, Pallas kernels, load(): pl.pallas_call(load_kernel, in_specs=[pl.BlockSpec(memory_space=pltpu.HBM...  3.27 us
    ppermute x6, waiting for transfers between devices, exchange(): return lax.ppermute(value, 'rows', pairs)  2.28 us
    pallas_call x1, Pallas kernels, new_update(): pl.pallas_call(update_kernel, in_specs=[INSIDE] * 2, out_specs=ANYWHERE,...  1.72 us
    pallas_call x1, Pallas kernels, new_moment(): pl.pallas_call(moment_kernel, in_specs=[INSIDE, INSIDE], out_specs=[INSID...  1.7 us
    pallas_call x1, Pallas kernels, scaled_rotation(): pl.pallas_call(functools.partial(scale_kernel, orders, own), in_specs=[IN...  1.58 us
    pallas_call x1, Pallas kernels, power_products(): pl.pallas_call(power_kernel, in_specs=[INSIDE] * len(operands), out_specs...  1.55 us
    pallas_call x2, Pallas kernels, transposed(): pl.pallas_call(transpose_kernel, in_specs=[INSIDE], out_specs=INSIDE, out...  1.28 us
  transfers between devices with their start and end apart: 8, of which 5 were waited for; matrix products, arithmetic and copies ran while one was open for 0% of the time, Pallas kernels for 33%

profile of v7, /device:TPU:0, one launch (start us, length us, event | category | flops | bytes accessed | tf_op | source)
XLA Modules:
  0.0 29.1 jit_solution(3649693128485290712)
XLA Ops:
  0.6 3.5 %collective-permute-start = (bf16[4,2880]{1,0:T(4,128)(2,1)}, bf16[4,2880]{1,0:T(4,128)(2,1)S(1)}, u32[]{:S(2)}, u32[]{:S(2)}) collective-permute-start(bf16[4,2880]{1,0:T(4,128)(2,1)} %refs_1_.1), channel_id=1, source_target_pairs={{0,9},{1,8},{2,11},{3,10},{4,13},{5,12},{6,15},{7,14},{8,1},{9,0},... | collective-permute-start | bytes 69128 | tf_op jit(solution)/shard_map/ppermute | solution.py:227
  4.2 1.6 %load.2 = (bf16[2880,384]{1,0:T(8,128)(2,1)S(1)}, bf16[4,2880]{1,0:T(4,128)(2,1)S(1)}) custom-call(bf16[2880,384]{1,0:T(8,128)(2,1)} %bitcast.8, bf16[4,2880]{1,0:T(4,128)(2,1)} %refs_1_.1), custom_call_target="tpu_custom_call" | custom-call | tf_op jit(solution)/shard_map/load/pallas_call | solution.py:48
  5.8 0.1 collective-permute-done
  6.0 0.6 %collective-permute-start.3 = (bf16[2880,384]{1,0:T(8,128)(2,1)S(1)}, bf16[2880,384]{1,0:T(8,128)(2,1)S(1)}, u32[]{:S(2)}, u32[]{:S(2)}) collective-permute-start(bf16[2880,384]{1,0:T(8,128)(2,1)S(1)} %get-tuple-element.48.value.grad), channel_id=1, source_target_pairs={{0,1},{1,0},{2,3},{3,2},{4,5},{5,4},{6,7},{7,6},{8,9},{9,8},{10,11... | collective-permute-start | bytes 6635528 | tf_op jit(solution)/shard_map/ppermute | solution.py:230
  6.6 1.7 %collective-permute-start.1 = (bf16[8,2880]{1,0:T(8,128)(2,1)S(1)}, bf16[8,2880]{1,0:T(8,128)(2,1)S(1)}, u32[]{:S(2)}, u32[]{:S(2)}) collective-permute-start(bf16[8,2880]{1,0:T(8,128)(2,1)S(1)} %pad_maximum_fusion.1), channel_id=1, source_target_pairs={{0,5},{1,2},{2,1},{3,6},{4,7},{5,0},{6,3},{7,4},{8,11},{9,12},{10,... | collective-permute-start | bytes 138248 | tf_op jit(solution)/shard_map/ppermute | solution.py:227
  8.3 0.6 %transpose.27.grad_rows = bf16[384,2880]{1,0:T(8,128)(2,1)S(1)} custom-call(bf16[2880,384]{1,0:T(8,128)(2,1)S(1)} %get-tuple-element.48.value.grad), custom_call_target="tpu_custom_call" | custom-call | tf_op jit(solution)/shard_map/transpose/pallas_call | solution.py:94
  8.9 1.2 %collective-permute-done.1 = bf16[8,2880]{1,0:T(8,128)(2,1)S(1)} collective-permute-done((bf16[8,2880]{1,0:T(8,128)(2,1)S(1)}, bf16[8,2880]{1,0:T(8,128)(2,1)S(1)}, u32[]{:S(2)}, u32[]{:S(2)}) %collective-permute-start.1) | collective-permute-done | bytes 46112 | tf_op jit(solution)/shard_map/ppermute | solution.py:227
  10.2 1.6 %collective-permute-start.2 = (bf16[16,2880]{1,0:T(8,128)(2,1)S(1)}, bf16[16,2880]{1,0:T(8,128)(2,1)S(1)}, u32[]{:S(2)}, u32[]{:S(2)}) collective-permute-start(bf16[16,2880]{1,0:T(8,128)(2,1)S(1)} %pad_maximum_fusion), channel_id=1, source_target_pairs={{0,3},{1,4},{2,7},{3,0},{4,1},{5,6},{6,5},{7,2},{8,13},{9,10},{10,... | collective-permute-start | bytes 276488 | tf_op jit(solution)/shard_map/ppermute | solution.py:227
  11.8 1.6 %load.3.moment = bf16[2880,384]{1,0:T(8,128)(2,1)S(1)} custom-call(bf16[2880,384]{1,0:T(8,128)(2,1)} %bitcast.9), custom_call_target="tpu_custom_call" | custom-call | tf_op jit(solution)/shard_map/load/pallas_call | solution.py:48
  13.4 0.0 collective-permute-done.3.value.other
  13.4 0.6 %transpose.28.other_rows = bf16[384,2880]{1,0:T(8,128)(2,1)S(1)} custom-call(bf16[2880,384]{1,0:T(8,128)(2,1)S(1)} %collective-permute-done.3.value.other), custom_call_target="tpu_custom_call" | custom-call | tf_op jit(solution)/shard_map/transpose/pallas_call | solution.py:94
  14.1 0.2 collective-permute-done.2
  14.3 1.6 %power.1 = (f32[32,384]{1,0:T(8,128)S(1)}, f32[16,2880]{1,0:T(8,128)S(1)}, bf16[16,2880]{1,0:T(8,128)(2,1)S(1)}) custom-call(bf16[32,2880]{1,0:T(8,128)(2,1)S(1)} %constant_dynamic-update-slice_fusion.basis, bf16[2880,384]{1,0:T(8,128)(2,1)S(1)} %get-tuple-element.48.value.grad, bf16[2880,384]{1,0:T(8,128)(2,1)S(1)} %collective-permute-done.3.value.other, ...), custom_call_target="tpu_custom_call" | custom-call | tf_op jit(solution)/shard_map/power/pallas_call | solution.py:122
  15.8 0.0 copy-start
  15.8 1.6 %collective-permute-start.5 = (bf16[16,2880]{1,0:T(8,128)(2,1)S(1)}, bf16[16,2880]{1,0:T(8,128)(2,1)S(1)}, u32[]{:S(2)}, u32[]{:S(2)}) collective-permute-start(bf16[16,2880]{1,0:T(8,128)(2,1)S(1)} %get-tuple-element.59), channel_id=1, source_target_pairs={{0,3},{1,4},{2,7},{3,0},{4,1},{5,6},{6,5},{7,2},{8,13},{9,10},{10,... | collective-permute-start | bytes 276488 | tf_op jit(solution)/shard_map/ppermute | solution.py:227
  17.4 1.7 %moment.1 = (bf16[2880,384]{1,0:T(8,128)(2,1)S(1)}, bf16[2880,384]{1,0:T(8,128)(2,1)}) custom-call(bf16[2880,384]{1,0:T(8,128)(2,1)S(1)} %get-tuple-element.48.value.grad, bf16[2880,384]{1,0:T(8,128)(2,1)S(1)} %load.3.moment), custom_call_target="tpu_custom_call" | custom-call | tf_op jit(solution)/shard_map/moment/pallas_call | solution.py:75
  19.1 0.3 collective-permute-start.4
  19.4 0.5 %collective-permute-done.5 = bf16[16,2880]{1,0:T(8,128)(2,1)S(1)} collective-permute-done((bf16[16,2880]{1,0:T(8,128)(2,1)S(1)}, bf16[16,2880]{1,0:T(8,128)(2,1)S(1)}, u32[]{:S(2)}, u32[]{:S(2)}) %collective-permute-start.5) | collective-permute-done | bytes 92192 | tf_op jit(solution)/shard_map/ppermute | solution.py:227
  19.9 1.7 %collective-permute-start.6 = (bf16[8,2880]{1,0:T(8,128)(2,1)S(1)}, bf16[8,2880]{1,0:T(8,128)(2,1)S(1)}, u32[]{:S(2)}, u32[]{:S(2)}) collective-permute-start(bf16[8,2880]{1,0:T(8,128)(2,1)S(1)} %slice.24), channel_id=1, source_target_pairs={{0,5},{1,2},{2,1},{3,6},{4,7},{5,0},{6,3},{7,4},{8,11},{9,12},{10,... | collective-permute-start | bytes 138248 | tf_op jit(solution)/shard_map/ppermute | solution.py:227
  21.6 0.0 collective-permute-done.4
  21.6 0.0 copy-done
  21.6 1.6 %scale.1 = (bf16[64,384]{1,0:T(8,128)(2,1)S(1)}, f32[64,384]{1,0:T(8,128)}) custom-call(bf16[64,2880]{1,0:T(8,128)(2,1)S(1)} %constant_dynamic-update-slice_fusion.2.basis, bf16[2880,384]{1,0:T(8,128)(2,1)S(1)} %get-tuple-element.48.value.grad, bf16[2880,384]{1,0:T(8,128)(2,1)S(1)} %get-tuple-element.68.moment, f32[32,384]{1,0:T(8,128)S(1)} %get-tuple-element.69.rot_half, ...), custom_call_target="tpu_custom_call" | custom-call | tf_op jit(solution)/shard_map/scale/pallas_call | solution.py:177
  23.2 0.3 collective-permute-done.6
  23.5 3.0 %collective-permute-start.7 = (bf16[4,2880]{1,0:T(4,128)(2,1)S(1)}, bf16[4,2880]{1,0:T(4,128)(2,1)S(1)}, u32[]{:S(2)}, u32[]{:S(2)}) collective-permute-start(bf16[4,2880]{1,0:T(4,128)(2,1)S(1)} %slice.25), channel_id=1, source_target_pairs={{0,9},{1,8},{2,11},{3,10},{4,13},{5,12},{6,15},{7,14},{8,1},{9,0},... | collective-permute-start | bytes 69128 | tf_op jit(solution)/shard_map/ppermute | solution.py:227
  26.5 1.7 %update.1 = bf16[2880,384]{1,0:T(8,128)(2,1)} custom-call(bf16[64,2880]{1,0:T(8,128)(2,1)S(1)} %constant_dynamic-update-slice_fusion.2.basis, bf16[64,384]{1,0:T(8,128)(2,1)S(1)} %get-tuple-element.74.scaled), custom_call_target="tpu_custom_call" | custom-call | tf_op jit(solution)/shard_map/update/pallas_call | solution.py:205
  28.2 0.0 collective-permute-done.7
  28.2 0.1 multiply_reduce_fusion
  28.4 0.7 %fusion = f32[4,2880]{1,0:T(4,128)} fusion(f32[4,2880]{1,0:T(4,128)S(1)} %slice.21, bf16[4,2880]{1,0:T(4,128)(2,1)S(1)} %collective-permute-done.7, f32[4]{0:T(128)S(1)} %add_sqrt_fusion), kind=kLoop, calls=%fused_computation.8 | loop fusion | flops 34560 | bytes 115216 | tf_op jit(solution)/shard_map/div | solution.py:280
  (13 shorter events, 0.2 us)
Async XLA Ops:
  0.6 5.3 %collective-permute-start = (bf16[4,2880]{1,0:T(4,128)(2,1)}, bf16[4,2880]{1,0:T(4,128)(2,1)S(1)}, u32[]{:S(2)}, u32[]{:S(2)}) collective-permute-start(bf16[4,2880]{1,0:T(4,128)(2,1)} %refs_1_.1), channel_id=1, source_target_pairs={{0,9},{1,8},{2,11},{3,10},{4,13},{5,12},{6,15},{7,14},{8,1},{9,0},... | collective-permute-start | bytes 69128 | tf_op jit(solution)/shard_map/ppermute | solution.py:227
  6.0 7.5 %collective-permute-start.3 = (bf16[2880,384]{1,0:T(8,128)(2,1)S(1)}, bf16[2880,384]{1,0:T(8,128)(2,1)S(1)}, u32[]{:S(2)}, u32[]{:S(2)}) collective-permute-start(bf16[2880,384]{1,0:T(8,128)(2,1)S(1)} %get-tuple-element.48.value.grad), channel_id=1, source_target_pairs={{0,1},{1,0},{2,3},{3,2},{4,5},{5,4},{6,7},{7,6},{8,9},{9,8},{10,11... | collective-permute-start | bytes 6635528 | tf_op jit(solution)/shard_map/ppermute | solution.py:230
  6.6 3.6 %collective-permute-start.1 = (bf16[8,2880]{1,0:T(8,128)(2,1)S(1)}, bf16[8,2880]{1,0:T(8,128)(2,1)S(1)}, u32[]{:S(2)}, u32[]{:S(2)}) collective-permute-start(bf16[8,2880]{1,0:T(8,128)(2,1)S(1)} %pad_maximum_fusion.1), channel_id=1, source_target_pairs={{0,5},{1,2},{2,1},{3,6},{4,7},{5,0},{6,3},{7,4},{8,11},{9,12},{10,... | collective-permute-start | bytes 138248 | tf_op jit(solution)/shard_map/ppermute | solution.py:227
  10.2 4.1 %collective-permute-start.2 = (bf16[16,2880]{1,0:T(8,128)(2,1)S(1)}, bf16[16,2880]{1,0:T(8,128)(2,1)S(1)}, u32[]{:S(2)}, u32[]{:S(2)}) collective-permute-start(bf16[16,2880]{1,0:T(8,128)(2,1)S(1)} %pad_maximum_fusion), channel_id=1, source_target_pairs={{0,3},{1,4},{2,7},{3,0},{4,1},{5,6},{6,5},{7,2},{8,13},{9,10},{10,... | collective-permute-start | bytes 276488 | tf_op jit(solution)/shard_map/ppermute | solution.py:227
  15.8 5.8 %copy-start = (f32[384,64]{0,1:T(8,128)S(1)}, f32[384,64]{0,1:T(8,128)}, u32[]{:S(2)}) copy-start(f32[384,64]{0,1:T(8,128)} %param.6) | copy-start | bytes 294916
  15.8 4.1 %collective-permute-start.5 = (bf16[16,2880]{1,0:T(8,128)(2,1)S(1)}, bf16[16,2880]{1,0:T(8,128)(2,1)S(1)}, u32[]{:S(2)}, u32[]{:S(2)}) collective-permute-start(bf16[16,2880]{1,0:T(8,128)(2,1)S(1)} %get-tuple-element.59), channel_id=1, source_target_pairs={{0,3},{1,4},{2,7},{3,0},{4,1},{5,6},{6,5},{7,2},{8,13},{9,10},{10,... | collective-permute-start | bytes 276488 | tf_op jit(solution)/shard_map/ppermute | solution.py:227
  19.1 2.5 %collective-permute-start.4 = (bf16[32,2880]{1,0:T(8,128)(2,1)S(1)}, bf16[32,2880]{1,0:T(8,128)(2,1)S(1)}, u32[]{:S(2)}, u32[]{:S(2)}) collective-permute-start(bf16[32,2880]{1,0:T(8,128)(2,1)S(1)} %constant_dynamic-update-slice_fusion.basis), channel_id=1, source_target_pairs={{0,1},{1,0},{2,3},{3,2},{4,5},{5,4},{6,7},{7,6},{8,9},{9,8},{10,11... | collective-permute-start | bytes 552968 | tf_op jit(solution)/shard_map/ppermute | solution.py:230
  19.9 3.6 %collective-permute-start.6 = (bf16[8,2880]{1,0:T(8,128)(2,1)S(1)}, bf16[8,2880]{1,0:T(8,128)(2,1)S(1)}, u32[]{:S(2)}, u32[]{:S(2)}) collective-permute-start(bf16[8,2880]{1,0:T(8,128)(2,1)S(1)} %slice.24), channel_id=1, source_target_pairs={{0,5},{1,2},{2,1},{3,6},{4,7},{5,0},{6,3},{7,4},{8,11},{9,12},{10,... | collective-permute-start | bytes 138248 | tf_op jit(solution)/shard_map/ppermute | solution.py:227
  23.5 4.7 %collective-permute-start.7 = (bf16[4,2880]{1,0:T(4,128)(2,1)S(1)}, bf16[4,2880]{1,0:T(4,128)(2,1)S(1)}, u32[]{:S(2)}, u32[]{:S(2)}) collective-permute-start(bf16[4,2880]{1,0:T(4,128)(2,1)S(1)} %slice.25), channel_id=1, source_target_pairs={{0,9},{1,8},{2,11},{3,10},{4,13},{5,12},{6,15},{7,14},{8,1},{9,0},... | collective-permute-start | bytes 69128 | tf_op jit(solution)/shard_map/ppermute | solution.py:227

commit v8 on v6

--- a/solution.py
+++ b/solution.py
@@ -86,35 +86,72 @@
     )(inside(grad), inside(moment))
 
 
-def power_kernel(basis, grad, other, rot, kept, sent):
+def transpose_kernel(*refs):
+    count = len(refs) // 2
+    for value, out in zip(refs[:count], refs[count:]):
+        out[...] = value[...].T
+
+
+def transposed(*values):
+    return pl.pallas_call(
+        transpose_kernel,
+        in_specs=[INSIDE] * len(values),
+        out_specs=[INSIDE] * len(values),
+        out_shape=[pltpu.VMEM(value.shape[::-1], value.dtype) for value in values],
+        compiler_params=PARAMS,
+        name="transpose",
+    )(*map(inside, values))
+
+
+def power_kernel(*refs):
+    *pieces, grad, other, grad_rows, other_rows, basis, rot, kept, sent = refs
+    basis[...] = jnp.concatenate([piece[...] for piece in pieces], 0)
     rot_own = dot(basis[...], grad[...], ((1,), (0,)))
     rot_other = dot(basis[...], other[...], ((1,), (0,)))
     rot[...] = rot_own
-    rot_own = rot_own.astype(jnp.bfloat16)
-    rot_other = rot_other.astype(jnp.bfloat16)
+    both = jnp.concatenate([rot_own, rot_other], 1).astype(jnp.bfloat16)
     half = kept.shape[0]
     for at, size in cuts(grad.shape[0], 768):
         part = pl.ds(at, size)
-        product = dot(rot_own, grad[part], ((1,), (1,))) + dot(rot_other, other[part], ((1,), (1,)))
+        rows = jnp.concatenate([grad_rows[:, part], other_rows[:, part]], 0)
+        product = dot(both, rows, ((1,), (0,)))
         kept[:, part] = product[:half]
         sent[:, part] = product[half:].astype(jnp.bfloat16)
 
 
-def power_products(basis, grad, other):
-    count, depth = basis.shape
-    rows = grad.shape[1]
+def power_products(pieces, grads):
+    depth, rows = grads[0].shape
+    count = sum(piece.shape[0] for piece in pieces)
     return pl.pallas_call(
         power_kernel,
-        in_specs=[INSIDE] * 3,
-        out_specs=[INSIDE] * 3,
+        in_specs=[INSIDE] * (len(pieces) + len(grads)),
+        out_specs=[INSIDE] * 4,
         out_shape=[
+            pltpu.VMEM((count, depth), jnp.bfloat16),
             pltpu.VMEM((count, rows), jnp.float32),
             pltpu.VMEM((count // 2, depth), jnp.float32),
             pltpu.VMEM((count // 2, depth), jnp.bfloat16),
         ],
         compiler_params=PARAMS,
         name="power",
-    )(inside(basis), inside(grad), inside(other))
+    )(*map(inside, (*pieces, *grads)))
+
+
+def normal_kernel(kept, come, out):
+    power = kept[...] + come[...].astype(jnp.float32)
+    square = jnp.mean(power * power, axis=1, keepdims=True)
+    out[...] = power / jnp.sqrt(square + 1e-06)
+
+
+def normalised(kept, come):
+    return pl.pallas_call(
+        normal_kernel,
+        in_specs=[INSIDE] * 2,
+        out_specs=INSIDE,
+        out_shape=jax.ShapeDtypeStruct(kept.shape, kept.dtype),
+        compiler_params=PARAMS,
+        name="normalise",
+    )(inside(kept), inside(come))
 
 
 def scale_kernel(orders, own, basis, grad, moment, rot_half, second, scaled, second_next, rot, mom):
@@ -220,16 +257,18 @@
     come, grad, held = tie(come, grad, held)
     other = across(grad)
     held = jnp.concatenate([held, come], 0)
-    for step in range(1, bits):
-        if step == bits - 1:
-            held, moment = tie(held, moment)
-        come = exchange(held, step)
-        if step == bits - 1:
-            (moment,) = load(moment)
-            come, moment, other = tie(come, moment, other)
-        held = jnp.concatenate([held, come], 0)
-
-    rot_half, kept, sent = power_products(held, grad, other)
+    for step in range(1, bits - 2):
+        held = jnp.concatenate([held, exchange(held, step)], 0)
+    first = exchange(held, bits - 2)
+    second_hand = exchange(held, bits - 1)
+    first, grad = tie(first, grad)
+    last = exchange(first, bits - 1)
+    second_hand, grad, other = tie(second_hand, grad, other)
+    grad_rows, other_rows = transposed(grad, other)
+    last, grad_rows, other_rows = tie(last, grad_rows, other_rows)
+    held, rot_half, kept, sent = power_products(
+        (held, first, second_hand, last), (grad, other, grad_rows, other_rows)
+    )
     come = exchange(sent, bits - 1)
     moment, _ = tie(moment, sent)
     moment_in, moment_next = new_moment(grad, moment)
@@ -237,9 +276,9 @@
     theirs = across(held)
     come, moment_in, moment_next = tie(come, moment_in, moment_next)
     for step in reversed(range(bits)):
-        kept = kept + come.astype(jnp.float32)
         if step == 0:
             break
+        kept = kept + come.astype(jnp.float32)
         half = kept.shape[0] // 2
         come = exchange(kept[half:].astype(jnp.bfloat16), step - 1)
         kept = kept[:half]
@@ -254,7 +293,7 @@
             scaled, kept = tie(scaled, kept)
             update = new_update(whole, scaled)
             come, update = tie(come, update)
-    basis_next = kept / jnp.sqrt(jnp.mean(kept * kept, axis=1, keepdims=True) + 1e-06)
+    basis_next = normalised(kept, come)
     return update.T, moment_next.T, second_next.T, basis_next
 
 

time: 29.8 us -> 28.9 us (0.970)
  starting transfers between devices: 13.9 us -> 15.5 us
  waiting for transfers between devices: 3.63 us -> 2.24 us
  other arithmetic: 0.97 us -> 0.06 us
    ppermute x6 -> x7, starting transfers between devices: 13 us -> 14.8 us  [exchange(): return lax.ppermute(value, 'rows', pairs)]
    pallas_call x2 -> x1, Pallas kernels: 3.27 us -> 1.64 us  [load(): pl.pallas_call(load_kernel, in_specs=[pl.BlockSpec(memory_space=pltpu.HBM...]
    pallas_call x1 -> x3, Pallas kernels: 2.08 us -> 3.52 us  [the longest x1 1.55 us: power_products(): pl.pallas_call(power_kernel, in_specs=[INSIDE] * (len(pieces) + len(grads...]
    ppermute x6 -> x7, waiting for transfers between devices: 3.62 us -> 2.23 us  [exchange(): return lax.ppermute(value, 'rows', pairs)]
    div x1 -> x0, other arithmetic: 0.71 us -> none  [shards(): kept / jnp.sqrt(jnp.mean(kept * kept, axis=1, keepdims=True) + 1e-06)]
  transfers between devices with their start and end apart: 8 -> 9, of which waited for: 5 -> 5; matrix products, arithmetic and copies ran while one was open for 1% -> 0% of each run, Pallas kernels for 28% -> 27%
where the time goes in v8:
time: 28.9 us; the launch traced here: 28.8 us
  starting transfers between devices  15.5 us (54%)
  Pallas kernels  10.2 us (35%)
  waiting for transfers between devices  2.24 us (8%)
  between operations  0.72 us (2%)
    ppermute x7, starting transfers between devices, exchange(): return lax.ppermute(value, 'rows', pairs)  14.8 us
    ppermute x7, waiting for transfers between devices, exchange(): return lax.ppermute(value, 'rows', pairs)  2.23 us
    pallas_call x1, Pallas kernels, new_update(): pl.pallas_call(update_kernel, in_specs=[INSIDE] * 2, out_specs=ANYWHERE,...  1.72 us
    pallas_call x1, Pallas kernels, new_moment(): pl.pallas_call(moment_kernel, in_specs=[INSIDE, INSIDE], out_specs=[INSID...  1.7 us
    pallas_call x1, Pallas kernels, load(): pl.pallas_call(load_kernel, in_specs=[pl.BlockSpec(memory_space=pltpu.HBM...  1.64 us
    pallas_call x1, Pallas kernels, scaled_rotation(): pl.pallas_call(functools.partial(scale_kernel, orders, own), in_specs=[IN...  1.57 us
    pallas_call x1, Pallas kernels, power_products(): pl.pallas_call(power_kernel, in_specs=[INSIDE] * (len(pieces) + len(grads...  1.55 us
    pallas_call x1, Pallas kernels, transposed(): pl.pallas_call(transpose_kernel, in_specs=[INSIDE] * len(values), out_spe...  1.22 us
  transfers between devices with their start and end apart: 9, of which 5 were waited for; matrix products, arithmetic and copies ran while one was open for 0% of the time, Pallas kernels for 27%

profile of v8, /device:TPU:0, one launch (start us, length us, event | category | flops | bytes accessed | tf_op | source)
XLA Modules:
  0.0 28.8 jit_solution(2999009046276326900)
XLA Ops:
  0.6 3.5 %collective-permute-start = (bf16[4,2880]{1,0:T(4,128)(2,1)}, bf16[4,2880]{1,0:T(4,128)(2,1)S(1)}, u32[]{:S(2)}, u32[]{:S(2)}) collective-permute-start(bf16[4,2880]{1,0:T(4,128)(2,1)} %refs_1_.1), channel_id=1, source_target_pairs={{0,9},{1,8},{2,11},{3,10},{4,13},{5,12},{6,15},{7,14},{8,1},{9,0},... | collective-permute-start | bytes 69128 | tf_op jit(solution)/shard_map/ppermute | solution.py:248
  4.2 1.6 %load.1 = (bf16[2880,384]{1,0:T(8,128)(2,1)S(1)}, bf16[4,2880]{1,0:T(4,128)(2,1)S(1)}) custom-call(bf16[2880,384]{1,0:T(8,128)(2,1)} %bitcast.9, bf16[4,2880]{1,0:T(4,128)(2,1)} %refs_1_.1), custom_call_target="tpu_custom_call" | custom-call | tf_op jit(solution)/shard_map/load/pallas_call | solution.py:48
  5.8 0.1 collective-permute-done
  6.0 0.6 %collective-permute-start.3 = (bf16[2880,384]{1,0:T(8,128)(2,1)S(1)}, bf16[2880,384]{1,0:T(8,128)(2,1)S(1)}, u32[]{:S(2)}, u32[]{:S(2)}) collective-permute-start(bf16[2880,384]{1,0:T(8,128)(2,1)S(1)} %get-tuple-element.49.refs_0_.refs_4_.grad), channel_id=1, source_target_pairs={{0,1},{1,0},{2,3},{3,2},{4,5},{5,4},{6,7},{7,6},{8,9},{9,8},{10,11... | collective-permute-start | bytes 6635528 | tf_op jit(solution)/shard_map/ppermute | solution.py:251
  6.6 1.7 %collective-permute-start.1 = (bf16[8,2880]{1,0:T(8,128)(2,1)S(1)}, bf16[8,2880]{1,0:T(8,128)(2,1)S(1)}, u32[]{:S(2)}, u32[]{:S(2)}) collective-permute-start(bf16[8,2880]{1,0:T(8,128)(2,1)S(1)} %pad_maximum_fusion.refs_0_), channel_id=1, source_target_pairs={{0,5},{1,2},{2,1},{3,6},{4,7},{5,0},{6,3},{7,4},{8,11},{9,12},{10,... | collective-permute-start | bytes 138248 | tf_op jit(solution)/shard_map/ppermute | solution.py:248
  8.3 1.2 %collective-permute-start.2 = (bf16[8,2880]{1,0:T(8,128)(2,1)S(1)}, bf16[8,2880]{1,0:T(8,128)(2,1)S(1)}, u32[]{:S(2)}, u32[]{:S(2)}) collective-permute-start(bf16[8,2880]{1,0:T(8,128)(2,1)S(1)} %pad_maximum_fusion.refs_0_), channel_id=1, source_target_pairs={{0,3},{1,4},{2,7},{3,0},{4,1},{5,6},{6,5},{7,2},{8,13},{9,10},{10,... | collective-permute-start | bytes 138248 | tf_op jit(solution)/shard_map/ppermute | solution.py:248
  9.5 0.7 %collective-permute-done.1.refs_1_ = bf16[8,2880]{1,0:T(8,128)(2,1)S(1)} collective-permute-done((bf16[8,2880]{1,0:T(8,128)(2,1)S(1)}, bf16[8,2880]{1,0:T(8,128)(2,1)S(1)}, u32[]{:S(2)}, u32[]{:S(2)}) %collective-permute-start.1) | collective-permute-done | bytes 46112 | tf_op jit(solution)/shard_map/ppermute | solution.py:248
  10.2 1.6 %collective-permute-start.4 = (bf16[8,2880]{1,0:T(8,128)(2,1)S(1)}, bf16[8,2880]{1,0:T(8,128)(2,1)S(1)}, u32[]{:S(2)}, u32[]{:S(2)}) collective-permute-start(bf16[8,2880]{1,0:T(8,128)(2,1)S(1)} %collective-permute-done.1.refs_1_), channel_id=1, source_target_pairs={{0,3},{1,4},{2,7},{3,0},{4,1},{5,6},{6,5},{7,2},{8,13},{9,10},{10,... | collective-permute-start | bytes 138248 | tf_op jit(solution)/shard_map/ppermute | solution.py:248
  11.7 0.0 collective-permute-done.2.refs_2_
  11.8 0.0 collective-permute-done.3.refs_1_.refs_5_
  11.8 1.2 %transpose.25 = (bf16[384,2880]{1,0:T(8,128)(2,1)S(1)}, bf16[384,2880]{1,0:T(8,128)(2,1)S(1)}) custom-call(bf16[2880,384]{1,0:T(8,128)(2,1)S(1)} %get-tuple-element.49.refs_0_.refs_4_.grad, bf16[2880,384]{1,0:T(8,128)(2,1)S(1)} %collective-permute-done.3.refs_1_.refs_5_), custom_call_target="tpu_custom_call" | custom-call | tf_op jit(solution)/shard_map/transpose/pallas_call | solution.py:96
  13.0 0.6 %collective-permute-done.4.refs_3_ = bf16[8,2880]{1,0:T(8,128)(2,1)S(1)} collective-permute-done((bf16[8,2880]{1,0:T(8,128)(2,1)S(1)}, bf16[8,2880]{1,0:T(8,128)(2,1)S(1)}, u32[]{:S(2)}, u32[]{:S(2)}) %collective-permute-start.4) | collective-permute-done | bytes 46112 | tf_op jit(solution)/shard_map/ppermute | solution.py:248
  13.7 0.0 copy-start
  13.7 1.6 %power.1 = (bf16[32,2880]{1,0:T(8,128)(2,1)S(1)}, f32[32,384]{1,0:T(8,128)S(1)}, f32[16,2880]{1,0:T(8,128)S(1)}, bf16[16,2880]{1,0:T(8,128)(2,1)S(1)}) custom-call(bf16[8,2880]{1,0:T(8,128)(2,1)S(1)} %pad_maximum_fusion.refs_0_, bf16[8,2880]{1,0:T(8,128)(2,1)S(1)} %collective-permute-done.1.refs_1_, bf16[8,2880]{1,0:T(8,128)(2,1)S(1)} %collective-permute-done.2.refs_2_, ...), custom_call_target="tpu_custom_call" | custom-call | tf_op jit(solution)/shard_map/power/pallas_call | solution.py:125
  15.2 1.7 %collective-permute-start.6 = (bf16[16,2880]{1,0:T(8,128)(2,1)S(1)}, bf16[16,2880]{1,0:T(8,128)(2,1)S(1)}, u32[]{:S(2)}, u32[]{:S(2)}) collective-permute-start(bf16[16,2880]{1,0:T(8,128)(2,1)S(1)} %get-tuple-element.57), channel_id=1, source_target_pairs={{0,3},{1,4},{2,7},{3,0},{4,1},{5,6},{6,5},{7,2},{8,13},{9,10},{10,... | collective-permute-start | bytes 276488 | tf_op jit(solution)/shard_map/ppermute | solution.py:248
  16.9 0.0 copy-done
  16.9 0.0 copy-start.1
  16.9 1.7 %moment.1 = (bf16[2880,384]{1,0:T(8,128)(2,1)S(1)}, bf16[2880,384]{1,0:T(8,128)(2,1)}) custom-call(bf16[2880,384]{1,0:T(8,128)(2,1)S(1)} %get-tuple-element.49.refs_0_.refs_4_.grad, bf16[2880,384]{1,0:T(8,128)(2,1)S(1)} %bitcast.6), custom_call_target="tpu_custom_call" | custom-call | tf_op jit(solution)/shard_map/moment/pallas_call | solution.py:75
  18.6 0.2 collective-permute-start.5
  18.8 0.5 %collective-permute-done.6 = bf16[16,2880]{1,0:T(8,128)(2,1)S(1)} collective-permute-done((bf16[16,2880]{1,0:T(8,128)(2,1)S(1)}, bf16[16,2880]{1,0:T(8,128)(2,1)S(1)}, u32[]{:S(2)}, u32[]{:S(2)}) %collective-permute-start.6) | collective-permute-done | bytes 92192 | tf_op jit(solution)/shard_map/ppermute | solution.py:248
  19.3 1.7 %collective-permute-start.7 = (bf16[8,2880]{1,0:T(8,128)(2,1)S(1)}, bf16[8,2880]{1,0:T(8,128)(2,1)S(1)}, u32[]{:S(2)}, u32[]{:S(2)}) collective-permute-start(bf16[8,2880]{1,0:T(8,128)(2,1)S(1)} %slice.24), channel_id=1, source_target_pairs={{0,5},{1,2},{2,1},{3,6},{4,7},{5,0},{6,3},{7,4},{8,11},{9,12},{10,... | collective-permute-start | bytes 138248 | tf_op jit(solution)/shard_map/ppermute | solution.py:248
  21.0 0.0 collective-permute-done.5
  21.0 0.0 copy-done.1
  21.0 1.6 %scale.1 = (bf16[64,384]{1,0:T(8,128)(2,1)S(1)}, f32[64,384]{1,0:T(8,128)}) custom-call(bf16[64,2880]{1,0:T(8,128)(2,1)S(1)} %constant_dynamic-update-slice_fusion.basis, bf16[2880,384]{1,0:T(8,128)(2,1)S(1)} %get-tuple-element.49.refs_0_.refs_4_.grad, bf16[2880,384]{1,0:T(8,128)(2,1)S(1)} %get-tuple-element.66.moment, ...), custom_call_target="tpu_custom_call" | custom-call | tf_op jit(solution)/shard_map/scale/pallas_call | solution.py:198
  22.6 0.3 collective-permute-done.7
  22.9 3.4 %collective-permute-start.8 = (bf16[4,2880]{1,0:T(4,128)(2,1)S(1)}, bf16[4,2880]{1,0:T(4,128)(2,1)S(1)}, u32[]{:S(2)}, u32[]{:S(2)}) collective-permute-start(bf16[4,2880]{1,0:T(4,128)(2,1)S(1)} %slice.25), channel_id=1, source_target_pairs={{0,9},{1,8},{2,11},{3,10},{4,13},{5,12},{6,15},{7,14},{8,1},{9,0},... | collective-permute-start | bytes 69128 | tf_op jit(solution)/shard_map/ppermute | solution.py:248
  26.3 1.7 %update.1 = bf16[2880,384]{1,0:T(8,128)(2,1)} custom-call(bf16[64,2880]{1,0:T(8,128)(2,1)S(1)} %constant_dynamic-update-slice_fusion.basis, bf16[64,384]{1,0:T(8,128)(2,1)S(1)} %get-tuple-element.72.scaled), custom_call_target="tpu_custom_call" | custom-call | tf_op jit(solution)/shard_map/update/pallas_call | solution.py:226
  28.0 0.0 collective-permute-done.8.come
  28.0 0.7 %normalise.1 = f32[4,2880]{1,0:T(4,128)} custom-call(f32[4,2880]{1,0:T(4,128)S(1)} %slice.21.kept, bf16[4,2880]{1,0:T(4,128)(2,1)S(1)} %collective-permute-done.8.come), custom_call_target="tpu_custom_call" | custom-call | tf_op jit(solution)/shard_map/normalise/pallas_call | solution.py:147
  (9 shorter events, 0.1 us)
Async XLA Ops:
  0.6 5.3 %collective-permute-start = (bf16[4,2880]{1,0:T(4,128)(2,1)}, bf16[4,2880]{1,0:T(4,128)(2,1)S(1)}, u32[]{:S(2)}, u32[]{:S(2)}) collective-permute-start(bf16[4,2880]{1,0:T(4,128)(2,1)} %refs_1_.1), channel_id=1, source_target_pairs={{0,9},{1,8},{2,11},{3,10},{4,13},{5,12},{6,15},{7,14},{8,1},{9,0},... | collective-permute-start | bytes 69128 | tf_op jit(solution)/shard_map/ppermute | solution.py:248
  6.0 5.8 %collective-permute-start.3 = (bf16[2880,384]{1,0:T(8,128)(2,1)S(1)}, bf16[2880,384]{1,0:T(8,128)(2,1)S(1)}, u32[]{:S(2)}, u32[]{:S(2)}) collective-permute-start(bf16[2880,384]{1,0:T(8,128)(2,1)S(1)} %get-tuple-element.49.refs_0_.refs_4_.grad), channel_id=1, source_target_pairs={{0,1},{1,0},{2,3},{3,2},{4,5},{5,4},{6,7},{7,6},{8,9},{9,8},{10,11... | collective-permute-start | bytes 6635528 | tf_op jit(solution)/shard_map/ppermute | solution.py:251
  6.6 3.6 %collective-permute-start.1 = (bf16[8,2880]{1,0:T(8,128)(2,1)S(1)}, bf16[8,2880]{1,0:T(8,128)(2,1)S(1)}, u32[]{:S(2)}, u32[]{:S(2)}) collective-permute-start(bf16[8,2880]{1,0:T(8,128)(2,1)S(1)} %pad_maximum_fusion.refs_0_), channel_id=1, source_target_pairs={{0,5},{1,2},{2,1},{3,6},{4,7},{5,0},{6,3},{7,4},{8,11},{9,12},{10,... | collective-permute-start | bytes 138248 | tf_op jit(solution)/shard_map/ppermute | solution.py:248
  8.3 3.5 %collective-permute-start.2 = (bf16[8,2880]{1,0:T(8,128)(2,1)S(1)}, bf16[8,2880]{1,0:T(8,128)(2,1)S(1)}, u32[]{:S(2)}, u32[]{:S(2)}) collective-permute-start(bf16[8,2880]{1,0:T(8,128)(2,1)S(1)} %pad_maximum_fusion.refs_0_), channel_id=1, source_target_pairs={{0,3},{1,4},{2,7},{3,0},{4,1},{5,6},{6,5},{7,2},{8,13},{9,10},{10,... | collective-permute-start | bytes 138248 | tf_op jit(solution)/shard_map/ppermute | solution.py:248
  10.2 3.5 %collective-permute-start.4 = (bf16[8,2880]{1,0:T(8,128)(2,1)S(1)}, bf16[8,2880]{1,0:T(8,128)(2,1)S(1)}, u32[]{:S(2)}, u32[]{:S(2)}) collective-permute-start(bf16[8,2880]{1,0:T(8,128)(2,1)S(1)} %collective-permute-done.1.refs_1_), channel_id=1, source_target_pairs={{0,3},{1,4},{2,7},{3,0},{4,1},{5,6},{6,5},{7,2},{8,13},{9,10},{10,... | collective-permute-start | bytes 138248 | tf_op jit(solution)/shard_map/ppermute | solution.py:248
  13.7 3.2 %copy-start = (bf16[384,2880]{0,1:T(8,128)(2,1)S(1)}, bf16[384,2880]{0,1:T(8,128)(2,1)}, u32[]{:S(2)}) copy-start(bf16[384,2880]{0,1:T(8,128)(2,1)} %param.5) | copy-start | bytes 6635524
  15.2 4.0 %collective-permute-start.6 = (bf16[16,2880]{1,0:T(8,128)(2,1)S(1)}, bf16[16,2880]{1,0:T(8,128)(2,1)S(1)}, u32[]{:S(2)}, u32[]{:S(2)}) collective-permute-start(bf16[16,2880]{1,0:T(8,128)(2,1)S(1)} %get-tuple-element.57), channel_id=1, source_target_pairs={{0,3},{1,4},{2,7},{3,0},{4,1},{5,6},{6,5},{7,2},{8,13},{9,10},{10,... | collective-permute-start | bytes 276488 | tf_op jit(solution)/shard_map/ppermute | solution.py:248
  16.9 4.1 %copy-start.1 = (f32[384,64]{0,1:T(8,128)S(1)}, f32[384,64]{0,1:T(8,128)}, u32[]{:S(2)}) copy-start(f32[384,64]{0,1:T(8,128)} %param.6) | copy-start | bytes 294916
  18.6 2.4 %collective-permute-start.5 = (bf16[32,2880]{1,0:T(8,128)(2,1)S(1)}, bf16[32,2880]{1,0:T(8,128)(2,1)S(1)}, u32[]{:S(2)}, u32[]{:S(2)}) collective-permute-start(bf16[32,2880]{1,0:T(8,128)(2,1)S(1)} %get-tuple-element.60), channel_id=1, source_target_pairs={{0,1},{1,0},{2,3},{3,2},{4,5},{5,4},{6,7},{7,6},{8,9},{9,8},{10,11... | collective-permute-start | bytes 552968 | tf_op jit(solution)/shard_map/ppermute | solution.py:251
  19.3 3.6 %collective-permute-start.7 = (bf16[8,2880]{1,0:T(8,128)(2,1)S(1)}, bf16[8,2880]{1,0:T(8,128)(2,1)S(1)}, u32[]{:S(2)}, u32[]{:S(2)}) collective-permute-start(bf16[8,2880]{1,0:T(8,128)(2,1)S(1)} %slice.24), channel_id=1, source_target_pairs={{0,5},{1,2},{2,1},{3,6},{4,7},{5,0},{6,3},{7,4},{8,11},{9,12},{10,... | collective-permute-start | bytes 138248 | tf_op jit(solution)/shard_map/ppermute | solution.py:248
  22.9 5.1 %collective-permute-start.8 = (bf16[4,2880]{1,0:T(4,128)(2,1)S(1)}, bf16[4,2880]{1,0:T(4,128)(2,1)S(1)}, u32[]{:S(2)}, u32[]{:S(2)}) collective-permute-start(bf16[4,2880]{1,0:T(4,128)(2,1)S(1)} %slice.25), channel_id=1, source_target_pairs={{0,9},{1,8},{2,11},{3,10},{4,13},{5,12},{6,15},{7,14},{8,1},{9,0},... | collective-permute-start | bytes 69128 | tf_op jit(solution)/shard_map/ppermute | solution.py:248

commit v9 on v8

--- a/solution.py
+++ b/solution.py
@@ -57,30 +57,18 @@
     return out
 
 
-def moment_kernel(grad, moment, held, stored, sems):
-    copies = []
-    for i, (at, size) in enumerate(cuts(grad.shape[0], 960)):
-        part = pl.ds(at, size)
-        held[part] = (
-            0.9 * moment[part].astype(jnp.float32) + 0.1 * grad[part].astype(jnp.float32)
-        ).astype(jnp.bfloat16)
-        copy = pltpu.make_async_copy(held.at[part], stored.at[part], sems.at[i])
-        copy.start()
-        copies.append(copy)
-    for copy in copies:
-        copy.wait()
+def moment_kernel(grad, moment, out):
+    out[...] = (0.9 * moment[...].astype(jnp.float32) + 0.1 * grad[...].astype(jnp.float32)).astype(
+        jnp.bfloat16
+    )
 
 
 def new_moment(grad, moment):
     return pl.pallas_call(
         moment_kernel,
         in_specs=[INSIDE, INSIDE],
-        out_specs=[INSIDE, ANYWHERE],
-        out_shape=[
-            pltpu.VMEM(grad.shape, grad.dtype),
-            jax.ShapeDtypeStruct(grad.shape, grad.dtype),
-        ],
-        scratch_shapes=[pltpu.SemaphoreType.DMA((len(cuts(grad.shape[0], 960)),))],
+        out_specs=INSIDE,
+        out_shape=pltpu.VMEM(grad.shape, grad.dtype),
         compiler_params=PARAMS,
         name="moment",
     )(inside(grad), inside(moment))
@@ -104,19 +92,20 @@
 
 
 def power_kernel(*refs):
-    *pieces, grad, other, grad_rows, other_rows, basis, rot, kept, sent = refs
+    *pieces, grad, other, grad_rows, other_rows, basis, rot, kept, sent, passed = refs
     basis[...] = jnp.concatenate([piece[...] for piece in pieces], 0)
     rot_own = dot(basis[...], grad[...], ((1,), (0,)))
     rot_other = dot(basis[...], other[...], ((1,), (0,)))
     rot[...] = rot_own
     both = jnp.concatenate([rot_own, rot_other], 1).astype(jnp.bfloat16)
-    half = kept.shape[0]
+    quarter = sent.shape[0]
     for at, size in cuts(grad.shape[0], 768):
         part = pl.ds(at, size)
         rows = jnp.concatenate([grad_rows[:, part], other_rows[:, part]], 0)
         product = dot(both, rows, ((1,), (0,)))
-        kept[:, part] = product[:half]
-        sent[:, part] = product[half:].astype(jnp.bfloat16)
+        kept[:, part] = product[: 2 * quarter]
+        sent[:, part] = product[2 * quarter : 3 * quarter].astype(jnp.bfloat16)
+        passed[:, part] = product[3 * quarter :].astype(jnp.bfloat16)
 
 
 def power_products(pieces, grads):
@@ -125,12 +114,13 @@
     return pl.pallas_call(
         power_kernel,
         in_specs=[INSIDE] * (len(pieces) + len(grads)),
-        out_specs=[INSIDE] * 4,
+        out_specs=[INSIDE] * 5,
         out_shape=[
             pltpu.VMEM((count, depth), jnp.bfloat16),
             pltpu.VMEM((count, rows), jnp.float32),
             pltpu.VMEM((count // 2, depth), jnp.float32),
-            pltpu.VMEM((count // 2, depth), jnp.bfloat16),
+            pltpu.VMEM((count // 4, depth), jnp.bfloat16),
+            pltpu.VMEM((count // 4, depth), jnp.bfloat16),
         ],
         compiler_params=PARAMS,
         name="power",
@@ -154,7 +144,11 @@
     )(inside(kept), inside(come))
 
 
-def scale_kernel(orders, own, basis, grad, moment, rot_half, second, scaled, second_next, rot, mom):
+def scale_kernel(
+    orders, own, basis, grad, moment, rot_half, second, scaled, second_next, stored, rot, mom, sem
+):
+    copy = pltpu.make_async_copy(moment, stored, sem)
+    copy.start()
     me = lax.axis_index("rows")
     core, chip = me & 1, me >> 1
     bits = len(orders[0])
@@ -191,6 +185,7 @@
                 rot[theirs] = jnp.where(first, ratio[own:], ratio[:own])
 
     scaled[...] = rot[...].astype(jnp.bfloat16)
+    copy.wait()
 
 
 def scaled_rotation(orders, own, basis, grad, moment, rot_half, second):
@@ -198,12 +193,13 @@
     return pl.pallas_call(
         functools.partial(scale_kernel, orders, own),
         in_specs=[INSIDE] * 5,
-        out_specs=[INSIDE] * 2,
+        out_specs=[INSIDE, INSIDE, ANYWHERE],
         out_shape=[
             pltpu.VMEM((count, rows), jnp.bfloat16),
             jax.ShapeDtypeStruct((count, rows), jnp.float32),
+            jax.ShapeDtypeStruct(moment.shape, moment.dtype),
         ],
-        scratch_shapes=[pltpu.VMEM((count, rows), jnp.float32)] * 2,
+        scratch_shapes=[pltpu.VMEM((count, rows), jnp.float32)] * 2 + [pltpu.SemaphoreType.DMA],
         compiler_params=PARAMS,
         name="scale",
     )(*map(inside, (basis, grad, moment, rot_half, second)))
@@ -266,30 +262,32 @@
     second_hand, grad, other = tie(second_hand, grad, other)
     grad_rows, other_rows = transposed(grad, other)
     last, grad_rows, other_rows = tie(last, grad_rows, other_rows)
-    held, rot_half, kept, sent = power_products(
+    held, rot_half, kept, sent, passed = power_products(
         (held, first, second_hand, last), (grad, other, grad_rows, other_rows)
     )
-    come = exchange(sent, bits - 1)
+    come = exchange(passed, bits - 1)
     moment, _ = tie(moment, sent)
-    moment_in, moment_next = new_moment(grad, moment)
-    held, _ = tie(held, moment_in)
+    moment = new_moment(grad, moment)
+    held, sent, moment = tie(held, sent, moment)
+    come_last = exchange(sent, bits - 1)
     theirs = across(held)
-    come, moment_in, moment_next = tie(come, moment_in, moment_next)
-    for step in reversed(range(bits)):
-        if step == 0:
-            break
+    come, moment = tie(come, moment)
+    quarter = sent.shape[0]
+    turned = kept[quarter:] + come.astype(jnp.float32)
+    come = exchange(turned.astype(jnp.bfloat16), bits - 2)
+    come_last, theirs, _ = tie(come_last, theirs, turned)
+    whole = jnp.concatenate([held, theirs], 0)
+    scaled, second_next, moment_next = scaled_rotation(
+        orders, own, whole, grad, moment, rot_half, second
+    )
+    come, scaled, second_next, moment_next = tie(come, scaled, second_next, moment_next)
+    kept = kept[:quarter] + come_last.astype(jnp.float32)
+    for step in reversed(range(bits - 2)):
         kept = kept + come.astype(jnp.float32)
         half = kept.shape[0] // 2
-        come = exchange(kept[half:].astype(jnp.bfloat16), step - 1)
+        come = exchange(kept[half:].astype(jnp.bfloat16), step)
         kept = kept[:half]
-        if step == bits - 1:
-            theirs, kept = tie(theirs, kept)
-            whole = jnp.concatenate([held, theirs], 0)
-            scaled, second_next = scaled_rotation(
-                orders, own, whole, grad, moment_in, rot_half, second
-            )
-            come, scaled, second_next = tie(come, scaled, second_next)
-        if step == bits - 2:
+        if step == 0:
             scaled, kept = tie(scaled, kept)
             update = new_update(whole, scaled)
             come, update = tie(come, update)

time: 28.9 us -> 30.3 us (1.048)
  waiting for transfers between devices: 2.24 us -> 2.95 us
  starting transfers between devices: 15.5 us -> 16 us
    pallas_call x1, Pallas kernels: 1.57 us -> 2.58 us  [scaled_rotation(): pl.pallas_call(functools.partial(scale_kernel, orders, own), in_specs=[IN...]
    pallas_call x1, Pallas kernels: 1.7 us -> 0.81 us  [new_moment(): pl.pallas_call(moment_kernel, in_specs=[INSIDE, INSIDE], out_specs=INSIDE...]
    ppermute x7 -> x8, waiting for transfers between devices: 2.23 us -> 2.95 us  [exchange(): return lax.ppermute(value, 'rows', pairs)]
    ppermute x7 -> x8, starting transfers between devices: 14.8 us -> 15.3 us  [exchange(): return lax.ppermute(value, 'rows', pairs)]
  transfers between devices with their start and end apart: 9 -> 10, of which waited for: 5 -> 4; matrix products, arithmetic and copies ran while one was open for 0% -> 0% of each run, Pallas kernels for 27% -> 26%
where the time goes in v9:
time: 30.3 us; the launch traced here: 30.1 us
  starting transfers between devices  16 us (53%)
  Pallas kernels  10.3 us (34%)
  waiting for transfers between devices  2.95 us (10%)
  between operations  0.72 us (2%)
    ppermute x8, starting transfers between devices, exchange(): return lax.ppermute(value, 'rows', pairs)  15.3 us
    ppermute x8, waiting for transfers between devices, exchange(): return lax.ppermute(value, 'rows', pairs)  2.95 us
    pallas_call x1, Pallas kernels, scaled_rotation(): pl.pallas_call(functools.partial(scale_kernel, orders, own), in_specs=[IN...  2.58 us
    pallas_call x1, Pallas kernels, new_update(): pl.pallas_call(update_kernel, in_specs=[INSIDE] * 2, out_specs=ANYWHERE,...  1.72 us
    pallas_call x1, Pallas kernels, load(): pl.pallas_call(load_kernel, in_specs=[pl.BlockSpec(memory_space=pltpu.HBM...  1.64 us
    pallas_call x1, Pallas kernels, power_products(): pl.pallas_call(power_kernel, in_specs=[INSIDE] * (len(pieces) + len(grads...  1.54 us
    pallas_call x1, Pallas kernels, transposed(): pl.pallas_call(transpose_kernel, in_specs=[INSIDE] * len(values), out_spe...  1.22 us
    pallas_call x1, Pallas kernels, new_moment(): pl.pallas_call(moment_kernel, in_specs=[INSIDE, INSIDE], out_specs=INSIDE...  0.81 us
  transfers between devices with their start and end apart: 10, of which 4 were waited for; matrix products, arithmetic and copies ran while one was open for 0% of the time, Pallas kernels for 26%

profile of v9, /device:TPU:0, one launch (start us, length us, event | category | flops | bytes accessed | tf_op | source)
XLA Modules:
  0.0 30.1 jit_solution(9921615137629205101)
XLA Ops:
  0.6 3.5 %collective-permute-start = (bf16[4,2880]{1,0:T(4,128)(2,1)}, bf16[4,2880]{1,0:T(4,128)(2,1)S(1)}, u32[]{:S(2)}, u32[]{:S(2)}) collective-permute-start(bf16[4,2880]{1,0:T(4,128)(2,1)} %refs_1_.1), channel_id=1, source_target_pairs={{0,9},{1,8},{2,11},{3,10},{4,13},{5,12},{6,15},{7,14},{8,1},{9,0},... | collective-permute-start | bytes 69128 | tf_op jit(solution)/shard_map/ppermute | solution.py:244
  4.2 1.6 %load.1 = (bf16[2880,384]{1,0:T(8,128)(2,1)S(1)}, bf16[4,2880]{1,0:T(4,128)(2,1)S(1)}) custom-call(bf16[2880,384]{1,0:T(8,128)(2,1)} %bitcast.9, bf16[4,2880]{1,0:T(4,128)(2,1)} %refs_1_.1), custom_call_target="tpu_custom_call" | custom-call | tf_op jit(solution)/shard_map/load/pallas_call | solution.py:48
  5.8 0.1 collective-permute-done
  6.0 0.6 %collective-permute-start.3 = (bf16[2880,384]{1,0:T(8,128)(2,1)S(1)}, bf16[2880,384]{1,0:T(8,128)(2,1)S(1)}, u32[]{:S(2)}, u32[]{:S(2)}) collective-permute-start(bf16[2880,384]{1,0:T(8,128)(2,1)S(1)} %get-tuple-element.51.refs_0_.refs_4_.grad), channel_id=1, source_target_pairs={{0,1},{1,0},{2,3},{3,2},{4,5},{5,4},{6,7},{7,6},{8,9},{9,8},{10,11... | collective-permute-start | bytes 6635528 | tf_op jit(solution)/shard_map/ppermute | solution.py:247
  6.6 1.7 %collective-permute-start.1 = (bf16[8,2880]{1,0:T(8,128)(2,1)S(1)}, bf16[8,2880]{1,0:T(8,128)(2,1)S(1)}, u32[]{:S(2)}, u32[]{:S(2)}) collective-permute-start(bf16[8,2880]{1,0:T(8,128)(2,1)S(1)} %pad_maximum_fusion.refs_0_), channel_id=1, source_target_pairs={{0,5},{1,2},{2,1},{3,6},{4,7},{5,0},{6,3},{7,4},{8,11},{9,12},{10,... | collective-permute-start | bytes 138248 | tf_op jit(solution)/shard_map/ppermute | solution.py:244
  8.3 1.2 %collective-permute-start.2 = (bf16[8,2880]{1,0:T(8,128)(2,1)S(1)}, bf16[8,2880]{1,0:T(8,128)(2,1)S(1)}, u32[]{:S(2)}, u32[]{:S(2)}) collective-permute-start(bf16[8,2880]{1,0:T(8,128)(2,1)S(1)} %pad_maximum_fusion.refs_0_), channel_id=1, source_target_pairs={{0,3},{1,4},{2,7},{3,0},{4,1},{5,6},{6,5},{7,2},{8,13},{9,10},{10,... | collective-permute-start | bytes 138248 | tf_op jit(solution)/shard_map/ppermute | solution.py:244
  9.5 0.7 %collective-permute-done.1.refs_1_ = bf16[8,2880]{1,0:T(8,128)(2,1)S(1)} collective-permute-done((bf16[8,2880]{1,0:T(8,128)(2,1)S(1)}, bf16[8,2880]{1,0:T(8,128)(2,1)S(1)}, u32[]{:S(2)}, u32[]{:S(2)}) %collective-permute-start.1) | collective-permute-done | bytes 46112 | tf_op jit(solution)/shard_map/ppermute | solution.py:244
  10.2 1.6 %collective-permute-start.4 = (bf16[8,2880]{1,0:T(8,128)(2,1)S(1)}, bf16[8,2880]{1,0:T(8,128)(2,1)S(1)}, u32[]{:S(2)}, u32[]{:S(2)}) collective-permute-start(bf16[8,2880]{1,0:T(8,128)(2,1)S(1)} %collective-permute-done.1.refs_1_), channel_id=1, source_target_pairs={{0,3},{1,4},{2,7},{3,0},{4,1},{5,6},{6,5},{7,2},{8,13},{9,10},{10,... | collective-permute-start | bytes 138248 | tf_op jit(solution)/shard_map/ppermute | solution.py:244
  11.7 0.0 collective-permute-done.2.refs_2_
  11.8 0.0 collective-permute-done.3.refs_1_.refs_5_
  11.8 1.2 %transpose.25 = (bf16[384,2880]{1,0:T(8,128)(2,1)S(1)}, bf16[384,2880]{1,0:T(8,128)(2,1)S(1)}) custom-call(bf16[2880,384]{1,0:T(8,128)(2,1)S(1)} %get-tuple-element.51.refs_0_.refs_4_.grad, bf16[2880,384]{1,0:T(8,128)(2,1)S(1)} %collective-permute-done.3.refs_1_.refs_5_), custom_call_target="tpu_custom_call" | custom-call | tf_op jit(solution)/shard_map/transpose/pallas_call | solution.py:84
  13.0 0.6 %collective-permute-done.4.refs_3_ = bf16[8,2880]{1,0:T(8,128)(2,1)S(1)} collective-permute-done((bf16[8,2880]{1,0:T(8,128)(2,1)S(1)}, bf16[8,2880]{1,0:T(8,128)(2,1)S(1)}, u32[]{:S(2)}, u32[]{:S(2)}) %collective-permute-start.4) | collective-permute-done | bytes 46112 | tf_op jit(solution)/shard_map/ppermute | solution.py:244
  13.7 0.0 copy-start
  13.7 1.5 %power.1 = (bf16[32,2880]{1,0:T(8,128)(2,1)S(1)}, f32[32,384]{1,0:T(8,128)S(1)}, f32[16,2880]{1,0:T(8,128)S(1)}, bf16[8,2880]{1,0:T(8,128)(2,1)S(1)}, bf16[8,2880]{1,0:T(8,128)(2,1)S(1)}) custom-call(bf16[8,2880]{1,0:T(8,128)(2,1)S(1)} %pad_maximum_fusion.refs_0_, bf16[8,2880]{1,0:T(8,128)(2,1)S(1)} %collective-permute-done.1.refs_1_, ...), custom_call_target="tpu_custom_call" | custom-call | tf_op jit(solution)/shard_map/power/pallas_call | solution.py:114
  15.2 0.0 copy-start.1
  15.2 1.7 %collective-permute-start.7 = (bf16[8,2880]{1,0:T(8,128)(2,1)S(1)}, bf16[8,2880]{1,0:T(8,128)(2,1)S(1)}, u32[]{:S(2)}, u32[]{:S(2)}) collective-permute-start(bf16[8,2880]{1,0:T(8,128)(2,1)S(1)} %get-tuple-element.64), channel_id=1, source_target_pairs={{0,3},{1,4},{2,7},{3,0},{4,1},{5,6},{6,5},{7,2},{8,13},{9,10},{10,... | collective-permute-start | bytes 138248 | tf_op jit(solution)/shard_map/ppermute | solution.py:244
  16.9 0.0 copy-done
  16.9 0.8 %moment.1 = bf16[2880,384]{1,0:T(8,128)(2,1)S(1)} custom-call(bf16[2880,384]{1,0:T(8,128)(2,1)S(1)} %get-tuple-element.51.refs_0_.refs_4_.grad, bf16[2880,384]{1,0:T(8,128)(2,1)S(1)} %bitcast.6), custom_call_target="tpu_custom_call" | custom-call | tf_op jit(solution)/shard_map/moment/pallas_call | solution.py:67
  17.7 0.2 collective-permute-start.6
  17.9 2.1 %collective-permute-start.5 = (bf16[8,2880]{1,0:T(8,128)(2,1)S(1)}, bf16[8,2880]{1,0:T(8,128)(2,1)S(1)}, u32[]{:S(2)}, u32[]{:S(2)}) collective-permute-start(bf16[8,2880]{1,0:T(8,128)(2,1)S(1)} %get-tuple-element.62), channel_id=1, source_target_pairs={{0,3},{1,4},{2,7},{3,0},{4,1},{5,6},{6,5},{7,2},{8,13},{9,10},{10,... | collective-permute-start | bytes 138248 | tf_op jit(solution)/shard_map/ppermute | solution.py:244
  20.0 0.0 collective-permute-done.7
  20.0 0.4 %collective-permute-start.8 = (bf16[8,2880]{1,0:T(8,128)(2,1)S(1)}, bf16[8,2880]{1,0:T(8,128)(2,1)S(1)}, u32[]{:S(2)}, u32[]{:S(2)}) collective-permute-start(bf16[8,2880]{1,0:T(8,128)(2,1)S(1)} %convert_add_fusion.1), channel_id=1, source_target_pairs={{0,5},{1,2},{2,1},{3,6},{4,7},{5,0},{6,3},{7,4},{8,11},{9,12},{10,... | collective-permute-start | bytes 138248 | tf_op jit(solution)/shard_map/ppermute | solution.py:244
  20.4 1.4 %collective-permute-done.5 = bf16[8,2880]{1,0:T(8,128)(2,1)S(1)} collective-permute-done((bf16[8,2880]{1,0:T(8,128)(2,1)S(1)}, bf16[8,2880]{1,0:T(8,128)(2,1)S(1)}, u32[]{:S(2)}, u32[]{:S(2)}) %collective-permute-start.5) | collective-permute-done | bytes 46112 | tf_op jit(solution)/shard_map/ppermute | solution.py:244
  21.9 0.0 collective-permute-done.6
  21.9 0.0 copy-done.1
  21.9 2.6 %scale.1 = (bf16[64,384]{1,0:T(8,128)(2,1)S(1)}, f32[64,384]{1,0:T(8,128)}, bf16[2880,384]{1,0:T(8,128)(2,1)}) custom-call(bf16[64,2880]{1,0:T(8,128)(2,1)S(1)} %constant_dynamic-update-slice_fusion.basis, bf16[2880,384]{1,0:T(8,128)(2,1)S(1)} %get-tuple-element.51.refs_0_.refs_4_.grad, bf16[2880,384]{1,0:T(8,128)(2,1)S(1)} %moment.1, ...), custom_call_target="tpu_custom_call" | custom-call | tf_op jit(solution)/shard_map/scale/pallas_call | solution.py:193
  24.5 0.0 collective-permute-done.8
  24.6 3.0 %collective-permute-start.9 = (bf16[4,2880]{1,0:T(4,128)(2,1)S(1)}, bf16[4,2880]{1,0:T(4,128)(2,1)S(1)}, u32[]{:S(2)}, u32[]{:S(2)}) collective-permute-start(bf16[4,2880]{1,0:T(4,128)(2,1)S(1)} %slice.22), channel_id=1, source_target_pairs={{0,9},{1,8},{2,11},{3,10},{4,13},{5,12},{6,15},{7,14},{8,1},{9,0},... | collective-permute-start | bytes 69128 | tf_op jit(solution)/shard_map/ppermute | solution.py:244
  27.6 1.7 %update.1 = bf16[2880,384]{1,0:T(8,128)(2,1)} custom-call(bf16[64,2880]{1,0:T(8,128)(2,1)S(1)} %constant_dynamic-update-slice_fusion.basis, bf16[64,384]{1,0:T(8,128)(2,1)S(1)} %get-tuple-element.76.scaled), custom_call_target="tpu_custom_call" | custom-call | tf_op jit(solution)/shard_map/update/pallas_call | solution.py:222
  29.3 0.0 collective-permute-done.9.come
  29.3 0.7 %normalise.1 = f32[4,2880]{1,0:T(4,128)} custom-call(f32[4,2880]{1,0:T(4,128)S(1)} %slice.18.kept, bf16[4,2880]{1,0:T(4,128)(2,1)S(1)} %collective-permute-done.9.come), custom_call_target="tpu_custom_call" | custom-call | tf_op jit(solution)/shard_map/normalise/pallas_call | solution.py:137
  (7 shorter events, 0.1 us)
Async XLA Ops:
  0.6 5.3 %collective-permute-start = (bf16[4,2880]{1,0:T(4,128)(2,1)}, bf16[4,2880]{1,0:T(4,128)(2,1)S(1)}, u32[]{:S(2)}, u32[]{:S(2)}) collective-permute-start(bf16[4,2880]{1,0:T(4,128)(2,1)} %refs_1_.1), channel_id=1, source_target_pairs={{0,9},{1,8},{2,11},{3,10},{4,13},{5,12},{6,15},{7,14},{8,1},{9,0},... | collective-permute-start | bytes 69128 | tf_op jit(solution)/shard_map/ppermute | solution.py:244
  6.0 5.8 %collective-permute-start.3 = (bf16[2880,384]{1,0:T(8,128)(2,1)S(1)}, bf16[2880,384]{1,0:T(8,128)(2,1)S(1)}, u32[]{:S(2)}, u32[]{:S(2)}) collective-permute-start(bf16[2880,384]{1,0:T(8,128)(2,1)S(1)} %get-tuple-element.51.refs_0_.refs_4_.grad), channel_id=1, source_target_pairs={{0,1},{1,0},{2,3},{3,2},{4,5},{5,4},{6,7},{7,6},{8,9},{9,8},{10,11... | collective-permute-start | bytes 6635528 | tf_op jit(solution)/shard_map/ppermute | solution.py:247
  6.6 3.6 %collective-permute-start.1 = (bf16[8,2880]{1,0:T(8,128)(2,1)S(1)}, bf16[8,2880]{1,0:T(8,128)(2,1)S(1)}, u32[]{:S(2)}, u32[]{:S(2)}) collective-permute-start(bf16[8,2880]{1,0:T(8,128)(2,1)S(1)} %pad_maximum_fusion.refs_0_), channel_id=1, source_target_pairs={{0,5},{1,2},{2,1},{3,6},{4,7},{5,0},{6,3},{7,4},{8,11},{9,12},{10,... | collective-permute-start | bytes 138248 | tf_op jit(solution)/shard_map/ppermute | solution.py:244
  8.3 3.5 %collective-permute-start.2 = (bf16[8,2880]{1,0:T(8,128)(2,1)S(1)}, bf16[8,2880]{1,0:T(8,128)(2,1)S(1)}, u32[]{:S(2)}, u32[]{:S(2)}) collective-permute-start(bf16[8,2880]{1,0:T(8,128)(2,1)S(1)} %pad_maximum_fusion.refs_0_), channel_id=1, source_target_pairs={{0,3},{1,4},{2,7},{3,0},{4,1},{5,6},{6,5},{7,2},{8,13},{9,10},{10,... | collective-permute-start | bytes 138248 | tf_op jit(solution)/shard_map/ppermute | solution.py:244
  10.2 3.5 %collective-permute-start.4 = (bf16[8,2880]{1,0:T(8,128)(2,1)S(1)}, bf16[8,2880]{1,0:T(8,128)(2,1)S(1)}, u32[]{:S(2)}, u32[]{:S(2)}) collective-permute-start(bf16[8,2880]{1,0:T(8,128)(2,1)S(1)} %collective-permute-done.1.refs_1_), channel_id=1, source_target_pairs={{0,3},{1,4},{2,7},{3,0},{4,1},{5,6},{6,5},{7,2},{8,13},{9,10},{10,... | collective-permute-start | bytes 138248 | tf_op jit(solution)/shard_map/ppermute | solution.py:244
  13.7 3.2 %copy-start = (bf16[384,2880]{0,1:T(8,128)(2,1)S(1)}, bf16[384,2880]{0,1:T(8,128)(2,1)}, u32[]{:S(2)}) copy-start(bf16[384,2880]{0,1:T(8,128)(2,1)} %param.5) | copy-start | bytes 6635524
  15.2 6.7 %copy-start.1 = (f32[384,64]{0,1:T(8,128)S(1)}, f32[384,64]{0,1:T(8,128)}, u32[]{:S(2)}) copy-start(f32[384,64]{0,1:T(8,128)} %param.6) | copy-start | bytes 294916
  15.2 4.8 %collective-permute-start.7 = (bf16[8,2880]{1,0:T(8,128)(2,1)S(1)}, bf16[8,2880]{1,0:T(8,128)(2,1)S(1)}, u32[]{:S(2)}, u32[]{:S(2)}) collective-permute-start(bf16[8,2880]{1,0:T(8,128)(2,1)S(1)} %get-tuple-element.64), channel_id=1, source_target_pairs={{0,3},{1,4},{2,7},{3,0},{4,1},{5,6},{6,5},{7,2},{8,13},{9,10},{10,... | collective-permute-start | bytes 138248 | tf_op jit(solution)/shard_map/ppermute | solution.py:244
  17.7 4.2 %collective-permute-start.6 = (bf16[32,2880]{1,0:T(8,128)(2,1)S(1)}, bf16[32,2880]{1,0:T(8,128)(2,1)S(1)}, u32[]{:S(2)}, u32[]{:S(2)}) collective-permute-start(bf16[32,2880]{1,0:T(8,128)(2,1)S(1)} %get-tuple-element.63), channel_id=1, source_target_pairs={{0,1},{1,0},{2,3},{3,2},{4,5},{5,4},{6,7},{7,6},{8,9},{9,8},{10,11... | collective-permute-start | bytes 552968 | tf_op jit(solution)/shard_map/ppermute | solution.py:247
  17.9 4.0 %collective-permute-start.5 = (bf16[8,2880]{1,0:T(8,128)(2,1)S(1)}, bf16[8,2880]{1,0:T(8,128)(2,1)S(1)}, u32[]{:S(2)}, u32[]{:S(2)}) collective-permute-start(bf16[8,2880]{1,0:T(8,128)(2,1)S(1)} %get-tuple-element.62), channel_id=1, source_target_pairs={{0,3},{1,4},{2,7},{3,0},{4,1},{5,6},{6,5},{7,2},{8,13},{9,10},{10,... | collective-permute-start | bytes 138248 | tf_op jit(solution)/shard_map/ppermute | solution.py:244
  20.0 4.5 %collective-permute-start.8 = (bf16[8,2880]{1,0:T(8,128)(2,1)S(1)}, bf16[8,2880]{1,0:T(8,128)(2,1)S(1)}, u32[]{:S(2)}, u32[]{:S(2)}) collective-permute-start(bf16[8,2880]{1,0:T(8,128)(2,1)S(1)} %convert_add_fusion.1), channel_id=1, source_target_pairs={{0,5},{1,2},{2,1},{3,6},{4,7},{5,0},{6,3},{7,4},{8,11},{9,12},{10,... | collective-permute-start | bytes 138248 | tf_op jit(solution)/shard_map/ppermute | solution.py:244
  24.6 4.8 %collective-permute-start.9 = (bf16[4,2880]{1,0:T(4,128)(2,1)S(1)}, bf16[4,2880]{1,0:T(4,128)(2,1)S(1)}, u32[]{:S(2)}, u32[]{:S(2)}) collective-permute-start(bf16[4,2880]{1,0:T(4,128)(2,1)S(1)} %slice.22), channel_id=1, source_target_pairs={{0,9},{1,8},{2,11},{3,10},{4,13},{5,12},{6,15},{7,14},{8,1},{9,0},... | collective-permute-start | bytes 69128 | tf_op jit(solution)/shard_map/ppermute | solution.py:244

commit v10 on v9

--- a/solution.py
+++ b/solution.py
@@ -32,16 +32,21 @@
     return lax.dot_general(left, right, (dims, ((), ())), preferred_element_type=jnp.float32)
 
 
-def load_kernel(*refs):
-    count = len(refs) // 2
-    sems = refs[-1]
-    copies = [
-        pltpu.make_async_copy(refs[i], refs[count + i], sems.at[i]) for i in range(count)
-    ]
-    for copy in copies:
-        copy.start()
-    for copy in copies:
+def start_copies(source, target, sems, size):
+    copies = []
+    for i, (at, rows) in enumerate(cuts(source.shape[0], size)):
+        part = pl.ds(at, rows)
+        copies.append(pltpu.make_async_copy(source.at[part], target.at[part], sems.at[i]))
+        copies[-1].start()
+    return copies
+
+
+def load_kernel(grad, basis, grad_in, basis_in, sems, sem):
+    last = pltpu.make_async_copy(basis, basis_in, sem)
+    last.start()
+    for copy in start_copies(grad, grad_in, sems, 720):
         copy.wait()
+    last.wait()
 
 
 def load(*values):
@@ -50,7 +55,10 @@
         in_specs=[pl.BlockSpec(memory_space=pltpu.HBM)] * len(values),
         out_specs=[INSIDE] * len(values),
         out_shape=[pltpu.VMEM(value.shape, value.dtype) for value in values],
-        scratch_shapes=[pltpu.SemaphoreType.DMA((len(values),))],
+        scratch_shapes=[
+            pltpu.SemaphoreType.DMA((len(cuts(values[0].shape[0], 720)),)),
+            pltpu.SemaphoreType.DMA,
+        ],
         compiler_params=PARAMS,
         name="load",
     )(*[pltpu.with_memory_space_constraint(value, pltpu.HBM) for value in values])
@@ -145,10 +153,9 @@
 
 
 def scale_kernel(
-    orders, own, basis, grad, moment, rot_half, second, scaled, second_next, stored, rot, mom, sem
+    orders, own, basis, grad, moment, rot_half, second, scaled, second_next, stored, rot, mom, sems
 ):
-    copy = pltpu.make_async_copy(moment, stored, sem)
-    copy.start()
+    copies = start_copies(moment, stored, sems, 720)
     me = lax.axis_index("rows")
     core, chip = me & 1, me >> 1
     bits = len(orders[0])
@@ -185,7 +192,8 @@
                 rot[theirs] = jnp.where(first, ratio[own:], ratio[:own])
 
     scaled[...] = rot[...].astype(jnp.bfloat16)
-    copy.wait()
+    for copy in copies:
+        copy.wait()
 
 
 def scaled_rotation(orders, own, basis, grad, moment, rot_half, second):
@@ -199,7 +207,11 @@
             jax.ShapeDtypeStruct((count, rows), jnp.float32),
             jax.ShapeDtypeStruct(moment.shape, moment.dtype),
         ],
-        scratch_shapes=[pltpu.VMEM((count, rows), jnp.float32)] * 2 + [pltpu.SemaphoreType.DMA],
+        scratch_shapes=[
+            pltpu.VMEM((count, rows), jnp.float32),
+            pltpu.VMEM((count, rows), jnp.float32),
+            pltpu.SemaphoreType.DMA((len(cuts(moment.shape[0], 720)),)),
+        ],
         compiler_params=PARAMS,
         name="scale",
     )(*map(inside, (basis, grad, moment, rot_half, second)))
@@ -275,7 +287,7 @@
     quarter = sent.shape[0]
     turned = kept[quarter:] + come.astype(jnp.float32)
     come = exchange(turned.astype(jnp.bfloat16), bits - 2)
-    come_last, theirs, _ = tie(come_last, theirs, turned)
+    theirs, _ = tie(theirs, turned)
     whole = jnp.concatenate([held, theirs], 0)
     scaled, second_next, moment_next = scaled_rotation(
         orders, own, whole, grad, moment, rot_half, second

time: 30.3 us -> 29.6 us (0.977)
  waiting for transfers between devices: 2.95 us -> 2.03 us
    ppermute x8, waiting for transfers between devices: 2.95 us -> 2.02 us  [exchange(): return lax.ppermute(value, 'rows', pairs)]
  transfers between devices with their start and end apart: 10 -> 10, of which waited for: 4 -> 5; matrix products, arithmetic and copies ran while one was open for 0% -> 0% of each run, Pallas kernels for 26% -> 27%
where the time goes in v10:
time: 29.6 us; the launch traced here: 29.1 us
  starting transfers between devices  16 us (54%)
  Pallas kernels  10.2 us (34%)
  waiting for transfers between devices  2.03 us (7%)
  between operations  0.71 us (2%)
    ppermute x8, starting transfers between devices, exchange(): return lax.ppermute(value, 'rows', pairs)  15.3 us
    pallas_call x1, Pallas kernels, scaled_rotation(): pl.pallas_call(functools.partial(scale_kernel, orders, own), in_specs=[IN...  2.59 us
    ppermute x8, waiting for transfers between devices, exchange(): return lax.ppermute(value, 'rows', pairs)  2.02 us
    pallas_call x1, Pallas kernels, new_update(): pl.pallas_call(update_kernel, in_specs=[INSIDE] * 2, out_specs=ANYWHERE,...  1.72 us
    pallas_call x1, Pallas kernels, load(): pl.pallas_call(load_kernel, in_specs=[pl.BlockSpec(memory_space=pltpu.HBM...  1.61 us
    pallas_call x1, Pallas kernels, power_products(): pl.pallas_call(power_kernel, in_specs=[INSIDE] * (len(pieces) + len(grads...  1.54 us
    pallas_call x1, Pallas kernels, transposed(): pl.pallas_call(transpose_kernel, in_specs=[INSIDE] * len(values), out_spe...  1.22 us
    pallas_call x1, Pallas kernels, new_moment(): pl.pallas_call(moment_kernel, in_specs=[INSIDE, INSIDE], out_specs=INSIDE...  0.81 us
  transfers between devices with their start and end apart: 10, of which 5 were waited for; matrix products, arithmetic and copies ran while one was open for 0% of the time, Pallas kernels for 27%

profile of v10, /device:TPU:0, one launch (start us, length us, event | category | flops | bytes accessed | tf_op | source)
XLA Modules:
  0.0 29.1 jit_solution(9874740763190304635)
XLA Ops:
  0.6 3.5 %collective-permute-start = (bf16[4,2880]{1,0:T(4,128)(2,1)}, bf16[4,2880]{1,0:T(4,128)(2,1)S(1)}, u32[]{:S(2)}, u32[]{:S(2)}) collective-permute-start(bf16[4,2880]{1,0:T(4,128)(2,1)} %basis.1), channel_id=1, source_target_pairs={{0,9},{1,8},{2,11},{3,10},{4,13},{5,12},{6,15},{7,14},{8,1},{9,0},... | collective-permute-start | bytes 69128 | tf_op jit(solution)/shard_map/ppermute | solution.py:256
  4.2 1.6 %load.1 = (bf16[2880,384]{1,0:T(8,128)(2,1)S(1)}, bf16[4,2880]{1,0:T(4,128)(2,1)S(1)}) custom-call(bf16[2880,384]{1,0:T(8,128)(2,1)} %bitcast.9, bf16[4,2880]{1,0:T(4,128)(2,1)} %basis.1), custom_call_target="tpu_custom_call" | custom-call | tf_op jit(solution)/shard_map/load/pallas_call | solution.py:53
  5.8 0.2 collective-permute-done
  6.0 0.6 %collective-permute-start.3 = (bf16[2880,384]{1,0:T(8,128)(2,1)S(1)}, bf16[2880,384]{1,0:T(8,128)(2,1)S(1)}, u32[]{:S(2)}, u32[]{:S(2)}) collective-permute-start(bf16[2880,384]{1,0:T(8,128)(2,1)S(1)} %get-tuple-element.50.refs_0_.refs_4_.grad), channel_id=1, source_target_pairs={{0,1},{1,0},{2,3},{3,2},{4,5},{5,4},{6,7},{7,6},{8,9},{9,8},{10,11... | collective-permute-start | bytes 6635528 | tf_op jit(solution)/shard_map/ppermute | solution.py:259
  6.6 1.7 %collective-permute-start.1 = (bf16[8,2880]{1,0:T(8,128)(2,1)S(1)}, bf16[8,2880]{1,0:T(8,128)(2,1)S(1)}, u32[]{:S(2)}, u32[]{:S(2)}) collective-permute-start(bf16[8,2880]{1,0:T(8,128)(2,1)S(1)} %pad_maximum_fusion.refs_0_), channel_id=1, source_target_pairs={{0,5},{1,2},{2,1},{3,6},{4,7},{5,0},{6,3},{7,4},{8,11},{9,12},{10,... | collective-permute-start | bytes 138248 | tf_op jit(solution)/shard_map/ppermute | solution.py:256
  8.3 1.2 %collective-permute-start.2 = (bf16[8,2880]{1,0:T(8,128)(2,1)S(1)}, bf16[8,2880]{1,0:T(8,128)(2,1)S(1)}, u32[]{:S(2)}, u32[]{:S(2)}) collective-permute-start(bf16[8,2880]{1,0:T(8,128)(2,1)S(1)} %pad_maximum_fusion.refs_0_), channel_id=1, source_target_pairs={{0,3},{1,4},{2,7},{3,0},{4,1},{5,6},{6,5},{7,2},{8,13},{9,10},{10,... | collective-permute-start | bytes 138248 | tf_op jit(solution)/shard_map/ppermute | solution.py:256
  9.5 0.6 %collective-permute-done.1.refs_1_ = bf16[8,2880]{1,0:T(8,128)(2,1)S(1)} collective-permute-done((bf16[8,2880]{1,0:T(8,128)(2,1)S(1)}, bf16[8,2880]{1,0:T(8,128)(2,1)S(1)}, u32[]{:S(2)}, u32[]{:S(2)}) %collective-permute-start.1) | collective-permute-done | bytes 46112 | tf_op jit(solution)/shard_map/ppermute | solution.py:256
  10.1 1.6 %collective-permute-start.4 = (bf16[8,2880]{1,0:T(8,128)(2,1)S(1)}, bf16[8,2880]{1,0:T(8,128)(2,1)S(1)}, u32[]{:S(2)}, u32[]{:S(2)}) collective-permute-start(bf16[8,2880]{1,0:T(8,128)(2,1)S(1)} %collective-permute-done.1.refs_1_), channel_id=1, source_target_pairs={{0,3},{1,4},{2,7},{3,0},{4,1},{5,6},{6,5},{7,2},{8,13},{9,10},{10,... | collective-permute-start | bytes 138248 | tf_op jit(solution)/shard_map/ppermute | solution.py:256
  11.7 0.1 collective-permute-done.2.refs_2_
  11.8 0.0 collective-permute-done.3.refs_1_.refs_5_
  11.8 1.2 %transpose.25 = (bf16[384,2880]{1,0:T(8,128)(2,1)S(1)}, bf16[384,2880]{1,0:T(8,128)(2,1)S(1)}) custom-call(bf16[2880,384]{1,0:T(8,128)(2,1)S(1)} %get-tuple-element.50.refs_0_.refs_4_.grad, bf16[2880,384]{1,0:T(8,128)(2,1)S(1)} %collective-permute-done.3.refs_1_.refs_5_), custom_call_target="tpu_custom_call" | custom-call | tf_op jit(solution)/shard_map/transpose/pallas_call | solution.py:92
  13.0 0.6 %collective-permute-done.4.refs_3_ = bf16[8,2880]{1,0:T(8,128)(2,1)S(1)} collective-permute-done((bf16[8,2880]{1,0:T(8,128)(2,1)S(1)}, bf16[8,2880]{1,0:T(8,128)(2,1)S(1)}, u32[]{:S(2)}, u32[]{:S(2)}) %collective-permute-start.4) | collective-permute-done | bytes 46112 | tf_op jit(solution)/shard_map/ppermute | solution.py:256
  13.6 0.0 copy-start
  13.6 1.5 %power.1 = (bf16[32,2880]{1,0:T(8,128)(2,1)S(1)}, f32[32,384]{1,0:T(8,128)S(1)}, f32[16,2880]{1,0:T(8,128)S(1)}, bf16[8,2880]{1,0:T(8,128)(2,1)S(1)}, bf16[8,2880]{1,0:T(8,128)(2,1)S(1)}) custom-call(bf16[8,2880]{1,0:T(8,128)(2,1)S(1)} %pad_maximum_fusion.refs_0_, bf16[8,2880]{1,0:T(8,128)(2,1)S(1)} %collective-permute-done.1.refs_1_, ...), custom_call_target="tpu_custom_call" | custom-call | tf_op jit(solution)/shard_map/power/pallas_call | solution.py:122
  15.2 0.0 copy-start.1
  15.2 1.7 %collective-permute-start.6 = (bf16[8,2880]{1,0:T(8,128)(2,1)S(1)}, bf16[8,2880]{1,0:T(8,128)(2,1)S(1)}, u32[]{:S(2)}, u32[]{:S(2)}) collective-permute-start(bf16[8,2880]{1,0:T(8,128)(2,1)S(1)} %get-tuple-element.62), channel_id=1, source_target_pairs={{0,3},{1,4},{2,7},{3,0},{4,1},{5,6},{6,5},{7,2},{8,13},{9,10},{10,... | collective-permute-start | bytes 138248 | tf_op jit(solution)/shard_map/ppermute | solution.py:256
  16.9 0.0 copy-done
  16.9 0.8 %moment.1 = bf16[2880,384]{1,0:T(8,128)(2,1)S(1)} custom-call(bf16[2880,384]{1,0:T(8,128)(2,1)S(1)} %get-tuple-element.50.refs_0_.refs_4_.grad, bf16[2880,384]{1,0:T(8,128)(2,1)S(1)} %bitcast.6), custom_call_target="tpu_custom_call" | custom-call | tf_op jit(solution)/shard_map/moment/pallas_call | solution.py:75
  17.7 0.2 collective-permute-start.8
  17.9 2.1 %collective-permute-start.5 = (bf16[8,2880]{1,0:T(8,128)(2,1)S(1)}, bf16[8,2880]{1,0:T(8,128)(2,1)S(1)}, u32[]{:S(2)}, u32[]{:S(2)}) collective-permute-start(bf16[8,2880]{1,0:T(8,128)(2,1)S(1)} %get-tuple-element.61), channel_id=1, source_target_pairs={{0,3},{1,4},{2,7},{3,0},{4,1},{5,6},{6,5},{7,2},{8,13},{9,10},{10,... | collective-permute-start | bytes 138248 | tf_op jit(solution)/shard_map/ppermute | solution.py:256
  20.0 0.0 collective-permute-done.6
  20.0 0.4 %collective-permute-start.7 = (bf16[8,2880]{1,0:T(8,128)(2,1)S(1)}, bf16[8,2880]{1,0:T(8,128)(2,1)S(1)}, u32[]{:S(2)}, u32[]{:S(2)}) collective-permute-start(bf16[8,2880]{1,0:T(8,128)(2,1)S(1)} %convert_add_fusion.1), channel_id=1, source_target_pairs={{0,5},{1,2},{2,1},{3,6},{4,7},{5,0},{6,3},{7,4},{8,11},{9,12},{10,... | collective-permute-start | bytes 138248 | tf_op jit(solution)/shard_map/ppermute | solution.py:256
  20.4 0.0 collective-permute-done.8
  20.5 0.0 copy-done.1
  20.5 2.6 %scale.1 = (bf16[64,384]{1,0:T(8,128)(2,1)S(1)}, f32[64,384]{1,0:T(8,128)}, bf16[2880,384]{1,0:T(8,128)(2,1)}) custom-call(bf16[64,2880]{1,0:T(8,128)(2,1)S(1)} %constant_dynamic-update-slice_fusion.basis, bf16[2880,384]{1,0:T(8,128)(2,1)S(1)} %get-tuple-element.50.refs_0_.refs_4_.grad, bf16[2880,384]{1,0:T(8,128)(2,1)S(1)} %moment.1, ...), custom_call_target="tpu_custom_call" | custom-call | tf_op jit(solution)/shard_map/scale/pallas_call | solution.py:201
  23.1 0.5 %collective-permute-done.7 = bf16[8,2880]{1,0:T(8,128)(2,1)S(1)} collective-permute-done((bf16[8,2880]{1,0:T(8,128)(2,1)S(1)}, bf16[8,2880]{1,0:T(8,128)(2,1)S(1)}, u32[]{:S(2)}, u32[]{:S(2)}) %collective-permute-start.7) | collective-permute-done | bytes 46112 | tf_op jit(solution)/shard_map/ppermute | solution.py:256
  23.6 0.0 collective-permute-done.5
  23.6 3.0 %collective-permute-start.9 = (bf16[4,2880]{1,0:T(4,128)(2,1)S(1)}, bf16[4,2880]{1,0:T(4,128)(2,1)S(1)}, u32[]{:S(2)}, u32[]{:S(2)}) collective-permute-start(bf16[4,2880]{1,0:T(4,128)(2,1)S(1)} %slice.22), channel_id=1, source_target_pairs={{0,9},{1,8},{2,11},{3,10},{4,13},{5,12},{6,15},{7,14},{8,1},{9,0},... | collective-permute-start | bytes 69128 | tf_op jit(solution)/shard_map/ppermute | solution.py:256
  26.6 1.7 %update.1 = bf16[2880,384]{1,0:T(8,128)(2,1)} custom-call(bf16[64,2880]{1,0:T(8,128)(2,1)S(1)} %constant_dynamic-update-slice_fusion.basis, bf16[64,384]{1,0:T(8,128)(2,1)S(1)} %get-tuple-element.74.scaled), custom_call_target="tpu_custom_call" | custom-call | tf_op jit(solution)/shard_map/update/pallas_call | solution.py:234
  28.4 0.0 collective-permute-done.9.come
  28.4 0.7 %normalise.1 = f32[4,2880]{1,0:T(4,128)} custom-call(f32[4,2880]{1,0:T(4,128)S(1)} %slice.18.kept, bf16[4,2880]{1,0:T(4,128)(2,1)S(1)} %collective-permute-done.9.come), custom_call_target="tpu_custom_call" | custom-call | tf_op jit(solution)/shard_map/normalise/pallas_call | solution.py:145
  (7 shorter events, 0.1 us)
Async XLA Ops:
  0.6 5.3 %collective-permute-start = (bf16[4,2880]{1,0:T(4,128)(2,1)}, bf16[4,2880]{1,0:T(4,128)(2,1)S(1)}, u32[]{:S(2)}, u32[]{:S(2)}) collective-permute-start(bf16[4,2880]{1,0:T(4,128)(2,1)} %basis.1), channel_id=1, source_target_pairs={{0,9},{1,8},{2,11},{3,10},{4,13},{5,12},{6,15},{7,14},{8,1},{9,0},... | collective-permute-start | bytes 69128 | tf_op jit(solution)/shard_map/ppermute | solution.py:256
  6.0 5.8 %collective-permute-start.3 = (bf16[2880,384]{1,0:T(8,128)(2,1)S(1)}, bf16[2880,384]{1,0:T(8,128)(2,1)S(1)}, u32[]{:S(2)}, u32[]{:S(2)}) collective-permute-start(bf16[2880,384]{1,0:T(8,128)(2,1)S(1)} %get-tuple-element.50.refs_0_.refs_4_.grad), channel_id=1, source_target_pairs={{0,1},{1,0},{2,3},{3,2},{4,5},{5,4},{6,7},{7,6},{8,9},{9,8},{10,11... | collective-permute-start | bytes 6635528 | tf_op jit(solution)/shard_map/ppermute | solution.py:259
  6.6 3.6 %collective-permute-start.1 = (bf16[8,2880]{1,0:T(8,128)(2,1)S(1)}, bf16[8,2880]{1,0:T(8,128)(2,1)S(1)}, u32[]{:S(2)}, u32[]{:S(2)}) collective-permute-start(bf16[8,2880]{1,0:T(8,128)(2,1)S(1)} %pad_maximum_fusion.refs_0_), channel_id=1, source_target_pairs={{0,5},{1,2},{2,1},{3,6},{4,7},{5,0},{6,3},{7,4},{8,11},{9,12},{10,... | collective-permute-start | bytes 138248 | tf_op jit(solution)/shard_map/ppermute | solution.py:256
  8.3 3.5 %collective-permute-start.2 = (bf16[8,2880]{1,0:T(8,128)(2,1)S(1)}, bf16[8,2880]{1,0:T(8,128)(2,1)S(1)}, u32[]{:S(2)}, u32[]{:S(2)}) collective-permute-start(bf16[8,2880]{1,0:T(8,128)(2,1)S(1)} %pad_maximum_fusion.refs_0_), channel_id=1, source_target_pairs={{0,3},{1,4},{2,7},{3,0},{4,1},{5,6},{6,5},{7,2},{8,13},{9,10},{10,... | collective-permute-start | bytes 138248 | tf_op jit(solution)/shard_map/ppermute | solution.py:256
  10.1 3.5 %collective-permute-start.4 = (bf16[8,2880]{1,0:T(8,128)(2,1)S(1)}, bf16[8,2880]{1,0:T(8,128)(2,1)S(1)}, u32[]{:S(2)}, u32[]{:S(2)}) collective-permute-start(bf16[8,2880]{1,0:T(8,128)(2,1)S(1)} %collective-permute-done.1.refs_1_), channel_id=1, source_target_pairs={{0,3},{1,4},{2,7},{3,0},{4,1},{5,6},{6,5},{7,2},{8,13},{9,10},{10,... | collective-permute-start | bytes 138248 | tf_op jit(solution)/shard_map/ppermute | solution.py:256
  13.6 3.3 %copy-start = (bf16[384,2880]{0,1:T(8,128)(2,1)S(1)}, bf16[384,2880]{0,1:T(8,128)(2,1)}, u32[]{:S(2)}) copy-start(bf16[384,2880]{0,1:T(8,128)(2,1)} %param.5) | copy-start | bytes 6635524
  15.2 5.3 %copy-start.1 = (f32[384,64]{0,1:T(8,128)S(1)}, f32[384,64]{0,1:T(8,128)}, u32[]{:S(2)}) copy-start(f32[384,64]{0,1:T(8,128)} %param.6) | copy-start | bytes 294916
  15.2 4.8 %collective-permute-start.6 = (bf16[8,2880]{1,0:T(8,128)(2,1)S(1)}, bf16[8,2880]{1,0:T(8,128)(2,1)S(1)}, u32[]{:S(2)}, u32[]{:S(2)}) collective-permute-start(bf16[8,2880]{1,0:T(8,128)(2,1)S(1)} %get-tuple-element.62), channel_id=1, source_target_pairs={{0,3},{1,4},{2,7},{3,0},{4,1},{5,6},{6,5},{7,2},{8,13},{9,10},{10,... | collective-permute-start | bytes 138248 | tf_op jit(solution)/shard_map/ppermute | solution.py:256
  17.7 2.7 %collective-permute-start.8 = (bf16[32,2880]{1,0:T(8,128)(2,1)S(1)}, bf16[32,2880]{1,0:T(8,128)(2,1)S(1)}, u32[]{:S(2)}, u32[]{:S(2)}) collective-permute-start(bf16[32,2880]{1,0:T(8,128)(2,1)S(1)} %get-tuple-element.65), channel_id=1, source_target_pairs={{0,1},{1,0},{2,3},{3,2},{4,5},{5,4},{6,7},{7,6},{8,9},{9,8},{10,11... | collective-permute-start | bytes 552968 | tf_op jit(solution)/shard_map/ppermute | solution.py:259
  17.9 5.7 %collective-permute-start.5 = (bf16[8,2880]{1,0:T(8,128)(2,1)S(1)}, bf16[8,2880]{1,0:T(8,128)(2,1)S(1)}, u32[]{:S(2)}, u32[]{:S(2)}) collective-permute-start(bf16[8,2880]{1,0:T(8,128)(2,1)S(1)} %get-tuple-element.61), channel_id=1, source_target_pairs={{0,3},{1,4},{2,7},{3,0},{4,1},{5,6},{6,5},{7,2},{8,13},{9,10},{10,... | collective-permute-start | bytes 138248 | tf_op jit(solution)/shard_map/ppermute | solution.py:256
  20.0 3.6 %collective-permute-start.7 = (bf16[8,2880]{1,0:T(8,128)(2,1)S(1)}, bf16[8,2880]{1,0:T(8,128)(2,1)S(1)}, u32[]{:S(2)}, u32[]{:S(2)}) collective-permute-start(bf16[8,2880]{1,0:T(8,128)(2,1)S(1)} %convert_add_fusion.1), channel_id=1, source_target_pairs={{0,5},{1,2},{2,1},{3,6},{4,7},{5,0},{6,3},{7,4},{8,11},{9,12},{10,... | collective-permute-start | bytes 138248 | tf_op jit(solution)/shard_map/ppermute | solution.py:256
  23.6 4.7 %collective-permute-start.9 = (bf16[4,2880]{1,0:T(4,128)(2,1)S(1)}, bf16[4,2880]{1,0:T(4,128)(2,1)S(1)}, u32[]{:S(2)}, u32[]{:S(2)}) collective-permute-start(bf16[4,2880]{1,0:T(4,128)(2,1)S(1)} %slice.22), channel_id=1, source_target_pairs={{0,9},{1,8},{2,11},{3,10},{4,13},{5,12},{6,15},{7,14},{8,1},{9,0},... | collective-permute-start | bytes 69128 | tf_op jit(solution)/shard_map/ppermute | solution.py:256

commit v11 on v10

--- a/solution.py
+++ b/solution.py
@@ -65,18 +65,30 @@
     return out
 
 
-def moment_kernel(grad, moment, out):
-    out[...] = (0.9 * moment[...].astype(jnp.float32) + 0.1 * grad[...].astype(jnp.float32)).astype(
-        jnp.bfloat16
-    )
+def moment_kernel(grad, moment, held, stored, sems):
+    copies = []
+    for i, (at, size) in enumerate(cuts(grad.shape[0], 960)):
+        part = pl.ds(at, size)
+        held[part] = (
+            0.9 * moment[part].astype(jnp.float32) + 0.1 * grad[part].astype(jnp.float32)
+        ).astype(jnp.bfloat16)
+        copy = pltpu.make_async_copy(held.at[part], stored.at[part], sems.at[i])
+        copy.start()
+        copies.append(copy)
+    for copy in copies:
+        copy.wait()
 
 
 def new_moment(grad, moment):
     return pl.pallas_call(
         moment_kernel,
         in_specs=[INSIDE, INSIDE],
-        out_specs=INSIDE,
-        out_shape=pltpu.VMEM(grad.shape, grad.dtype),
+        out_specs=[INSIDE, ANYWHERE],
+        out_shape=[
+            pltpu.VMEM(grad.shape, grad.dtype),
+            jax.ShapeDtypeStruct(grad.shape, grad.dtype),
+        ],
+        scratch_shapes=[pltpu.SemaphoreType.DMA((len(cuts(grad.shape[0], 960)),))],
         compiler_params=PARAMS,
         name="moment",
     )(inside(grad), inside(moment))
@@ -153,9 +165,8 @@
 
 
 def scale_kernel(
-    orders, own, basis, grad, moment, rot_half, second, scaled, second_next, stored, rot, mom, sems
+    orders, own, basis, grad, moment, rot_half, second, scaled, second_next, rot, mom
 ):
-    copies = start_copies(moment, stored, sems, 720)
     me = lax.axis_index("rows")
     core, chip = me & 1, me >> 1
     bits = len(orders[0])
@@ -192,8 +203,6 @@
                 rot[theirs] = jnp.where(first, ratio[own:], ratio[:own])
 
     scaled[...] = rot[...].astype(jnp.bfloat16)
-    for copy in copies:
-        copy.wait()
 
 
 def scaled_rotation(orders, own, basis, grad, moment, rot_half, second):
@@ -201,17 +210,12 @@
     return pl.pallas_call(
         functools.partial(scale_kernel, orders, own),
         in_specs=[INSIDE] * 5,
-        out_specs=[INSIDE, INSIDE, ANYWHERE],
+        out_specs=[INSIDE, INSIDE],
         out_shape=[
             pltpu.VMEM((count, rows), jnp.bfloat16),
             jax.ShapeDtypeStruct((count, rows), jnp.float32),
-            jax.ShapeDtypeStruct(moment.shape, moment.dtype),
-        ],
-        scratch_shapes=[
-            pltpu.VMEM((count, rows), jnp.float32),
-            pltpu.VMEM((count, rows), jnp.float32),
-            pltpu.SemaphoreType.DMA((len(cuts(moment.shape[0], 720)),)),
-        ],
+        ],
+        scratch_shapes=[pltpu.VMEM((count, rows), jnp.float32)] * 2,
         compiler_params=PARAMS,
         name="scale",
     )(*map(inside, (basis, grad, moment, rot_half, second)))
@@ -279,8 +283,8 @@
     )
     come = exchange(passed, bits - 1)
     moment, _ = tie(moment, sent)
-    moment = new_moment(grad, moment)
-    held, sent, moment = tie(held, sent, moment)
+    moment, moment_next = new_moment(grad, moment)
+    held, sent, moment, moment_next = tie(held, sent, moment, moment_next)
     come_last = exchange(sent, bits - 1)
     theirs = across(held)
     come, moment = tie(come, moment)
@@ -289,10 +293,10 @@
     come = exchange(turned.astype(jnp.bfloat16), bits - 2)
     theirs, _ = tie(theirs, turned)
     whole = jnp.concatenate([held, theirs], 0)
-    scaled, second_next, moment_next = scaled_rotation(
+    scaled, second_next = scaled_rotation(
         orders, own, whole, grad, moment, rot_half, second
     )
-    come, scaled, second_next, moment_next = tie(come, scaled, second_next, moment_next)
+    come, scaled, second_next = tie(come, scaled, second_next)
     kept = kept[:quarter] + come_last.astype(jnp.float32)
     for step in reversed(range(bits - 2)):
         kept = kept + come.astype(jnp.float32)

time: 29.6 us -> 30.3 us (1.024)
  waiting for transfers between devices: 2.03 us -> 3.43 us
  starting transfers between devices: 16 us -> 15.4 us
    ppermute x8, waiting for transfers between devices: 2.02 us -> 3.43 us  [exchange(): return lax.ppermute(value, 'rows', pairs)]
    pallas_call x1, Pallas kernels: 2.59 us -> 1.54 us  [scaled_rotation(): pl.pallas_call(functools.partial(scale_kernel, orders, own), in_specs=[IN...]
    pallas_call x1, Pallas kernels: 0.81 us -> 1.7 us  [new_moment(): pl.pallas_call(moment_kernel, in_specs=[INSIDE, INSIDE], out_specs=[INSID...]
    ppermute x8, starting transfers between devices: 15.3 us -> 14.7 us  [exchange(): return lax.ppermute(value, 'rows', pairs)]
  transfers between devices with their start and end apart: 10 -> 10, of which waited for: 5 -> 5; matrix products, arithmetic and copies ran while one was open for 0% -> 0% of each run, Pallas kernels for 27% -> 26%
where the time goes in v11:
time: 30.3 us; the launch traced here: 29.8 us
  starting transfers between devices  15.4 us (51%)
  Pallas kernels  10.1 us (33%)
  waiting for transfers between devices  3.43 us (11%)
  between operations  0.71 us (2%)
    ppermute x8, starting transfers between devices, exchange(): return lax.ppermute(value, 'rows', pairs)  14.7 us
    ppermute x8, waiting for transfers between devices, exchange(): return lax.ppermute(value, 'rows', pairs)  3.43 us
    pallas_call x1, Pallas kernels, new_update(): pl.pallas_call(update_kernel, in_specs=[INSIDE] * 2, out_specs=ANYWHERE,...  1.72 us
    pallas_call x1, Pallas kernels, new_moment(): pl.pallas_call(moment_kernel, in_specs=[INSIDE, INSIDE], out_specs=[INSID...  1.7 us
    pallas_call x1, Pallas kernels, load(): pl.pallas_call(load_kernel, in_specs=[pl.BlockSpec(memory_space=pltpu.HBM...  1.61 us
    pallas_call x1, Pallas kernels, scaled_rotation(): pl.pallas_call(functools.partial(scale_kernel, orders, own), in_specs=[IN...  1.54 us
    pallas_call x1, Pallas kernels, power_products(): pl.pallas_call(power_kernel, in_specs=[INSIDE] * (len(pieces) + len(grads...  1.54 us
    pallas_call x1, Pallas kernels, transposed(): pl.pallas_call(transpose_kernel, in_specs=[INSIDE] * len(values), out_spe...  1.22 us
  transfers between devices with their start and end apart: 10, of which 5 were waited for; matrix products, arithmetic and copies ran while one was open for 0% of the time, Pallas kernels for 26%

profile of v11, /device:TPU:0, one launch (start us, length us, event | category | flops | bytes accessed | tf_op | source)
XLA Modules:
  0.0 29.8 jit_solution(8840443456678597595)
XLA Ops:
  0.6 3.5 %collective-permute-start = (bf16[4,2880]{1,0:T(4,128)(2,1)}, bf16[4,2880]{1,0:T(4,128)(2,1)S(1)}, u32[]{:S(2)}, u32[]{:S(2)}) collective-permute-start(bf16[4,2880]{1,0:T(4,128)(2,1)} %basis.1), channel_id=1, source_target_pairs={{0,9},{1,8},{2,11},{3,10},{4,13},{5,12},{6,15},{7,14},{8,1},{9,0},... | collective-permute-start | bytes 69128 | tf_op jit(solution)/shard_map/ppermute | solution.py:260
  4.2 1.6 %load.1 = (bf16[2880,384]{1,0:T(8,128)(2,1)S(1)}, bf16[4,2880]{1,0:T(4,128)(2,1)S(1)}) custom-call(bf16[2880,384]{1,0:T(8,128)(2,1)} %bitcast.9, bf16[4,2880]{1,0:T(4,128)(2,1)} %basis.1), custom_call_target="tpu_custom_call" | custom-call | tf_op jit(solution)/shard_map/load/pallas_call | solution.py:53
  5.8 0.2 collective-permute-done
  6.0 0.6 %collective-permute-start.3 = (bf16[2880,384]{1,0:T(8,128)(2,1)S(1)}, bf16[2880,384]{1,0:T(8,128)(2,1)S(1)}, u32[]{:S(2)}, u32[]{:S(2)}) collective-permute-start(bf16[2880,384]{1,0:T(8,128)(2,1)S(1)} %get-tuple-element.51.refs_0_.refs_4_.grad), channel_id=1, source_target_pairs={{0,1},{1,0},{2,3},{3,2},{4,5},{5,4},{6,7},{7,6},{8,9},{9,8},{10,11... | collective-permute-start | bytes 6635528 | tf_op jit(solution)/shard_map/ppermute | solution.py:263
  6.6 1.7 %collective-permute-start.1 = (bf16[8,2880]{1,0:T(8,128)(2,1)S(1)}, bf16[8,2880]{1,0:T(8,128)(2,1)S(1)}, u32[]{:S(2)}, u32[]{:S(2)}) collective-permute-start(bf16[8,2880]{1,0:T(8,128)(2,1)S(1)} %pad_maximum_fusion.refs_0_), channel_id=1, source_target_pairs={{0,5},{1,2},{2,1},{3,6},{4,7},{5,0},{6,3},{7,4},{8,11},{9,12},{10,... | collective-permute-start | bytes 138248 | tf_op jit(solution)/shard_map/ppermute | solution.py:260
  8.3 1.2 %collective-permute-start.2 = (bf16[8,2880]{1,0:T(8,128)(2,1)S(1)}, bf16[8,2880]{1,0:T(8,128)(2,1)S(1)}, u32[]{:S(2)}, u32[]{:S(2)}) collective-permute-start(bf16[8,2880]{1,0:T(8,128)(2,1)S(1)} %pad_maximum_fusion.refs_0_), channel_id=1, source_target_pairs={{0,3},{1,4},{2,7},{3,0},{4,1},{5,6},{6,5},{7,2},{8,13},{9,10},{10,... | collective-permute-start | bytes 138248 | tf_op jit(solution)/shard_map/ppermute | solution.py:260
  9.5 0.6 %collective-permute-done.1.refs_1_ = bf16[8,2880]{1,0:T(8,128)(2,1)S(1)} collective-permute-done((bf16[8,2880]{1,0:T(8,128)(2,1)S(1)}, bf16[8,2880]{1,0:T(8,128)(2,1)S(1)}, u32[]{:S(2)}, u32[]{:S(2)}) %collective-permute-start.1) | collective-permute-done | bytes 46112 | tf_op jit(solution)/shard_map/ppermute | solution.py:260
  10.1 1.6 %collective-permute-start.4 = (bf16[8,2880]{1,0:T(8,128)(2,1)S(1)}, bf16[8,2880]{1,0:T(8,128)(2,1)S(1)}, u32[]{:S(2)}, u32[]{:S(2)}) collective-permute-start(bf16[8,2880]{1,0:T(8,128)(2,1)S(1)} %collective-permute-done.1.refs_1_), channel_id=1, source_target_pairs={{0,3},{1,4},{2,7},{3,0},{4,1},{5,6},{6,5},{7,2},{8,13},{9,10},{10,... | collective-permute-start | bytes 138248 | tf_op jit(solution)/shard_map/ppermute | solution.py:260
  11.7 0.1 collective-permute-done.2.refs_2_
  11.8 0.0 collective-permute-done.3.refs_1_.refs_5_
  11.8 1.2 %transpose.25 = (bf16[384,2880]{1,0:T(8,128)(2,1)S(1)}, bf16[384,2880]{1,0:T(8,128)(2,1)S(1)}) custom-call(bf16[2880,384]{1,0:T(8,128)(2,1)S(1)} %get-tuple-element.51.refs_0_.refs_4_.grad, bf16[2880,384]{1,0:T(8,128)(2,1)S(1)} %collective-permute-done.3.refs_1_.refs_5_), custom_call_target="tpu_custom_call" | custom-call | tf_op jit(solution)/shard_map/transpose/pallas_call | solution.py:104
  13.0 0.6 %collective-permute-done.4.refs_3_ = bf16[8,2880]{1,0:T(8,128)(2,1)S(1)} collective-permute-done((bf16[8,2880]{1,0:T(8,128)(2,1)S(1)}, bf16[8,2880]{1,0:T(8,128)(2,1)S(1)}, u32[]{:S(2)}, u32[]{:S(2)}) %collective-permute-start.4) | collective-permute-done | bytes 46112 | tf_op jit(solution)/shard_map/ppermute | solution.py:260
  13.6 0.0 copy-start
  13.6 1.5 %power.1 = (bf16[32,2880]{1,0:T(8,128)(2,1)S(1)}, f32[32,384]{1,0:T(8,128)S(1)}, f32[16,2880]{1,0:T(8,128)S(1)}, bf16[8,2880]{1,0:T(8,128)(2,1)S(1)}, bf16[8,2880]{1,0:T(8,128)(2,1)S(1)}) custom-call(bf16[8,2880]{1,0:T(8,128)(2,1)S(1)} %pad_maximum_fusion.refs_0_, bf16[8,2880]{1,0:T(8,128)(2,1)S(1)} %collective-permute-done.1.refs_1_, ...), custom_call_target="tpu_custom_call" | custom-call | tf_op jit(solution)/shard_map/power/pallas_call | solution.py:134
  15.2 0.0 copy-start.1
  15.2 1.7 %collective-permute-start.6 = (bf16[8,2880]{1,0:T(8,128)(2,1)S(1)}, bf16[8,2880]{1,0:T(8,128)(2,1)S(1)}, u32[]{:S(2)}, u32[]{:S(2)}) collective-permute-start(bf16[8,2880]{1,0:T(8,128)(2,1)S(1)} %get-tuple-element.65), channel_id=1, source_target_pairs={{0,3},{1,4},{2,7},{3,0},{4,1},{5,6},{6,5},{7,2},{8,13},{9,10},{10,... | collective-permute-start | bytes 138248 | tf_op jit(solution)/shard_map/ppermute | solution.py:260
  16.9 0.0 copy-done
  16.9 1.7 %moment.1 = (bf16[2880,384]{1,0:T(8,128)(2,1)S(1)}, bf16[2880,384]{1,0:T(8,128)(2,1)}) custom-call(bf16[2880,384]{1,0:T(8,128)(2,1)S(1)} %get-tuple-element.51.refs_0_.refs_4_.grad, bf16[2880,384]{1,0:T(8,128)(2,1)S(1)} %bitcast.6), custom_call_target="tpu_custom_call" | custom-call | tf_op jit(solution)/shard_map/moment/pallas_call | solution.py:83
  18.6 0.2 collective-permute-start.8
  18.8 2.1 %collective-permute-start.5 = (bf16[8,2880]{1,0:T(8,128)(2,1)S(1)}, bf16[8,2880]{1,0:T(8,128)(2,1)S(1)}, u32[]{:S(2)}, u32[]{:S(2)}) collective-permute-start(bf16[8,2880]{1,0:T(8,128)(2,1)S(1)} %get-tuple-element.64), channel_id=1, source_target_pairs={{0,3},{1,4},{2,7},{3,0},{4,1},{5,6},{6,5},{7,2},{8,13},{9,10},{10,... | collective-permute-start | bytes 138248 | tf_op jit(solution)/shard_map/ppermute | solution.py:260
  20.9 0.0 collective-permute-done.6
  20.9 0.1 collective-permute-start.7
  21.0 0.0 collective-permute-done.8
  21.0 0.0 copy-done.1
  21.0 1.5 %scale.1 = (bf16[64,384]{1,0:T(8,128)(2,1)S(1)}, f32[64,384]{1,0:T(8,128)}) custom-call(bf16[64,2880]{1,0:T(8,128)(2,1)S(1)} %constant_dynamic-update-slice_fusion.basis, bf16[2880,384]{1,0:T(8,128)(2,1)S(1)} %get-tuple-element.51.refs_0_.refs_4_.grad, bf16[2880,384]{1,0:T(8,128)(2,1)S(1)} %get-tuple-element.70.moment, ...), custom_call_target="tpu_custom_call" | custom-call | tf_op jit(solution)/shard_map/scale/pallas_call | solution.py:210
  22.6 1.9 %collective-permute-done.7 = bf16[8,2880]{1,0:T(8,128)(2,1)S(1)} collective-permute-done((bf16[8,2880]{1,0:T(8,128)(2,1)S(1)}, bf16[8,2880]{1,0:T(8,128)(2,1)S(1)}, u32[]{:S(2)}, u32[]{:S(2)}) %collective-permute-start.7) | collective-permute-done | bytes 46112 | tf_op jit(solution)/shard_map/ppermute | solution.py:260
  24.5 0.0 collective-permute-done.5
  24.5 2.8 %collective-permute-start.9 = (bf16[4,2880]{1,0:T(4,128)(2,1)S(1)}, bf16[4,2880]{1,0:T(4,128)(2,1)S(1)}, u32[]{:S(2)}, u32[]{:S(2)}) collective-permute-start(bf16[4,2880]{1,0:T(4,128)(2,1)S(1)} %slice.22), channel_id=1, source_target_pairs={{0,9},{1,8},{2,11},{3,10},{4,13},{5,12},{6,15},{7,14},{8,1},{9,0},... | collective-permute-start | bytes 69128 | tf_op jit(solution)/shard_map/ppermute | solution.py:260
  27.3 1.7 %update.1 = bf16[2880,384]{1,0:T(8,128)(2,1)} custom-call(bf16[64,2880]{1,0:T(8,128)(2,1)S(1)} %constant_dynamic-update-slice_fusion.basis, bf16[64,384]{1,0:T(8,128)(2,1)S(1)} %get-tuple-element.76.scaled), custom_call_target="tpu_custom_call" | custom-call | tf_op jit(solution)/shard_map/update/pallas_call | solution.py:238
  29.0 0.0 collective-permute-done.9.come
  29.0 0.7 %normalise.1 = f32[4,2880]{1,0:T(4,128)} custom-call(f32[4,2880]{1,0:T(4,128)S(1)} %slice.18.kept, bf16[4,2880]{1,0:T(4,128)(2,1)S(1)} %collective-permute-done.9.come), custom_call_target="tpu_custom_call" | custom-call | tf_op jit(solution)/shard_map/normalise/pallas_call | solution.py:157
  (7 shorter events, 0.1 us)
Async XLA Ops:
  0.6 5.3 %collective-permute-start = (bf16[4,2880]{1,0:T(4,128)(2,1)}, bf16[4,2880]{1,0:T(4,128)(2,1)S(1)}, u32[]{:S(2)}, u32[]{:S(2)}) collective-permute-start(bf16[4,2880]{1,0:T(4,128)(2,1)} %basis.1), channel_id=1, source_target_pairs={{0,9},{1,8},{2,11},{3,10},{4,13},{5,12},{6,15},{7,14},{8,1},{9,0},... | collective-permute-start | bytes 69128 | tf_op jit(solution)/shard_map/ppermute | solution.py:260
  6.0 5.8 %collective-permute-start.3 = (bf16[2880,384]{1,0:T(8,128)(2,1)S(1)}, bf16[2880,384]{1,0:T(8,128)(2,1)S(1)}, u32[]{:S(2)}, u32[]{:S(2)}) collective-permute-start(bf16[2880,384]{1,0:T(8,128)(2,1)S(1)} %get-tuple-element.51.refs_0_.refs_4_.grad), channel_id=1, source_target_pairs={{0,1},{1,0},{2,3},{3,2},{4,5},{5,4},{6,7},{7,6},{8,9},{9,8},{10,11... | collective-permute-start | bytes 6635528 | tf_op jit(solution)/shard_map/ppermute | solution.py:263
  6.6 3.6 %collective-permute-start.1 = (bf16[8,2880]{1,0:T(8,128)(2,1)S(1)}, bf16[8,2880]{1,0:T(8,128)(2,1)S(1)}, u32[]{:S(2)}, u32[]{:S(2)}) collective-permute-start(bf16[8,2880]{1,0:T(8,128)(2,1)S(1)} %pad_maximum_fusion.refs_0_), channel_id=1, source_target_pairs={{0,5},{1,2},{2,1},{3,6},{4,7},{5,0},{6,3},{7,4},{8,11},{9,12},{10,... | collective-permute-start | bytes 138248 | tf_op jit(solution)/shard_map/ppermute | solution.py:260
  8.3 3.5 %collective-permute-start.2 = (bf16[8,2880]{1,0:T(8,128)(2,1)S(1)}, bf16[8,2880]{1,0:T(8,128)(2,1)S(1)}, u32[]{:S(2)}, u32[]{:S(2)}) collective-permute-start(bf16[8,2880]{1,0:T(8,128)(2,1)S(1)} %pad_maximum_fusion.refs_0_), channel_id=1, source_target_pairs={{0,3},{1,4},{2,7},{3,0},{4,1},{5,6},{6,5},{7,2},{8,13},{9,10},{10,... | collective-permute-start | bytes 138248 | tf_op jit(solution)/shard_map/ppermute | solution.py:260
  10.1 3.5 %collective-permute-start.4 = (bf16[8,2880]{1,0:T(8,128)(2,1)S(1)}, bf16[8,2880]{1,0:T(8,128)(2,1)S(1)}, u32[]{:S(2)}, u32[]{:S(2)}) collective-permute-start(bf16[8,2880]{1,0:T(8,128)(2,1)S(1)} %collective-permute-done.1.refs_1_), channel_id=1, source_target_pairs={{0,3},{1,4},{2,7},{3,0},{4,1},{5,6},{6,5},{7,2},{8,13},{9,10},{10,... | collective-permute-start | bytes 138248 | tf_op jit(solution)/shard_map/ppermute | solution.py:260
  13.6 3.3 %copy-start = (bf16[384,2880]{0,1:T(8,128)(2,1)S(1)}, bf16[384,2880]{0,1:T(8,128)(2,1)}, u32[]{:S(2)}) copy-start(bf16[384,2880]{0,1:T(8,128)(2,1)} %param.5) | copy-start | bytes 6635524
  15.2 5.8 %copy-start.1 = (f32[384,64]{0,1:T(8,128)S(1)}, f32[384,64]{0,1:T(8,128)}, u32[]{:S(2)}) copy-start(f32[384,64]{0,1:T(8,128)} %param.6) | copy-start | bytes 294916
  15.2 5.7 %collective-permute-start.6 = (bf16[8,2880]{1,0:T(8,128)(2,1)S(1)}, bf16[8,2880]{1,0:T(8,128)(2,1)S(1)}, u32[]{:S(2)}, u32[]{:S(2)}) collective-permute-start(bf16[8,2880]{1,0:T(8,128)(2,1)S(1)} %get-tuple-element.65), channel_id=1, source_target_pairs={{0,3},{1,4},{2,7},{3,0},{4,1},{5,6},{6,5},{7,2},{8,13},{9,10},{10,... | collective-permute-start | bytes 138248 | tf_op jit(solution)/shard_map/ppermute | solution.py:260
  18.6 2.4 %collective-permute-start.8 = (bf16[32,2880]{1,0:T(8,128)(2,1)S(1)}, bf16[32,2880]{1,0:T(8,128)(2,1)S(1)}, u32[]{:S(2)}, u32[]{:S(2)}) collective-permute-start(bf16[32,2880]{1,0:T(8,128)(2,1)S(1)} %get-tuple-element.68), channel_id=1, source_target_pairs={{0,1},{1,0},{2,3},{3,2},{4,5},{5,4},{6,7},{7,6},{8,9},{9,8},{10,11... | collective-permute-start | bytes 552968 | tf_op jit(solution)/shard_map/ppermute | solution.py:263
  18.8 5.7 %collective-permute-start.5 = (bf16[8,2880]{1,0:T(8,128)(2,1)S(1)}, bf16[8,2880]{1,0:T(8,128)(2,1)S(1)}, u32[]{:S(2)}, u32[]{:S(2)}) collective-permute-start(bf16[8,2880]{1,0:T(8,128)(2,1)S(1)} %get-tuple-element.64), channel_id=1, source_target_pairs={{0,3},{1,4},{2,7},{3,0},{4,1},{5,6},{6,5},{7,2},{8,13},{9,10},{10,... | collective-permute-start | bytes 138248 | tf_op jit(solution)/shard_map/ppermute | solution.py:260
  20.9 3.6 %collective-permute-start.7 = (bf16[8,2880]{1,0:T(8,128)(2,1)S(1)}, bf16[8,2880]{1,0:T(8,128)(2,1)S(1)}, u32[]{:S(2)}, u32[]{:S(2)}) collective-permute-start(bf16[8,2880]{1,0:T(8,128)(2,1)S(1)} %convert_add_fusion.1), channel_id=1, source_target_pairs={{0,5},{1,2},{2,1},{3,6},{4,7},{5,0},{6,3},{7,4},{8,11},{9,12},{10,... | collective-permute-start | bytes 138248 | tf_op jit(solution)/shard_map/ppermute | solution.py:260
  24.5 4.5 %collective-permute-start.9 = (bf16[4,2880]{1,0:T(4,128)(2,1)S(1)}, bf16[4,2880]{1,0:T(4,128)(2,1)S(1)}, u32[]{:S(2)}, u32[]{:S(2)}) collective-permute-start(bf16[4,2880]{1,0:T(4,128)(2,1)S(1)} %slice.22), channel_id=1, source_target_pairs={{0,9},{1,8},{2,11},{3,10},{4,13},{5,12},{6,15},{7,14},{8,1},{9,0},... | collective-permute-start | bytes 69128 | tf_op jit(solution)/shard_map/ppermute | solution.py:260

commit v12 on v8

--- a/solution.py
+++ b/solution.py
@@ -57,10 +57,11 @@
     return out
 
 
-def moment_kernel(grad, moment, held, stored, sems):
+def moment_kernel(begin, grad, moment, *refs):
+    held, stored, sems = refs[-3:]
     copies = []
-    for i, (at, size) in enumerate(cuts(grad.shape[0], 960)):
-        part = pl.ds(at, size)
+    for i, (at, size) in enumerate(cuts(grad.shape[0] // 2, 720)):
+        part = pl.ds(begin + at, size)
         held[part] = (
             0.9 * moment[part].astype(jnp.float32) + 0.1 * grad[part].astype(jnp.float32)
         ).astype(jnp.bfloat16)
@@ -71,19 +72,25 @@
         copy.wait()
 
 
-def new_moment(grad, moment):
-    return pl.pallas_call(
-        moment_kernel,
-        in_specs=[INSIDE, INSIDE],
+def half_moment(grad, moment, *so_far):
+    more = len(so_far) > 0
+    half = grad.shape[0] // 2
+    values = [inside(grad), inside(moment)]
+    if more:
+        values += [inside(so_far[0]), so_far[1]]
+    return pl.pallas_call(
+        functools.partial(moment_kernel, half if more else 0),
+        in_specs=[INSIDE, INSIDE] + [INSIDE, ANYWHERE] * more,
         out_specs=[INSIDE, ANYWHERE],
         out_shape=[
             pltpu.VMEM(grad.shape, grad.dtype),
             jax.ShapeDtypeStruct(grad.shape, grad.dtype),
         ],
-        scratch_shapes=[pltpu.SemaphoreType.DMA((len(cuts(grad.shape[0], 960)),))],
+        input_output_aliases={2: 0, 3: 1} if more else {},
+        scratch_shapes=[pltpu.SemaphoreType.DMA((len(cuts(half, 720)),))],
         compiler_params=PARAMS,
         name="moment",
-    )(inside(grad), inside(moment))
+    )(*values)
 
 
 def transpose_kernel(*refs):
@@ -271,9 +278,10 @@
     )
     come = exchange(sent, bits - 1)
     moment, _ = tie(moment, sent)
-    moment_in, moment_next = new_moment(grad, moment)
-    held, _ = tie(held, moment_in)
+    first_half = half_moment(grad, moment)
+    held, *first_half = tie(held, *first_half)
     theirs = across(held)
+    moment_in, moment_next = half_moment(grad, moment, *first_half)
     come, moment_in, moment_next = tie(come, moment_in, moment_next)
     for step in reversed(range(bits)):
         if step == 0:

time: 28.9 us -> 29.3 us (1.014)
  Pallas kernels: 10.2 us -> 10.9 us
    pallas_call x1 -> x2, Pallas kernels: 1.7 us -> 2.46 us  [half_moment(): pl.pallas_call(functools.partial(moment_kernel, half if more else 0), in_...]
  transfers between devices with their start and end apart: 9 -> 9, of which waited for: 5 -> 4; matrix products, arithmetic and copies ran while one was open for 0% -> 0% of each run, Pallas kernels for 27% -> 29%
where the time goes in v12:
time: 29.3 us; the launch traced here: 29.2 us
  starting transfers between devices  15.3 us (52%)
  Pallas kernels  10.9 us (37%)
  waiting for transfers between devices  2.09 us (7%)
  between operations  0.74 us (3%)
    ppermute x7, starting transfers between devices, exchange(): return lax.ppermute(value, 'rows', pairs)  14.5 us
    pallas_call x2, Pallas kernels, half_moment(): pl.pallas_call(functools.partial(moment_kernel, half if more else 0), in_...  2.46 us
    ppermute x7, waiting for transfers between devices, exchange(): return lax.ppermute(value, 'rows', pairs)  2.08 us
    pallas_call x1, Pallas kernels, new_update(): pl.pallas_call(update_kernel, in_specs=[INSIDE] * 2, out_specs=ANYWHERE,...  1.72 us
    pallas_call x1, Pallas kernels, load(): pl.pallas_call(load_kernel, in_specs=[pl.BlockSpec(memory_space=pltpu.HBM...  1.64 us
    pallas_call x1, Pallas kernels, scaled_rotation(): pl.pallas_call(functools.partial(scale_kernel, orders, own), in_specs=[IN...  1.57 us
    pallas_call x1, Pallas kernels, power_products(): pl.pallas_call(power_kernel, in_specs=[INSIDE] * (len(pieces) + len(grads...  1.55 us
    pallas_call x1, Pallas kernels, transposed(): pl.pallas_call(transpose_kernel, in_specs=[INSIDE] * len(values), out_spe...  1.22 us
  transfers between devices with their start and end apart: 9, of which 4 were waited for; matrix products, arithmetic and copies ran while one was open for 0% of the time, Pallas kernels for 29%

profile of v12, /device:TPU:0, one launch (start us, length us, event | category | flops | bytes accessed | tf_op | source)
XLA Modules:
  0.0 29.2 jit_solution(4238841456370675665)
XLA Ops:
  0.6 3.5 %collective-permute-start = (bf16[4,2880]{1,0:T(4,128)(2,1)}, bf16[4,2880]{1,0:T(4,128)(2,1)S(1)}, u32[]{:S(2)}, u32[]{:S(2)}) collective-permute-start(bf16[4,2880]{1,0:T(4,128)(2,1)} %refs_1_.1), channel_id=1, source_target_pairs={{0,9},{1,8},{2,11},{3,10},{4,13},{5,12},{6,15},{7,14},{8,1},{9,0},... | collective-permute-start | bytes 69128 | tf_op jit(solution)/shard_map/ppermute | solution.py:255
  4.2 1.6 %load.1 = (bf16[2880,384]{1,0:T(8,128)(2,1)S(1)}, bf16[4,2880]{1,0:T(4,128)(2,1)S(1)}) custom-call(bf16[2880,384]{1,0:T(8,128)(2,1)} %bitcast.10, bf16[4,2880]{1,0:T(4,128)(2,1)} %refs_1_.1), custom_call_target="tpu_custom_call" | custom-call | tf_op jit(solution)/shard_map/load/pallas_call | solution.py:48
  5.8 0.1 collective-permute-done
  6.0 0.6 %collective-permute-start.3 = (bf16[2880,384]{1,0:T(8,128)(2,1)S(1)}, bf16[2880,384]{1,0:T(8,128)(2,1)S(1)}, u32[]{:S(2)}, u32[]{:S(2)}) collective-permute-start(bf16[2880,384]{1,0:T(8,128)(2,1)S(1)} %get-tuple-element.53.refs_0_.refs_4_.grad), channel_id=1, source_target_pairs={{0,1},{1,0},{2,3},{3,2},{4,5},{5,4},{6,7},{7,6},{8,9},{9,8},{10,11... | collective-permute-start | bytes 6635528 | tf_op jit(solution)/shard_map/ppermute | solution.py:258
  6.6 1.7 %collective-permute-start.1 = (bf16[8,2880]{1,0:T(8,128)(2,1)S(1)}, bf16[8,2880]{1,0:T(8,128)(2,1)S(1)}, u32[]{:S(2)}, u32[]{:S(2)}) collective-permute-start(bf16[8,2880]{1,0:T(8,128)(2,1)S(1)} %pad_maximum_fusion.refs_0_), channel_id=1, source_target_pairs={{0,5},{1,2},{2,1},{3,6},{4,7},{5,0},{6,3},{7,4},{8,11},{9,12},{10,... | collective-permute-start | bytes 138248 | tf_op jit(solution)/shard_map/ppermute | solution.py:255
  8.3 1.2 %collective-permute-start.2 = (bf16[8,2880]{1,0:T(8,128)(2,1)S(1)}, bf16[8,2880]{1,0:T(8,128)(2,1)S(1)}, u32[]{:S(2)}, u32[]{:S(2)}) collective-permute-start(bf16[8,2880]{1,0:T(8,128)(2,1)S(1)} %pad_maximum_fusion.refs_0_), channel_id=1, source_target_pairs={{0,3},{1,4},{2,7},{3,0},{4,1},{5,6},{6,5},{7,2},{8,13},{9,10},{10,... | collective-permute-start | bytes 138248 | tf_op jit(solution)/shard_map/ppermute | solution.py:255
  9.5 0.7 %collective-permute-done.1.refs_1_ = bf16[8,2880]{1,0:T(8,128)(2,1)S(1)} collective-permute-done((bf16[8,2880]{1,0:T(8,128)(2,1)S(1)}, bf16[8,2880]{1,0:T(8,128)(2,1)S(1)}, u32[]{:S(2)}, u32[]{:S(2)}) %collective-permute-start.1) | collective-permute-done | bytes 46112 | tf_op jit(solution)/shard_map/ppermute | solution.py:255
  10.2 1.6 %collective-permute-start.4 = (bf16[8,2880]{1,0:T(8,128)(2,1)S(1)}, bf16[8,2880]{1,0:T(8,128)(2,1)S(1)}, u32[]{:S(2)}, u32[]{:S(2)}) collective-permute-start(bf16[8,2880]{1,0:T(8,128)(2,1)S(1)} %collective-permute-done.1.refs_1_), channel_id=1, source_target_pairs={{0,3},{1,4},{2,7},{3,0},{4,1},{5,6},{6,5},{7,2},{8,13},{9,10},{10,... | collective-permute-start | bytes 138248 | tf_op jit(solution)/shard_map/ppermute | solution.py:255
  11.7 0.0 collective-permute-done.2.refs_2_
  11.8 0.0 collective-permute-done.3.refs_1_.refs_5_
  11.8 1.2 %transpose.25 = (bf16[384,2880]{1,0:T(8,128)(2,1)S(1)}, bf16[384,2880]{1,0:T(8,128)(2,1)S(1)}) custom-call(bf16[2880,384]{1,0:T(8,128)(2,1)S(1)} %get-tuple-element.53.refs_0_.refs_4_.grad, bf16[2880,384]{1,0:T(8,128)(2,1)S(1)} %collective-permute-done.3.refs_1_.refs_5_), custom_call_target="tpu_custom_call" | custom-call | tf_op jit(solution)/shard_map/transpose/pallas_call | solution.py:103
  13.0 0.6 %collective-permute-done.4.refs_3_ = bf16[8,2880]{1,0:T(8,128)(2,1)S(1)} collective-permute-done((bf16[8,2880]{1,0:T(8,128)(2,1)S(1)}, bf16[8,2880]{1,0:T(8,128)(2,1)S(1)}, u32[]{:S(2)}, u32[]{:S(2)}) %collective-permute-start.4) | collective-permute-done | bytes 46112 | tf_op jit(solution)/shard_map/ppermute | solution.py:255
  13.7 0.0 copy-start
  13.7 1.6 %power.1 = (bf16[32,2880]{1,0:T(8,128)(2,1)S(1)}, f32[32,384]{1,0:T(8,128)S(1)}, f32[16,2880]{1,0:T(8,128)S(1)}, bf16[16,2880]{1,0:T(8,128)(2,1)S(1)}) custom-call(bf16[8,2880]{1,0:T(8,128)(2,1)S(1)} %pad_maximum_fusion.refs_0_, bf16[8,2880]{1,0:T(8,128)(2,1)S(1)} %collective-permute-done.1.refs_1_, bf16[8,2880]{1,0:T(8,128)(2,1)S(1)} %collective-permute-done.2.refs_2_, ...), custom_call_target="tpu_custom_call" | custom-call | tf_op jit(solution)/shard_map/power/pallas_call | solution.py:132
  15.2 1.7 %collective-permute-start.6 = (bf16[16,2880]{1,0:T(8,128)(2,1)S(1)}, bf16[16,2880]{1,0:T(8,128)(2,1)S(1)}, u32[]{:S(2)}, u32[]{:S(2)}) collective-permute-start(bf16[16,2880]{1,0:T(8,128)(2,1)S(1)} %get-tuple-element.61), channel_id=1, source_target_pairs={{0,3},{1,4},{2,7},{3,0},{4,1},{5,6},{6,5},{7,2},{8,13},{9,10},{10,... | collective-permute-start | bytes 276488 | tf_op jit(solution)/shard_map/ppermute | solution.py:255
  16.9 0.0 copy-done
  16.9 1.2 %moment.2 = (bf16[2880,384]{1,0:T(8,128)(2,1)S(1)}, bf16[2880,384]{1,0:T(8,128)(2,1)}) custom-call(bf16[2880,384]{1,0:T(8,128)(2,1)S(1)} %get-tuple-element.53.refs_0_.refs_4_.grad, bf16[2880,384]{1,0:T(8,128)(2,1)S(1)} %bitcast.6), custom_call_target="tpu_custom_call" | custom-call | tf_op jit(solution)/shard_map/moment/pallas_call | solution.py:81
  18.1 0.2 collective-permute-start.5
  18.3 0.0 copy-start.1
  18.3 1.2 %moment.3 = (bf16[2880,384]{1,0:T(8,128)(2,1)S(1)}, bf16[2880,384]{1,0:T(8,128)(2,1)}) custom-call(bf16[2880,384]{1,0:T(8,128)(2,1)S(1)} %get-tuple-element.53.refs_0_.refs_4_.grad, bf16[2880,384]{1,0:T(8,128)(2,1)S(1)} %bitcast.7, bf16[2880,384]{1,0:T(8,128)(2,1)S(1)} %get-tuple-element.67.refs_0_, ...), custom_call_target="tpu_custom_call", output_to_operand_aliasing={{0}: (2, {}), {1}: (3, {})} | custom-call | tf_op jit(solution)/shard_map/moment/pallas_call | solution.py:81
  19.6 0.0 collective-permute-done.6
  19.6 1.4 %collective-permute-start.7 = (bf16[8,2880]{1,0:T(8,128)(2,1)S(1)}, bf16[8,2880]{1,0:T(8,128)(2,1)S(1)}, u32[]{:S(2)}, u32[]{:S(2)}) collective-permute-start(bf16[8,2880]{1,0:T(8,128)(2,1)S(1)} %slice.24), channel_id=1, source_target_pairs={{0,5},{1,2},{2,1},{3,6},{4,7},{5,0},{6,3},{7,4},{8,11},{9,12},{10,... | collective-permute-start | bytes 138248 | tf_op jit(solution)/shard_map/ppermute | solution.py:255
  21.0 0.0 collective-permute-done.5
  21.0 0.0 copy-done.1
  21.0 1.6 %scale.1 = (bf16[64,384]{1,0:T(8,128)(2,1)S(1)}, f32[64,384]{1,0:T(8,128)}) custom-call(bf16[64,2880]{1,0:T(8,128)(2,1)S(1)} %constant_dynamic-update-slice_fusion.basis, bf16[2880,384]{1,0:T(8,128)(2,1)S(1)} %get-tuple-element.53.refs_0_.refs_4_.grad, bf16[2880,384]{1,0:T(8,128)(2,1)S(1)} %get-tuple-element.74.moment, ...), custom_call_target="tpu_custom_call" | custom-call | tf_op jit(solution)/shard_map/scale/pallas_call | solution.py:205
  22.6 0.6 %collective-permute-done.7 = bf16[8,2880]{1,0:T(8,128)(2,1)S(1)} collective-permute-done((bf16[8,2880]{1,0:T(8,128)(2,1)S(1)}, bf16[8,2880]{1,0:T(8,128)(2,1)S(1)}, u32[]{:S(2)}, u32[]{:S(2)}) %collective-permute-start.7) | collective-permute-done | bytes 46112 | tf_op jit(solution)/shard_map/ppermute | solution.py:255
  23.2 3.5 %collective-permute-start.8 = (bf16[4,2880]{1,0:T(4,128)(2,1)S(1)}, bf16[4,2880]{1,0:T(4,128)(2,1)S(1)}, u32[]{:S(2)}, u32[]{:S(2)}) collective-permute-start(bf16[4,2880]{1,0:T(4,128)(2,1)S(1)} %slice.25), channel_id=1, source_target_pairs={{0,9},{1,8},{2,11},{3,10},{4,13},{5,12},{6,15},{7,14},{8,1},{9,0},... | collective-permute-start | bytes 69128 | tf_op jit(solution)/shard_map/ppermute | solution.py:255
  26.7 1.7 %update.1 = bf16[2880,384]{1,0:T(8,128)(2,1)} custom-call(bf16[64,2880]{1,0:T(8,128)(2,1)S(1)} %constant_dynamic-update-slice_fusion.basis, bf16[64,384]{1,0:T(8,128)(2,1)S(1)} %get-tuple-element.80.scaled), custom_call_target="tpu_custom_call" | custom-call | tf_op jit(solution)/shard_map/update/pallas_call | solution.py:233
  28.4 0.0 collective-permute-done.8.come
  28.4 0.7 %normalise.1 = f32[4,2880]{1,0:T(4,128)} custom-call(f32[4,2880]{1,0:T(4,128)S(1)} %slice.21.kept, bf16[4,2880]{1,0:T(4,128)(2,1)S(1)} %collective-permute-done.8.come), custom_call_target="tpu_custom_call" | custom-call | tf_op jit(solution)/shard_map/normalise/pallas_call | solution.py:154
  (9 shorter events, 0.1 us)
Async XLA Ops:
  0.6 5.3 %collective-permute-start = (bf16[4,2880]{1,0:T(4,128)(2,1)}, bf16[4,2880]{1,0:T(4,128)(2,1)S(1)}, u32[]{:S(2)}, u32[]{:S(2)}) collective-permute-start(bf16[4,2880]{1,0:T(4,128)(2,1)} %refs_1_.1), channel_id=1, source_target_pairs={{0,9},{1,8},{2,11},{3,10},{4,13},{5,12},{6,15},{7,14},{8,1},{9,0},... | collective-permute-start | bytes 69128 | tf_op jit(solution)/shard_map/ppermute | solution.py:255
  6.0 5.8 %collective-permute-start.3 = (bf16[2880,384]{1,0:T(8,128)(2,1)S(1)}, bf16[2880,384]{1,0:T(8,128)(2,1)S(1)}, u32[]{:S(2)}, u32[]{:S(2)}) collective-permute-start(bf16[2880,384]{1,0:T(8,128)(2,1)S(1)} %get-tuple-element.53.refs_0_.refs_4_.grad), channel_id=1, source_target_pairs={{0,1},{1,0},{2,3},{3,2},{4,5},{5,4},{6,7},{7,6},{8,9},{9,8},{10,11... | collective-permute-start | bytes 6635528 | tf_op jit(solution)/shard_map/ppermute | solution.py:258
  6.6 3.6 %collective-permute-start.1 = (bf16[8,2880]{1,0:T(8,128)(2,1)S(1)}, bf16[8,2880]{1,0:T(8,128)(2,1)S(1)}, u32[]{:S(2)}, u32[]{:S(2)}) collective-permute-start(bf16[8,2880]{1,0:T(8,128)(2,1)S(1)} %pad_maximum_fusion.refs_0_), channel_id=1, source_target_pairs={{0,5},{1,2},{2,1},{3,6},{4,7},{5,0},{6,3},{7,4},{8,11},{9,12},{10,... | collective-permute-start | bytes 138248 | tf_op jit(solution)/shard_map/ppermute | solution.py:255
  8.3 3.5 %collective-permute-start.2 = (bf16[8,2880]{1,0:T(8,128)(2,1)S(1)}, bf16[8,2880]{1,0:T(8,128)(2,1)S(1)}, u32[]{:S(2)}, u32[]{:S(2)}) collective-permute-start(bf16[8,2880]{1,0:T(8,128)(2,1)S(1)} %pad_maximum_fusion.refs_0_), channel_id=1, source_target_pairs={{0,3},{1,4},{2,7},{3,0},{4,1},{5,6},{6,5},{7,2},{8,13},{9,10},{10,... | collective-permute-start | bytes 138248 | tf_op jit(solution)/shard_map/ppermute | solution.py:255
  10.2 3.5 %collective-permute-start.4 = (bf16[8,2880]{1,0:T(8,128)(2,1)S(1)}, bf16[8,2880]{1,0:T(8,128)(2,1)S(1)}, u32[]{:S(2)}, u32[]{:S(2)}) collective-permute-start(bf16[8,2880]{1,0:T(8,128)(2,1)S(1)} %collective-permute-done.1.refs_1_), channel_id=1, source_target_pairs={{0,3},{1,4},{2,7},{3,0},{4,1},{5,6},{6,5},{7,2},{8,13},{9,10},{10,... | collective-permute-start | bytes 138248 | tf_op jit(solution)/shard_map/ppermute | solution.py:255
  13.7 3.2 %copy-start = (bf16[384,2880]{0,1:T(8,128)(2,1)S(1)}, bf16[384,2880]{0,1:T(8,128)(2,1)}, u32[]{:S(2)}) copy-start(bf16[384,2880]{0,1:T(8,128)(2,1)} %param.5) | copy-start | bytes 6635524
  15.2 4.3 %collective-permute-start.6 = (bf16[16,2880]{1,0:T(8,128)(2,1)S(1)}, bf16[16,2880]{1,0:T(8,128)(2,1)S(1)}, u32[]{:S(2)}, u32[]{:S(2)}) collective-permute-start(bf16[16,2880]{1,0:T(8,128)(2,1)S(1)} %get-tuple-element.61), channel_id=1, source_target_pairs={{0,3},{1,4},{2,7},{3,0},{4,1},{5,6},{6,5},{7,2},{8,13},{9,10},{10,... | collective-permute-start | bytes 276488 | tf_op jit(solution)/shard_map/ppermute | solution.py:255
  18.1 2.9 %collective-permute-start.5 = (bf16[32,2880]{1,0:T(8,128)(2,1)S(1)}, bf16[32,2880]{1,0:T(8,128)(2,1)S(1)}, u32[]{:S(2)}, u32[]{:S(2)}) collective-permute-start(bf16[32,2880]{1,0:T(8,128)(2,1)S(1)} %get-tuple-element.65), channel_id=1, source_target_pairs={{0,1},{1,0},{2,3},{3,2},{4,5},{5,4},{6,7},{7,6},{8,9},{9,8},{10,11... | collective-permute-start | bytes 552968 | tf_op jit(solution)/shard_map/ppermute | solution.py:258
  18.3 2.7 %copy-start.1 = (f32[384,64]{0,1:T(8,128)S(1)}, f32[384,64]{0,1:T(8,128)}, u32[]{:S(2)}) copy-start(f32[384,64]{0,1:T(8,128)} %param.6) | copy-start | bytes 294916
  19.6 3.6 %collective-permute-start.7 = (bf16[8,2880]{1,0:T(8,128)(2,1)S(1)}, bf16[8,2880]{1,0:T(8,128)(2,1)S(1)}, u32[]{:S(2)}, u32[]{:S(2)}) collective-permute-start(bf16[8,2880]{1,0:T(8,128)(2,1)S(1)} %slice.24), channel_id=1, source_target_pairs={{0,5},{1,2},{2,1},{3,6},{4,7},{5,0},{6,3},{7,4},{8,11},{9,12},{10,... | collective-permute-start | bytes 138248 | tf_op jit(solution)/shard_map/ppermute | solution.py:255
  23.2 5.2 %collective-permute-start.8 = (bf16[4,2880]{1,0:T(4,128)(2,1)S(1)}, bf16[4,2880]{1,0:T(4,128)(2,1)S(1)}, u32[]{:S(2)}, u32[]{:S(2)}) collective-permute-start(bf16[4,2880]{1,0:T(4,128)(2,1)S(1)} %slice.25), channel_id=1, source_target_pairs={{0,9},{1,8},{2,11},{3,10},{4,13},{5,12},{6,15},{7,14},{8,1},{9,0},... | collective-permute-start | bytes 69128 | tf_op jit(solution)/shard_map/ppermute | solution.py:255

commit v13 on v8

--- a/solution.py
+++ b/solution.py
@@ -154,7 +154,14 @@
     )(inside(kept), inside(come))
 
 
-def scale_kernel(orders, own, basis, grad, moment, rot_half, second, scaled, second_next, rot, mom):
+def early(depth):
+    return depth // 3 // 128 * 128
+
+
+def scale_kernel(
+    orders, own, basis, grad, moment, rot_half, second, scaled, second_next, update, *scratch
+):
+    rot, mom, value_in, held, sems = scratch
     me = lax.axis_index("rows")
     core, chip = me & 1, me >> 1
     bits = len(orders[0])
@@ -185,56 +192,76 @@
 
                 turned = joined(rot)
                 value = 0.95 * second[tile] + 0.05 * turned * turned
-                second_next[tile] = value
+                value_in[tile] = value
                 ratio = joined(mom) / (jnp.sqrt(value) + 1e-08)
                 rot[mine] = jnp.where(first, ratio[:own], ratio[own:])
                 rot[theirs] = jnp.where(first, ratio[own:], ratio[:own])
 
+    copies = [pltpu.make_async_copy(value_in, second_next, sems.at[0])]
+    copies[0].start()
     scaled[...] = rot[...].astype(jnp.bfloat16)
+    part = pl.ds(0, held.shape[0])
+    held[...] = dot(basis[:, part], scaled[...], ((0,), (0,))).astype(jnp.bfloat16)
+    copies.append(pltpu.make_async_copy(held, update.at[part], sems.at[1]))
+    copies[1].start()
+    for copy in copies:
+        copy.wait()
 
 
 def scaled_rotation(orders, own, basis, grad, moment, rot_half, second):
-    count, rows = basis.shape[0], grad.shape[1]
+    count, depth = basis.shape
+    rows = grad.shape[1]
     return pl.pallas_call(
         functools.partial(scale_kernel, orders, own),
         in_specs=[INSIDE] * 5,
-        out_specs=[INSIDE] * 2,
+        out_specs=[INSIDE, ANYWHERE, ANYWHERE],
         out_shape=[
             pltpu.VMEM((count, rows), jnp.bfloat16),
             jax.ShapeDtypeStruct((count, rows), jnp.float32),
-        ],
-        scratch_shapes=[pltpu.VMEM((count, rows), jnp.float32)] * 2,
+            jax.ShapeDtypeStruct((depth, rows), jnp.bfloat16),
+        ],
+        scratch_shapes=[
+            pltpu.VMEM((count, rows), jnp.float32),
+            pltpu.VMEM((count, rows), jnp.float32),
+            pltpu.VMEM((count, rows), jnp.float32),
+            pltpu.VMEM((early(depth), rows), jnp.bfloat16),
+            pltpu.SemaphoreType.DMA((2,)),
+        ],
         compiler_params=PARAMS,
         name="scale",
     )(*map(inside, (basis, grad, moment, rot_half, second)))
 
 
-def update_kernel(basis, scaled, out, held, sems):
+def update_kernel(basis, scaled, so_far, out, held, sems):
+    first = early(out.shape[0])
     copies = []
-    for i, (at, size) in enumerate(cuts(out.shape[0], 640)):
-        part = pl.ds(at, size)
-        held[part] = dot(basis[:, part], scaled[...], ((0,), (0,))).astype(jnp.bfloat16)
-        copy = pltpu.make_async_copy(held.at[part], out.at[part], sems.at[i])
+    for i, (at, size) in enumerate(cuts(out.shape[0] - first, 768)):
+        part = pl.ds(first + at, size)
+        here = pl.ds(at, size)
+        held[here] = dot(basis[:, part], scaled[...], ((0,), (0,))).astype(jnp.bfloat16)
+        copy = pltpu.make_async_copy(held.at[here], out.at[part], sems.at[i])
         copy.start()
         copies.append(copy)
     for copy in copies:
         copy.wait()
 
 
-def new_update(basis, scaled):
-    depth, rows = basis.shape[1], scaled.shape[1]
+def rest_of_update(basis, scaled, so_far):
+    depth, rows = so_far.shape
+    later = depth - early(depth)
     return pl.pallas_call(
         update_kernel,
-        in_specs=[INSIDE] * 2,
+        in_specs=[INSIDE, INSIDE, ANYWHERE],
         out_specs=ANYWHERE,
         out_shape=jax.ShapeDtypeStruct((depth, rows), jnp.bfloat16),
+        input_output_aliases={2: 0},
         scratch_shapes=[
-            pltpu.VMEM((depth, rows), jnp.bfloat16),
-            pltpu.SemaphoreType.DMA((len(cuts(depth, 640)),)),
+            pltpu.VMEM((later, rows), jnp.bfloat16),
+            pltpu.SemaphoreType.DMA((len(cuts(later, 768)),)),
         ],
         compiler_params=PARAMS,
         name="update",
-    )(inside(basis), inside(scaled))
+    )(inside(basis), inside(scaled), so_far)
 
 
 def shards(n, grad, moment, second, basis):
@@ -285,13 +312,13 @@
         if step == bits - 1:
             theirs, kept = tie(theirs, kept)
             whole = jnp.concatenate([held, theirs], 0)
-            scaled, second_next = scaled_rotation(
+            scaled, second_next, update = scaled_rotation(
                 orders, own, whole, grad, moment_in, rot_half, second
             )
-            come, scaled, second_next = tie(come, scaled, second_next)
+            come, scaled, second_next, update = tie(come, scaled, second_next, update)
         if step == bits - 2:
             scaled, kept = tie(scaled, kept)
-            update = new_update(whole, scaled)
+            update = rest_of_update(whole, scaled, update)
             come, update = tie(come, update)
     basis_next = normalised(kept, come)
     return update.T, moment_next.T, second_next.T, basis_next

time: 28.9 us -> 29.3 us (1.014)
  Pallas kernels: 10.2 us -> 10.5 us
    pallas_call x1, Pallas kernels: 1.57 us -> 2.17 us  [scaled_rotation(): pl.pallas_call(functools.partial(scale_kernel, orders, own), in_specs=[IN...]
  transfers between devices with their start and end apart: 9 -> 9, of which waited for: 5 -> 5; matrix products, arithmetic and copies ran while one was open for 0% -> 0% of each run, Pallas kernels for 27% -> 28%
where the time goes in v13:
time: 29.3 us; the launch traced here: 29.1 us
  starting transfers between devices  15.6 us (53%)
  Pallas kernels  10.5 us (36%)
  waiting for transfers between devices  2.1 us (7%)
  between operations  0.73 us (2%)
    ppermute x7, starting transfers between devices, exchange(): return lax.ppermute(value, 'rows', pairs)  14.8 us
    pallas_call x1, Pallas kernels, scaled_rotation(): pl.pallas_call(functools.partial(scale_kernel, orders, own), in_specs=[IN...  2.17 us
    ppermute x7, waiting for transfers between devices, exchange(): return lax.ppermute(value, 'rows', pairs)  2.1 us
    pallas_call x1, Pallas kernels, new_moment(): pl.pallas_call(moment_kernel, in_specs=[INSIDE, INSIDE], out_specs=[INSID...  1.7 us
    pallas_call x1, Pallas kernels, load(): pl.pallas_call(load_kernel, in_specs=[pl.BlockSpec(memory_space=pltpu.HBM...  1.64 us
    pallas_call x1, Pallas kernels, power_products(): pl.pallas_call(power_kernel, in_specs=[INSIDE] * (len(pieces) + len(grads...  1.55 us
    pallas_call x1, Pallas kernels, rest_of_update(): pl.pallas_call(update_kernel, in_specs=[INSIDE, INSIDE, ANYWHERE], out_sp...  1.52 us
    pallas_call x1, Pallas kernels, transposed(): pl.pallas_call(transpose_kernel, in_specs=[INSIDE] * len(values), out_spe...  1.22 us
  transfers between devices with their start and end apart: 9, of which 5 were waited for; matrix products, arithmetic and copies ran while one was open for 0% of the time, Pallas kernels for 28%

profile of v13, /device:TPU:0, one launch (start us, length us, event | category | flops | bytes accessed | tf_op | source)
XLA Modules:
  0.0 29.1 jit_solution(13986659559108324214)
XLA Ops:
  0.6 3.5 %collective-permute-start = (bf16[4,2880]{1,0:T(4,128)(2,1)}, bf16[4,2880]{1,0:T(4,128)(2,1)S(1)}, u32[]{:S(2)}, u32[]{:S(2)}) collective-permute-start(bf16[4,2880]{1,0:T(4,128)(2,1)} %refs_1_.1), channel_id=1, source_target_pairs={{0,9},{1,8},{2,11},{3,10},{4,13},{5,12},{6,15},{7,14},{8,1},{9,0},... | collective-permute-start | bytes 69128 | tf_op jit(solution)/shard_map/ppermute | solution.py:275
  4.2 1.6 %load.1 = (bf16[2880,384]{1,0:T(8,128)(2,1)S(1)}, bf16[4,2880]{1,0:T(4,128)(2,1)S(1)}) custom-call(bf16[2880,384]{1,0:T(8,128)(2,1)} %bitcast.8, bf16[4,2880]{1,0:T(4,128)(2,1)} %refs_1_.1), custom_call_target="tpu_custom_call" | custom-call | tf_op jit(solution)/shard_map/load/pallas_call | solution.py:48
  5.8 0.1 collective-permute-done
  6.0 0.6 %collective-permute-start.3 = (bf16[2880,384]{1,0:T(8,128)(2,1)S(1)}, bf16[2880,384]{1,0:T(8,128)(2,1)S(1)}, u32[]{:S(2)}, u32[]{:S(2)}) collective-permute-start(bf16[2880,384]{1,0:T(8,128)(2,1)S(1)} %get-tuple-element.51.refs_0_.refs_4_.grad), channel_id=1, source_target_pairs={{0,1},{1,0},{2,3},{3,2},{4,5},{5,4},{6,7},{7,6},{8,9},{9,8},{10,11... | collective-permute-start | bytes 6635528 | tf_op jit(solution)/shard_map/ppermute | solution.py:278
  6.6 1.7 %collective-permute-start.1 = (bf16[8,2880]{1,0:T(8,128)(2,1)S(1)}, bf16[8,2880]{1,0:T(8,128)(2,1)S(1)}, u32[]{:S(2)}, u32[]{:S(2)}) collective-permute-start(bf16[8,2880]{1,0:T(8,128)(2,1)S(1)} %pad_maximum_fusion.refs_0_), channel_id=1, source_target_pairs={{0,5},{1,2},{2,1},{3,6},{4,7},{5,0},{6,3},{7,4},{8,11},{9,12},{10,... | collective-permute-start | bytes 138248 | tf_op jit(solution)/shard_map/ppermute | solution.py:275
  8.3 1.2 %collective-permute-start.2 = (bf16[8,2880]{1,0:T(8,128)(2,1)S(1)}, bf16[8,2880]{1,0:T(8,128)(2,1)S(1)}, u32[]{:S(2)}, u32[]{:S(2)}) collective-permute-start(bf16[8,2880]{1,0:T(8,128)(2,1)S(1)} %pad_maximum_fusion.refs_0_), channel_id=1, source_target_pairs={{0,3},{1,4},{2,7},{3,0},{4,1},{5,6},{6,5},{7,2},{8,13},{9,10},{10,... | collective-permute-start | bytes 138248 | tf_op jit(solution)/shard_map/ppermute | solution.py:275
  9.5 0.7 %collective-permute-done.1.refs_1_ = bf16[8,2880]{1,0:T(8,128)(2,1)S(1)} collective-permute-done((bf16[8,2880]{1,0:T(8,128)(2,1)S(1)}, bf16[8,2880]{1,0:T(8,128)(2,1)S(1)}, u32[]{:S(2)}, u32[]{:S(2)}) %collective-permute-start.1) | collective-permute-done | bytes 46112 | tf_op jit(solution)/shard_map/ppermute | solution.py:275
  10.2 1.6 %collective-permute-start.4 = (bf16[8,2880]{1,0:T(8,128)(2,1)S(1)}, bf16[8,2880]{1,0:T(8,128)(2,1)S(1)}, u32[]{:S(2)}, u32[]{:S(2)}) collective-permute-start(bf16[8,2880]{1,0:T(8,128)(2,1)S(1)} %collective-permute-done.1.refs_1_), channel_id=1, source_target_pairs={{0,3},{1,4},{2,7},{3,0},{4,1},{5,6},{6,5},{7,2},{8,13},{9,10},{10,... | collective-permute-start | bytes 138248 | tf_op jit(solution)/shard_map/ppermute | solution.py:275
  11.7 0.0 collective-permute-done.2.refs_2_
  11.8 0.0 collective-permute-done.3.refs_1_.refs_5_
  11.8 1.2 %transpose.25 = (bf16[384,2880]{1,0:T(8,128)(2,1)S(1)}, bf16[384,2880]{1,0:T(8,128)(2,1)S(1)}) custom-call(bf16[2880,384]{1,0:T(8,128)(2,1)S(1)} %get-tuple-element.51.refs_0_.refs_4_.grad, bf16[2880,384]{1,0:T(8,128)(2,1)S(1)} %collective-permute-done.3.refs_1_.refs_5_), custom_call_target="tpu_custom_call" | custom-call | tf_op jit(solution)/shard_map/transpose/pallas_call | solution.py:96
  13.0 0.6 %collective-permute-done.4.refs_3_ = bf16[8,2880]{1,0:T(8,128)(2,1)S(1)} collective-permute-done((bf16[8,2880]{1,0:T(8,128)(2,1)S(1)}, bf16[8,2880]{1,0:T(8,128)(2,1)S(1)}, u32[]{:S(2)}, u32[]{:S(2)}) %collective-permute-start.4) | collective-permute-done | bytes 46112 | tf_op jit(solution)/shard_map/ppermute | solution.py:275
  13.7 0.0 copy-start
  13.7 1.6 %power.1 = (bf16[32,2880]{1,0:T(8,128)(2,1)S(1)}, f32[32,384]{1,0:T(8,128)S(1)}, f32[16,2880]{1,0:T(8,128)S(1)}, bf16[16,2880]{1,0:T(8,128)(2,1)S(1)}) custom-call(bf16[8,2880]{1,0:T(8,128)(2,1)S(1)} %pad_maximum_fusion.refs_0_, bf16[8,2880]{1,0:T(8,128)(2,1)S(1)} %collective-permute-done.1.refs_1_, bf16[8,2880]{1,0:T(8,128)(2,1)S(1)} %collective-permute-done.2.refs_2_, ...), custom_call_target="tpu_custom_call" | custom-call | tf_op jit(solution)/shard_map/power/pallas_call | solution.py:125
  15.2 1.7 %collective-permute-start.6 = (bf16[16,2880]{1,0:T(8,128)(2,1)S(1)}, bf16[16,2880]{1,0:T(8,128)(2,1)S(1)}, u32[]{:S(2)}, u32[]{:S(2)}) collective-permute-start(bf16[16,2880]{1,0:T(8,128)(2,1)S(1)} %get-tuple-element.59), channel_id=1, source_target_pairs={{0,3},{1,4},{2,7},{3,0},{4,1},{5,6},{6,5},{7,2},{8,13},{9,10},{10,... | collective-permute-start | bytes 276488 | tf_op jit(solution)/shard_map/ppermute | solution.py:275
  16.9 0.0 copy-done
  16.9 0.0 copy-start.1
  16.9 1.7 %moment.1 = (bf16[2880,384]{1,0:T(8,128)(2,1)S(1)}, bf16[2880,384]{1,0:T(8,128)(2,1)}) custom-call(bf16[2880,384]{1,0:T(8,128)(2,1)S(1)} %get-tuple-element.51.refs_0_.refs_4_.grad, bf16[2880,384]{1,0:T(8,128)(2,1)S(1)} %bitcast.6), custom_call_target="tpu_custom_call" | custom-call | tf_op jit(solution)/shard_map/moment/pallas_call | solution.py:75
  18.6 0.2 collective-permute-start.5
  18.8 0.5 %collective-permute-done.6 = bf16[16,2880]{1,0:T(8,128)(2,1)S(1)} collective-permute-done((bf16[16,2880]{1,0:T(8,128)(2,1)S(1)}, bf16[16,2880]{1,0:T(8,128)(2,1)S(1)}, u32[]{:S(2)}, u32[]{:S(2)}) %collective-permute-start.6) | collective-permute-done | bytes 92192 | tf_op jit(solution)/shard_map/ppermute | solution.py:275
  19.3 1.7 %collective-permute-start.7 = (bf16[8,2880]{1,0:T(8,128)(2,1)S(1)}, bf16[8,2880]{1,0:T(8,128)(2,1)S(1)}, u32[]{:S(2)}, u32[]{:S(2)}) collective-permute-start(bf16[8,2880]{1,0:T(8,128)(2,1)S(1)} %slice.24), channel_id=1, source_target_pairs={{0,5},{1,2},{2,1},{3,6},{4,7},{5,0},{6,3},{7,4},{8,11},{9,12},{10,... | collective-permute-start | bytes 138248 | tf_op jit(solution)/shard_map/ppermute | solution.py:275
  21.0 0.0 collective-permute-done.5
  21.0 0.0 copy-done.1
  21.0 2.2 %scale.1 = (bf16[64,384]{1,0:T(8,128)(2,1)S(1)}, f32[64,384]{1,0:T(8,128)}, bf16[2880,384]{1,0:T(8,128)(2,1)}) custom-call(bf16[64,2880]{1,0:T(8,128)(2,1)S(1)} %constant_dynamic-update-slice_fusion.basis, bf16[2880,384]{1,0:T(8,128)(2,1)S(1)} %get-tuple-element.51.refs_0_.refs_4_.grad, bf16[2880,384]{1,0:T(8,128)(2,1)S(1)} %get-tuple-element.68.moment, ...), custom_call_target="tpu_custom_call" | custom-call | tf_op jit(solution)/shard_map/scale/pallas_call | solution.py:214
  23.2 0.0 collective-permute-done.7
  23.3 3.5 %collective-permute-start.8 = (bf16[4,2880]{1,0:T(4,128)(2,1)S(1)}, bf16[4,2880]{1,0:T(4,128)(2,1)S(1)}, u32[]{:S(2)}, u32[]{:S(2)}) collective-permute-start(bf16[4,2880]{1,0:T(4,128)(2,1)S(1)} %slice.25), channel_id=1, source_target_pairs={{0,9},{1,8},{2,11},{3,10},{4,13},{5,12},{6,15},{7,14},{8,1},{9,0},... | collective-permute-start | bytes 69128 | tf_op jit(solution)/shard_map/ppermute | solution.py:275
  26.7 1.5 %update.1 = bf16[2880,384]{1,0:T(8,128)(2,1)} custom-call(bf16[64,2880]{1,0:T(8,128)(2,1)S(1)} %constant_dynamic-update-slice_fusion.basis, bf16[64,384]{1,0:T(8,128)(2,1)S(1)} %get-tuple-element.75.scaled, bf16[2880,384]{1,0:T(8,128)(2,1)} %get-tuple-element.76.so_far), custom_call_target="tpu_custom_call", output_to_operand_aliasing={{}: (2, {})} | custom-call | tf_op jit(solution)/shard_map/update/pallas_call | solution.py:252
  28.3 0.1 collective-permute-done.8.come
  28.4 0.7 %normalise.1 = f32[4,2880]{1,0:T(4,128)} custom-call(f32[4,2880]{1,0:T(4,128)S(1)} %slice.21.kept, bf16[4,2880]{1,0:T(4,128)(2,1)S(1)} %collective-permute-done.8.come), custom_call_target="tpu_custom_call" | custom-call | tf_op jit(solution)/shard_map/normalise/pallas_call | solution.py:147
  (9 shorter events, 0.1 us)
Async XLA Ops:
  0.6 5.3 %collective-permute-start = (bf16[4,2880]{1,0:T(4,128)(2,1)}, bf16[4,2880]{1,0:T(4,128)(2,1)S(1)}, u32[]{:S(2)}, u32[]{:S(2)}) collective-permute-start(bf16[4,2880]{1,0:T(4,128)(2,1)} %refs_1_.1), channel_id=1, source_target_pairs={{0,9},{1,8},{2,11},{3,10},{4,13},{5,12},{6,15},{7,14},{8,1},{9,0},... | collective-permute-start | bytes 69128 | tf_op jit(solution)/shard_map/ppermute | solution.py:275
  6.0 5.8 %collective-permute-start.3 = (bf16[2880,384]{1,0:T(8,128)(2,1)S(1)}, bf16[2880,384]{1,0:T(8,128)(2,1)S(1)}, u32[]{:S(2)}, u32[]{:S(2)}) collective-permute-start(bf16[2880,384]{1,0:T(8,128)(2,1)S(1)} %get-tuple-element.51.refs_0_.refs_4_.grad), channel_id=1, source_target_pairs={{0,1},{1,0},{2,3},{3,2},{4,5},{5,4},{6,7},{7,6},{8,9},{9,8},{10,11... | collective-permute-start | bytes 6635528 | tf_op jit(solution)/shard_map/ppermute | solution.py:278
  6.6 3.6 %collective-permute-start.1 = (bf16[8,2880]{1,0:T(8,128)(2,1)S(1)}, bf16[8,2880]{1,0:T(8,128)(2,1)S(1)}, u32[]{:S(2)}, u32[]{:S(2)}) collective-permute-start(bf16[8,2880]{1,0:T(8,128)(2,1)S(1)} %pad_maximum_fusion.refs_0_), channel_id=1, source_target_pairs={{0,5},{1,2},{2,1},{3,6},{4,7},{5,0},{6,3},{7,4},{8,11},{9,12},{10,... | collective-permute-start | bytes 138248 | tf_op jit(solution)/shard_map/ppermute | solution.py:275
  8.3 3.5 %collective-permute-start.2 = (bf16[8,2880]{1,0:T(8,128)(2,1)S(1)}, bf16[8,2880]{1,0:T(8,128)(2,1)S(1)}, u32[]{:S(2)}, u32[]{:S(2)}) collective-permute-start(bf16[8,2880]{1,0:T(8,128)(2,1)S(1)} %pad_maximum_fusion.refs_0_), channel_id=1, source_target_pairs={{0,3},{1,4},{2,7},{3,0},{4,1},{5,6},{6,5},{7,2},{8,13},{9,10},{10,... | collective-permute-start | bytes 138248 | tf_op jit(solution)/shard_map/ppermute | solution.py:275
  10.2 3.5 %collective-permute-start.4 = (bf16[8,2880]{1,0:T(8,128)(2,1)S(1)}, bf16[8,2880]{1,0:T(8,128)(2,1)S(1)}, u32[]{:S(2)}, u32[]{:S(2)}) collective-permute-start(bf16[8,2880]{1,0:T(8,128)(2,1)S(1)} %collective-permute-done.1.refs_1_), channel_id=1, source_target_pairs={{0,3},{1,4},{2,7},{3,0},{4,1},{5,6},{6,5},{7,2},{8,13},{9,10},{10,... | collective-permute-start | bytes 138248 | tf_op jit(solution)/shard_map/ppermute | solution.py:275
  13.7 3.2 %copy-start = (bf16[384,2880]{0,1:T(8,128)(2,1)S(1)}, bf16[384,2880]{0,1:T(8,128)(2,1)}, u32[]{:S(2)}) copy-start(bf16[384,2880]{0,1:T(8,128)(2,1)} %param.5) | copy-start | bytes 6635524
  15.2 4.0 %collective-permute-start.6 = (bf16[16,2880]{1,0:T(8,128)(2,1)S(1)}, bf16[16,2880]{1,0:T(8,128)(2,1)S(1)}, u32[]{:S(2)}, u32[]{:S(2)}) collective-permute-start(bf16[16,2880]{1,0:T(8,128)(2,1)S(1)} %get-tuple-element.59), channel_id=1, source_target_pairs={{0,3},{1,4},{2,7},{3,0},{4,1},{5,6},{6,5},{7,2},{8,13},{9,10},{10,... | collective-permute-start | bytes 276488 | tf_op jit(solution)/shard_map/ppermute | solution.py:275
  16.9 4.1 %copy-start.1 = (f32[384,64]{0,1:T(8,128)S(1)}, f32[384,64]{0,1:T(8,128)}, u32[]{:S(2)}) copy-start(f32[384,64]{0,1:T(8,128)} %param.6) | copy-start | bytes 294916
  18.6 2.4 %collective-permute-start.5 = (bf16[32,2880]{1,0:T(8,128)(2,1)S(1)}, bf16[32,2880]{1,0:T(8,128)(2,1)S(1)}, u32[]{:S(2)}, u32[]{:S(2)}) collective-permute-start(bf16[32,2880]{1,0:T(8,128)(2,1)S(1)} %get-tuple-element.62), channel_id=1, source_target_pairs={{0,1},{1,0},{2,3},{3,2},{4,5},{5,4},{6,7},{7,6},{8,9},{9,8},{10,11... | collective-permute-start | bytes 552968 | tf_op jit(solution)/shard_map/ppermute | solution.py:278
  19.3 3.9 %collective-permute-start.7 = (bf16[8,2880]{1,0:T(8,128)(2,1)S(1)}, bf16[8,2880]{1,0:T(8,128)(2,1)S(1)}, u32[]{:S(2)}, u32[]{:S(2)}) collective-permute-start(bf16[8,2880]{1,0:T(8,128)(2,1)S(1)} %slice.24), channel_id=1, source_target_pairs={{0,5},{1,2},{2,1},{3,6},{4,7},{5,0},{6,3},{7,4},{8,11},{9,12},{10,... | collective-permute-start | bytes 138248 | tf_op jit(solution)/shard_map/ppermute | solution.py:275
  23.3 5.1 %collective-permute-start.8 = (bf16[4,2880]{1,0:T(4,128)(2,1)S(1)}, bf16[4,2880]{1,0:T(4,128)(2,1)S(1)}, u32[]{:S(2)}, u32[]{:S(2)}) collective-permute-start(bf16[4,2880]{1,0:T(4,128)(2,1)S(1)} %slice.25), channel_id=1, source_target_pairs={{0,9},{1,8},{2,11},{3,10},{4,13},{5,12},{6,15},{7,14},{8,1},{9,0},... | collective-permute-start | bytes 69128 | tf_op jit(solution)/shard_map/ppermute | solution.py:275

commit v14 on v8

--- a/solution.py
+++ b/solution.py
@@ -271,9 +271,8 @@
     )
     come = exchange(sent, bits - 1)
     moment, _ = tie(moment, sent)
+    theirs = across(held)
     moment_in, moment_next = new_moment(grad, moment)
-    held, _ = tie(held, moment_in)
-    theirs = across(held)
     come, moment_in, moment_next = tie(come, moment_in, moment_next)
     for step in reversed(range(bits)):
         if step == 0:

time: 28.9 us -> 28.9 us (level)
  no operation moved by 1% of the time
where the time goes in v14:
time: 28.9 us; the launch traced here: 28.8 us
  starting transfers between devices  15.5 us (54%)
  Pallas kernels  10.2 us (35%)
  waiting for transfers between devices  2.28 us (8%)
  between operations  0.74 us (3%)
    ppermute x7, starting transfers between devices, exchange(): return lax.ppermute(value, 'rows', pairs)  14.8 us
    ppermute x7, waiting for transfers between devices, exchange(): return lax.ppermute(value, 'rows', pairs)  2.28 us
    pallas_call x1, Pallas kernels, new_update(): pl.pallas_call(update_kernel, in_specs=[INSIDE] * 2, out_specs=ANYWHERE,...  1.72 us
    pallas_call x1, Pallas kernels, new_moment(): pl.pallas_call(moment_kernel, in_specs=[INSIDE, INSIDE], out_specs=[INSID...  1.7 us
    pallas_call x1, Pallas kernels, load(): pl.pallas_call(load_kernel, in_specs=[pl.BlockSpec(memory_space=pltpu.HBM...  1.64 us
    pallas_call x1, Pallas kernels, scaled_rotation(): pl.pallas_call(functools.partial(scale_kernel, orders, own), in_specs=[IN...  1.57 us
    pallas_call x1, Pallas kernels, power_products(): pl.pallas_call(power_kernel, in_specs=[INSIDE] * (len(pieces) + len(grads...  1.55 us
    pallas_call x1, Pallas kernels, transposed(): pl.pallas_call(transpose_kernel, in_specs=[INSIDE] * len(values), out_spe...  1.22 us
  transfers between devices with their start and end apart: 9, of which 5 were waited for; matrix products, arithmetic and copies ran while one was open for 0% of the time, Pallas kernels for 27%

profile of v14, /device:TPU:0, one launch (start us, length us, event | category | flops | bytes accessed | tf_op | source)
XLA Modules:
  0.0 28.8 jit_solution(10010703756053171545)
XLA Ops:
  0.6 3.5 %collective-permute-start = (bf16[4,2880]{1,0:T(4,128)(2,1)}, bf16[4,2880]{1,0:T(4,128)(2,1)S(1)}, u32[]{:S(2)}, u32[]{:S(2)}) collective-permute-start(bf16[4,2880]{1,0:T(4,128)(2,1)} %refs_1_.1), channel_id=1, source_target_pairs={{0,9},{1,8},{2,11},{3,10},{4,13},{5,12},{6,15},{7,14},{8,1},{9,0},... | collective-permute-start | bytes 69128 | tf_op jit(solution)/shard_map/ppermute | solution.py:248
  4.2 1.6 %load.1 = (bf16[2880,384]{1,0:T(8,128)(2,1)S(1)}, bf16[4,2880]{1,0:T(4,128)(2,1)S(1)}) custom-call(bf16[2880,384]{1,0:T(8,128)(2,1)} %bitcast.9, bf16[4,2880]{1,0:T(4,128)(2,1)} %refs_1_.1), custom_call_target="tpu_custom_call" | custom-call | tf_op jit(solution)/shard_map/load/pallas_call | solution.py:48
  5.8 0.1 collective-permute-done
  6.0 0.6 %collective-permute-start.3 = (bf16[2880,384]{1,0:T(8,128)(2,1)S(1)}, bf16[2880,384]{1,0:T(8,128)(2,1)S(1)}, u32[]{:S(2)}, u32[]{:S(2)}) collective-permute-start(bf16[2880,384]{1,0:T(8,128)(2,1)S(1)} %get-tuple-element.48.refs_0_.refs_4_.grad), channel_id=1, source_target_pairs={{0,1},{1,0},{2,3},{3,2},{4,5},{5,4},{6,7},{7,6},{8,9},{9,8},{10,11... | collective-permute-start | bytes 6635528 | tf_op jit(solution)/shard_map/ppermute | solution.py:251
  6.6 1.7 %collective-permute-start.1 = (bf16[8,2880]{1,0:T(8,128)(2,1)S(1)}, bf16[8,2880]{1,0:T(8,128)(2,1)S(1)}, u32[]{:S(2)}, u32[]{:S(2)}) collective-permute-start(bf16[8,2880]{1,0:T(8,128)(2,1)S(1)} %pad_maximum_fusion.refs_0_), channel_id=1, source_target_pairs={{0,5},{1,2},{2,1},{3,6},{4,7},{5,0},{6,3},{7,4},{8,11},{9,12},{10,... | collective-permute-start | bytes 138248 | tf_op jit(solution)/shard_map/ppermute | solution.py:248
  8.3 1.2 %collective-permute-start.2 = (bf16[8,2880]{1,0:T(8,128)(2,1)S(1)}, bf16[8,2880]{1,0:T(8,128)(2,1)S(1)}, u32[]{:S(2)}, u32[]{:S(2)}) collective-permute-start(bf16[8,2880]{1,0:T(8,128)(2,1)S(1)} %pad_maximum_fusion.refs_0_), channel_id=1, source_target_pairs={{0,3},{1,4},{2,7},{3,0},{4,1},{5,6},{6,5},{7,2},{8,13},{9,10},{10,... | collective-permute-start | bytes 138248 | tf_op jit(solution)/shard_map/ppermute | solution.py:248
  9.5 0.7 %collective-permute-done.1.refs_1_ = bf16[8,2880]{1,0:T(8,128)(2,1)S(1)} collective-permute-done((bf16[8,2880]{1,0:T(8,128)(2,1)S(1)}, bf16[8,2880]{1,0:T(8,128)(2,1)S(1)}, u32[]{:S(2)}, u32[]{:S(2)}) %collective-permute-start.1) | collective-permute-done | bytes 46112 | tf_op jit(solution)/shard_map/ppermute | solution.py:248
  10.2 1.6 %collective-permute-start.4 = (bf16[8,2880]{1,0:T(8,128)(2,1)S(1)}, bf16[8,2880]{1,0:T(8,128)(2,1)S(1)}, u32[]{:S(2)}, u32[]{:S(2)}) collective-permute-start(bf16[8,2880]{1,0:T(8,128)(2,1)S(1)} %collective-permute-done.1.refs_1_), channel_id=1, source_target_pairs={{0,3},{1,4},{2,7},{3,0},{4,1},{5,6},{6,5},{7,2},{8,13},{9,10},{10,... | collective-permute-start | bytes 138248 | tf_op jit(solution)/shard_map/ppermute | solution.py:248
  11.7 0.0 collective-permute-done.2.refs_2_
  11.8 0.0 collective-permute-done.3.refs_1_.refs_5_
  11.8 1.2 %transpose.25 = (bf16[384,2880]{1,0:T(8,128)(2,1)S(1)}, bf16[384,2880]{1,0:T(8,128)(2,1)S(1)}) custom-call(bf16[2880,384]{1,0:T(8,128)(2,1)S(1)} %get-tuple-element.48.refs_0_.refs_4_.grad, bf16[2880,384]{1,0:T(8,128)(2,1)S(1)} %collective-permute-done.3.refs_1_.refs_5_), custom_call_target="tpu_custom_call" | custom-call | tf_op jit(solution)/shard_map/transpose/pallas_call | solution.py:96
  13.0 0.6 %collective-permute-done.4.refs_3_ = bf16[8,2880]{1,0:T(8,128)(2,1)S(1)} collective-permute-done((bf16[8,2880]{1,0:T(8,128)(2,1)S(1)}, bf16[8,2880]{1,0:T(8,128)(2,1)S(1)}, u32[]{:S(2)}, u32[]{:S(2)}) %collective-permute-start.4) | collective-permute-done | bytes 46112 | tf_op jit(solution)/shard_map/ppermute | solution.py:248
  13.7 0.0 copy-start
  13.7 1.6 %power.1 = (bf16[32,2880]{1,0:T(8,128)(2,1)S(1)}, f32[32,384]{1,0:T(8,128)S(1)}, f32[16,2880]{1,0:T(8,128)S(1)}, bf16[16,2880]{1,0:T(8,128)(2,1)S(1)}) custom-call(bf16[8,2880]{1,0:T(8,128)(2,1)S(1)} %pad_maximum_fusion.refs_0_, bf16[8,2880]{1,0:T(8,128)(2,1)S(1)} %collective-permute-done.1.refs_1_, bf16[8,2880]{1,0:T(8,128)(2,1)S(1)} %collective-permute-done.2.refs_2_, ...), custom_call_target="tpu_custom_call" | custom-call | tf_op jit(solution)/shard_map/power/pallas_call | solution.py:125
  15.2 1.7 %collective-permute-start.6 = (bf16[16,2880]{1,0:T(8,128)(2,1)S(1)}, bf16[16,2880]{1,0:T(8,128)(2,1)S(1)}, u32[]{:S(2)}, u32[]{:S(2)}) collective-permute-start(bf16[16,2880]{1,0:T(8,128)(2,1)S(1)} %get-tuple-element.57), channel_id=1, source_target_pairs={{0,3},{1,4},{2,7},{3,0},{4,1},{5,6},{6,5},{7,2},{8,13},{9,10},{10,... | collective-permute-start | bytes 276488 | tf_op jit(solution)/shard_map/ppermute | solution.py:248
  16.9 0.1 collective-permute-start.5
  17.0 0.0 copy-done
  17.0 0.0 copy-start.1
  17.0 1.7 %moment.1 = (bf16[2880,384]{1,0:T(8,128)(2,1)S(1)}, bf16[2880,384]{1,0:T(8,128)(2,1)}) custom-call(bf16[2880,384]{1,0:T(8,128)(2,1)S(1)} %get-tuple-element.48.refs_0_.refs_4_.grad, bf16[2880,384]{1,0:T(8,128)(2,1)S(1)} %bitcast.6), custom_call_target="tpu_custom_call" | custom-call | tf_op jit(solution)/shard_map/moment/pallas_call | solution.py:75
  18.7 0.5 %collective-permute-done.6 = bf16[16,2880]{1,0:T(8,128)(2,1)S(1)} collective-permute-done((bf16[16,2880]{1,0:T(8,128)(2,1)S(1)}, bf16[16,2880]{1,0:T(8,128)(2,1)S(1)}, u32[]{:S(2)}, u32[]{:S(2)}) %collective-permute-start.6) | collective-permute-done | bytes 92192 | tf_op jit(solution)/shard_map/ppermute | solution.py:248
  19.3 1.7 %collective-permute-start.7 = (bf16[8,2880]{1,0:T(8,128)(2,1)S(1)}, bf16[8,2880]{1,0:T(8,128)(2,1)S(1)}, u32[]{:S(2)}, u32[]{:S(2)}) collective-permute-start(bf16[8,2880]{1,0:T(8,128)(2,1)S(1)} %slice.24), channel_id=1, source_target_pairs={{0,5},{1,2},{2,1},{3,6},{4,7},{5,0},{6,3},{7,4},{8,11},{9,12},{10,... | collective-permute-start | bytes 138248 | tf_op jit(solution)/shard_map/ppermute | solution.py:248
  21.0 0.0 collective-permute-done.5
  21.0 0.0 copy-done.1
  21.0 1.6 %scale.1 = (bf16[64,384]{1,0:T(8,128)(2,1)S(1)}, f32[64,384]{1,0:T(8,128)}) custom-call(bf16[64,2880]{1,0:T(8,128)(2,1)S(1)} %constant_dynamic-update-slice_fusion.basis, bf16[2880,384]{1,0:T(8,128)(2,1)S(1)} %get-tuple-element.48.refs_0_.refs_4_.grad, bf16[2880,384]{1,0:T(8,128)(2,1)S(1)} %get-tuple-element.64.moment, ...), custom_call_target="tpu_custom_call" | custom-call | tf_op jit(solution)/shard_map/scale/pallas_call | solution.py:198
  22.6 0.3 collective-permute-done.7
  22.9 3.4 %collective-permute-start.8 = (bf16[4,2880]{1,0:T(4,128)(2,1)S(1)}, bf16[4,2880]{1,0:T(4,128)(2,1)S(1)}, u32[]{:S(2)}, u32[]{:S(2)}) collective-permute-start(bf16[4,2880]{1,0:T(4,128)(2,1)S(1)} %slice.25), channel_id=1, source_target_pairs={{0,9},{1,8},{2,11},{3,10},{4,13},{5,12},{6,15},{7,14},{8,1},{9,0},... | collective-permute-start | bytes 69128 | tf_op jit(solution)/shard_map/ppermute | solution.py:248
  26.3 1.7 %update.1 = bf16[2880,384]{1,0:T(8,128)(2,1)} custom-call(bf16[64,2880]{1,0:T(8,128)(2,1)S(1)} %constant_dynamic-update-slice_fusion.basis, bf16[64,384]{1,0:T(8,128)(2,1)S(1)} %get-tuple-element.70.scaled), custom_call_target="tpu_custom_call" | custom-call | tf_op jit(solution)/shard_map/update/pallas_call | solution.py:226
  28.0 0.0 collective-permute-done.8.come
  28.0 0.7 %normalise.1 = f32[4,2880]{1,0:T(4,128)} custom-call(f32[4,2880]{1,0:T(4,128)S(1)} %slice.21.kept, bf16[4,2880]{1,0:T(4,128)(2,1)S(1)} %collective-permute-done.8.come), custom_call_target="tpu_custom_call" | custom-call | tf_op jit(solution)/shard_map/normalise/pallas_call | solution.py:147
  (9 shorter events, 0.1 us)
Async XLA Ops:
  0.6 5.3 %collective-permute-start = (bf16[4,2880]{1,0:T(4,128)(2,1)}, bf16[4,2880]{1,0:T(4,128)(2,1)S(1)}, u32[]{:S(2)}, u32[]{:S(2)}) collective-permute-start(bf16[4,2880]{1,0:T(4,128)(2,1)} %refs_1_.1), channel_id=1, source_target_pairs={{0,9},{1,8},{2,11},{3,10},{4,13},{5,12},{6,15},{7,14},{8,1},{9,0},... | collective-permute-start | bytes 69128 | tf_op jit(solution)/shard_map/ppermute | solution.py:248
  6.0 5.8 %collective-permute-start.3 = (bf16[2880,384]{1,0:T(8,128)(2,1)S(1)}, bf16[2880,384]{1,0:T(8,128)(2,1)S(1)}, u32[]{:S(2)}, u32[]{:S(2)}) collective-permute-start(bf16[2880,384]{1,0:T(8,128)(2,1)S(1)} %get-tuple-element.48.refs_0_.refs_4_.grad), channel_id=1, source_target_pairs={{0,1},{1,0},{2,3},{3,2},{4,5},{5,4},{6,7},{7,6},{8,9},{9,8},{10,11... | collective-permute-start | bytes 6635528 | tf_op jit(solution)/shard_map/ppermute | solution.py:251
  6.6 3.6 %collective-permute-start.1 = (bf16[8,2880]{1,0:T(8,128)(2,1)S(1)}, bf16[8,2880]{1,0:T(8,128)(2,1)S(1)}, u32[]{:S(2)}, u32[]{:S(2)}) collective-permute-start(bf16[8,2880]{1,0:T(8,128)(2,1)S(1)} %pad_maximum_fusion.refs_0_), channel_id=1, source_target_pairs={{0,5},{1,2},{2,1},{3,6},{4,7},{5,0},{6,3},{7,4},{8,11},{9,12},{10,... | collective-permute-start | bytes 138248 | tf_op jit(solution)/shard_map/ppermute | solution.py:248
  8.3 3.5 %collective-permute-start.2 = (bf16[8,2880]{1,0:T(8,128)(2,1)S(1)}, bf16[8,2880]{1,0:T(8,128)(2,1)S(1)}, u32[]{:S(2)}, u32[]{:S(2)}) collective-permute-start(bf16[8,2880]{1,0:T(8,128)(2,1)S(1)} %pad_maximum_fusion.refs_0_), channel_id=1, source_target_pairs={{0,3},{1,4},{2,7},{3,0},{4,1},{5,6},{6,5},{7,2},{8,13},{9,10},{10,... | collective-permute-start | bytes 138248 | tf_op jit(solution)/shard_map/ppermute | solution.py:248
  10.2 3.5 %collective-permute-start.4 = (bf16[8,2880]{1,0:T(8,128)(2,1)S(1)}, bf16[8,2880]{1,0:T(8,128)(2,1)S(1)}, u32[]{:S(2)}, u32[]{:S(2)}) collective-permute-start(bf16[8,2880]{1,0:T(8,128)(2,1)S(1)} %collective-permute-done.1.refs_1_), channel_id=1, source_target_pairs={{0,3},{1,4},{2,7},{3,0},{4,1},{5,6},{6,5},{7,2},{8,13},{9,10},{10,... | collective-permute-start | bytes 138248 | tf_op jit(solution)/shard_map/ppermute | solution.py:248
  13.7 3.3 %copy-start = (bf16[384,2880]{0,1:T(8,128)(2,1)S(1)}, bf16[384,2880]{0,1:T(8,128)(2,1)}, u32[]{:S(2)}) copy-start(bf16[384,2880]{0,1:T(8,128)(2,1)} %param.5) | copy-start | bytes 6635524
  15.2 4.0 %collective-permute-start.6 = (bf16[16,2880]{1,0:T(8,128)(2,1)S(1)}, bf16[16,2880]{1,0:T(8,128)(2,1)S(1)}, u32[]{:S(2)}, u32[]{:S(2)}) collective-permute-start(bf16[16,2880]{1,0:T(8,128)(2,1)S(1)} %get-tuple-element.57), channel_id=1, source_target_pairs={{0,3},{1,4},{2,7},{3,0},{4,1},{5,6},{6,5},{7,2},{8,13},{9,10},{10,... | collective-permute-start | bytes 276488 | tf_op jit(solution)/shard_map/ppermute | solution.py:248
  16.9 4.1 %collective-permute-start.5 = (bf16[32,2880]{1,0:T(8,128)(2,1)S(1)}, bf16[32,2880]{1,0:T(8,128)(2,1)S(1)}, u32[]{:S(2)}, u32[]{:S(2)}) collective-permute-start(bf16[32,2880]{1,0:T(8,128)(2,1)S(1)} %get-tuple-element.55), channel_id=1, source_target_pairs={{0,1},{1,0},{2,3},{3,2},{4,5},{5,4},{6,7},{7,6},{8,9},{9,8},{10,11... | collective-permute-start | bytes 552968 | tf_op jit(solution)/shard_map/ppermute | solution.py:251
  17.0 4.0 %copy-start.1 = (f32[384,64]{0,1:T(8,128)S(1)}, f32[384,64]{0,1:T(8,128)}, u32[]{:S(2)}) copy-start(f32[384,64]{0,1:T(8,128)} %param.6) | copy-start | bytes 294916
  19.3 3.6 %collective-permute-start.7 = (bf16[8,2880]{1,0:T(8,128)(2,1)S(1)}, bf16[8,2880]{1,0:T(8,128)(2,1)S(1)}, u32[]{:S(2)}, u32[]{:S(2)}) collective-permute-start(bf16[8,2880]{1,0:T(8,128)(2,1)S(1)} %slice.24), channel_id=1, source_target_pairs={{0,5},{1,2},{2,1},{3,6},{4,7},{5,0},{6,3},{7,4},{8,11},{9,12},{10,... | collective-permute-start | bytes 138248 | tf_op jit(solution)/shard_map/ppermute | solution.py:248
  22.9 5.1 %collective-permute-start.8 = (bf16[4,2880]{1,0:T(4,128)(2,1)S(1)}, bf16[4,2880]{1,0:T(4,128)(2,1)S(1)}, u32[]{:S(2)}, u32[]{:S(2)}) collective-permute-start(bf16[4,2880]{1,0:T(4,128)(2,1)S(1)} %slice.25), channel_id=1, source_target_pairs={{0,9},{1,8},{2,11},{3,10},{4,13},{5,12},{6,15},{7,14},{8,1},{9,0},... | collective-permute-start | bytes 69128 | tf_op jit(solution)/shard_map/ppermute | solution.py:248

commit v15 on v14

--- a/solution.py
+++ b/solution.py
@@ -158,7 +158,7 @@
     me = lax.axis_index("rows")
     core, chip = me & 1, me >> 1
     bits = len(orders[0])
-    parity = functools.reduce(lambda a, b: a ^ b, [(me >> b) & 1 for b in range(bits + 1)])
+    parity = functools.reduce(lambda a, b: a ^ b, [(me >> b) & 1 for b in range(bits)])
     count = rot_half.shape[0]
     rot[:count] = rot_half[...]
     rot[count:] = dot(basis[count:], grad[...], ((1,), (0,)))
@@ -174,7 +174,7 @@
             for offset in range(1 << bits):
                 mine = pl.ds(place(offset, orders[half]), own)
                 theirs = pl.ds(count + place(offset, orders[1 - half]), own)
-                first = core == odd(offset)
+                first = core == odd(offset & ((1 << (bits - 1)) - 1))
                 tile = pl.ds(pl.multiple_of((chip ^ offset) * 2 * own, 2 * own), 2 * own)
 
                 def joined(ref):
@@ -243,9 +243,12 @@
     far, near = (bits - 1,), tuple(reversed(range(bits - 1)))
     orders = (far + near, far + near[-1:] + near[:-1])
 
+    def partner(i, step):
+        bit = orders[odd(i & (n // 2 - 1))][step]
+        return i ^ (2 << bit) ^ (bit != far[0])
+
     def exchange(value, step):
-        pairs = [(i, i ^ (2 << orders[odd(i)][step]) ^ 1) for i in range(n)]
-        return lax.ppermute(value, "rows", pairs)
+        return lax.ppermute(value, "rows", [(i, partner(i, step)) for i in range(n)])
 
     def across(value):
         return lax.ppermute(value, "rows", [(i, i ^ 1) for i in range(n)])

time: 28.9 us -> 29.3 us (1.014)
    ppermute x7, starting transfers between devices: 14.8 us -> 15.6 us  [exchange(): lax.ppermute(value, 'rows', [(i, partner(i, step)) for i in range(n)])]
    ppermute x2, starting transfers between devices: 0.71 us -> 0.01 us  [across(): return lax.ppermute(value, 'rows', [(i, i ^ 1) for i in range(n)])]
  transfers between devices with their start and end apart: 9 -> 9, of which waited for: 5 -> 6; matrix products, arithmetic and copies ran while one was open for 0% -> 0% of each run, Pallas kernels for 27% -> 27%
where the time goes in v15:
time: 29.3 us; the launch traced here: 29.2 us
  starting transfers between devices  15.6 us (53%)
  Pallas kernels  10.2 us (35%)
  waiting for transfers between devices  2.52 us (9%)
  between operations  0.73 us (2%)
    ppermute x7, starting transfers between devices, exchange(): lax.ppermute(value, 'rows', [(i, partner(i, step)) for i in range(n)])  15.6 us
    ppermute x7, waiting for transfers between devices, exchange(): lax.ppermute(value, 'rows', [(i, partner(i, step)) for i in range(n)])  2.51 us
    pallas_call x1, Pallas kernels, new_update(): pl.pallas_call(update_kernel, in_specs=[INSIDE] * 2, out_specs=ANYWHERE,...  1.72 us
    pallas_call x1, Pallas kernels, new_moment(): pl.pallas_call(moment_kernel, in_specs=[INSIDE, INSIDE], out_specs=[INSID...  1.7 us
    pallas_call x1, Pallas kernels, load(): pl.pallas_call(load_kernel, in_specs=[pl.BlockSpec(memory_space=pltpu.HBM...  1.64 us
    pallas_call x1, Pallas kernels, scaled_rotation(): pl.pallas_call(functools.partial(scale_kernel, orders, own), in_specs=[IN...  1.58 us
    pallas_call x1, Pallas kernels, power_products(): pl.pallas_call(power_kernel, in_specs=[INSIDE] * (len(pieces) + len(grads...  1.55 us
    pallas_call x1, Pallas kernels, transposed(): pl.pallas_call(transpose_kernel, in_specs=[INSIDE] * len(values), out_spe...  1.22 us
  transfers between devices with their start and end apart: 9, of which 6 were waited for; matrix products, arithmetic and copies ran while one was open for 0% of the time, Pallas kernels for 27%

profile of v15, /device:TPU:0, one launch (start us, length us, event | category | flops | bytes accessed | tf_op | source)
XLA Modules:
  0.0 29.2 jit_solution(4313828713758074229)
XLA Ops:
  0.6 4.1 %collective-permute-start = (bf16[4,2880]{1,0:T(4,128)(2,1)}, bf16[4,2880]{1,0:T(4,128)(2,1)S(1)}, u32[]{:S(2)}, u32[]{:S(2)}) collective-permute-start(bf16[4,2880]{1,0:T(4,128)(2,1)} %refs_1_.1), channel_id=1, source_target_pairs={{0,8},{1,9},{2,10},{3,11},{4,12},{5,13},{6,14},{7,15},{8,0},{9,1},... | collective-permute-start | bytes 69128 | tf_op jit(solution)/shard_map/ppermute | solution.py:251
  4.7 1.6 %load.1 = (bf16[2880,384]{1,0:T(8,128)(2,1)S(1)}, bf16[4,2880]{1,0:T(4,128)(2,1)S(1)}) custom-call(bf16[2880,384]{1,0:T(8,128)(2,1)} %bitcast.9, bf16[4,2880]{1,0:T(4,128)(2,1)} %refs_1_.1), custom_call_target="tpu_custom_call" | custom-call | tf_op jit(solution)/shard_map/load/pallas_call | solution.py:48
  6.4 0.4 %collective-permute-done = bf16[4,2880]{1,0:T(4,128)(2,1)S(1)} collective-permute-done((bf16[4,2880]{1,0:T(4,128)(2,1)}, bf16[4,2880]{1,0:T(4,128)(2,1)S(1)}, u32[]{:S(2)}, u32[]{:S(2)}) %collective-permute-start) | collective-permute-done | bytes 23072 | tf_op jit(solution)/shard_map/ppermute | solution.py:251
  6.7 0.0 collective-permute-start.3
  6.8 2.1 %collective-permute-start.1 = (bf16[8,2880]{1,0:T(8,128)(2,1)S(1)}, bf16[8,2880]{1,0:T(8,128)(2,1)S(1)}, u32[]{:S(2)}, u32[]{:S(2)}) collective-permute-start(bf16[8,2880]{1,0:T(8,128)(2,1)S(1)} %pad_maximum_fusion.refs_0_), channel_id=1, source_target_pairs={{0,5},{1,2},{2,1},{3,6},{4,7},{5,0},{6,3},{7,4},{8,13},{9,10},{10,... | collective-permute-start | bytes 138248 | tf_op jit(solution)/shard_map/ppermute | solution.py:251
  8.9 1.1 %collective-permute-start.2 = (bf16[8,2880]{1,0:T(8,128)(2,1)S(1)}, bf16[8,2880]{1,0:T(8,128)(2,1)S(1)}, u32[]{:S(2)}, u32[]{:S(2)}) collective-permute-start(bf16[8,2880]{1,0:T(8,128)(2,1)S(1)} %pad_maximum_fusion.refs_0_), channel_id=1, source_target_pairs={{0,3},{1,4},{2,7},{3,0},{4,1},{5,6},{6,5},{7,2},{8,11},{9,12},{10,... | collective-permute-start | bytes 138248 | tf_op jit(solution)/shard_map/ppermute | solution.py:251
  10.0 0.7 %collective-permute-done.1.refs_1_ = bf16[8,2880]{1,0:T(8,128)(2,1)S(1)} collective-permute-done((bf16[8,2880]{1,0:T(8,128)(2,1)S(1)}, bf16[8,2880]{1,0:T(8,128)(2,1)S(1)}, u32[]{:S(2)}, u32[]{:S(2)}) %collective-permute-start.1) | collective-permute-done | bytes 46112 | tf_op jit(solution)/shard_map/ppermute | solution.py:251
  10.6 1.8 %collective-permute-start.4 = (bf16[8,2880]{1,0:T(8,128)(2,1)S(1)}, bf16[8,2880]{1,0:T(8,128)(2,1)S(1)}, u32[]{:S(2)}, u32[]{:S(2)}) collective-permute-start(bf16[8,2880]{1,0:T(8,128)(2,1)S(1)} %collective-permute-done.1.refs_1_), channel_id=1, source_target_pairs={{0,3},{1,4},{2,7},{3,0},{4,1},{5,6},{6,5},{7,2},{8,11},{9,12},{10,... | collective-permute-start | bytes 138248 | tf_op jit(solution)/shard_map/ppermute | solution.py:251
  12.4 0.0 collective-permute-done.2.refs_2_
  12.4 0.0 collective-permute-done.3.refs_1_.refs_5_
  12.4 1.2 %transpose.25 = (bf16[384,2880]{1,0:T(8,128)(2,1)S(1)}, bf16[384,2880]{1,0:T(8,128)(2,1)S(1)}) custom-call(bf16[2880,384]{1,0:T(8,128)(2,1)S(1)} %get-tuple-element.48.refs_0_.refs_4_.grad, bf16[2880,384]{1,0:T(8,128)(2,1)S(1)} %collective-permute-done.3.refs_1_.refs_5_), custom_call_target="tpu_custom_call" | custom-call | tf_op jit(solution)/shard_map/transpose/pallas_call | solution.py:96
  13.6 0.5 %collective-permute-done.4.refs_3_ = bf16[8,2880]{1,0:T(8,128)(2,1)S(1)} collective-permute-done((bf16[8,2880]{1,0:T(8,128)(2,1)S(1)}, bf16[8,2880]{1,0:T(8,128)(2,1)S(1)}, u32[]{:S(2)}, u32[]{:S(2)}) %collective-permute-start.4) | collective-permute-done | bytes 46112 | tf_op jit(solution)/shard_map/ppermute | solution.py:251
  14.2 0.0 copy-start
  14.2 1.6 %power.1 = (bf16[32,2880]{1,0:T(8,128)(2,1)S(1)}, f32[32,384]{1,0:T(8,128)S(1)}, f32[16,2880]{1,0:T(8,128)S(1)}, bf16[16,2880]{1,0:T(8,128)(2,1)S(1)}) custom-call(bf16[8,2880]{1,0:T(8,128)(2,1)S(1)} %pad_maximum_fusion.refs_0_, bf16[8,2880]{1,0:T(8,128)(2,1)S(1)} %collective-permute-done.1.refs_1_, bf16[8,2880]{1,0:T(8,128)(2,1)S(1)} %collective-permute-done.2.refs_2_, ...), custom_call_target="tpu_custom_call" | custom-call | tf_op jit(solution)/shard_map/power/pallas_call | solution.py:125
  15.7 2.0 %collective-permute-start.6 = (bf16[16,2880]{1,0:T(8,128)(2,1)S(1)}, bf16[16,2880]{1,0:T(8,128)(2,1)S(1)}, u32[]{:S(2)}, u32[]{:S(2)}) collective-permute-start(bf16[16,2880]{1,0:T(8,128)(2,1)S(1)} %get-tuple-element.57), channel_id=1, source_target_pairs={{0,3},{1,4},{2,7},{3,0},{4,1},{5,6},{6,5},{7,2},{8,11},{9,12},{10,... | collective-permute-start | bytes 276488 | tf_op jit(solution)/shard_map/ppermute | solution.py:251
  17.7 0.0 collective-permute-start.5
  17.7 0.0 copy-done
  17.7 0.0 copy-start.1
  17.7 1.7 %moment.1 = (bf16[2880,384]{1,0:T(8,128)(2,1)S(1)}, bf16[2880,384]{1,0:T(8,128)(2,1)}) custom-call(bf16[2880,384]{1,0:T(8,128)(2,1)S(1)} %get-tuple-element.48.refs_0_.refs_4_.grad, bf16[2880,384]{1,0:T(8,128)(2,1)S(1)} %bitcast.6), custom_call_target="tpu_custom_call" | custom-call | tf_op jit(solution)/shard_map/moment/pallas_call | solution.py:75
  19.5 0.5 %collective-permute-done.6 = bf16[16,2880]{1,0:T(8,128)(2,1)S(1)} collective-permute-done((bf16[16,2880]{1,0:T(8,128)(2,1)S(1)}, bf16[16,2880]{1,0:T(8,128)(2,1)S(1)}, u32[]{:S(2)}, u32[]{:S(2)}) %collective-permute-start.6) | collective-permute-done | bytes 92192 | tf_op jit(solution)/shard_map/ppermute | solution.py:251
  20.0 1.5 %collective-permute-start.7 = (bf16[8,2880]{1,0:T(8,128)(2,1)S(1)}, bf16[8,2880]{1,0:T(8,128)(2,1)S(1)}, u32[]{:S(2)}, u32[]{:S(2)}) collective-permute-start(bf16[8,2880]{1,0:T(8,128)(2,1)S(1)} %slice.24), channel_id=1, source_target_pairs={{0,5},{1,2},{2,1},{3,6},{4,7},{5,0},{6,3},{7,4},{8,13},{9,10},{10,... | collective-permute-start | bytes 138248 | tf_op jit(solution)/shard_map/ppermute | solution.py:251
  21.6 0.0 collective-permute-done.5
  21.6 0.0 copy-done.1
  21.6 1.6 %scale.1 = (bf16[64,384]{1,0:T(8,128)(2,1)S(1)}, f32[64,384]{1,0:T(8,128)}) custom-call(bf16[64,2880]{1,0:T(8,128)(2,1)S(1)} %constant_dynamic-update-slice_fusion.basis, bf16[2880,384]{1,0:T(8,128)(2,1)S(1)} %get-tuple-element.48.refs_0_.refs_4_.grad, bf16[2880,384]{1,0:T(8,128)(2,1)S(1)} %get-tuple-element.64.moment, ...), custom_call_target="tpu_custom_call" | custom-call | tf_op jit(solution)/shard_map/scale/pallas_call | solution.py:198
  23.2 0.4 %collective-permute-done.7 = bf16[8,2880]{1,0:T(8,128)(2,1)S(1)} collective-permute-done((bf16[8,2880]{1,0:T(8,128)(2,1)S(1)}, bf16[8,2880]{1,0:T(8,128)(2,1)S(1)}, u32[]{:S(2)}, u32[]{:S(2)}) %collective-permute-start.7) | collective-permute-done | bytes 46112 | tf_op jit(solution)/shard_map/ppermute | solution.py:251
  23.6 3.0 %collective-permute-start.8 = (bf16[4,2880]{1,0:T(4,128)(2,1)S(1)}, bf16[4,2880]{1,0:T(4,128)(2,1)S(1)}, u32[]{:S(2)}, u32[]{:S(2)}) collective-permute-start(bf16[4,2880]{1,0:T(4,128)(2,1)S(1)} %slice.25), channel_id=1, source_target_pairs={{0,8},{1,9},{2,10},{3,11},{4,12},{5,13},{6,14},{7,15},{8,0},{9,1},... | collective-permute-start | bytes 69128 | tf_op jit(solution)/shard_map/ppermute | solution.py:251
  26.6 1.7 %update.1 = bf16[2880,384]{1,0:T(8,128)(2,1)} custom-call(bf16[64,2880]{1,0:T(8,128)(2,1)S(1)} %constant_dynamic-update-slice_fusion.basis, bf16[64,384]{1,0:T(8,128)(2,1)S(1)} %get-tuple-element.70.scaled), custom_call_target="tpu_custom_call" | custom-call | tf_op jit(solution)/shard_map/update/pallas_call | solution.py:226
  28.4 0.1 collective-permute-done.8.come
  28.4 0.7 %normalise.1 = f32[4,2880]{1,0:T(4,128)} custom-call(f32[4,2880]{1,0:T(4,128)S(1)} %slice.21.kept, bf16[4,2880]{1,0:T(4,128)(2,1)S(1)} %collective-permute-done.8.come), custom_call_target="tpu_custom_call" | custom-call | tf_op jit(solution)/shard_map/normalise/pallas_call | solution.py:147
  (9 shorter events, 0.1 us)
Async XLA Ops:
  0.6 6.1 %collective-permute-start = (bf16[4,2880]{1,0:T(4,128)(2,1)}, bf16[4,2880]{1,0:T(4,128)(2,1)S(1)}, u32[]{:S(2)}, u32[]{:S(2)}) collective-permute-start(bf16[4,2880]{1,0:T(4,128)(2,1)} %refs_1_.1), channel_id=1, source_target_pairs={{0,8},{1,9},{2,10},{3,11},{4,12},{5,13},{6,14},{7,15},{8,0},{9,1},... | collective-permute-start | bytes 69128 | tf_op jit(solution)/shard_map/ppermute | solution.py:251
  6.7 5.7 %collective-permute-start.3 = (bf16[2880,384]{1,0:T(8,128)(2,1)S(1)}, bf16[2880,384]{1,0:T(8,128)(2,1)S(1)}, u32[]{:S(2)}, u32[]{:S(2)}) collective-permute-start(bf16[2880,384]{1,0:T(8,128)(2,1)S(1)} %get-tuple-element.48.refs_0_.refs_4_.grad), channel_id=1, source_target_pairs={{0,1},{1,0},{2,3},{3,2},{4,5},{5,4},{6,7},{7,6},{8,9},{9,8},{10,11... | collective-permute-start | bytes 6635528 | tf_op jit(solution)/shard_map/ppermute | solution.py:254
  6.8 3.8 %collective-permute-start.1 = (bf16[8,2880]{1,0:T(8,128)(2,1)S(1)}, bf16[8,2880]{1,0:T(8,128)(2,1)S(1)}, u32[]{:S(2)}, u32[]{:S(2)}) collective-permute-start(bf16[8,2880]{1,0:T(8,128)(2,1)S(1)} %pad_maximum_fusion.refs_0_), channel_id=1, source_target_pairs={{0,5},{1,2},{2,1},{3,6},{4,7},{5,0},{6,3},{7,4},{8,13},{9,10},{10,... | collective-permute-start | bytes 138248 | tf_op jit(solution)/shard_map/ppermute | solution.py:251
  8.9 3.6 %collective-permute-start.2 = (bf16[8,2880]{1,0:T(8,128)(2,1)S(1)}, bf16[8,2880]{1,0:T(8,128)(2,1)S(1)}, u32[]{:S(2)}, u32[]{:S(2)}) collective-permute-start(bf16[8,2880]{1,0:T(8,128)(2,1)S(1)} %pad_maximum_fusion.refs_0_), channel_id=1, source_target_pairs={{0,3},{1,4},{2,7},{3,0},{4,1},{5,6},{6,5},{7,2},{8,11},{9,12},{10,... | collective-permute-start | bytes 138248 | tf_op jit(solution)/shard_map/ppermute | solution.py:251
  10.6 3.6 %collective-permute-start.4 = (bf16[8,2880]{1,0:T(8,128)(2,1)S(1)}, bf16[8,2880]{1,0:T(8,128)(2,1)S(1)}, u32[]{:S(2)}, u32[]{:S(2)}) collective-permute-start(bf16[8,2880]{1,0:T(8,128)(2,1)S(1)} %collective-permute-done.1.refs_1_), channel_id=1, source_target_pairs={{0,3},{1,4},{2,7},{3,0},{4,1},{5,6},{6,5},{7,2},{8,11},{9,12},{10,... | collective-permute-start | bytes 138248 | tf_op jit(solution)/shard_map/ppermute | solution.py:251
  14.2 3.6 %copy-start = (bf16[384,2880]{0,1:T(8,128)(2,1)S(1)}, bf16[384,2880]{0,1:T(8,128)(2,1)}, u32[]{:S(2)}) copy-start(bf16[384,2880]{0,1:T(8,128)(2,1)} %param.5) | copy-start | bytes 6635524
  15.7 4.2 %collective-permute-start.6 = (bf16[16,2880]{1,0:T(8,128)(2,1)S(1)}, bf16[16,2880]{1,0:T(8,128)(2,1)S(1)}, u32[]{:S(2)}, u32[]{:S(2)}) collective-permute-start(bf16[16,2880]{1,0:T(8,128)(2,1)S(1)} %get-tuple-element.57), channel_id=1, source_target_pairs={{0,3},{1,4},{2,7},{3,0},{4,1},{5,6},{6,5},{7,2},{8,11},{9,12},{10,... | collective-permute-start | bytes 276488 | tf_op jit(solution)/shard_map/ppermute | solution.py:251
  17.7 3.9 %collective-permute-start.5 = (bf16[32,2880]{1,0:T(8,128)(2,1)S(1)}, bf16[32,2880]{1,0:T(8,128)(2,1)S(1)}, u32[]{:S(2)}, u32[]{:S(2)}) collective-permute-start(bf16[32,2880]{1,0:T(8,128)(2,1)S(1)} %get-tuple-element.55), channel_id=1, source_target_pairs={{0,1},{1,0},{2,3},{3,2},{4,5},{5,4},{6,7},{7,6},{8,9},{9,8},{10,11... | collective-permute-start | bytes 552968 | tf_op jit(solution)/shard_map/ppermute | solution.py:254
  17.7 3.8 %copy-start.1 = (f32[384,64]{0,1:T(8,128)S(1)}, f32[384,64]{0,1:T(8,128)}, u32[]{:S(2)}) copy-start(f32[384,64]{0,1:T(8,128)} %param.6) | copy-start | bytes 294916
  20.0 3.6 %collective-permute-start.7 = (bf16[8,2880]{1,0:T(8,128)(2,1)S(1)}, bf16[8,2880]{1,0:T(8,128)(2,1)S(1)}, u32[]{:S(2)}, u32[]{:S(2)}) collective-permute-start(bf16[8,2880]{1,0:T(8,128)(2,1)S(1)} %slice.24), channel_id=1, source_target_pairs={{0,5},{1,2},{2,1},{3,6},{4,7},{5,0},{6,3},{7,4},{8,13},{9,10},{10,... | collective-permute-start | bytes 138248 | tf_op jit(solution)/shard_map/ppermute | solution.py:251
  23.6 4.8 %collective-permute-start.8 = (bf16[4,2880]{1,0:T(4,128)(2,1)S(1)}, bf16[4,2880]{1,0:T(4,128)(2,1)S(1)}, u32[]{:S(2)}, u32[]{:S(2)}) collective-permute-start(bf16[4,2880]{1,0:T(4,128)(2,1)S(1)} %slice.25), channel_id=1, source_target_pairs={{0,8},{1,9},{2,10},{3,11},{4,12},{5,13},{6,14},{7,15},{8,0},{9,1},... | collective-permute-start | bytes 69128 | tf_op jit(solution)/shard_map/ppermute | solution.py:251

commit v16 on v13

--- a/solution.py
+++ b/solution.py
@@ -155,7 +155,7 @@
 
 
 def early(depth):
-    return depth // 3 // 128 * 128
+    return min(256, depth)
 
 
 def scale_kernel(
@@ -235,7 +235,7 @@
 def update_kernel(basis, scaled, so_far, out, held, sems):
     first = early(out.shape[0])
     copies = []
-    for i, (at, size) in enumerate(cuts(out.shape[0] - first, 768)):
+    for i, (at, size) in enumerate(cuts(out.shape[0] - first, 384)):
         part = pl.ds(first + at, size)
         here = pl.ds(at, size)
         held[here] = dot(basis[:, part], scaled[...], ((0,), (0,))).astype(jnp.bfloat16)
@@ -257,7 +257,7 @@
         input_output_aliases={2: 0},
         scratch_shapes=[
             pltpu.VMEM((later, rows), jnp.bfloat16),
-            pltpu.SemaphoreType.DMA((len(cuts(later, 768)),)),
+            pltpu.SemaphoreType.DMA((len(cuts(later, 384)),)),
         ],
         compiler_params=PARAMS,
         name="update",
@@ -298,9 +298,8 @@
     )
     come = exchange(sent, bits - 1)
     moment, _ = tie(moment, sent)
+    theirs = across(held)
     moment_in, moment_next = new_moment(grad, moment)
-    held, _ = tie(held, moment_in)
-    theirs = across(held)
     come, moment_in, moment_next = tie(come, moment_in, moment_next)
     for step in reversed(range(bits)):
         if step == 0:

time: 29.3 us -> 29 us (0.990)
    pallas_call x1, Pallas kernels: 2.17 us -> 1.87 us  [scaled_rotation(): pl.pallas_call(functools.partial(scale_kernel, orders, own), in_specs=[IN...]
  transfers between devices with their start and end apart: 9 -> 9, of which waited for: 5 -> 4; matrix products, arithmetic and copies ran while one was open for 0% -> 0% of each run, Pallas kernels for 28% -> 28%
where the time goes in v16:
time: 29 us; the launch traced here: 28.8 us
  starting transfers between devices  15.6 us (54%)
  Pallas kernels  10.3 us (36%)
  waiting for transfers between devices  2.02 us (7%)
  between operations  0.75 us (3%)
    ppermute x7, starting transfers between devices, exchange(): return lax.ppermute(value, 'rows', pairs)  14.8 us
    ppermute x7, waiting for transfers between devices, exchange(): return lax.ppermute(value, 'rows', pairs)  2.02 us
    pallas_call x1, Pallas kernels, scaled_rotation(): pl.pallas_call(functools.partial(scale_kernel, orders, own), in_specs=[IN...  1.87 us
    pallas_call x1, Pallas kernels, new_moment(): pl.pallas_call(moment_kernel, in_specs=[INSIDE, INSIDE], out_specs=[INSID...  1.7 us
    pallas_call x1, Pallas kernels, load(): pl.pallas_call(load_kernel, in_specs=[pl.BlockSpec(memory_space=pltpu.HBM...  1.64 us
    pallas_call x1, Pallas kernels, rest_of_update(): pl.pallas_call(update_kernel, in_specs=[INSIDE, INSIDE, ANYWHERE], out_sp...  1.61 us
    pallas_call x1, Pallas kernels, power_products(): pl.pallas_call(power_kernel, in_specs=[INSIDE] * (len(pieces) + len(grads...  1.55 us
    pallas_call x1, Pallas kernels, transposed(): pl.pallas_call(transpose_kernel, in_specs=[INSIDE] * len(values), out_spe...  1.22 us
  transfers between devices with their start and end apart: 9, of which 4 were waited for; matrix products, arithmetic and copies ran while one was open for 0% of the time, Pallas kernels for 28%

profile of v16, /device:TPU:0, one launch (start us, length us, event | category | flops | bytes accessed | tf_op | source)
XLA Modules:
  0.0 28.8 jit_solution(26991174487734676)
XLA Ops:
  0.6 3.5 %collective-permute-start = (bf16[4,2880]{1,0:T(4,128)(2,1)}, bf16[4,2880]{1,0:T(4,128)(2,1)S(1)}, u32[]{:S(2)}, u32[]{:S(2)}) collective-permute-start(bf16[4,2880]{1,0:T(4,128)(2,1)} %refs_1_.1), channel_id=1, source_target_pairs={{0,9},{1,8},{2,11},{3,10},{4,13},{5,12},{6,15},{7,14},{8,1},{9,0},... | collective-permute-start | bytes 69128 | tf_op jit(solution)/shard_map/ppermute | solution.py:275
  4.2 1.6 %load.1 = (bf16[2880,384]{1,0:T(8,128)(2,1)S(1)}, bf16[4,2880]{1,0:T(4,128)(2,1)S(1)}) custom-call(bf16[2880,384]{1,0:T(8,128)(2,1)} %bitcast.8, bf16[4,2880]{1,0:T(4,128)(2,1)} %refs_1_.1), custom_call_target="tpu_custom_call" | custom-call | tf_op jit(solution)/shard_map/load/pallas_call | solution.py:48
  5.8 0.1 collective-permute-done
  6.0 0.6 %collective-permute-start.3 = (bf16[2880,384]{1,0:T(8,128)(2,1)S(1)}, bf16[2880,384]{1,0:T(8,128)(2,1)S(1)}, u32[]{:S(2)}, u32[]{:S(2)}) collective-permute-start(bf16[2880,384]{1,0:T(8,128)(2,1)S(1)} %get-tuple-element.50.refs_0_.refs_4_.grad), channel_id=1, source_target_pairs={{0,1},{1,0},{2,3},{3,2},{4,5},{5,4},{6,7},{7,6},{8,9},{9,8},{10,11... | collective-permute-start | bytes 6635528 | tf_op jit(solution)/shard_map/ppermute | solution.py:278
  6.6 1.7 %collective-permute-start.1 = (bf16[8,2880]{1,0:T(8,128)(2,1)S(1)}, bf16[8,2880]{1,0:T(8,128)(2,1)S(1)}, u32[]{:S(2)}, u32[]{:S(2)}) collective-permute-start(bf16[8,2880]{1,0:T(8,128)(2,1)S(1)} %pad_maximum_fusion.refs_0_), channel_id=1, source_target_pairs={{0,5},{1,2},{2,1},{3,6},{4,7},{5,0},{6,3},{7,4},{8,11},{9,12},{10,... | collective-permute-start | bytes 138248 | tf_op jit(solution)/shard_map/ppermute | solution.py:275
  8.3 1.2 %collective-permute-start.2 = (bf16[8,2880]{1,0:T(8,128)(2,1)S(1)}, bf16[8,2880]{1,0:T(8,128)(2,1)S(1)}, u32[]{:S(2)}, u32[]{:S(2)}) collective-permute-start(bf16[8,2880]{1,0:T(8,128)(2,1)S(1)} %pad_maximum_fusion.refs_0_), channel_id=1, source_target_pairs={{0,3},{1,4},{2,7},{3,0},{4,1},{5,6},{6,5},{7,2},{8,13},{9,10},{10,... | collective-permute-start | bytes 138248 | tf_op jit(solution)/shard_map/ppermute | solution.py:275
  9.5 0.7 %collective-permute-done.1.refs_1_ = bf16[8,2880]{1,0:T(8,128)(2,1)S(1)} collective-permute-done((bf16[8,2880]{1,0:T(8,128)(2,1)S(1)}, bf16[8,2880]{1,0:T(8,128)(2,1)S(1)}, u32[]{:S(2)}, u32[]{:S(2)}) %collective-permute-start.1) | collective-permute-done | bytes 46112 | tf_op jit(solution)/shard_map/ppermute | solution.py:275
  10.2 1.6 %collective-permute-start.4 = (bf16[8,2880]{1,0:T(8,128)(2,1)S(1)}, bf16[8,2880]{1,0:T(8,128)(2,1)S(1)}, u32[]{:S(2)}, u32[]{:S(2)}) collective-permute-start(bf16[8,2880]{1,0:T(8,128)(2,1)S(1)} %collective-permute-done.1.refs_1_), channel_id=1, source_target_pairs={{0,3},{1,4},{2,7},{3,0},{4,1},{5,6},{6,5},{7,2},{8,13},{9,10},{10,... | collective-permute-start | bytes 138248 | tf_op jit(solution)/shard_map/ppermute | solution.py:275
  11.7 0.0 collective-permute-done.2.refs_2_
  11.8 0.0 collective-permute-done.3.refs_1_.refs_5_
  11.8 1.2 %transpose.25 = (bf16[384,2880]{1,0:T(8,128)(2,1)S(1)}, bf16[384,2880]{1,0:T(8,128)(2,1)S(1)}) custom-call(bf16[2880,384]{1,0:T(8,128)(2,1)S(1)} %get-tuple-element.50.refs_0_.refs_4_.grad, bf16[2880,384]{1,0:T(8,128)(2,1)S(1)} %collective-permute-done.3.refs_1_.refs_5_), custom_call_target="tpu_custom_call" | custom-call | tf_op jit(solution)/shard_map/transpose/pallas_call | solution.py:96
  13.0 0.6 %collective-permute-done.4.refs_3_ = bf16[8,2880]{1,0:T(8,128)(2,1)S(1)} collective-permute-done((bf16[8,2880]{1,0:T(8,128)(2,1)S(1)}, bf16[8,2880]{1,0:T(8,128)(2,1)S(1)}, u32[]{:S(2)}, u32[]{:S(2)}) %collective-permute-start.4) | collective-permute-done | bytes 46112 | tf_op jit(solution)/shard_map/ppermute | solution.py:275
  13.7 0.0 copy-start
  13.7 1.6 %power.1 = (bf16[32,2880]{1,0:T(8,128)(2,1)S(1)}, f32[32,384]{1,0:T(8,128)S(1)}, f32[16,2880]{1,0:T(8,128)S(1)}, bf16[16,2880]{1,0:T(8,128)(2,1)S(1)}) custom-call(bf16[8,2880]{1,0:T(8,128)(2,1)S(1)} %pad_maximum_fusion.refs_0_, bf16[8,2880]{1,0:T(8,128)(2,1)S(1)} %collective-permute-done.1.refs_1_, bf16[8,2880]{1,0:T(8,128)(2,1)S(1)} %collective-permute-done.2.refs_2_, ...), custom_call_target="tpu_custom_call" | custom-call | tf_op jit(solution)/shard_map/power/pallas_call | solution.py:125
  15.2 1.7 %collective-permute-start.6 = (bf16[16,2880]{1,0:T(8,128)(2,1)S(1)}, bf16[16,2880]{1,0:T(8,128)(2,1)S(1)}, u32[]{:S(2)}, u32[]{:S(2)}) collective-permute-start(bf16[16,2880]{1,0:T(8,128)(2,1)S(1)} %get-tuple-element.59), channel_id=1, source_target_pairs={{0,3},{1,4},{2,7},{3,0},{4,1},{5,6},{6,5},{7,2},{8,13},{9,10},{10,... | collective-permute-start | bytes 276488 | tf_op jit(solution)/shard_map/ppermute | solution.py:275
  16.9 0.1 collective-permute-start.5
  17.0 0.0 copy-done
  17.0 0.0 copy-start.1
  17.0 1.7 %moment.1 = (bf16[2880,384]{1,0:T(8,128)(2,1)S(1)}, bf16[2880,384]{1,0:T(8,128)(2,1)}) custom-call(bf16[2880,384]{1,0:T(8,128)(2,1)S(1)} %get-tuple-element.50.refs_0_.refs_4_.grad, bf16[2880,384]{1,0:T(8,128)(2,1)S(1)} %bitcast.6), custom_call_target="tpu_custom_call" | custom-call | tf_op jit(solution)/shard_map/moment/pallas_call | solution.py:75
  18.7 0.5 %collective-permute-done.6 = bf16[16,2880]{1,0:T(8,128)(2,1)S(1)} collective-permute-done((bf16[16,2880]{1,0:T(8,128)(2,1)S(1)}, bf16[16,2880]{1,0:T(8,128)(2,1)S(1)}, u32[]{:S(2)}, u32[]{:S(2)}) %collective-permute-start.6) | collective-permute-done | bytes 92192 | tf_op jit(solution)/shard_map/ppermute | solution.py:275
  19.3 1.7 %collective-permute-start.7 = (bf16[8,2880]{1,0:T(8,128)(2,1)S(1)}, bf16[8,2880]{1,0:T(8,128)(2,1)S(1)}, u32[]{:S(2)}, u32[]{:S(2)}) collective-permute-start(bf16[8,2880]{1,0:T(8,128)(2,1)S(1)} %slice.24), channel_id=1, source_target_pairs={{0,5},{1,2},{2,1},{3,6},{4,7},{5,0},{6,3},{7,4},{8,11},{9,12},{10,... | collective-permute-start | bytes 138248 | tf_op jit(solution)/shard_map/ppermute | solution.py:275
  21.0 0.0 collective-permute-done.5
  21.0 0.0 copy-done.1
  21.0 1.9 %scale.1 = (bf16[64,384]{1,0:T(8,128)(2,1)S(1)}, f32[64,384]{1,0:T(8,128)}, bf16[2880,384]{1,0:T(8,128)(2,1)}) custom-call(bf16[64,2880]{1,0:T(8,128)(2,1)S(1)} %constant_dynamic-update-slice_fusion.basis, bf16[2880,384]{1,0:T(8,128)(2,1)S(1)} %get-tuple-element.50.refs_0_.refs_4_.grad, bf16[2880,384]{1,0:T(8,128)(2,1)S(1)} %get-tuple-element.66.moment, ...), custom_call_target="tpu_custom_call" | custom-call | tf_op jit(solution)/shard_map/scale/pallas_call | solution.py:214
  22.9 0.0 collective-permute-done.7
  22.9 3.5 %collective-permute-start.8 = (bf16[4,2880]{1,0:T(4,128)(2,1)S(1)}, bf16[4,2880]{1,0:T(4,128)(2,1)S(1)}, u32[]{:S(2)}, u32[]{:S(2)}) collective-permute-start(bf16[4,2880]{1,0:T(4,128)(2,1)S(1)} %slice.25), channel_id=1, source_target_pairs={{0,9},{1,8},{2,11},{3,10},{4,13},{5,12},{6,15},{7,14},{8,1},{9,0},... | collective-permute-start | bytes 69128 | tf_op jit(solution)/shard_map/ppermute | solution.py:275
  26.4 1.6 %update.1 = bf16[2880,384]{1,0:T(8,128)(2,1)} custom-call(bf16[64,2880]{1,0:T(8,128)(2,1)S(1)} %constant_dynamic-update-slice_fusion.basis, bf16[64,384]{1,0:T(8,128)(2,1)S(1)} %get-tuple-element.73.scaled, bf16[2880,384]{1,0:T(8,128)(2,1)} %get-tuple-element.74.so_far), custom_call_target="tpu_custom_call", output_to_operand_aliasing={{}: (2, {})} | custom-call | tf_op jit(solution)/shard_map/update/pallas_call | solution.py:252
  28.0 0.0 collective-permute-done.8.come
  28.1 0.7 %normalise.1 = f32[4,2880]{1,0:T(4,128)} custom-call(f32[4,2880]{1,0:T(4,128)S(1)} %slice.21.kept, bf16[4,2880]{1,0:T(4,128)(2,1)S(1)} %collective-permute-done.8.come), custom_call_target="tpu_custom_call" | custom-call | tf_op jit(solution)/shard_map/normalise/pallas_call | solution.py:147
  (9 shorter events, 0.1 us)
Async XLA Ops:
  0.6 5.3 %collective-permute-start = (bf16[4,2880]{1,0:T(4,128)(2,1)}, bf16[4,2880]{1,0:T(4,128)(2,1)S(1)}, u32[]{:S(2)}, u32[]{:S(2)}) collective-permute-start(bf16[4,2880]{1,0:T(4,128)(2,1)} %refs_1_.1), channel_id=1, source_target_pairs={{0,9},{1,8},{2,11},{3,10},{4,13},{5,12},{6,15},{7,14},{8,1},{9,0},... | collective-permute-start | bytes 69128 | tf_op jit(solution)/shard_map/ppermute | solution.py:275
  6.0 5.8 %collective-permute-start.3 = (bf16[2880,384]{1,0:T(8,128)(2,1)S(1)}, bf16[2880,384]{1,0:T(8,128)(2,1)S(1)}, u32[]{:S(2)}, u32[]{:S(2)}) collective-permute-start(bf16[2880,384]{1,0:T(8,128)(2,1)S(1)} %get-tuple-element.50.refs_0_.refs_4_.grad), channel_id=1, source_target_pairs={{0,1},{1,0},{2,3},{3,2},{4,5},{5,4},{6,7},{7,6},{8,9},{9,8},{10,11... | collective-permute-start | bytes 6635528 | tf_op jit(solution)/shard_map/ppermute | solution.py:278
  6.6 3.6 %collective-permute-start.1 = (bf16[8,2880]{1,0:T(8,128)(2,1)S(1)}, bf16[8,2880]{1,0:T(8,128)(2,1)S(1)}, u32[]{:S(2)}, u32[]{:S(2)}) collective-permute-start(bf16[8,2880]{1,0:T(8,128)(2,1)S(1)} %pad_maximum_fusion.refs_0_), channel_id=1, source_target_pairs={{0,5},{1,2},{2,1},{3,6},{4,7},{5,0},{6,3},{7,4},{8,11},{9,12},{10,... | collective-permute-start | bytes 138248 | tf_op jit(solution)/shard_map/ppermute | solution.py:275
  8.3 3.5 %collective-permute-start.2 = (bf16[8,2880]{1,0:T(8,128)(2,1)S(1)}, bf16[8,2880]{1,0:T(8,128)(2,1)S(1)}, u32[]{:S(2)}, u32[]{:S(2)}) collective-permute-start(bf16[8,2880]{1,0:T(8,128)(2,1)S(1)} %pad_maximum_fusion.refs_0_), channel_id=1, source_target_pairs={{0,3},{1,4},{2,7},{3,0},{4,1},{5,6},{6,5},{7,2},{8,13},{9,10},{10,... | collective-permute-start | bytes 138248 | tf_op jit(solution)/shard_map/ppermute | solution.py:275
  10.2 3.5 %collective-permute-start.4 = (bf16[8,2880]{1,0:T(8,128)(2,1)S(1)}, bf16[8,2880]{1,0:T(8,128)(2,1)S(1)}, u32[]{:S(2)}, u32[]{:S(2)}) collective-permute-start(bf16[8,2880]{1,0:T(8,128)(2,1)S(1)} %collective-permute-done.1.refs_1_), channel_id=1, source_target_pairs={{0,3},{1,4},{2,7},{3,0},{4,1},{5,6},{6,5},{7,2},{8,13},{9,10},{10,... | collective-permute-start | bytes 138248 | tf_op jit(solution)/shard_map/ppermute | solution.py:275
  13.7 3.3 %copy-start = (bf16[384,2880]{0,1:T(8,128)(2,1)S(1)}, bf16[384,2880]{0,1:T(8,128)(2,1)}, u32[]{:S(2)}) copy-start(bf16[384,2880]{0,1:T(8,128)(2,1)} %param.5) | copy-start | bytes 6635524
  15.2 4.0 %collective-permute-start.6 = (bf16[16,2880]{1,0:T(8,128)(2,1)S(1)}, bf16[16,2880]{1,0:T(8,128)(2,1)S(1)}, u32[]{:S(2)}, u32[]{:S(2)}) collective-permute-start(bf16[16,2880]{1,0:T(8,128)(2,1)S(1)} %get-tuple-element.59), channel_id=1, source_target_pairs={{0,3},{1,4},{2,7},{3,0},{4,1},{5,6},{6,5},{7,2},{8,13},{9,10},{10,... | collective-permute-start | bytes 276488 | tf_op jit(solution)/shard_map/ppermute | solution.py:275
  16.9 4.1 %collective-permute-start.5 = (bf16[32,2880]{1,0:T(8,128)(2,1)S(1)}, bf16[32,2880]{1,0:T(8,128)(2,1)S(1)}, u32[]{:S(2)}, u32[]{:S(2)}) collective-permute-start(bf16[32,2880]{1,0:T(8,128)(2,1)S(1)} %get-tuple-element.57), channel_id=1, source_target_pairs={{0,1},{1,0},{2,3},{3,2},{4,5},{5,4},{6,7},{7,6},{8,9},{9,8},{10,11... | collective-permute-start | bytes 552968 | tf_op jit(solution)/shard_map/ppermute | solution.py:278
  17.0 4.0 %copy-start.1 = (f32[384,64]{0,1:T(8,128)S(1)}, f32[384,64]{0,1:T(8,128)}, u32[]{:S(2)}) copy-start(f32[384,64]{0,1:T(8,128)} %param.6) | copy-start | bytes 294916
  19.3 3.6 %collective-permute-start.7 = (bf16[8,2880]{1,0:T(8,128)(2,1)S(1)}, bf16[8,2880]{1,0:T(8,128)(2,1)S(1)}, u32[]{:S(2)}, u32[]{:S(2)}) collective-permute-start(bf16[8,2880]{1,0:T(8,128)(2,1)S(1)} %slice.24), channel_id=1, source_target_pairs={{0,5},{1,2},{2,1},{3,6},{4,7},{5,0},{6,3},{7,4},{8,11},{9,12},{10,... | collective-permute-start | bytes 138248 | tf_op jit(solution)/shard_map/ppermute | solution.py:275
  22.9 5.1 %collective-permute-start.8 = (bf16[4,2880]{1,0:T(4,128)(2,1)S(1)}, bf16[4,2880]{1,0:T(4,128)(2,1)S(1)}, u32[]{:S(2)}, u32[]{:S(2)}) collective-permute-start(bf16[4,2880]{1,0:T(4,128)(2,1)S(1)} %slice.25), channel_id=1, source_target_pairs={{0,9},{1,8},{2,11},{3,10},{4,13},{5,12},{6,15},{7,14},{8,1},{9,0},... | collective-permute-start | bytes 69128 | tf_op jit(solution)/shard_map/ppermute | solution.py:275

commit v17 on v16

--- a/solution.py
+++ b/solution.py
@@ -165,7 +165,7 @@
     me = lax.axis_index("rows")
     core, chip = me & 1, me >> 1
     bits = len(orders[0])
-    parity = functools.reduce(lambda a, b: a ^ b, [(me >> b) & 1 for b in range(bits + 1)])
+    parity = functools.reduce(lambda a, b: a ^ b, [(me >> b) & 1 for b in range(bits)])
     count = rot_half.shape[0]
     rot[:count] = rot_half[...]
     rot[count:] = dot(basis[count:], grad[...], ((1,), (0,)))
@@ -181,7 +181,7 @@
             for offset in range(1 << bits):
                 mine = pl.ds(place(offset, orders[half]), own)
                 theirs = pl.ds(count + place(offset, orders[1 - half]), own)
-                first = core == odd(offset)
+                first = core == odd(offset & ((1 << (bits - 1)) - 1))
                 tile = pl.ds(pl.multiple_of((chip ^ offset) * 2 * own, 2 * own), 2 * own)
 
                 def joined(ref):
@@ -270,9 +270,12 @@
     far, near = (bits - 1,), tuple(reversed(range(bits - 1)))
     orders = (far + near, far + near[-1:] + near[:-1])
 
+    def partner(i, step):
+        bit = orders[odd(i & (n // 2 - 1))][step]
+        return i ^ (2 << bit) ^ (bit != far[0])
+
     def exchange(value, step):
-        pairs = [(i, i ^ (2 << orders[odd(i)][step]) ^ 1) for i in range(n)]
-        return lax.ppermute(value, "rows", pairs)
+        return lax.ppermute(value, "rows", [(i, partner(i, step)) for i in range(n)])
 
     def across(value):
         return lax.ppermute(value, "rows", [(i, i ^ 1) for i in range(n)])

time: 29 us -> 29.3 us (1.010)
  waiting for transfers between devices: 2.02 us -> 2.33 us
    ppermute x7, starting transfers between devices: 14.8 us -> 15.6 us  [exchange(): lax.ppermute(value, 'rows', [(i, partner(i, step)) for i in range(n)])]
    ppermute x2, starting transfers between devices: 0.71 us -> 0.01 us  [across(): return lax.ppermute(value, 'rows', [(i, i ^ 1) for i in range(n)])]
    ppermute x7, waiting for transfers between devices: 2.02 us -> 2.32 us  [exchange(): lax.ppermute(value, 'rows', [(i, partner(i, step)) for i in range(n)])]
  transfers between devices with their start and end apart: 9 -> 9, of which waited for: 4 -> 6; matrix products, arithmetic and copies ran while one was open for 0% -> 0% of each run, Pallas kernels for 28% -> 28%
where the time goes in v17:
time: 29.3 us; the launch traced here: 29.2 us
  starting transfers between devices  15.6 us (53%)
  Pallas kernels  10.3 us (35%)
  waiting for transfers between devices  2.33 us (8%)
  between operations  0.74 us (3%)
    ppermute x7, starting transfers between devices, exchange(): lax.ppermute(value, 'rows', [(i, partner(i, step)) for i in range(n)])  15.6 us
    ppermute x7, waiting for transfers between devices, exchange(): lax.ppermute(value, 'rows', [(i, partner(i, step)) for i in range(n)])  2.32 us
    pallas_call x1, Pallas kernels, scaled_rotation(): pl.pallas_call(functools.partial(scale_kernel, orders, own), in_specs=[IN...  1.87 us
    pallas_call x1, Pallas kernels, new_moment(): pl.pallas_call(moment_kernel, in_specs=[INSIDE, INSIDE], out_specs=[INSID...  1.7 us
    pallas_call x1, Pallas kernels, load(): pl.pallas_call(load_kernel, in_specs=[pl.BlockSpec(memory_space=pltpu.HBM...  1.64 us
    pallas_call x1, Pallas kernels, rest_of_update(): pl.pallas_call(update_kernel, in_specs=[INSIDE, INSIDE, ANYWHERE], out_sp...  1.61 us
    pallas_call x1, Pallas kernels, power_products(): pl.pallas_call(power_kernel, in_specs=[INSIDE] * (len(pieces) + len(grads...  1.55 us
    pallas_call x1, Pallas kernels, transposed(): pl.pallas_call(transpose_kernel, in_specs=[INSIDE] * len(values), out_spe...  1.22 us
  transfers between devices with their start and end apart: 9, of which 6 were waited for; matrix products, arithmetic and copies ran while one was open for 0% of the time, Pallas kernels for 28%

profile of v17, /device:TPU:0, one launch (start us, length us, event | category | flops | bytes accessed | tf_op | source)
XLA Modules:
  0.0 29.2 jit_solution(14926787884005159508)
XLA Ops:
  0.6 4.1 %collective-permute-start = (bf16[4,2880]{1,0:T(4,128)(2,1)}, bf16[4,2880]{1,0:T(4,128)(2,1)S(1)}, u32[]{:S(2)}, u32[]{:S(2)}) collective-permute-start(bf16[4,2880]{1,0:T(4,128)(2,1)} %refs_1_.1), channel_id=1, source_target_pairs={{0,8},{1,9},{2,10},{3,11},{4,12},{5,13},{6,14},{7,15},{8,0},{9,1},... | collective-permute-start | bytes 69128 | tf_op jit(solution)/shard_map/ppermute | solution.py:278
  4.7 1.6 %load.1 = (bf16[2880,384]{1,0:T(8,128)(2,1)S(1)}, bf16[4,2880]{1,0:T(4,128)(2,1)S(1)}) custom-call(bf16[2880,384]{1,0:T(8,128)(2,1)} %bitcast.8, bf16[4,2880]{1,0:T(4,128)(2,1)} %refs_1_.1), custom_call_target="tpu_custom_call" | custom-call | tf_op jit(solution)/shard_map/load/pallas_call | solution.py:48
  6.4 0.4 %collective-permute-done = bf16[4,2880]{1,0:T(4,128)(2,1)S(1)} collective-permute-done((bf16[4,2880]{1,0:T(4,128)(2,1)}, bf16[4,2880]{1,0:T(4,128)(2,1)S(1)}, u32[]{:S(2)}, u32[]{:S(2)}) %collective-permute-start) | collective-permute-done | bytes 23072 | tf_op jit(solution)/shard_map/ppermute | solution.py:278
  6.7 0.0 collective-permute-start.3
  6.8 2.1 %collective-permute-start.1 = (bf16[8,2880]{1,0:T(8,128)(2,1)S(1)}, bf16[8,2880]{1,0:T(8,128)(2,1)S(1)}, u32[]{:S(2)}, u32[]{:S(2)}) collective-permute-start(bf16[8,2880]{1,0:T(8,128)(2,1)S(1)} %pad_maximum_fusion.refs_0_), channel_id=1, source_target_pairs={{0,5},{1,2},{2,1},{3,6},{4,7},{5,0},{6,3},{7,4},{8,13},{9,10},{10,... | collective-permute-start | bytes 138248 | tf_op jit(solution)/shard_map/ppermute | solution.py:278
  8.9 1.1 %collective-permute-start.2 = (bf16[8,2880]{1,0:T(8,128)(2,1)S(1)}, bf16[8,2880]{1,0:T(8,128)(2,1)S(1)}, u32[]{:S(2)}, u32[]{:S(2)}) collective-permute-start(bf16[8,2880]{1,0:T(8,128)(2,1)S(1)} %pad_maximum_fusion.refs_0_), channel_id=1, source_target_pairs={{0,3},{1,4},{2,7},{3,0},{4,1},{5,6},{6,5},{7,2},{8,11},{9,12},{10,... | collective-permute-start | bytes 138248 | tf_op jit(solution)/shard_map/ppermute | solution.py:278
  10.0 0.7 %collective-permute-done.1.refs_1_ = bf16[8,2880]{1,0:T(8,128)(2,1)S(1)} collective-permute-done((bf16[8,2880]{1,0:T(8,128)(2,1)S(1)}, bf16[8,2880]{1,0:T(8,128)(2,1)S(1)}, u32[]{:S(2)}, u32[]{:S(2)}) %collective-permute-start.1) | collective-permute-done | bytes 46112 | tf_op jit(solution)/shard_map/ppermute | solution.py:278
  10.6 1.8 %collective-permute-start.4 = (bf16[8,2880]{1,0:T(8,128)(2,1)S(1)}, bf16[8,2880]{1,0:T(8,128)(2,1)S(1)}, u32[]{:S(2)}, u32[]{:S(2)}) collective-permute-start(bf16[8,2880]{1,0:T(8,128)(2,1)S(1)} %collective-permute-done.1.refs_1_), channel_id=1, source_target_pairs={{0,3},{1,4},{2,7},{3,0},{4,1},{5,6},{6,5},{7,2},{8,11},{9,12},{10,... | collective-permute-start | bytes 138248 | tf_op jit(solution)/shard_map/ppermute | solution.py:278
  12.4 0.0 collective-permute-done.2.refs_2_
  12.4 0.0 collective-permute-done.3.refs_1_.refs_5_
  12.4 1.2 %transpose.25 = (bf16[384,2880]{1,0:T(8,128)(2,1)S(1)}, bf16[384,2880]{1,0:T(8,128)(2,1)S(1)}) custom-call(bf16[2880,384]{1,0:T(8,128)(2,1)S(1)} %get-tuple-element.50.refs_0_.refs_4_.grad, bf16[2880,384]{1,0:T(8,128)(2,1)S(1)} %collective-permute-done.3.refs_1_.refs_5_), custom_call_target="tpu_custom_call" | custom-call | tf_op jit(solution)/shard_map/transpose/pallas_call | solution.py:96
  13.6 0.5 %collective-permute-done.4.refs_3_ = bf16[8,2880]{1,0:T(8,128)(2,1)S(1)} collective-permute-done((bf16[8,2880]{1,0:T(8,128)(2,1)S(1)}, bf16[8,2880]{1,0:T(8,128)(2,1)S(1)}, u32[]{:S(2)}, u32[]{:S(2)}) %collective-permute-start.4) | collective-permute-done | bytes 46112 | tf_op jit(solution)/shard_map/ppermute | solution.py:278
  14.2 0.0 copy-start
  14.2 1.6 %power.1 = (bf16[32,2880]{1,0:T(8,128)(2,1)S(1)}, f32[32,384]{1,0:T(8,128)S(1)}, f32[16,2880]{1,0:T(8,128)S(1)}, bf16[16,2880]{1,0:T(8,128)(2,1)S(1)}) custom-call(bf16[8,2880]{1,0:T(8,128)(2,1)S(1)} %pad_maximum_fusion.refs_0_, bf16[8,2880]{1,0:T(8,128)(2,1)S(1)} %collective-permute-done.1.refs_1_, bf16[8,2880]{1,0:T(8,128)(2,1)S(1)} %collective-permute-done.2.refs_2_, ...), custom_call_target="tpu_custom_call" | custom-call | tf_op jit(solution)/shard_map/power/pallas_call | solution.py:125
  15.7 2.0 %collective-permute-start.6 = (bf16[16,2880]{1,0:T(8,128)(2,1)S(1)}, bf16[16,2880]{1,0:T(8,128)(2,1)S(1)}, u32[]{:S(2)}, u32[]{:S(2)}) collective-permute-start(bf16[16,2880]{1,0:T(8,128)(2,1)S(1)} %get-tuple-element.59), channel_id=1, source_target_pairs={{0,3},{1,4},{2,7},{3,0},{4,1},{5,6},{6,5},{7,2},{8,11},{9,12},{10,... | collective-permute-start | bytes 276488 | tf_op jit(solution)/shard_map/ppermute | solution.py:278
  17.7 0.0 collective-permute-start.5
  17.7 0.0 copy-done
  17.7 0.0 copy-start.1
  17.7 1.7 %moment.1 = (bf16[2880,384]{1,0:T(8,128)(2,1)S(1)}, bf16[2880,384]{1,0:T(8,128)(2,1)}) custom-call(bf16[2880,384]{1,0:T(8,128)(2,1)S(1)} %get-tuple-element.50.refs_0_.refs_4_.grad, bf16[2880,384]{1,0:T(8,128)(2,1)S(1)} %bitcast.6), custom_call_target="tpu_custom_call" | custom-call | tf_op jit(solution)/shard_map/moment/pallas_call | solution.py:75
  19.5 0.5 %collective-permute-done.6 = bf16[16,2880]{1,0:T(8,128)(2,1)S(1)} collective-permute-done((bf16[16,2880]{1,0:T(8,128)(2,1)S(1)}, bf16[16,2880]{1,0:T(8,128)(2,1)S(1)}, u32[]{:S(2)}, u32[]{:S(2)}) %collective-permute-start.6) | collective-permute-done | bytes 92192 | tf_op jit(solution)/shard_map/ppermute | solution.py:278
  20.0 1.5 %collective-permute-start.7 = (bf16[8,2880]{1,0:T(8,128)(2,1)S(1)}, bf16[8,2880]{1,0:T(8,128)(2,1)S(1)}, u32[]{:S(2)}, u32[]{:S(2)}) collective-permute-start(bf16[8,2880]{1,0:T(8,128)(2,1)S(1)} %slice.24), channel_id=1, source_target_pairs={{0,5},{1,2},{2,1},{3,6},{4,7},{5,0},{6,3},{7,4},{8,13},{9,10},{10,... | collective-permute-start | bytes 138248 | tf_op jit(solution)/shard_map/ppermute | solution.py:278
  21.6 0.0 collective-permute-done.5
  21.6 0.0 copy-done.1
  21.6 1.9 %scale.1 = (bf16[64,384]{1,0:T(8,128)(2,1)S(1)}, f32[64,384]{1,0:T(8,128)}, bf16[2880,384]{1,0:T(8,128)(2,1)}) custom-call(bf16[64,2880]{1,0:T(8,128)(2,1)S(1)} %constant_dynamic-update-slice_fusion.basis, bf16[2880,384]{1,0:T(8,128)(2,1)S(1)} %get-tuple-element.50.refs_0_.refs_4_.grad, bf16[2880,384]{1,0:T(8,128)(2,1)S(1)} %get-tuple-element.66.moment, ...), custom_call_target="tpu_custom_call" | custom-call | tf_op jit(solution)/shard_map/scale/pallas_call | solution.py:214
  23.5 0.1 collective-permute-done.7
  23.6 3.0 %collective-permute-start.8 = (bf16[4,2880]{1,0:T(4,128)(2,1)S(1)}, bf16[4,2880]{1,0:T(4,128)(2,1)S(1)}, u32[]{:S(2)}, u32[]{:S(2)}) collective-permute-start(bf16[4,2880]{1,0:T(4,128)(2,1)S(1)} %slice.25), channel_id=1, source_target_pairs={{0,8},{1,9},{2,10},{3,11},{4,12},{5,13},{6,14},{7,15},{8,0},{9,1},... | collective-permute-start | bytes 69128 | tf_op jit(solution)/shard_map/ppermute | solution.py:278
  26.6 1.6 %update.1 = bf16[2880,384]{1,0:T(8,128)(2,1)} custom-call(bf16[64,2880]{1,0:T(8,128)(2,1)S(1)} %constant_dynamic-update-slice_fusion.basis, bf16[64,384]{1,0:T(8,128)(2,1)S(1)} %get-tuple-element.73.scaled, bf16[2880,384]{1,0:T(8,128)(2,1)} %get-tuple-element.74.so_far), custom_call_target="tpu_custom_call", output_to_operand_aliasing={{}: (2, {})} | custom-call | tf_op jit(solution)/shard_map/update/pallas_call | solution.py:252
  28.3 0.2 collective-permute-done.8.come
  28.4 0.7 %normalise.1 = f32[4,2880]{1,0:T(4,128)} custom-call(f32[4,2880]{1,0:T(4,128)S(1)} %slice.21.kept, bf16[4,2880]{1,0:T(4,128)(2,1)S(1)} %collective-permute-done.8.come), custom_call_target="tpu_custom_call" | custom-call | tf_op jit(solution)/shard_map/normalise/pallas_call | solution.py:147
  (9 shorter events, 0.1 us)
Async XLA Ops:
  0.6 6.1 %collective-permute-start = (bf16[4,2880]{1,0:T(4,128)(2,1)}, bf16[4,2880]{1,0:T(4,128)(2,1)S(1)}, u32[]{:S(2)}, u32[]{:S(2)}) collective-permute-start(bf16[4,2880]{1,0:T(4,128)(2,1)} %refs_1_.1), channel_id=1, source_target_pairs={{0,8},{1,9},{2,10},{3,11},{4,12},{5,13},{6,14},{7,15},{8,0},{9,1},... | collective-permute-start | bytes 69128 | tf_op jit(solution)/shard_map/ppermute | solution.py:278
  6.7 5.7 %collective-permute-start.3 = (bf16[2880,384]{1,0:T(8,128)(2,1)S(1)}, bf16[2880,384]{1,0:T(8,128)(2,1)S(1)}, u32[]{:S(2)}, u32[]{:S(2)}) collective-permute-start(bf16[2880,384]{1,0:T(8,128)(2,1)S(1)} %get-tuple-element.50.refs_0_.refs_4_.grad), channel_id=1, source_target_pairs={{0,1},{1,0},{2,3},{3,2},{4,5},{5,4},{6,7},{7,6},{8,9},{9,8},{10,11... | collective-permute-start | bytes 6635528 | tf_op jit(solution)/shard_map/ppermute | solution.py:281
  6.8 3.8 %collective-permute-start.1 = (bf16[8,2880]{1,0:T(8,128)(2,1)S(1)}, bf16[8,2880]{1,0:T(8,128)(2,1)S(1)}, u32[]{:S(2)}, u32[]{:S(2)}) collective-permute-start(bf16[8,2880]{1,0:T(8,128)(2,1)S(1)} %pad_maximum_fusion.refs_0_), channel_id=1, source_target_pairs={{0,5},{1,2},{2,1},{3,6},{4,7},{5,0},{6,3},{7,4},{8,13},{9,10},{10,... | collective-permute-start | bytes 138248 | tf_op jit(solution)/shard_map/ppermute | solution.py:278
  8.9 3.6 %collective-permute-start.2 = (bf16[8,2880]{1,0:T(8,128)(2,1)S(1)}, bf16[8,2880]{1,0:T(8,128)(2,1)S(1)}, u32[]{:S(2)}, u32[]{:S(2)}) collective-permute-start(bf16[8,2880]{1,0:T(8,128)(2,1)S(1)} %pad_maximum_fusion.refs_0_), channel_id=1, source_target_pairs={{0,3},{1,4},{2,7},{3,0},{4,1},{5,6},{6,5},{7,2},{8,11},{9,12},{10,... | collective-permute-start | bytes 138248 | tf_op jit(solution)/shard_map/ppermute | solution.py:278
  10.6 3.6 %collective-permute-start.4 = (bf16[8,2880]{1,0:T(8,128)(2,1)S(1)}, bf16[8,2880]{1,0:T(8,128)(2,1)S(1)}, u32[]{:S(2)}, u32[]{:S(2)}) collective-permute-start(bf16[8,2880]{1,0:T(8,128)(2,1)S(1)} %collective-permute-done.1.refs_1_), channel_id=1, source_target_pairs={{0,3},{1,4},{2,7},{3,0},{4,1},{5,6},{6,5},{7,2},{8,11},{9,12},{10,... | collective-permute-start | bytes 138248 | tf_op jit(solution)/shard_map/ppermute | solution.py:278
  14.2 3.6 %copy-start = (bf16[384,2880]{0,1:T(8,128)(2,1)S(1)}, bf16[384,2880]{0,1:T(8,128)(2,1)}, u32[]{:S(2)}) copy-start(bf16[384,2880]{0,1:T(8,128)(2,1)} %param.5) | copy-start | bytes 6635524
  15.7 4.2 %collective-permute-start.6 = (bf16[16,2880]{1,0:T(8,128)(2,1)S(1)}, bf16[16,2880]{1,0:T(8,128)(2,1)S(1)}, u32[]{:S(2)}, u32[]{:S(2)}) collective-permute-start(bf16[16,2880]{1,0:T(8,128)(2,1)S(1)} %get-tuple-element.59), channel_id=1, source_target_pairs={{0,3},{1,4},{2,7},{3,0},{4,1},{5,6},{6,5},{7,2},{8,11},{9,12},{10,... | collective-permute-start | bytes 276488 | tf_op jit(solution)/shard_map/ppermute | solution.py:278
  17.7 3.9 %collective-permute-start.5 = (bf16[32,2880]{1,0:T(8,128)(2,1)S(1)}, bf16[32,2880]{1,0:T(8,128)(2,1)S(1)}, u32[]{:S(2)}, u32[]{:S(2)}) collective-permute-start(bf16[32,2880]{1,0:T(8,128)(2,1)S(1)} %get-tuple-element.57), channel_id=1, source_target_pairs={{0,1},{1,0},{2,3},{3,2},{4,5},{5,4},{6,7},{7,6},{8,9},{9,8},{10,11... | collective-permute-start | bytes 552968 | tf_op jit(solution)/shard_map/ppermute | solution.py:281
  17.7 3.8 %copy-start.1 = (f32[384,64]{0,1:T(8,128)S(1)}, f32[384,64]{0,1:T(8,128)}, u32[]{:S(2)}) copy-start(f32[384,64]{0,1:T(8,128)} %param.6) | copy-start | bytes 294916
  20.0 3.6 %collective-permute-start.7 = (bf16[8,2880]{1,0:T(8,128)(2,1)S(1)}, bf16[8,2880]{1,0:T(8,128)(2,1)S(1)}, u32[]{:S(2)}, u32[]{:S(2)}) collective-permute-start(bf16[8,2880]{1,0:T(8,128)(2,1)S(1)} %slice.24), channel_id=1, source_target_pairs={{0,5},{1,2},{2,1},{3,6},{4,7},{5,0},{6,3},{7,4},{8,13},{9,10},{10,... | collective-permute-start | bytes 138248 | tf_op jit(solution)/shard_map/ppermute | solution.py:278
  23.6 4.8 %collective-permute-start.8 = (bf16[4,2880]{1,0:T(4,128)(2,1)S(1)}, bf16[4,2880]{1,0:T(4,128)(2,1)S(1)}, u32[]{:S(2)}, u32[]{:S(2)}) collective-permute-start(bf16[4,2880]{1,0:T(4,128)(2,1)S(1)} %slice.25), channel_id=1, source_target_pairs={{0,8},{1,9},{2,10},{3,11},{4,12},{5,13},{6,14},{7,15},{8,0},{9,1},... | collective-permute-start | bytes 69128 | tf_op jit(solution)/shard_map/ppermute | solution.py:278

commit v18 on v14

--- a/solution.py
+++ b/solution.py
@@ -241,7 +241,7 @@
     bits = n.bit_length() - 2
     own = basis.shape[0]
     far, near = (bits - 1,), tuple(reversed(range(bits - 1)))
-    orders = (far + near, far + near[-1:] + near[:-1])
+    orders = (far + near[-1:] + near[:-1], far + near)
 
     def exchange(value, step):
         pairs = [(i, i ^ (2 << orders[odd(i)][step]) ^ 1) for i in range(n)]

time: 28.9 us -> 28.7 us (level)
  starting transfers between devices: 15.5 us -> 15.1 us
  transfers between devices with their start and end apart: 9 -> 9, of which waited for: 5 -> 5; matrix products, arithmetic and copies ran while one was open for 0% -> 0% of each run, Pallas kernels for 27% -> 28%
where the time goes in v18:
time: 28.7 us; the launch traced here: 28.5 us
  starting transfers between devices  15.1 us (53%)
  Pallas kernels  10.2 us (36%)
  waiting for transfers between devices  2.37 us (8%)
  between operations  0.74 us (3%)
    ppermute x7, starting transfers between devices, exchange(): return lax.ppermute(value, 'rows', pairs)  14.5 us
    ppermute x7, waiting for transfers between devices, exchange(): return lax.ppermute(value, 'rows', pairs)  2.37 us
    pallas_call x1, Pallas kernels, new_update(): pl.pallas_call(update_kernel, in_specs=[INSIDE] * 2, out_specs=ANYWHERE,...  1.72 us
    pallas_call x1, Pallas kernels, new_moment(): pl.pallas_call(moment_kernel, in_specs=[INSIDE, INSIDE], out_specs=[INSID...  1.7 us
    pallas_call x1, Pallas kernels, load(): pl.pallas_call(load_kernel, in_specs=[pl.BlockSpec(memory_space=pltpu.HBM...  1.64 us
    pallas_call x1, Pallas kernels, scaled_rotation(): pl.pallas_call(functools.partial(scale_kernel, orders, own), in_specs=[IN...  1.57 us
    pallas_call x1, Pallas kernels, power_products(): pl.pallas_call(power_kernel, in_specs=[INSIDE] * (len(pieces) + len(grads...  1.55 us
    pallas_call x1, Pallas kernels, transposed(): pl.pallas_call(transpose_kernel, in_specs=[INSIDE] * len(values), out_spe...  1.22 us
  transfers between devices with their start and end apart: 9, of which 5 were waited for; matrix products, arithmetic and copies ran while one was open for 0% of the time, Pallas kernels for 28%

profile of v18, /device:TPU:0, one launch (start us, length us, event | category | flops | bytes accessed | tf_op | source)
XLA Modules:
  0.0 28.5 jit_solution(10769847670447542811)
XLA Ops:
  0.6 3.5 %collective-permute-start = (bf16[4,2880]{1,0:T(4,128)(2,1)}, bf16[4,2880]{1,0:T(4,128)(2,1)S(1)}, u32[]{:S(2)}, u32[]{:S(2)}) collective-permute-start(bf16[4,2880]{1,0:T(4,128)(2,1)} %refs_1_.1), channel_id=1, source_target_pairs={{0,9},{1,8},{2,11},{3,10},{4,13},{5,12},{6,15},{7,14},{8,1},{9,0},... | collective-permute-start | bytes 69128 | tf_op jit(solution)/shard_map/ppermute | solution.py:248
  4.2 1.6 %load.1 = (bf16[2880,384]{1,0:T(8,128)(2,1)S(1)}, bf16[4,2880]{1,0:T(4,128)(2,1)S(1)}) custom-call(bf16[2880,384]{1,0:T(8,128)(2,1)} %bitcast.9, bf16[4,2880]{1,0:T(4,128)(2,1)} %refs_1_.1), custom_call_target="tpu_custom_call" | custom-call | tf_op jit(solution)/shard_map/load/pallas_call | solution.py:48
  5.8 0.1 collective-permute-done
  6.0 0.6 %collective-permute-start.3 = (bf16[2880,384]{1,0:T(8,128)(2,1)S(1)}, bf16[2880,384]{1,0:T(8,128)(2,1)S(1)}, u32[]{:S(2)}, u32[]{:S(2)}) collective-permute-start(bf16[2880,384]{1,0:T(8,128)(2,1)S(1)} %get-tuple-element.48.refs_0_.refs_4_.grad), channel_id=1, source_target_pairs={{0,1},{1,0},{2,3},{3,2},{4,5},{5,4},{6,7},{7,6},{8,9},{9,8},{10,11... | collective-permute-start | bytes 6635528 | tf_op jit(solution)/shard_map/ppermute | solution.py:251
  6.6 1.6 %collective-permute-start.1 = (bf16[8,2880]{1,0:T(8,128)(2,1)S(1)}, bf16[8,2880]{1,0:T(8,128)(2,1)S(1)}, u32[]{:S(2)}, u32[]{:S(2)}) collective-permute-start(bf16[8,2880]{1,0:T(8,128)(2,1)S(1)} %pad_maximum_fusion.refs_0_), channel_id=1, source_target_pairs={{0,3},{1,4},{2,7},{3,0},{4,1},{5,6},{6,5},{7,2},{8,13},{9,10},{10,... | collective-permute-start | bytes 138248 | tf_op jit(solution)/shard_map/ppermute | solution.py:248
  8.2 1.3 %collective-permute-start.2 = (bf16[8,2880]{1,0:T(8,128)(2,1)S(1)}, bf16[8,2880]{1,0:T(8,128)(2,1)S(1)}, u32[]{:S(2)}, u32[]{:S(2)}) collective-permute-start(bf16[8,2880]{1,0:T(8,128)(2,1)S(1)} %pad_maximum_fusion.refs_0_), channel_id=1, source_target_pairs={{0,5},{1,2},{2,1},{3,6},{4,7},{5,0},{6,3},{7,4},{8,11},{9,12},{10,... | collective-permute-start | bytes 138248 | tf_op jit(solution)/shard_map/ppermute | solution.py:248
  9.5 0.7 %collective-permute-done.1.refs_1_ = bf16[8,2880]{1,0:T(8,128)(2,1)S(1)} collective-permute-done((bf16[8,2880]{1,0:T(8,128)(2,1)S(1)}, bf16[8,2880]{1,0:T(8,128)(2,1)S(1)}, u32[]{:S(2)}, u32[]{:S(2)}) %collective-permute-start.1) | collective-permute-done | bytes 46112 | tf_op jit(solution)/shard_map/ppermute | solution.py:248
  10.2 1.6 %collective-permute-start.4 = (bf16[8,2880]{1,0:T(8,128)(2,1)S(1)}, bf16[8,2880]{1,0:T(8,128)(2,1)S(1)}, u32[]{:S(2)}, u32[]{:S(2)}) collective-permute-start(bf16[8,2880]{1,0:T(8,128)(2,1)S(1)} %collective-permute-done.1.refs_1_), channel_id=1, source_target_pairs={{0,5},{1,2},{2,1},{3,6},{4,7},{5,0},{6,3},{7,4},{8,11},{9,12},{10,... | collective-permute-start | bytes 138248 | tf_op jit(solution)/shard_map/ppermute | solution.py:248
  11.8 0.0 collective-permute-done.2.refs_2_
  11.8 0.0 collective-permute-done.3.refs_1_.refs_5_
  11.8 1.2 %transpose.25 = (bf16[384,2880]{1,0:T(8,128)(2,1)S(1)}, bf16[384,2880]{1,0:T(8,128)(2,1)S(1)}) custom-call(bf16[2880,384]{1,0:T(8,128)(2,1)S(1)} %get-tuple-element.48.refs_0_.refs_4_.grad, bf16[2880,384]{1,0:T(8,128)(2,1)S(1)} %collective-permute-done.3.refs_1_.refs_5_), custom_call_target="tpu_custom_call" | custom-call | tf_op jit(solution)/shard_map/transpose/pallas_call | solution.py:96
  13.0 0.6 %collective-permute-done.4.refs_3_ = bf16[8,2880]{1,0:T(8,128)(2,1)S(1)} collective-permute-done((bf16[8,2880]{1,0:T(8,128)(2,1)S(1)}, bf16[8,2880]{1,0:T(8,128)(2,1)S(1)}, u32[]{:S(2)}, u32[]{:S(2)}) %collective-permute-start.4) | collective-permute-done | bytes 46112 | tf_op jit(solution)/shard_map/ppermute | solution.py:248
  13.7 0.0 copy-start
  13.7 1.6 %power.1 = (bf16[32,2880]{1,0:T(8,128)(2,1)S(1)}, f32[32,384]{1,0:T(8,128)S(1)}, f32[16,2880]{1,0:T(8,128)S(1)}, bf16[16,2880]{1,0:T(8,128)(2,1)S(1)}) custom-call(bf16[8,2880]{1,0:T(8,128)(2,1)S(1)} %pad_maximum_fusion.refs_0_, bf16[8,2880]{1,0:T(8,128)(2,1)S(1)} %collective-permute-done.1.refs_1_, bf16[8,2880]{1,0:T(8,128)(2,1)S(1)} %collective-permute-done.2.refs_2_, ...), custom_call_target="tpu_custom_call" | custom-call | tf_op jit(solution)/shard_map/power/pallas_call | solution.py:125
  15.2 1.8 %collective-permute-start.6 = (bf16[16,2880]{1,0:T(8,128)(2,1)S(1)}, bf16[16,2880]{1,0:T(8,128)(2,1)S(1)}, u32[]{:S(2)}, u32[]{:S(2)}) collective-permute-start(bf16[16,2880]{1,0:T(8,128)(2,1)S(1)} %get-tuple-element.57), channel_id=1, source_target_pairs={{0,5},{1,2},{2,1},{3,6},{4,7},{5,0},{6,3},{7,4},{8,11},{9,12},{10,... | collective-permute-start | bytes 276488 | tf_op jit(solution)/shard_map/ppermute | solution.py:248
  17.1 0.0 collective-permute-start.5
  17.1 0.0 copy-done
  17.1 0.0 copy-start.1
  17.1 1.7 %moment.1 = (bf16[2880,384]{1,0:T(8,128)(2,1)S(1)}, bf16[2880,384]{1,0:T(8,128)(2,1)}) custom-call(bf16[2880,384]{1,0:T(8,128)(2,1)S(1)} %get-tuple-element.48.refs_0_.refs_4_.grad, bf16[2880,384]{1,0:T(8,128)(2,1)S(1)} %bitcast.6), custom_call_target="tpu_custom_call" | custom-call | tf_op jit(solution)/shard_map/moment/pallas_call | solution.py:75
  18.8 0.5 %collective-permute-done.6 = bf16[16,2880]{1,0:T(8,128)(2,1)S(1)} collective-permute-done((bf16[16,2880]{1,0:T(8,128)(2,1)S(1)}, bf16[16,2880]{1,0:T(8,128)(2,1)S(1)}, u32[]{:S(2)}, u32[]{:S(2)}) %collective-permute-start.6) | collective-permute-done | bytes 92192 | tf_op jit(solution)/shard_map/ppermute | solution.py:248
  19.4 1.5 %collective-permute-start.7 = (bf16[8,2880]{1,0:T(8,128)(2,1)S(1)}, bf16[8,2880]{1,0:T(8,128)(2,1)S(1)}, u32[]{:S(2)}, u32[]{:S(2)}) collective-permute-start(bf16[8,2880]{1,0:T(8,128)(2,1)S(1)} %slice.24), channel_id=1, source_target_pairs={{0,3},{1,4},{2,7},{3,0},{4,1},{5,6},{6,5},{7,2},{8,13},{9,10},{10,... | collective-permute-start | bytes 138248 | tf_op jit(solution)/shard_map/ppermute | solution.py:248
  20.9 0.0 collective-permute-done.5
  20.9 0.0 copy-done.1
  20.9 1.6 %scale.1 = (bf16[64,384]{1,0:T(8,128)(2,1)S(1)}, f32[64,384]{1,0:T(8,128)}) custom-call(bf16[64,2880]{1,0:T(8,128)(2,1)S(1)} %constant_dynamic-update-slice_fusion.basis, bf16[2880,384]{1,0:T(8,128)(2,1)S(1)} %get-tuple-element.48.refs_0_.refs_4_.grad, bf16[2880,384]{1,0:T(8,128)(2,1)S(1)} %get-tuple-element.64.moment, ...), custom_call_target="tpu_custom_call" | custom-call | tf_op jit(solution)/shard_map/scale/pallas_call | solution.py:198
  22.5 0.4 %collective-permute-done.7 = bf16[8,2880]{1,0:T(8,128)(2,1)S(1)} collective-permute-done((bf16[8,2880]{1,0:T(8,128)(2,1)S(1)}, bf16[8,2880]{1,0:T(8,128)(2,1)S(1)}, u32[]{:S(2)}, u32[]{:S(2)}) %collective-permute-start.7) | collective-permute-done | bytes 46112 | tf_op jit(solution)/shard_map/ppermute | solution.py:248
  23.0 3.1 %collective-permute-start.8 = (bf16[4,2880]{1,0:T(4,128)(2,1)S(1)}, bf16[4,2880]{1,0:T(4,128)(2,1)S(1)}, u32[]{:S(2)}, u32[]{:S(2)}) collective-permute-start(bf16[4,2880]{1,0:T(4,128)(2,1)S(1)} %slice.25), channel_id=1, source_target_pairs={{0,9},{1,8},{2,11},{3,10},{4,13},{5,12},{6,15},{7,14},{8,1},{9,0},... | collective-permute-start | bytes 69128 | tf_op jit(solution)/shard_map/ppermute | solution.py:248
  26.1 1.7 %update.1 = bf16[2880,384]{1,0:T(8,128)(2,1)} custom-call(bf16[64,2880]{1,0:T(8,128)(2,1)S(1)} %constant_dynamic-update-slice_fusion.basis, bf16[64,384]{1,0:T(8,128)(2,1)S(1)} %get-tuple-element.70.scaled), custom_call_target="tpu_custom_call" | custom-call | tf_op jit(solution)/shard_map/update/pallas_call | solution.py:226
  27.8 0.0 collective-permute-done.8.come
  27.8 0.7 %normalise.1 = f32[4,2880]{1,0:T(4,128)} custom-call(f32[4,2880]{1,0:T(4,128)S(1)} %slice.21.kept, bf16[4,2880]{1,0:T(4,128)(2,1)S(1)} %collective-permute-done.8.come), custom_call_target="tpu_custom_call" | custom-call | tf_op jit(solution)/shard_map/normalise/pallas_call | solution.py:147
  (9 shorter events, 0.1 us)
Async XLA Ops:
  0.6 5.3 %collective-permute-start = (bf16[4,2880]{1,0:T(4,128)(2,1)}, bf16[4,2880]{1,0:T(4,128)(2,1)S(1)}, u32[]{:S(2)}, u32[]{:S(2)}) collective-permute-start(bf16[4,2880]{1,0:T(4,128)(2,1)} %refs_1_.1), channel_id=1, source_target_pairs={{0,9},{1,8},{2,11},{3,10},{4,13},{5,12},{6,15},{7,14},{8,1},{9,0},... | collective-permute-start | bytes 69128 | tf_op jit(solution)/shard_map/ppermute | solution.py:248
  6.0 5.8 %collective-permute-start.3 = (bf16[2880,384]{1,0:T(8,128)(2,1)S(1)}, bf16[2880,384]{1,0:T(8,128)(2,1)S(1)}, u32[]{:S(2)}, u32[]{:S(2)}) collective-permute-start(bf16[2880,384]{1,0:T(8,128)(2,1)S(1)} %get-tuple-element.48.refs_0_.refs_4_.grad), channel_id=1, source_target_pairs={{0,1},{1,0},{2,3},{3,2},{4,5},{5,4},{6,7},{7,6},{8,9},{9,8},{10,11... | collective-permute-start | bytes 6635528 | tf_op jit(solution)/shard_map/ppermute | solution.py:251
  6.6 3.6 %collective-permute-start.1 = (bf16[8,2880]{1,0:T(8,128)(2,1)S(1)}, bf16[8,2880]{1,0:T(8,128)(2,1)S(1)}, u32[]{:S(2)}, u32[]{:S(2)}) collective-permute-start(bf16[8,2880]{1,0:T(8,128)(2,1)S(1)} %pad_maximum_fusion.refs_0_), channel_id=1, source_target_pairs={{0,3},{1,4},{2,7},{3,0},{4,1},{5,6},{6,5},{7,2},{8,13},{9,10},{10,... | collective-permute-start | bytes 138248 | tf_op jit(solution)/shard_map/ppermute | solution.py:248
  8.2 3.6 %collective-permute-start.2 = (bf16[8,2880]{1,0:T(8,128)(2,1)S(1)}, bf16[8,2880]{1,0:T(8,128)(2,1)S(1)}, u32[]{:S(2)}, u32[]{:S(2)}) collective-permute-start(bf16[8,2880]{1,0:T(8,128)(2,1)S(1)} %pad_maximum_fusion.refs_0_), channel_id=1, source_target_pairs={{0,5},{1,2},{2,1},{3,6},{4,7},{5,0},{6,3},{7,4},{8,11},{9,12},{10,... | collective-permute-start | bytes 138248 | tf_op jit(solution)/shard_map/ppermute | solution.py:248
  10.2 3.5 %collective-permute-start.4 = (bf16[8,2880]{1,0:T(8,128)(2,1)S(1)}, bf16[8,2880]{1,0:T(8,128)(2,1)S(1)}, u32[]{:S(2)}, u32[]{:S(2)}) collective-permute-start(bf16[8,2880]{1,0:T(8,128)(2,1)S(1)} %collective-permute-done.1.refs_1_), channel_id=1, source_target_pairs={{0,5},{1,2},{2,1},{3,6},{4,7},{5,0},{6,3},{7,4},{8,11},{9,12},{10,... | collective-permute-start | bytes 138248 | tf_op jit(solution)/shard_map/ppermute | solution.py:248
  13.7 3.4 %copy-start = (bf16[384,2880]{0,1:T(8,128)(2,1)S(1)}, bf16[384,2880]{0,1:T(8,128)(2,1)}, u32[]{:S(2)}) copy-start(bf16[384,2880]{0,1:T(8,128)(2,1)} %param.5) | copy-start | bytes 6635524
  15.2 4.1 %collective-permute-start.6 = (bf16[16,2880]{1,0:T(8,128)(2,1)S(1)}, bf16[16,2880]{1,0:T(8,128)(2,1)S(1)}, u32[]{:S(2)}, u32[]{:S(2)}) collective-permute-start(bf16[16,2880]{1,0:T(8,128)(2,1)S(1)} %get-tuple-element.57), channel_id=1, source_target_pairs={{0,5},{1,2},{2,1},{3,6},{4,7},{5,0},{6,3},{7,4},{8,11},{9,12},{10,... | collective-permute-start | bytes 276488 | tf_op jit(solution)/shard_map/ppermute | solution.py:248
  17.1 3.9 %collective-permute-start.5 = (bf16[32,2880]{1,0:T(8,128)(2,1)S(1)}, bf16[32,2880]{1,0:T(8,128)(2,1)S(1)}, u32[]{:S(2)}, u32[]{:S(2)}) collective-permute-start(bf16[32,2880]{1,0:T(8,128)(2,1)S(1)} %get-tuple-element.55), channel_id=1, source_target_pairs={{0,1},{1,0},{2,3},{3,2},{4,5},{5,4},{6,7},{7,6},{8,9},{9,8},{10,11... | collective-permute-start | bytes 552968 | tf_op jit(solution)/shard_map/ppermute | solution.py:251
  17.1 3.8 %copy-start.1 = (f32[384,64]{0,1:T(8,128)S(1)}, f32[384,64]{0,1:T(8,128)}, u32[]{:S(2)}) copy-start(f32[384,64]{0,1:T(8,128)} %param.6) | copy-start | bytes 294916
  19.4 3.6 %collective-permute-start.7 = (bf16[8,2880]{1,0:T(8,128)(2,1)S(1)}, bf16[8,2880]{1,0:T(8,128)(2,1)S(1)}, u32[]{:S(2)}, u32[]{:S(2)}) collective-permute-start(bf16[8,2880]{1,0:T(8,128)(2,1)S(1)} %slice.24), channel_id=1, source_target_pairs={{0,3},{1,4},{2,7},{3,0},{4,1},{5,6},{6,5},{7,2},{8,13},{9,10},{10,... | collective-permute-start | bytes 138248 | tf_op jit(solution)/shard_map/ppermute | solution.py:248
  23.0 4.8 %collective-permute-start.8 = (bf16[4,2880]{1,0:T(4,128)(2,1)S(1)}, bf16[4,2880]{1,0:T(4,128)(2,1)S(1)}, u32[]{:S(2)}, u32[]{:S(2)}) collective-permute-start(bf16[4,2880]{1,0:T(4,128)(2,1)S(1)} %slice.25), channel_id=1, source_target_pairs={{0,9},{1,8},{2,11},{3,10},{4,13},{5,12},{6,15},{7,14},{8,1},{9,0},... | collective-permute-start | bytes 69128 | tf_op jit(solution)/shard_map/ppermute | solution.py:248
